TPU v7x, 32 devices: a whole 2x2x4 slice. The times are simulated.
32 devices in a mesh: acq: 8 (over y, x, core), strip: 4 (over z).
Axes of the slice: x: 2, y: 2, z: 4, core: 2. Of those that a mesh axis runs over, the one named last changes fastest.
Arguments:
- raw_echoes: float32 [8, 2, 1024, 2048], P('acq', None, 'strip'), may hold values from -6 to 6
- range_filter: float32 [2, 2048], replicated, may hold values from -5 to 5
- azimuth_filter: float32 [2, 1024, 2048], P(None, None, 'strip'), may hold values from -5 to 5
- pair_mask: int32 [8, 2], P('acq'), may hold values 0 or 1
- inversion: float32 [8, 8, 2], P(None, 'acq'), may hold values from -2 to 2
Outputs:
- epoch_gradients: float32 [8, 2, 512, 256], P('acq', None, 'strip')
Inputs may be any that keep to these rules, and one draw needn't show every extreme that they name: `pair_mask`: 1 where the pair is in the network, 0 where it is not.
All inputs are finite; a program needn't handle non-finite values. No bound on the sum of `pair_mask` on one device may be relied on, other than what follows from the above.
Results may differ from a plain program's by a relative error of at most 0.00014.
Values sent between devices are 32-bit elements; how exact they have to be, the bound alone decides.
No kernel may reach another device: no remote copies, remote signals or barrier semaphores. Data moves between devices by JAX's collectives and lax.ppermute only.
A program may use at most 128 MiB of HBM per device.

v0:
```python
import math

import jax
import jax.numpy as jnp
from jax import lax
from jax.sharding import PartitionSpec as P

LOOK = 4


def shifted(block, axis, distance):
    devices = range(lax.axis_size(axis))
    route = [(i - distance, i) for i in devices if i - distance in devices]
    return lax.ppermute(block, axis, route)


def split_length(length):
    first = 1
    for factor in range(1, length + 1):
        if length % factor == 0 and factor * factor <= length:
            first = factor
    return (first, length // first)


def block_table(size, sign):
    index = jnp.arange(size, dtype=jnp.int32)
    product = index[:, None] * index[None, :] % size
    angle = sign * 2.0 * math.pi / size * product.astype(jnp.float32)
    cosine = jnp.cos(angle)
    sine = jnp.sin(angle)
    from_real = jnp.stack([cosine, sine], axis=1)
    from_imag = jnp.stack([-sine, cosine], axis=1)
    return jnp.stack([from_real, from_imag])


def twiddle(first, second, sign):
    row_index = jnp.arange(first, dtype=jnp.int32)[:, None]
    col_index = jnp.arange(second, dtype=jnp.int32)[None, :]
    product = row_index * col_index % (first * second)
    angle = sign * 2.0 * math.pi / (first * second) * product.astype(jnp.float32)
    return (jnp.cos(angle), jnp.sin(angle))


def complex_times(left_real, left_imag, right_real, right_imag):
    return (
        left_real * right_real - left_imag * right_imag,
        left_real * right_imag + left_imag * right_real,
    )


def turn_stacked(field, turn_cos, turn_sin):
    real_part, imag_part = complex_times(field[0], field[1], turn_cos, turn_sin)
    return jnp.stack([real_part, imag_part])


def dft_last(field, sign):
    length = field.shape[-1]
    first, second = split_length(length)
    rows = field.shape[1]
    field = field.reshape(2, rows, first, second)
    field = jnp.einsum(
        "cnpq,cpdk->dnkq", field, block_table(first, sign), precision=lax.Precision.HIGHEST
    )
    turn_cos, turn_sin = twiddle(first, second, sign)
    field = turn_stacked(field, turn_cos, turn_sin)
    field = jnp.einsum(
        "cnkq,cqdm->dnmk", field, block_table(second, sign), precision=lax.Precision.HIGHEST
    )
    return field.reshape(2, rows, length)


def dft_rows(field, sign):
    length = field.shape[1]
    columns = field.shape[2]
    first, second = split_length(length)
    field = field.reshape(2, first, second, columns)
    field = jnp.einsum(
        "cpqn,cpdk->dkqn", field, block_table(first, sign), precision=lax.Precision.HIGHEST
    )
    turn_cos, turn_sin = twiddle(first, second, sign)
    field = turn_stacked(field, turn_cos[:, :, None], turn_sin[:, :, None])
    field = jnp.einsum(
        "ckqn,cqdm->dmkn", field, block_table(second, sign), precision=lax.Precision.HIGHEST
    )
    return field.reshape(2, length, columns)


def azimuth_forward(received):
    return dft_rows(received[:, :, 0, :], -1.0)[:, :, None, :]


def multilook(field):
    rows, cols = field.shape
    summed = field.reshape(rows // LOOK, LOOK, cols // LOOK, LOOK).sum(axis=(1, 3)) / LOOK
    return summed.T


def per_device(raw_echoes, range_filter, azimuth_filter, pair_mask, inversion):
    pulses = raw_echoes.shape[2]
    samples = raw_echoes.shape[3]
    spectrum = dft_last(raw_echoes[0], -1.0)
    spectrum = turn_stacked(spectrum, range_filter[0][None, :], range_filter[1][None, :])
    pressed = dft_last(spectrum, 1.0) / samples
    strips = lax.axis_size("strip")
    strip_width = samples // strips
    stacked = pressed.reshape(2, pulses, strips, strip_width)
    turned = azimuth_forward(
        lax.all_to_all(stacked, "strip", split_axis=2, concat_axis=1, tiled=True)
    )
    filtered = turn_stacked(turned[:, :, 0, :], azimuth_filter[0], azimuth_filter[1])
    image = dft_rows(filtered, 1.0)
    length = image.shape[1]
    scene = image / length
    prior_first = shifted(scene, "acq", 1)
    prior_second = shifted(scene, "acq", 2)

    def looked_pair(earlier):
        product_real = earlier[0] * scene[0] + earlier[1] * scene[1]
        product_imag = earlier[1] * scene[0] - earlier[0] * scene[1]
        return jnp.stack([multilook(product_real), multilook(product_imag)])

    looked = jnp.stack([looked_pair(prior_first), looked_pair(prior_second)])
    following = shifted(looked[:, :, 0, :], "strip", -1)
    extended = jnp.concatenate([looked, following[:, :, None, :]], axis=2)
    range_slope = (
        extended[:, 1, 1:, :] * extended[:, 0, :-1, :]
        - extended[:, 0, 1:, :] * extended[:, 1, :-1, :]
    )
    azimuth_slope = (
        looked[:, 1, :, 1:] * looked[:, 0, :, :-1] - looked[:, 0, :, 1:] * looked[:, 1, :, :-1]
    )
    azimuth_slope = jnp.pad(azimuth_slope, ((0, 0), (0, 0), (0, 1)))
    slopes = jnp.stack([azimuth_slope, range_slope], axis=1)
    epoch_index = lax.axis_index("acq")
    lags = jnp.array([1, 2], dtype=jnp.int32)
    usable = pair_mask[0].astype(jnp.float32) * (epoch_index >= lags).astype(jnp.float32)
    weights = inversion[:, 0, :] * usable[None, :]
    return lax.psum_scatter(
        jnp.einsum("cl,ldra->cdra", weights, slopes, precision=lax.Precision.HIGHEST),
        "acq",
        scatter_dimension=0,
        tiled=True,
    )


def solution(mesh):
    return jax.shard_map(
        per_device,
        mesh=mesh,
        in_specs=(
            P("acq", None, "strip", None),
            P(),
            P(None, None, "strip"),
            P("acq", None),
            P(None, "acq", None),
        ),
        out_specs=P("acq", None, "strip", None),
        check_vma=False,
    )
```

profile of v0, /device:TPU:0, one launch (start us, length us, event | category | flops | bytes accessed | tf_op | source)
XLA Modules:
  0.0 773.0 jit_solution(11800765396202063409)
XLA Ops:
  7.8 5.4 copy.58
  13.1 8.3 %fusion.25 = f32[2,256,32,64]{1,2,3,0:T(8,128)S(1)} fusion(f32[2,256,32,64]{1,3,2,0:T(8,128)} %bitcast.211, f32[1,32,2,32]{1,3,0,2:T(8,128)S(1)} %get-tuple-element.38, f32[1,32,2,32]{1,3,0,2:T(8,128)S(1)} %get-tuple-element.37), kind=kOutput, calls=%fused_computation.33 | convolution fusion | flops 805310464 | bytes 8404992 | tf_op jit(solution)/shard_map/cnpq,cpdk->dnkq/dot_general | solution.py:61
  23.0 5.9 fusion.28
  33.5 5.0 multiply_subtract_fusion.3
  44.0 5.9 fusion.12
  54.7 6.3 all-to-all-start
  61.2 93.2 %all-to-all-done = f32[2,256,4,512]{1,3,0,2:T(8,128)} async-done(((f32[2,256,4,512]{1,3,0,2:T(8,128)}), f32[2,256,4,512]{1,3,0,2:T(8,128)}, u32[]{:S(2)}, u32[]{:S(2)}) %all-to-all-start) | async-done | bytes 4194336 | tf_op jit(solution)/shard_map/all_to_all | solution.py:108
  154.5 5.5 copy.74
  159.9 8.3 %fusion.31 = f32[2,32,32,512]{3,1,2,0:T(8,128)S(1)} fusion(f32[2,32,32,512]{3,2,1,0:T(8,128)} %bitcast.213, f32[1,32,2,32]{1,3,0,2:T(8,128)S(1)} %get-tuple-element.38, f32[1,32,2,32]{1,3,0,2:T(8,128)S(1)} %get-tuple-element.37), kind=kOutput, calls=%fused_computation.35 | convolution fusion | flops 805310464 | bytes 8404992 | tf_op jit(solution)/shard_map/cpqn,cpdk->dkqn/dot_general | solution.py:77
  169.6 6.0 fusion.34
  188.7 6.2 bitcast_multiply_fusion
  194.9 4.4 copy.84
  202.6 4.1 collective-permute-start.1
  212.4 83.7 %collective-permute-done.1 = f32[2,1024,512]{2,1,0:T(8,128)} collective-permute-done((f32[2,1024,512]{2,1,0:T(8,128)}, f32[2,1024,512]{2,1,0:T(8,128)}, u32[]{:S(2)}, u32[]{:S(2)}) %collective-permute-start.1) | collective-permute-done | bytes 4194336 | tf_op jit(solution)/shard_map/ppermute | solution.py:14
  296.0 7.8 %fusion.45 = (f32[1,1024,512]{2,1,0:T(8,128)}, f32[1,1024,512]{2,1,0:T(8,128)}, f32[1,1024,512]{2,1,0:T(8,128)}, f32[1,1024,512]{2,1,0:T(8,128)S(1)}) fusion(f32[1,32,32,512]{3,2,1,0:T(8,128)S(1)} %copy.86, f32[1,32,32,512]{3,2,1,0:T(8,128)S(1)} %copy.85, f32[2,1024,512]{2,1,0:T(8,128)} %collective-permute-done.1, f32[2,1024,512]{2,1,0:T(8,128)} %collective-permute-done), kind=kLoop, calls=%fused_computation.45 | loop fusion | flops 6291456 | bytes 20971520 | tf_op jit(solution)/shard_map/add | solution.py:118
  303.8 71.6 %sub.72 = f32[256,4,128,4]{3,2,1,0:T(8,128)} reshape(f32[1,1024,512]{2,1,0:T(8,128)} %get-tuple-element.8) | data formatting | bytes 4194304 | tf_op jit(solution)/shard_map/sub | solution.py:119
  375.4 20.8 %reduce_sum.39 = f32[256,128]{1,0:T(8,128)S(1)} reduce(f32[256,4,128,4]{3,2,1,0:T(8,128)} %sub.72, f32[]{:T(128)} %constant.98.clone.1), dimensions={1,3}, to_apply=%region_3.4 | reduce | flops 491520 | bytes 2228228 | tf_op jit(solution)/shard_map/reduce_sum | solution.py:94
  396.3 71.4 %add.244 = f32[256,4,128,4]{3,2,1,0:T(8,128)} reshape(f32[1,1024,512]{2,1,0:T(8,128)} %get-tuple-element.7) | data formatting | bytes 4194304 | tf_op jit(solution)/shard_map/add | solution.py:118
  467.7 20.8 %reduce_sum.38 = f32[256,128]{1,0:T(8,128)S(1)} reduce(f32[256,4,128,4]{3,2,1,0:T(8,128)} %add.244, f32[]{:T(128)} %constant.98.clone.1), dimensions={1,3}, to_apply=%region_2.3 | reduce | flops 491520 | bytes 2228228 | tf_op jit(solution)/shard_map/reduce_sum | solution.py:94
  488.8 71.4 %sub.70 = f32[256,4,128,4]{3,2,1,0:T(8,128)} reshape(f32[1,1024,512]{2,1,0:T(8,128)} %get-tuple-element.23) | data formatting | bytes 4194304 | tf_op jit(solution)/shard_map/sub | solution.py:119
  560.3 20.8 %reduce_sum.37 = f32[256,128]{1,0:T(8,128)S(1)} reduce(f32[256,4,128,4]{3,2,1,0:T(8,128)} %sub.70, f32[]{:T(128)} %constant.98.clone.1), dimensions={1,3}, to_apply=%region_1.2 | reduce | flops 491520 | bytes 2228228 | tf_op jit(solution)/shard_map/reduce_sum | solution.py:94
  581.2 70.6 %add.242 = f32[256,4,128,4]{3,2,1,0:T(8,128)} reshape(f32[1,1024,512]{2,1,0:T(8,128)S(1)} %get-tuple-element.24) | data formatting | bytes 4194304 | tf_op jit(solution)/shard_map/add | solution.py:118
  651.8 20.8 %reduce_sum.36 = f32[256,128]{1,0:T(8,128)S(1)} reduce(f32[256,4,128,4]{3,2,1,0:T(8,128)} %add.242, f32[]{:T(128)} %constant.98.clone.1), dimensions={1,3}, to_apply=%region_0.1 | reduce | flops 491520 | bytes 2228228 | tf_op jit(solution)/shard_map/reduce_sum | solution.py:94
  684.6 81.3 %reduce-scatter.2.cloned.1.call-done = f32[1,2,128,256]{3,2,1,0:T(8,128)} async-done(((f32[8,2,128,256]{3,2,1,0:T(8,128)}), f32[1,2,128,256]{3,2,1,0:T(8,128)}) %reduce-scatter.2.cloned.1.call-update) | async-done | bytes 262160 | tf_op jit(solution)/shard_map/reduce_scatter | solution.py:138
  (84 shorter events, 53.6 us)
Async XLA Ops:
  30.6 2.6 copy-start.2
  54.7 99.7 %all-to-all-start = ((f32[2,256,4,512]{1,3,0,2:T(8,128)}), f32[2,256,4,512]{1,3,0,2:T(8,128)}, u32[]{:S(2)}, u32[]{:S(2)}) async-start(f32[2,256,4,512]{1,3,0,2:T(8,128)} %copy.73), calls=%async_computation | async-start | bytes 8388608 | tf_op jit(solution)/shard_map/all_to_all | solution.py:108
  61.1 704.8 %reduce-scatter.2.cloned.1.call-start = ((), (), s32[]{:S(2)}) async-start(), calls=%async_computation.2 | async-start | bytes 2359296 | tf_op jit(solution)/shard_map/reduce_scatter | solution.py:138
  177.4 2.2 copy-start.1
  194.9 4.4 copy-start
  194.9 11.7 %copy-start.5 = (s32[1,2]{1,0:T(1,128)S(1)}, s32[1,2]{1,0:T(1,128)}, u32[]{:S(2)}) copy-start(s32[1,2]{1,0:T(1,128)} %param.9) | copy-start | bytes 28
  194.9 11.7 %copy-start.6 = (s32[2]{0:T(128)S(1)}, s32[2]{0:T(128)}, u32[]{:S(2)}) copy-start(s32[2]{0:T(128)} %constant.119.clone) | copy-start | bytes 28
  199.3 13.0 %collective-permute-start = (f32[2,1024,512]{2,1,0:T(8,128)}, f32[2,1024,512]{2,1,0:T(8,128)}, u32[]{:S(2)}, u32[]{:S(2)}) collective-permute-start(f32[2,1024,512]{2,1,0:T(8,128)} %bitcast.65), channel_id=1, source_target_pairs={{0,4},{4,8},{8,12},{12,16},{16,20},{20,24},{24,28},{1,5},{5,9},{9,... | collective-permute-start | bytes 12582920 | tf_op jit(solution)/shard_map/ppermute | solution.py:14
  202.6 93.5 %collective-permute-start.1 = (f32[2,1024,512]{2,1,0:T(8,128)}, f32[2,1024,512]{2,1,0:T(8,128)}, u32[]{:S(2)}, u32[]{:S(2)}) collective-permute-start(f32[2,1024,512]{2,1,0:T(8,128)} %bitcast.65), channel_id=1, source_target_pairs={{0,8},{4,12},{8,16},{12,20},{16,24},{20,28},{1,9},{5,13},{9,17},{1... | collective-permute-start | bytes 12582920 | tf_op jit(solution)/shard_map/ppermute | solution.py:14
  672.5 7.7 copy-start.3
  672.5 7.7 copy-start.4
  674.2 5.5 collective-permute-start.2
Sparse Core Ops, SparseCore 0:
  684.7 81.0 reduce-scatter.1
where the time goes:
time: 778 us; the launch traced here: 773 us
  local copies, waits for them, and re-layouts  325 us (42%)
  waiting for transfers between devices  262 us (34%)
  other arithmetic  106 us (14%)
  matrix products  50.7 us (7%)
  starting transfers between devices  15.2 us (2%)
  between operations  14.2 us (2%)
    sub x2, local copies, waits for them, and re-layouts, looked_pair(): product_imag = earlier[1] * scene[0] - earlier[0] * scene[1]  143 us
    add x2, local copies, waits for them, and re-layouts, looked_pair(): product_real = earlier[0] * scene[0] + earlier[1] * scene[1]  142 us
    all_to_all x1, waiting for transfers between devices, per_device(): lax.all_to_all(stacked, 'strip', split_axis=2, concat_axis=1, tiled=True)  93.2 us
    ppermute x3, waiting for transfers between devices, shifted(): return lax.ppermute(block, axis, route)  87.5 us
    reduce_sum x4, other arithmetic, multilook(): field.reshape(rows // LOOK, LOOK, cols // LOOK, LOOK).sum(axis=(1, 3))  83.1 us
    reduce_scatter x1, waiting for transfers between devices, per_device(): lax.psum_scatter(jnp.einsum('cl,ldra->cdra', weights, slopes, precision=l...  81.3 us
  transfers between devices with their start and end apart: 5, of which 4 were waited for; matrix products, arithmetic and copies ran while one was open for 1% of the time, Pallas kernels for 0%

commit v1 on v0

v1 whole, which is shorter than its diff:
```python
import functools
import math

import jax
import jax.numpy as jnp
import ml_dtypes
import numpy as np
from jax import lax
from jax.experimental import pallas as pl
from jax.experimental.pallas import tpu as pltpu
from jax.sharding import PartitionSpec as P

LOOK = 4
RADIX = 8
ROWS = 8
VMEM_BYTES = 48 * 1024 * 1024
OWNERS = ("strip", "acq")


def add(left, right):
    return (left[0] + right[0], left[1] + right[1])


def sub(left, right):
    return (left[0] - right[0], left[1] - right[1])


def turn(value, sign):
    if sign > 0:
        return (-value[1], value[0])
    return (value[1], -value[0])


def dft4(x0, x1, x2, x3, sign):
    a, b = add(x0, x2), sub(x0, x2)
    c, d = add(x1, x3), turn(sub(x1, x3), sign)
    return [add(a, c), add(b, d), sub(a, c), sub(b, d)]


def dft8(x, sign):
    even = dft4(x[0], x[2], x[4], x[6], sign)
    odd = dft4(x[1], x[3], x[5], x[7], sign)
    half = math.sqrt(0.5)
    o1, o3 = odd[1], odd[3]
    t1 = add(o1, turn(o1, sign))
    t3 = sub(turn(o3, sign), o3)
    odd = [
        odd[0],
        (t1[0] * half, t1[1] * half),
        turn(odd[2], sign),
        (t3[0] * half, t3[1] * half),
    ]
    return [add(e, o) for e, o in zip(even, odd)] + [sub(e, o) for e, o in zip(even, odd)]


def two_parts(value):
    high = value.astype(jnp.bfloat16)
    low = (value - high.astype(jnp.float32)).astype(jnp.bfloat16)
    return high, low


def three_products(left_high, left_low, right_high, right_low, contract):
    def product(left, right):
        return lax.dot_general(
            left, right, (contract, ((), ())), preferred_element_type=jnp.float32
        )

    return (
        product(left_high, right_high)
        + product(left_high, right_low)
        + product(left_low, right_high)
    )


def host_parts(table):
    table = np.asarray(table, np.float64)
    high = table.astype(np.float32).astype(ml_dtypes.bfloat16)
    low = (table - high.astype(np.float64)).astype(np.float32).astype(ml_dtypes.bfloat16)
    return high, low


def unit(exponent, size, sign):
    angle = sign * 2.0 * np.pi / size * (exponent % size)
    return np.cos(angle), np.sin(angle)


def real_form(cosine, sine):
    top = np.concatenate([cosine, sine], axis=-1)
    bottom = np.concatenate([-sine, cosine], axis=-1)
    return np.concatenate([top, bottom], axis=-2)


class Plan:
    def __init__(self, strips, epochs, pulses, samples):
        self.strips, self.epochs = strips, epochs
        self.pulses, self.samples = pulses, samples
        self.azimuth = pulses * strips
        self.base = samples // RADIX
        self.owned = samples // (strips * epochs)
        self.parts = 2 if self.owned % (2 * LOOK * ROWS) == 0 else 1
        self.rows = self.owned // self.parts
        self.looks = self.rows // LOOK
        self.planes = self.looks % ROWS == 0
        self.blocks = self.base // self.owned
        self.lanes = self.azimuth // RADIX
        self.azimuth_looks = self.azimuth // LOOK

    def tile_shift(self, part, block, tile):
        start = block * self.owned + part * self.rows
        if self.planes:
            plane, look = divmod(tile * ROWS, self.looks)
            return start + LOOK * look + plane
        return start + tile * ROWS

    def tile_stride(self):
        return LOOK if self.planes else 1


def lag_vectors(range_filter, plan):
    base, samples = plan.base, plan.samples
    field = range_filter.reshape(2, base, RADIX).transpose(2, 0, 1).reshape(RADIX, 2 * base)
    index = np.arange(base)
    table = real_form(*unit(index[:, None] * index[None, :], base, -1.0)) / samples
    sums = jnp.dot(
        field, jnp.asarray(table.astype(np.float32)), precision=lax.Precision.HIGHEST
    ).reshape(RADIX, 2, base)
    lag = np.arange(2 * base)
    lag = np.where(lag <= base, lag, lag - 2 * base)
    turn_cos, turn_sin = unit(lag[None, :] * np.arange(RADIX)[:, None], samples, -1.0)
    turn_cos = jnp.asarray(turn_cos.astype(np.float32))
    turn_sin = jnp.asarray(turn_sin.astype(np.float32))
    real = jnp.concatenate([sums[:, 0], sums[:, 0]], axis=1)
    imag = jnp.concatenate([sums[:, 1], sums[:, 1]], axis=1)
    return jnp.stack(
        [real * turn_cos - imag * turn_sin, real * turn_sin + imag * turn_cos], axis=1
    )


def compress_kernel(plan, part, lag_ref, raw_ref, out_ref, t_high, t_low, y_high, y_low, z_ref):
    base, blocks = plan.base, plan.blocks
    tiles = plan.rows // ROWS
    chunk = blocks * plan.rows

    def build(d, carry):
        spread = [
            pltpu.roll(
                jnp.broadcast_to(lag_ref[d, c : c + 1, :], (ROWS, 2 * base)),
                0,
                1,
                stride=plan.tile_stride(),
                stride_axis=0,
            )
            for c in range(2)
        ]
        for pair in range(blocks * tiles // 2):
            real, imag = [], []
            for at in (2 * pair, 2 * pair + 1):
                shift = plan.tile_shift(part, at // tiles, at % tiles)
                real.append(pltpu.roll(spread[0], shift, 1)[:, :base])
                imag.append(pltpu.roll(spread[1], shift, 1)[:, :base])
            real_high, real_low = two_parts(jnp.concatenate(real, axis=0))
            imag_high, imag_low = two_parts(jnp.concatenate(imag, axis=0))
            top = pl.ds(pair * 2 * ROWS, 2 * ROWS)
            bottom = pl.ds(chunk + pair * 2 * ROWS, 2 * ROWS)
            t_high[d, top, :base] = real_high
            t_high[d, top, base:] = -imag_high
            t_high[d, bottom, :base] = imag_high
            t_high[d, bottom, base:] = real_high
            t_low[d, top, :base] = real_low
            t_low[d, top, base:] = -imag_low
            t_low[d, bottom, :base] = imag_low
            t_low[d, bottom, base:] = real_low
        return carry

    lax.fori_loop(0, RADIX, build, 0)

    def spread_pulses(at, carry):
        rows = pl.ds(at * 2 * ROWS, 2 * ROWS)
        x = [
            tuple(raw_ref[c, rows, a * base : (a + 1) * base] for c in range(2))
            for a in range(RADIX)
        ]
        for d, value in enumerate(dft8(x, -1.0)):
            for c in range(2):
                high, low = two_parts(value[c])
                y_high[d, rows, c * base : (c + 1) * base] = high
                y_low[d, rows, c * base : (c + 1) * base] = low
        return carry

    lax.fori_loop(0, plan.pulses // (2 * ROWS), spread_pulses, 0)

    def multiply(d, carry):
        z_ref[d] = three_products(t_high[d], t_low[d], y_high[d], y_low[d], ((1,), (1,)))
        return carry

    lax.fori_loop(0, RADIX, multiply, 0)

    for block in range(blocks):
        for tile in range(tiles):
            top = (block * tiles + tile) * ROWS
            z = [
                (z_ref[d, top : top + ROWS, :], z_ref[d, chunk + top : chunk + top + ROWS, :])
                for d in range(RADIX)
            ]
            for a, value in enumerate(dft8(z, 1.0)):
                for c in range(2):
                    out_ref[a * blocks + block, c, tile * ROWS : (tile + 1) * ROWS, :] = value[c]


def compress(plan, part, lags, raw):
    chunk = plan.blocks * plan.rows
    whole = pl.BlockSpec(memory_space=pltpu.VMEM)
    bytes_moved = 4 * (raw.size + raw.size // plan.parts)
    return pl.pallas_call(
        functools.partial(compress_kernel, plan, part),
        out_shape=jax.ShapeDtypeStruct(
            (plan.strips * plan.epochs, 2, plan.rows, plan.pulses), jnp.float32
        ),
        in_specs=[whole, whole],
        out_specs=whole,
        scratch_shapes=[
            pltpu.VMEM((RADIX, 2 * chunk, 2 * plan.base), jnp.bfloat16),
            pltpu.VMEM((RADIX, 2 * chunk, 2 * plan.base), jnp.bfloat16),
            pltpu.VMEM((RADIX, plan.pulses, 2 * plan.base), jnp.bfloat16),
            pltpu.VMEM((RADIX, plan.pulses, 2 * plan.base), jnp.bfloat16),
            pltpu.VMEM((RADIX, 2 * chunk, plan.pulses), jnp.float32),
        ],
        compiler_params=pltpu.CompilerParams(vmem_limit_bytes=VMEM_BYTES),
        cost_estimate=pl.CostEstimate(
            flops=6 * RADIX * 4 * chunk * plan.base * plan.pulses,
            bytes_accessed=bytes_moved,
            transcendentals=0,
        ),
        name="range_compress",
    )(lags, raw)


def focus_kernel(
    plan, field_ref, filter_ref, fh_ref, fl_ref, bh_ref, bl_ref, sum_ref, looked_ref,
    y_high, y_low, z_ref, scene_ref, product_ref,
):
    rows, lanes, epochs, looks = plan.rows, plan.lanes, plan.epochs, plan.looks
    per_block = field_ref.shape[-1] // lanes

    def forward(j, carry):
        for top in range(0, rows, ROWS):
            x = []
            for a in range(RADIX):
                strip, start = a // per_block, a % per_block * lanes
                x.append(
                    tuple(
                        field_ref[strip, j, c, top : top + ROWS, start : start + lanes]
                        for c in range(2)
                    )
                )
            for d, value in enumerate(dft8(x, -1.0)):
                for c in range(2):
                    at = pl.ds(pl.multiple_of(j * rows + top, ROWS), ROWS)
                    z_ref[d, at, c * lanes : (c + 1) * lanes] = value[c]
        return carry

    lax.fori_loop(0, epochs, forward, 0)

    def filtered(d, carry):
        y_high[...], y_low[...] = two_parts(z_ref[d])
        spectrum = three_products(
            y_high[...], y_low[...], fh_ref[d], fl_ref[d], ((1,), (0,))
        ).reshape(epochs, rows, 2 * lanes)
        real, imag = spectrum[:, :, :lanes], spectrum[:, :, lanes:]
        by_real, by_imag = filter_ref[0, d][None], filter_ref[1, d][None]
        real, imag = real * by_real - imag * by_imag, real * by_imag + imag * by_real
        for c, value in enumerate((real, imag)):
            high, low = two_parts(value.reshape(epochs * rows, lanes))
            y_high[:, c * lanes : (c + 1) * lanes] = high
            y_low[:, c * lanes : (c + 1) * lanes] = low
        z_ref[d] = three_products(
            y_high[...], y_low[...], bh_ref[d], bl_ref[d], ((1,), (0,))
        )
        return carry

    lax.fori_loop(0, RADIX, filtered, 0)

    scene_ref[0] = jnp.zeros_like(scene_ref[0])
    scene_ref[1] = jnp.zeros_like(scene_ref[1])

    def backward(j, carry):
        for top in range(0, rows, ROWS):
            at = pl.ds(pl.multiple_of(j * rows + top, ROWS), ROWS)
            z = [
                tuple(z_ref[d, at, c * lanes : (c + 1) * lanes] for c in range(2))
                for d in range(RADIX)
            ]
            for a, value in enumerate(dft8(z, 1.0)):
                for c in range(2):
                    scene_ref[j + 2, c, top : top + ROWS, a * lanes : (a + 1) * lanes] = value[c]
        return carry

    lax.fori_loop(0, epochs, backward, 0)

    def look(value):
        if plan.planes:
            return sum(value[q * looks : (q + 1) * looks] for q in range(1, LOOK)) + value[:looks]
        return value.reshape(looks, LOOK, value.shape[-1]).sum(axis=1)

    def interfere(j, carry):
        for a in range(RADIX):
            columns = pl.ds(a * lanes, lanes)
            later = (scene_ref[j + 2, 0, :, columns], scene_ref[j + 2, 1, :, columns])
            for lag in (1, 2):
                earlier = (
                    scene_ref[j + 2 - lag, 0, :, columns],
                    scene_ref[j + 2 - lag, 1, :, columns],
                )
                real = earlier[0] * later[0] + earlier[1] * later[1]
                imag = earlier[1] * later[0] - earlier[0] * later[1]
                product_ref[j, lag - 1, 0, :, columns] = look(real)
                product_ref[j, lag - 1, 1, :, columns] = look(imag)
        return carry

    lax.fori_loop(0, epochs, interfere, 0)

    total = epochs * 4 * looks
    products = product_ref[...].reshape(total, plan.azimuth)
    high, low = two_parts(products)
    weights = sum_ref[...]
    looked = jnp.dot(high, weights, preferred_element_type=jnp.float32) + jnp.dot(
        low, weights, preferred_element_type=jnp.float32
    )
    looked_ref[...] = looked.reshape(looked_ref.shape)


def focus(plan, field, spectrum):
    lanes = plan.lanes
    b = np.arange(lanes)[None, :, None]
    k = RADIX * np.arange(lanes)[None, None, :] + np.arange(RADIX)[:, None, None]
    cosine, sine = unit(b * k, plan.azimuth, -1.0)
    ahead = host_parts(real_form(cosine, sine))
    cosine, sine = cosine.swapaxes(1, 2), -sine.swapaxes(1, 2)
    back = host_parts(real_form(cosine, sine) / plan.azimuth)
    sums = (np.arange(plan.azimuth)[:, None] // LOOK == np.arange(plan.azimuth_looks)[None, :]) / LOOK
    sums = sums.astype(ml_dtypes.bfloat16)
    total = plan.epochs * plan.rows
    whole = pl.BlockSpec(memory_space=pltpu.VMEM)
    return pl.pallas_call(
        functools.partial(focus_kernel, plan),
        out_shape=jax.ShapeDtypeStruct(
            (plan.epochs, 2, 2, plan.looks, plan.azimuth_looks), jnp.float32
        ),
        in_specs=[whole] * 7,
        out_specs=whole,
        scratch_shapes=[
            pltpu.VMEM((total, 2 * lanes), jnp.bfloat16),
            pltpu.VMEM((total, 2 * lanes), jnp.bfloat16),
            pltpu.VMEM((RADIX, total, 2 * lanes), jnp.float32),
            pltpu.VMEM((plan.epochs + 2, 2, plan.rows, plan.azimuth), jnp.float32),
            pltpu.VMEM((plan.epochs, 2, 2, plan.looks, plan.azimuth), jnp.float32),
        ],
        compiler_params=pltpu.CompilerParams(vmem_limit_bytes=VMEM_BYTES),
        cost_estimate=pl.CostEstimate(
            flops=2 * 6 * RADIX * total * 4 * lanes * lanes,
            bytes_accessed=4 * field.size + 4 * 1024 * 1024,
            transcendentals=0,
        ),
        name="azimuth_focus",
    )(field, spectrum, *ahead, *back, sums)


def slope_kernel(plan, weight_ref, looked_ref, halo_ref, out_ref, slope_ref):
    epochs = plan.epochs
    columns = plan.azimuth_looks
    inner = lax.broadcasted_iota(jnp.int32, (plan.looks * plan.parts, columns), 1) < columns - 1

    def slopes(at, carry):
        j, lag = at // 2, at % 2
        real, imag = looked_ref[j, lag, 0], looked_ref[j, lag, 1]
        next_real = pltpu.roll(real, columns - 1, 1)
        next_imag = pltpu.roll(imag, columns - 1, 1)
        slope_ref[at, 0] = jnp.where(inner, next_imag * real - next_real * imag, 0.0)
        next_real = jnp.concatenate([real[1:], halo_ref[j, lag, 0]], axis=0)
        next_imag = jnp.concatenate([imag[1:], halo_ref[j, lag, 1]], axis=0)
        slope_ref[at, 1] = next_imag * real - next_real * imag
        return carry

    lax.fori_loop(0, 2 * epochs, slopes, 0)

    def epoch(e, carry):
        total = weight_ref[e, 0] * slope_ref[0]
        for at in range(1, 2 * epochs):
            total = total + weight_ref[e, at] * slope_ref[at]
        out_ref[e] = total
        return carry

    lax.fori_loop(0, epochs, epoch, 0)


def slopes_to_epochs(plan, weights, looked, halo):
    whole = pl.BlockSpec(memory_space=pltpu.VMEM)
    looks = plan.looks * plan.parts
    return pl.pallas_call(
        functools.partial(slope_kernel, plan),
        out_shape=jax.ShapeDtypeStruct(
            (plan.epochs, 2, looks, plan.azimuth_looks), jnp.float32
        ),
        in_specs=[pl.BlockSpec(memory_space=pltpu.SMEM), whole, whole],
        out_specs=whole,
        scratch_shapes=[
            pltpu.VMEM((2 * plan.epochs, 2, looks, plan.azimuth_looks), jnp.float32)
        ],
        compiler_params=pltpu.CompilerParams(vmem_limit_bytes=VMEM_BYTES),
        cost_estimate=pl.CostEstimate(
            flops=8 * looked.size * plan.epochs, bytes_accessed=5 * looked.size, transcendentals=0
        ),
        name="slopes_to_epochs",
    )(weights, looked, halo)


def own_filter(plan, azimuth_filter):
    start = lax.axis_index("acq") * plan.owned
    own = lax.dynamic_slice_in_dim(azimuth_filter, start, plan.owned, axis=2)
    own = own.reshape(2, plan.lanes, RADIX, plan.parts, plan.looks, LOOK)
    order = (3, 0, 2, 5, 4, 1) if plan.planes else (3, 0, 2, 4, 5, 1)
    return own.transpose(order).reshape(plan.parts, 2, RADIX, plan.rows, plan.lanes)


def exchange(plan, block):
    received = lax.all_to_all(block, OWNERS, split_axis=0, concat_axis=0, tiled=True)
    join = max(1, plan.lanes // plan.pulses)
    received = received.reshape(
        plan.strips // join, join, plan.epochs, 2, plan.rows, plan.pulses
    )
    if join > 1:
        received = received.transpose(0, 2, 3, 4, 1, 5)
    return received.reshape(
        plan.strips // join, plan.epochs, 2, plan.rows, join * plan.pulses
    )


def per_device(raw_echoes, range_filter, azimuth_filter, pair_mask, inversion):
    strips, epochs = lax.axis_size("strip"), lax.axis_size("acq")
    plan = Plan(strips, epochs, raw_echoes.shape[2], raw_echoes.shape[3])

    lags = jnp.array([1, 2], dtype=jnp.int32)
    usable = pair_mask[0].astype(jnp.float32) * (lax.axis_index("acq") >= lags).astype(jnp.float32)
    weights = lax.all_gather(inversion[:, 0, :] * usable[None, :], "acq", axis=1, tiled=False)
    weights = weights.reshape(epochs, 2 * epochs)

    vectors = lag_vectors(range_filter, plan)
    spectrum = own_filter(plan, azimuth_filter)
    looked = []
    fields = [
        exchange(plan, compress(plan, part, vectors, raw_echoes[0])) for part in range(plan.parts)
    ]
    for part in range(plan.parts):
        looked.append(focus(plan, fields[part], spectrum[part]))

    owners = strips * epochs
    device = [i % epochs * strips + i // epochs for i in range(owners)]
    halo = lax.ppermute(
        looked[0][:, :, :, :1, :],
        ("acq", "strip"),
        [(device[i], device[i - 1]) for i in range(1, owners)],
    )
    looked = jnp.concatenate(looked, axis=3)
    gradients = slopes_to_epochs(plan, weights, looked, halo)
    gathered = lax.all_to_all(gradients, "acq", split_axis=0, concat_axis=0, tiled=True)
    gathered = gathered.reshape(epochs, 2, looked.shape[3], plan.azimuth_looks)
    return gathered.swapaxes(0, 1).reshape(1, 2, -1, plan.azimuth_looks)


def solution(mesh):
    return jax.shard_map(
        per_device,
        mesh=mesh,
        in_specs=(
            P("acq", None, "strip", None),
            P(),
            P(None, None, "strip"),
            P("acq", None),
            P(None, "acq", None),
        ),
        out_specs=P("acq", None, "strip", None),
        check_vma=False,
    )
```

time: 778 us -> 149 us (0.19)
  local copies, waits for them, and re-layouts: 325 us -> 32.8 us
  waiting for transfers between devices: 262 us -> 40.9 us
  other arithmetic: 106 us -> 0.91 us
  matrix products: 50.7 us -> 2.21 us
  Pallas kernels: 0 us -> 38.9 us
  blocking collectives: 0 us -> 19.3 us
  between operations: 14.2 us -> 0.16 us
    sub x2 -> x0, local copies, waits for them, and re-layouts: 143 us -> none  [looked_pair(): product_imag = earlier[1] * scene[0] - earlier[0] * scene[1]]
    add x2 -> x0, local copies, waits for them, and re-layouts: 142 us -> none  [looked_pair(): product_real = earlier[0] * scene[0] + earlier[1] * scene[1]]
    ppermute x3 -> x1, waiting for transfers between devices: 87.5 us -> 0.01 us  [per_device(): lax.ppermute(looked[0][:, :, :, :1, :], ('acq', 'strip'), [(device[i], de...]
    reduce_sum x4 -> x0, other arithmetic: 83.1 us -> none  [multilook(): field.reshape(rows // LOOK, LOOK, cols // LOOK, LOOK).sum(axis=(1, 3))]
    reduce_scatter x1 -> x0, waiting for transfers between devices: 81.3 us -> none  [per_device(): lax.psum_scatter(jnp.einsum('cl,ldra->cdra', weights, slopes, precision=l...]
    all_to_all x1 -> x2, waiting for transfers between devices: 93.2 us -> 40.9 us  [exchange(): lax.all_to_all(block, OWNERS, split_axis=0, concat_axis=0, tiled=True)]
    dot_general x9 -> x1, matrix products: 50.7 us -> 2.21 us  [lag_vectors(): jnp.dot(field, jnp.asarray(table.astype(np.float32)), precision=lax.Preci...]
    pallas_call x0 -> x5, Pallas kernels: none -> 38.9 us  [the longest x2 19.9 us: compress(): pl.pallas_call(functools.partial(compress_kernel, plan, part), out_shape=...]
  transfers between devices with their start and end apart: 5 -> 3, of which waited for: 4 -> 2; matrix products, arithmetic and copies ran while one was open for 1% -> 17% of each run, Pallas kernels for 0% -> 18%
where the time goes in v1:
time: 149 us; the launch traced here: 148 us
  waiting for transfers between devices  40.9 us (27%)
  Pallas kernels  38.9 us (26%)
  local copies, waits for them, and re-layouts  32.8 us (22%)
  blocking collectives  19.3 us (13%)
  starting transfers between devices  12.7 us (9%)
  matrix products  2.21 us (1%)
    all_to_all x2, waiting for transfers between devices, exchange(): lax.all_to_all(block, OWNERS, split_axis=0, concat_axis=0, tiled=True)  40.9 us
    pallas_call x2, Pallas kernels, compress(): pl.pallas_call(functools.partial(compress_kernel, plan, part), out_shape=...  19.9 us
    pallas_call x2, Pallas kernels, focus(): pl.pallas_call(functools.partial(focus_kernel, plan), out_shape=jax.Shape...  16.7 us
    slice x3, local copies, waits for them, and re-layouts, per_device(): looked.append(focus(plan, fields[part], spectrum[part]))  14.9 us
    all_to_all x2, starting transfers between devices, exchange(): lax.all_to_all(block, OWNERS, split_axis=0, concat_axis=0, tiled=True)  11.4 us
    all_to_all x1, blocking collectives, per_device(): lax.all_to_all(gradients, 'acq', split_axis=0, concat_axis=0, tiled=True)  10.2 us
    all_gather x1, blocking collectives, per_device(): lax.all_gather(inversion[:, 0, :] * usable[None, :], 'acq', axis=1, tiled...  9.07 us
    reshape x1, local copies, waits for them, and re-layouts, own_filter(): own = own.reshape(2, plan.lanes, RADIX, plan.parts, plan.looks, LOOK)  7.04 us
  transfers between devices with their start and end apart: 3, of which 2 were waited for; matrix products, arithmetic and copies ran while one was open for 17% of the time, Pallas kernels for 18%

profile of v1, /device:TPU:0, one launch (start us, length us, event | category | flops | bytes accessed | tf_op | source)
XLA Modules:
  0.0 147.9 jit_solution(5374183030710107945)
XLA Ops:
  0.9 2.2 %convolution_bitcast_fusion = f32[8,2,256]{2,0,1:T(8,128)S(1)} fusion(f32[2,256,512]{2,1,0:T(8,128)} %constant.45, f32[8,512,1]{0,1,2:T(8,128)S(1)} %bitcast.35), kind=kOutput, calls=%fused_computation | convolution fusion | flops 25165824 | bytes 1081344 | tf_op jit(solution)/shard_map/dot_general | solution.py:124
  4.0 9.9 %range_compress.2 = f32[32,2,32,256]{3,2,1,0:T(8,128)} custom-call(f32[8,2,512]{2,1,0:T(2,128)S(1)} %pad_maximum_fusion.1.lag_ref, f32[2,256,2048]{2,1,0:T(8,128)} %bitcast.31), custom_call_target="tpu_custom_call" | custom-call | flops 1610612736 | bytes 6291456 | tf_op jit(solution)/shard_map/range_compress/pallas_call | solution.py:214
  13.9 7.3 %all-to-all-start = ((f32[32,2,32,256]{3,2,1,0:T(8,128)}), f32[32,2,32,256]{3,2,1,0:T(8,128)S(1)}, u32[]{:S(2)}, u32[]{:S(2)}) async-start(f32[32,2,32,256]{3,2,1,0:T(8,128)} %range_compress.2), calls=%async_computation | async-start | bytes 4194304 | tf_op jit(solution)/shard_map/all_to_all | solution.py:426
  21.2 10.0 %range_compress.3 = f32[32,2,32,256]{3,2,1,0:T(8,128)} custom-call(f32[8,2,512]{2,1,0:T(2,128)S(1)} %pad_maximum_fusion.1.lag_ref, f32[2,256,2048]{2,1,0:T(8,128)} %bitcast.32), custom_call_target="tpu_custom_call" | custom-call | flops 1610612736 | bytes 6291456 | tf_op jit(solution)/shard_map/range_compress/pallas_call | solution.py:214
  31.2 38.9 %all-to-all-done = f32[32,2,32,256]{3,2,1,0:T(8,128)S(1)} async-done(((f32[32,2,32,256]{3,2,1,0:T(8,128)}), f32[32,2,32,256]{3,2,1,0:T(8,128)S(1)}, u32[]{:S(2)}, u32[]{:S(2)}) %all-to-all-start) | async-done | bytes 2097184 | tf_op jit(solution)/shard_map/all_to_all | solution.py:426
  70.1 4.1 %all-to-all-start.1 = ((f32[32,2,32,256]{3,2,1,0:T(8,128)}), f32[32,2,32,256]{3,2,1,0:T(8,128)}, u32[]{:S(2)}, u32[]{:S(2)}) async-start(f32[32,2,32,256]{3,2,1,0:T(8,128)} %range_compress.3), calls=%async_computation.1 | async-start | bytes 4194304 | tf_op jit(solution)/shard_map/all_to_all | solution.py:426
  74.2 1.6 %constant_dynamic-slice_fusion = f32[2,1024,64]{2,1,0:T(8,128)S(1)} fusion(f32[2,1024,512]{2,1,0:T(8,128)} %param.21, s32[]{:T(128)S(6)} %select_n.3), kind=kLoop, calls=%fused_computation.16 | loop fusion | bytes 1048580 | tf_op jit(solution)/shard_map/dynamic_slice | solution.py:419
  75.8 1.2 copy.32
  77.0 7.0 %reshape.32 = f32[2,128,8,2,8,4]{2,1,5,4,3,0:T(8,128)} reshape(f32[2,1024,64]{1,2,0:T(8,128)} %copy.32) | data formatting | bytes 1048576 | tf_op jit(solution)/shard_map/reshape | solution.py:420
  84.0 7.8 %fusion.7 = (f32[1,2,8,4,8,128]{2,5,3,4,0,1:T(8,128)}, f32[1,2,8,4,8,128]{2,5,3,4,0,1:T(8,128)}) fusion(f32[2,2,8,4,8,128]{2,5,3,4,0,1:T(8,128)} %bitcast.30), kind=kLoop, calls=%fused_computation.17 | loop fusion | bytes 1048576 | tf_op jit(solution)/shard_map/slice | solution.py:454
  91.9 3.6 %copy.33 = f32[1,2,8,4,8,128]{5,4,3,2,1,0:T(8,128)} copy(f32[1,2,8,4,8,128]{2,5,3,4,0,1:T(8,128)} %get-tuple-element.5) | data formatting | bytes 524288 | tf_op jit(solution)/shard_map/slice | solution.py:454
  95.5 3.5 %copy.34 = f32[1,2,8,4,8,128]{5,4,3,2,1,0:T(8,128)} copy(f32[1,2,8,4,8,128]{2,5,3,4,0,1:T(8,128)} %get-tuple-element.6) | data formatting | bytes 524288 | tf_op jit(solution)/shard_map/slice | solution.py:454
  99.0 9.1 %all_gather.4 = f32[8,8,2]{0,2,1:T(2,128)S(1)} all-gather(f32[8,1,2]{0,2,1:T(2,128)S(1)} %broadcast_multiply_fusion), channel_id=1, replica_groups=mesh['acq'=8,'strip'=4] {'acq'}, dimensions={1}, use_global_device_ids=true | all-gather | bytes 576 | tf_op jit(solution)/shard_map/all_gather | solution.py:444
  108.2 1.2 copy-done.3
  109.4 1.0 copy-done.5
  110.5 0.9 copy-done.8
  111.4 8.4 %azimuth_focus.2 = f32[8,2,2,8,256]{4,3,2,1,0:T(8,128)S(1)} custom-call(f32[4,8,2,32,256]{4,3,2,1,0:T(8,128)} %bitcast.33, f32[2,8,32,128]{3,2,1,0:T(8,128)S(1)} %bitcast.29, bf16[8,256,256]{2,1,0:T(8,128)(2,1)S(1)} %copy-done, bf16[8,256,256]{2,1,0:T(8,128)(2,1)S(1)} %copy-done.1, bf16[8,256,256]{2,1,0:T(8,128)(2,1)S(1)} %copy-done.2, ...), custom_call_target="tpu_custom_call" | custom-call | flops 1610612736 | bytes 6291456 | tf_op jit(solution)/shard_map/azimuth_focus/pallas_call | solution.py:344
  119.8 1.3 collective-permute-start
  121.1 2.0 %all-to-all-done.1 = f32[32,2,32,256]{3,2,1,0:T(8,128)} async-done(((f32[32,2,32,256]{3,2,1,0:T(8,128)}), f32[32,2,32,256]{3,2,1,0:T(8,128)}, u32[]{:S(2)}, u32[]{:S(2)}) %all-to-all-start.1) | async-done | bytes 2097184 | tf_op jit(solution)/shard_map/all_to_all | solution.py:426
  123.1 1.2 copy-done.4
  124.3 1.0 copy-done.6
  126.3 8.4 %azimuth_focus.3 = f32[8,2,2,8,256]{4,3,2,1,0:T(8,128)S(1)} custom-call(f32[4,8,2,32,256]{4,3,2,1,0:T(8,128)} %bitcast.13.field_ref, f32[2,8,32,128]{3,2,1,0:T(8,128)S(1)} %bitcast.28, bf16[8,256,256]{2,1,0:T(8,128)(2,1)S(1)} %copy-done, bf16[8,256,256]{2,1,0:T(8,128)(2,1)S(1)} %copy-done.1, bf16[8,256,256]{2,1,0:T(8,128)(2,1)S(1)} %copy-done.2, ...), custom_call_target="tpu_custom_call" | custom-call | flops 1610612736 | bytes 6291456 | tf_op jit(solution)/shard_map/azimuth_focus/pallas_call | solution.py:344
  134.7 2.2 %slopes_to_epochs.1 = f32[8,2,16,256]{3,2,1,0:T(8,128)S(1)} custom-call(f32[8,16]{1,0:T(8,128)S(1)} %copy.35.weight_ref, f32[8,2,2,16,256]{4,3,2,1,0:T(8,128)S(1)} %pad_maximum_fusion.looked_ref, f32[8,2,2,1,256]{4,3,2,1,0:T(1,128)S(1)} %collective-permute-done.halo_ref), custom_call_target="tpu_custom_call" | custom-call | flops 8388608 | bytes 655360 | tf_op jit(solution)/shard_map/slopes_to_epochs/pallas_call | solution.py:399
  137.0 10.2 %all_to_all.15 = f32[8,2,16,256]{3,2,1,0:T(8,128)S(1)} all-to-all(f32[8,2,16,256]{3,2,1,0:T(8,128)S(1)} %slopes_to_epochs.1), channel_id=1, replica_groups=mesh['acq'=8,'strip'=4] {'acq'}, dimensions={0} | all-to-all | bytes 524288 | tf_op jit(solution)/shard_map/all_to_all | solution.py:465
  (34 shorter events, 3.6 us)
Async XLA Ops:
  13.9 56.2 %all-to-all-start = ((f32[32,2,32,256]{3,2,1,0:T(8,128)}), f32[32,2,32,256]{3,2,1,0:T(8,128)S(1)}, u32[]{:S(2)}, u32[]{:S(2)}) async-start(f32[32,2,32,256]{3,2,1,0:T(8,128)} %range_compress.2), calls=%async_computation | async-start | bytes 4194304 | tf_op jit(solution)/shard_map/all_to_all | solution.py:426
  70.1 13.9 %copy-start.9 = (f32[32,2,32,256]{3,2,1,0:T(8,128)}, f32[32,2,32,256]{3,2,1,0:T(8,128)S(1)}, u32[]{:S(2)}) copy-start(f32[32,2,32,256]{3,2,1,0:T(8,128)S(1)} %all-to-all-done) | copy-start | bytes 6291460
  70.1 53.0 %all-to-all-start.1 = ((f32[32,2,32,256]{3,2,1,0:T(8,128)}), f32[32,2,32,256]{3,2,1,0:T(8,128)}, u32[]{:S(2)}, u32[]{:S(2)}) async-start(f32[32,2,32,256]{3,2,1,0:T(8,128)} %range_compress.3), calls=%async_computation.1 | async-start | bytes 4194304 | tf_op jit(solution)/shard_map/all_to_all | solution.py:426
  91.8 7.1 %copy-start.11 = (s32[1,2]{1,0:T(1,128)S(1)}, s32[1,2]{1,0:T(1,128)}, u32[]{:S(2)}) copy-start(s32[1,2]{1,0:T(1,128)} %param.22) | copy-start | bytes 28
  91.8 7.1 %copy-start.12 = (s32[2]{0:T(128)S(1)}, s32[2]{0:T(128)}, u32[]{:S(2)}) copy-start(s32[2]{0:T(128)} %constant.32.clone) | copy-start | bytes 28
  91.8 7.1 %copy-start.10 = (f32[8,1,2]{0,2,1:T(2,128)S(1)}, f32[8,1,2]{0,2,1:T(2,128)}, u32[]{:S(2)}) copy-start(f32[8,1,2]{0,2,1:T(2,128)} %param.23) | copy-start | bytes 196
  91.8 16.3 %copy-start = (bf16[8,256,256]{2,1,0:T(8,128)(2,1)S(1)}, bf16[8,256,256]{2,1,0:T(8,128)(2,1)}, u32[]{:S(2)}) copy-start(bf16[8,256,256]{2,1,0:T(8,128)(2,1)} %constant.36.clone.fh_ref) | copy-start | bytes 3145732
  91.8 16.3 %copy-start.1 = (bf16[8,256,256]{2,1,0:T(8,128)(2,1)S(1)}, bf16[8,256,256]{2,1,0:T(8,128)(2,1)}, u32[]{:S(2)}) copy-start(bf16[8,256,256]{2,1,0:T(8,128)(2,1)} %constant.37.clone.fl_ref) | copy-start | bytes 3145732
  91.9 16.3 %copy-start.2 = (bf16[8,256,256]{2,1,0:T(8,128)(2,1)S(1)}, bf16[8,256,256]{2,1,0:T(8,128)(2,1)}, u32[]{:S(2)}) copy-start(bf16[8,256,256]{2,1,0:T(8,128)(2,1)} %constant.38.clone.bh_ref) | copy-start | bytes 3145732
  108.2 1.2 copy-start.3
  109.4 1.0 copy-start.5
  110.5 0.9 copy-start.8
  119.8 14.9 %collective-permute-start = (f32[8,2,2,1,256]{4,3,2,1,0:T(1,128)S(1)}, f32[8,2,2,1,256]{4,3,2,1,0:T(1,128)S(1)}, u32[]{:S(2)}, u32[]{:S(2)}) collective-permute-start(f32[8,2,2,1,256]{4,3,2,1,0:T(1,128)S(1)} %slice.28), channel_id=1, source_target_pairs={{4,0},{8,4},{12,8},{16,12},{20,16},{24,20},{28,24},{1,28},{5,1},{9... | collective-permute-start | bytes 98312 | tf_op jit(solution)/shard_map/ppermute | solution.py:458
  123.1 1.2 copy-start.4
  124.3 1.0 copy-start.6
  125.4 0.9 copy-start.7

commit v2 on v1

--- a/solution.py
+++ b/solution.py
@@ -116,41 +116,78 @@
         return LOOK if self.planes else 1
 
 
-def lag_vectors(range_filter, plan):
+def lag_tables(plan):
     base, samples = plan.base, plan.samples
-    field = range_filter.reshape(2, base, RADIX).transpose(2, 0, 1).reshape(RADIX, 2 * base)
     index = np.arange(base)
-    table = real_form(*unit(index[:, None] * index[None, :], base, -1.0)) / samples
-    sums = jnp.dot(
-        field, jnp.asarray(table.astype(np.float32)), precision=lax.Precision.HIGHEST
-    ).reshape(RADIX, 2, base)
-    lag = np.arange(2 * base)
-    lag = np.where(lag <= base, lag, lag - 2 * base)
-    turn_cos, turn_sin = unit(lag[None, :] * np.arange(RADIX)[:, None], samples, -1.0)
-    turn_cos = jnp.asarray(turn_cos.astype(np.float32))
-    turn_sin = jnp.asarray(turn_sin.astype(np.float32))
-    real = jnp.concatenate([sums[:, 0], sums[:, 0]], axis=1)
-    imag = jnp.concatenate([sums[:, 1], sums[:, 1]], axis=1)
-    return jnp.stack(
-        [real * turn_cos - imag * turn_sin, real * turn_sin + imag * turn_cos], axis=1
-    )
-
-
-def compress_kernel(plan, part, lag_ref, raw_ref, out_ref, t_high, t_low, y_high, y_low, z_ref):
+    table = host_parts(real_form(*unit(index[:, None] * index[None, :], samples, -1.0)) / samples)
+    block = np.arange(RADIX)[:, None]
+    turns = np.stack(
+        unit(block * index[None, :], RADIX, -1.0)
+        + tuple(np.broadcast_to(part, (RADIX, base)) for part in unit(block, RADIX, 1.0))
+    )
+    return table + (turns.astype(np.float32),)
+
+
+def lag_vectors(plan, filter_ref, table_high, table_low, turn_ref):
+    base = plan.base
+    lane = lax.broadcasted_iota(jnp.int32, (RADIX, base), 1)
+    chosen = lane % RADIX == lax.broadcasted_iota(jnp.int32, (RADIX, base), 0)
+    rows = []
+    for e in range(RADIX):
+        both = []
+        for c in range(2):
+            block = jnp.broadcast_to(filter_ref[c : c + 1, e * base : (e + 1) * base], (RADIX, base))
+            both.append(jnp.where(chosen, block, 0.0))
+        rows.append(jnp.concatenate(both, axis=1))
+    high, low = two_parts(jnp.concatenate(rows, axis=0))
+    sums = three_products(high, low, table_high[...], table_low[...], ((1,), (0,)))
+    real, imag = 0.0, 0.0
+    for e in range(RADIX):
+        part_real = sums[e * RADIX : (e + 1) * RADIX, :base]
+        part_imag = sums[e * RADIX : (e + 1) * RADIX, base:]
+        cosine, sine = turn_ref[0, e : e + 1, :], turn_ref[1, e : e + 1, :]
+        real = real + part_real * cosine - part_imag * sine
+        imag = imag + part_real * sine + part_imag * cosine
+    cosine, sine = turn_ref[2], turn_ref[3]
+    return (
+        jnp.concatenate([real, real * cosine - imag * sine], axis=1),
+        jnp.concatenate([imag, real * sine + imag * cosine], axis=1),
+    )
+
+
+def fetch(copies):
+    for copy in copies:
+        copy.start()
+    return copies
+
+
+def compress_kernel(
+    plan, part, filter_ref, table_high, table_low, turn_ref, raw_ref, out_ref,
+    raw, t_high, t_low, y_high, y_low, z_ref, sems,
+):
     base, blocks = plan.base, plan.blocks
     tiles = plan.rows // ROWS
     chunk = blocks * plan.rows
-
-    def build(d, carry):
+    pieces = sems.shape[0]
+    piece = plan.pulses // pieces
+
+    def raw_copy(at):
+        rows = pl.ds(at * piece, piece)
+        return pltpu.make_async_copy(raw_ref.at[:, rows, :], raw.at[:, rows, :], sems.at[at])
+
+    fetch([raw_copy(at) for at in range(pieces)])
+    lags = lag_vectors(plan, filter_ref, table_high, table_low, turn_ref)
+
+    for d in range(RADIX):
         spread = [
             pltpu.roll(
-                jnp.broadcast_to(lag_ref[d, c : c + 1, :], (ROWS, 2 * base)),
+                jnp.broadcast_to(lag[d : d + 1, :], (ROWS, 2 * base)),
                 0,
                 1,
                 stride=plan.tile_stride(),
                 stride_axis=0,
             )
-            for c in range(2)
+            for lag in lags
         ]
         for pair in range(blocks * tiles // 2):
             real, imag = [], []
@@ -170,14 +207,11 @@
             t_low[d, top, base:] = -imag_low
             t_low[d, bottom, :base] = imag_low
             t_low[d, bottom, base:] = real_low
-        return carry
-
-    lax.fori_loop(0, RADIX, build, 0)
 
     def spread_pulses(at, carry):
-        rows = pl.ds(at * 2 * ROWS, 2 * ROWS)
+        rows = pl.ds(pl.multiple_of(at * 2 * ROWS, 2 * ROWS), 2 * ROWS)
         x = [
-            tuple(raw_ref[c, rows, a * base : (a + 1) * base] for c in range(2))
+            tuple(raw[c, rows, a * base : (a + 1) * base] for c in range(2))
             for a in range(RADIX)
         ]
         for d, value in enumerate(dft8(x, -1.0)):
@@ -187,13 +221,13 @@
                 y_low[d, rows, c * base : (c + 1) * base] = low
         return carry
 
-    lax.fori_loop(0, plan.pulses // (2 * ROWS), spread_pulses, 0)
-
-    def multiply(d, carry):
+    steps = piece // (2 * ROWS)
+    for at in range(pieces):
+        raw_copy(at).wait()
+        lax.fori_loop(at * steps, (at + 1) * steps, spread_pulses, 0)
+
+    for d in range(RADIX):
         z_ref[d] = three_products(t_high[d], t_low[d], y_high[d], y_low[d], ((1,), (1,)))
-        return carry
-
-    lax.fori_loop(0, RADIX, multiply, 0)
 
     for block in range(blocks):
         for tile in range(tiles):
@@ -207,7 +241,7 @@
                     out_ref[a * blocks + block, c, tile * ROWS : (tile + 1) * ROWS, :] = value[c]
 
 
-def compress(plan, part, lags, raw):
+def compress(plan, part, range_filter, raw):
     chunk = plan.blocks * plan.rows
     whole = pl.BlockSpec(memory_space=pltpu.VMEM)
     bytes_moved = 4 * (raw.size + raw.size // plan.parts)
@@ -216,14 +250,16 @@
         out_shape=jax.ShapeDtypeStruct(
             (plan.strips * plan.epochs, 2, plan.rows, plan.pulses), jnp.float32
         ),
-        in_specs=[whole, whole],
+        in_specs=[whole] * 4 + [pl.BlockSpec(memory_space=pl.ANY)],
         out_specs=whole,
         scratch_shapes=[
+            pltpu.VMEM(raw.shape, jnp.float32),
             pltpu.VMEM((RADIX, 2 * chunk, 2 * plan.base), jnp.bfloat16),
             pltpu.VMEM((RADIX, 2 * chunk, 2 * plan.base), jnp.bfloat16),
             pltpu.VMEM((RADIX, plan.pulses, 2 * plan.base), jnp.bfloat16),
             pltpu.VMEM((RADIX, plan.pulses, 2 * plan.base), jnp.bfloat16),
             pltpu.VMEM((RADIX, 2 * chunk, plan.pulses), jnp.float32),
+            pltpu.SemaphoreType.DMA((4,)),
         ],
         compiler_params=pltpu.CompilerParams(vmem_limit_bytes=VMEM_BYTES),
         cost_estimate=pl.CostEstimate(
@@ -232,17 +268,45 @@
             transcendentals=0,
         ),
         name="range_compress",
-    )(lags, raw)
-
-
-def focus_kernel(
-    plan, field_ref, filter_ref, fh_ref, fl_ref, bh_ref, bl_ref, sum_ref, looked_ref,
-    y_high, y_low, z_ref, scene_ref, product_ref,
-):
+    )(range_filter, *lag_tables(plan), raw)
+
+
+def focus_kernel(plan, part, final, *refs):
+    field_any, filter_any, fh_any, fl_any, bh_any, bl_any, sum_any = refs[:7]
+    if final:
+        weight_ref, before_ref, halo_ref, out_ref = refs[7:11]
+    else:
+        (out_ref,) = refs[7:8]
+    scratch = refs[11 if final else 8 :]
+    (
+        field_ref, filter_ref, fh_ref, fl_ref, bh_ref, bl_ref, sum_ref,
+        z_ref, scene_ref, product_ref, field_sems, table_sems,
+    ) = scratch[:12]
     rows, lanes, epochs, looks = plan.rows, plan.lanes, plan.epochs, plan.looks
     per_block = field_ref.shape[-1] // lanes
 
+    def field_copy(j):
+        return pltpu.make_async_copy(field_any.at[:, j], field_ref.at[:, j], field_sems.at[j])
+
+    fetch([field_copy(j) for j in range(epochs)])
+    tables = fetch(
+        [
+            pltpu.make_async_copy(source, target, table_sems.at[at])
+            for at, (source, target) in enumerate(
+                (
+                    (fh_any, fh_ref),
+                    (fl_any, fl_ref),
+                    (filter_any.at[part], filter_ref),
+                    (bh_any, bh_ref),
+                    (bl_any, bl_ref),
+                    (sum_any, sum_ref),
+                )
+            )
+        ]
+    )
+
     def forward(j, carry):
+        field_copy(j).wait()
         for top in range(0, rows, ROWS):
             x = []
             for a in range(RADIX):
@@ -260,25 +324,20 @@
         return carry
 
     lax.fori_loop(0, epochs, forward, 0)
-
-    def filtered(d, carry):
-        y_high[...], y_low[...] = two_parts(z_ref[d])
-        spectrum = three_products(
-            y_high[...], y_low[...], fh_ref[d], fl_ref[d], ((1,), (0,))
-        ).reshape(epochs, rows, 2 * lanes)
+    for copy in tables:
+        copy.wait()
+
+    for d in range(RADIX):
+        high, low = two_parts(z_ref[d])
+        spectrum = three_products(high, low, fh_ref[d], fl_ref[d], ((1,), (0,)))
+        spectrum = spectrum.reshape(epochs, rows, 2 * lanes)
         real, imag = spectrum[:, :, :lanes], spectrum[:, :, lanes:]
         by_real, by_imag = filter_ref[0, d][None], filter_ref[1, d][None]
-        real, imag = real * by_real - imag * by_imag, real * by_imag + imag * by_real
-        for c, value in enumerate((real, imag)):
-            high, low = two_parts(value.reshape(epochs * rows, lanes))
-            y_high[:, c * lanes : (c + 1) * lanes] = high
-            y_low[:, c * lanes : (c + 1) * lanes] = low
-        z_ref[d] = three_products(
-            y_high[...], y_low[...], bh_ref[d], bl_ref[d], ((1,), (0,))
+        spectrum = jnp.concatenate(
+            [real * by_real - imag * by_imag, real * by_imag + imag * by_real], axis=2
         )
-        return carry
-
-    lax.fori_loop(0, RADIX, filtered, 0)
+        high, low = two_parts(spectrum.reshape(epochs * rows, 2 * lanes))
+        z_ref[d] = three_products(high, low, bh_ref[d], bl_ref[d], ((1,), (0,)))
 
     scene_ref[0] = jnp.zeros_like(scene_ref[0])
     scene_ref[1] = jnp.zeros_like(scene_ref[1])
@@ -326,46 +385,18 @@
     looked = jnp.dot(high, weights, preferred_element_type=jnp.float32) + jnp.dot(
         low, weights, preferred_element_type=jnp.float32
     )
-    looked_ref[...] = looked.reshape(looked_ref.shape)
-
-
-def focus(plan, field, spectrum):
-    lanes = plan.lanes
-    b = np.arange(lanes)[None, :, None]
-    k = RADIX * np.arange(lanes)[None, None, :] + np.arange(RADIX)[:, None, None]
-    cosine, sine = unit(b * k, plan.azimuth, -1.0)
-    ahead = host_parts(real_form(cosine, sine))
-    cosine, sine = cosine.swapaxes(1, 2), -sine.swapaxes(1, 2)
-    back = host_parts(real_form(cosine, sine) / plan.azimuth)
-    sums = (np.arange(plan.azimuth)[:, None] // LOOK == np.arange(plan.azimuth_looks)[None, :]) / LOOK
-    sums = sums.astype(ml_dtypes.bfloat16)
-    total = plan.epochs * plan.rows
-    whole = pl.BlockSpec(memory_space=pltpu.VMEM)
-    return pl.pallas_call(
-        functools.partial(focus_kernel, plan),
-        out_shape=jax.ShapeDtypeStruct(
-            (plan.epochs, 2, 2, plan.looks, plan.azimuth_looks), jnp.float32
-        ),
-        in_specs=[whole] * 7,
-        out_specs=whole,
-        scratch_shapes=[
-            pltpu.VMEM((total, 2 * lanes), jnp.bfloat16),
-            pltpu.VMEM((total, 2 * lanes), jnp.bfloat16),
-            pltpu.VMEM((RADIX, total, 2 * lanes), jnp.float32),
-            pltpu.VMEM((plan.epochs + 2, 2, plan.rows, plan.azimuth), jnp.float32),
-            pltpu.VMEM((plan.epochs, 2, 2, plan.looks, plan.azimuth), jnp.float32),
-        ],
-        compiler_params=pltpu.CompilerParams(vmem_limit_bytes=VMEM_BYTES),
-        cost_estimate=pl.CostEstimate(
-            flops=2 * 6 * RADIX * total * 4 * lanes * lanes,
-            bytes_accessed=4 * field.size + 4 * 1024 * 1024,
-            transcendentals=0,
-        ),
-        name="azimuth_focus",
-    )(field, spectrum, *ahead, *back, sums)
-
-
-def slope_kernel(plan, weight_ref, looked_ref, halo_ref, out_ref, slope_ref):
+    looked = looked.reshape(epochs, 2, 2, looks, plan.azimuth_looks)
+    if final:
+        looked_ref, slope_ref = scratch[12:]
+        for at, before in enumerate(before_ref):
+            looked_ref[:, :, :, at * looks : (at + 1) * looks, :] = before[...]
+        looked_ref[:, :, :, part * looks :, :] = looked
+        slopes_and_sums(plan, weight_ref, looked_ref, halo_ref, out_ref, slope_ref)
+    else:
+        out_ref[...] = looked
+
+
+def slopes_and_sums(plan, weight_ref, looked_ref, halo_ref, out_ref, slope_ref):
     epochs = plan.epochs
     columns = plan.azimuth_looks
     inner = lax.broadcasted_iota(jnp.int32, (plan.looks * plan.parts, columns), 1) < columns - 1
@@ -391,6 +422,75 @@
         return carry
 
     lax.fori_loop(0, epochs, epoch, 0)
+
+
+def focus_tables(plan):
+    lanes = plan.lanes
+    b = np.arange(lanes)[None, :, None]
+    k = RADIX * np.arange(lanes)[None, None, :] + np.arange(RADIX)[:, None, None]
+    cosine, sine = unit(b * k, plan.azimuth, -1.0)
+    ahead = host_parts(real_form(cosine, sine))
+    cosine, sine = cosine.swapaxes(1, 2), -sine.swapaxes(1, 2)
+    back = host_parts(real_form(cosine, sine) / plan.azimuth)
+    sums = (np.arange(plan.azimuth)[:, None] // LOOK == np.arange(plan.azimuth_looks)[None, :]) / LOOK
+    return ahead + back + (sums.astype(ml_dtypes.bfloat16),)
+
+
+def focus(plan, part, field, spectrum, finish=None):
+    lanes = plan.lanes
+    total = plan.epochs * plan.rows
+    tables = focus_tables(plan)
+    whole = pl.BlockSpec(memory_space=pltpu.VMEM)
+    looked = (plan.epochs, 2, 2, plan.looks, plan.azimuth_looks)
+    gradients = (plan.epochs, 2, plan.looks * plan.parts, plan.azimuth_looks)
+    operands = [field, spectrum, *tables]
+    in_specs = [pl.BlockSpec(memory_space=pl.ANY)] * 7
+    scratch = [
+        pltpu.VMEM(field.shape, jnp.float32),
+        pltpu.VMEM(spectrum.shape[1:], jnp.float32),
+        *[pltpu.VMEM(table.shape, jnp.bfloat16) for table in tables],
+        pltpu.VMEM((RADIX, total, 2 * lanes), jnp.float32),
+        pltpu.VMEM((plan.epochs + 2, 2, plan.rows, plan.azimuth), jnp.float32),
+        pltpu.VMEM((plan.epochs, 2, 2, plan.looks, plan.azimuth), jnp.float32),
+        pltpu.SemaphoreType.DMA((plan.epochs,)),
+        pltpu.SemaphoreType.DMA((6,)),
+    ]
+    shape = looked
+    if finish is not None:
+        weights, before, halo = finish
+        shape = gradients
+        operands += [weights, before, halo]
+        in_specs += [pl.BlockSpec(memory_space=pltpu.SMEM), [whole] * len(before), whole]
+        scratch += [
+            pltpu.VMEM((plan.epochs, 2, 2, plan.looks * plan.parts, plan.azimuth_looks), jnp.float32),
+            pltpu.VMEM((2 * plan.epochs,) + gradients[1:], jnp.float32),
+        ]
+    return pl.pallas_call(
+        functools.partial(focus_kernel_flat, plan, part, len(before) if finish else None),
+        out_shape=jax.ShapeDtypeStruct(shape, jnp.float32),
+        in_specs=jax.tree.leaves(in_specs),
+        out_specs=whole,
+        scratch_shapes=scratch,
+        compiler_params=pltpu.CompilerParams(vmem_limit_bytes=VMEM_BYTES),
+        cost_estimate=pl.CostEstimate(
+            flops=2 * 6 * RADIX * total * 4 * lanes * lanes,
+            bytes_accessed=4 * field.size + 4 * 1024 * 1024,
+            transcendentals=0,
+        ),
+        name="azimuth_focus",
+    )(*jax.tree.leaves(operands))
+
+
+def focus_kernel_flat(plan, part, count, *refs):
+    if count is None:
+        focus_kernel(plan, part, False, *refs)
+        return
+    before = refs[8 : 8 + count]
+    focus_kernel(plan, part, True, *refs[:8], before, *refs[8 + count :])
+
+
+def slope_kernel(plan, weight_ref, looked_ref, halo_ref, out_ref, slope_ref):
+    slopes_and_sums(plan, weight_ref, looked_ref, halo_ref, out_ref, slope_ref)
 
 
 def slopes_to_epochs(plan, weights, looked, halo):
@@ -444,26 +544,26 @@
     weights = lax.all_gather(inversion[:, 0, :] * usable[None, :], "acq", axis=1, tiled=False)
     weights = weights.reshape(epochs, 2 * epochs)
 
-    vectors = lag_vectors(range_filter, plan)
     spectrum = own_filter(plan, azimuth_filter)
-    looked = []
     fields = [
-        exchange(plan, compress(plan, part, vectors, raw_echoes[0])) for part in range(plan.parts)
+        exchange(plan, compress(plan, part, range_filter, raw_echoes[0]))
+        for part in range(plan.parts)
     ]
-    for part in range(plan.parts):
-        looked.append(focus(plan, fields[part], spectrum[part]))
+    before = [focus(plan, part, fields[part], spectrum) for part in range(max(1, plan.parts - 1))]
 
     owners = strips * epochs
     device = [i % epochs * strips + i // epochs for i in range(owners)]
     halo = lax.ppermute(
-        looked[0][:, :, :, :1, :],
+        before[0][:, :, :, :1, :],
         ("acq", "strip"),
         [(device[i], device[i - 1]) for i in range(1, owners)],
     )
-    looked = jnp.concatenate(looked, axis=3)
-    gradients = slopes_to_epochs(plan, weights, looked, halo)
+    if plan.parts > 1:
+        gradients = focus(plan, plan.parts - 1, fields[-1], spectrum, (weights, before, halo))
+    else:
+        gradients = slopes_to_epochs(plan, weights, before[0], halo)
     gathered = lax.all_to_all(gradients, "acq", split_axis=0, concat_axis=0, tiled=True)
-    gathered = gathered.reshape(epochs, 2, looked.shape[3], plan.azimuth_looks)
+    gathered = gathered.reshape(epochs, 2, plan.looks * plan.parts, plan.azimuth_looks)
     return gathered.swapaxes(0, 1).reshape(1, 2, -1, plan.azimuth_looks)
 
 

time: 149 us -> 141 us (0.946)
  waiting for transfers between devices: 40.9 us -> 55.9 us
  Pallas kernels: 38.9 us -> 25.4 us
  local copies, waits for them, and re-layouts: 32.8 us -> 24.3 us
  matrix products: 2.21 us -> 0 us
  blocking collectives: 19.3 us -> 21.4 us
    all_to_all x2, waiting for transfers between devices: 40.9 us -> 55.9 us  [exchange(): lax.all_to_all(block, OWNERS, split_axis=0, concat_axis=0, tiled=True)]
    slice x4 -> x1, local copies, waits for them, and re-layouts: 14.9 us -> 0.02 us  [per_device(): before[0][:, :, :, :1, :]]
    pallas_call x2, Pallas kernels: 19.9 us -> 12.3 us  [compress(): pl.pallas_call(functools.partial(compress_kernel, plan, part), out_shape=...]
    pallas_call x3 -> x2, Pallas kernels: 19 us -> 13.1 us  [focus(): pl.pallas_call(functools.partial(focus_kernel_flat, plan, part, len(befor...]
    transpose x0 -> x1, local copies, waits for them, and re-layouts: none -> 5.3 us  [own_filter(): own.transpose(order).reshape(plan.parts, 2, RADIX, plan.rows, plan.lanes)]
    dot_general x1 -> x0, matrix products: 2.21 us -> none  [lag_vectors(): jnp.dot(field, jnp.asarray(table.astype(np.float32)), precision=lax.Preci...]
    all_gather x1, blocking collectives: 9.07 us -> 11.1 us  [per_device(): lax.all_gather(inversion[:, 0, :] * usable[None, :], 'acq', axis=1, tiled...]
    unnamed x26 -> x38, local copies, waits for them, and re-layouts: 6.46 us -> 8.5 us
  transfers between devices with their start and end apart: 3 -> 3, of which waited for: 2 -> 2; matrix products, arithmetic and copies ran while one was open for 17% -> 11% of each run, Pallas kernels for 18% -> 8%
where the time goes in v2:
time: 141 us; the launch traced here: 140 us
  waiting for transfers between devices  55.9 us (40%)
  Pallas kernels  25.4 us (18%)
  local copies, waits for them, and re-layouts  24.3 us (17%)
  blocking collectives  21.4 us (15%)
  starting transfers between devices  12.7 us (9%)
    all_to_all x2, waiting for transfers between devices, exchange(): lax.all_to_all(block, OWNERS, split_axis=0, concat_axis=0, tiled=True)  55.9 us
    pallas_call x2, Pallas kernels, focus(): pl.pallas_call(functools.partial(focus_kernel_flat, plan, part, len(befor...  13.1 us
    pallas_call x2, Pallas kernels, compress(): pl.pallas_call(functools.partial(compress_kernel, plan, part), out_shape=...  12.3 us
    all_to_all x2, starting transfers between devices, exchange(): lax.all_to_all(block, OWNERS, split_axis=0, concat_axis=0, tiled=True)  11.4 us
    all_gather x1, blocking collectives, per_device(): lax.all_gather(inversion[:, 0, :] * usable[None, :], 'acq', axis=1, tiled...  11.1 us
    all_to_all x1, blocking collectives, per_device(): lax.all_to_all(gradients, 'acq', split_axis=0, concat_axis=0, tiled=True)  10.2 us
    unnamed x38, local copies, waits for them, and re-layouts  8.5 us
    reshape x1, local copies, waits for them, and re-layouts, own_filter(): own = own.reshape(2, plan.lanes, RADIX, plan.parts, plan.looks, LOOK)  7.05 us
  transfers between devices with their start and end apart: 3, of which 2 were waited for; matrix products, arithmetic and copies ran while one was open for 11% of the time, Pallas kernels for 8%

profile of v2, /device:TPU:0, one launch (start us, length us, event | category | flops | bytes accessed | tf_op | source)
XLA Modules:
  0.0 140.1 jit_solution(10679807971044469744)
XLA Ops:
  0.0 1.0 copy-done.6
  1.0 1.0 copy-done.8
  2.1 0.8 copy-done.11
  2.8 0.7 copy-done.13
  3.6 6.2 %range_compress.3 = f32[32,2,32,256]{3,2,1,0:T(8,128)} custom-call(f32[2,2048]{1,0:T(2,128)S(1)} %copy-done.13, bf16[512,512]{1,0:T(8,128)(2,1)S(1)} %copy-done.6, bf16[512,512]{1,0:T(8,128)(2,1)S(1)} %copy-done.8, f32[4,8,256]{2,1,0:T(8,128)S(1)} %copy-done.11, f32[2,256,2048]{2,1,0:T(8,128)} %bitcast.15), custom_call_target="tpu_custom_call" | custom-call | flops 1610612736 | bytes 6291456 | tf_op jit(solution)/shard_map/range_compress/pallas_call | solution.py:248
  9.8 7.3 %all-to-all-start.1 = ((f32[32,2,32,256]{3,2,1,0:T(8,128)}), f32[32,2,32,256]{3,2,1,0:T(8,128)S(1)}, u32[]{:S(2)}, u32[]{:S(2)}) async-start(f32[32,2,32,256]{3,2,1,0:T(8,128)} %range_compress.3), calls=%async_computation.1 | async-start | bytes 4194304 | tf_op jit(solution)/shard_map/all_to_all | solution.py:526
  17.1 6.1 %range_compress.2 = f32[32,2,32,256]{3,2,1,0:T(8,128)} custom-call(f32[2,2048]{1,0:T(2,128)S(1)} %copy-done.14, bf16[512,512]{1,0:T(8,128)(2,1)S(1)} %copy-done.7, bf16[512,512]{1,0:T(8,128)(2,1)S(1)} %copy-done.9, f32[4,8,256]{2,1,0:T(8,128)S(1)} %copy-done.12, f32[2,256,2048]{2,1,0:T(8,128)} %bitcast.16), custom_call_target="tpu_custom_call" | custom-call | flops 1610612736 | bytes 6291456 | tf_op jit(solution)/shard_map/range_compress/pallas_call | solution.py:248
  23.2 42.7 %all-to-all-done.1 = f32[32,2,32,256]{3,2,1,0:T(8,128)S(1)} async-done(((f32[32,2,32,256]{3,2,1,0:T(8,128)}), f32[32,2,32,256]{3,2,1,0:T(8,128)S(1)}, u32[]{:S(2)}, u32[]{:S(2)}) %all-to-all-start.1) | async-done | bytes 2097184 | tf_op jit(solution)/shard_map/all_to_all | solution.py:526
  66.0 4.1 %all-to-all-start = ((f32[32,2,32,256]{3,2,1,0:T(8,128)}), f32[32,2,32,256]{3,2,1,0:T(8,128)}, u32[]{:S(2)}, u32[]{:S(2)}) async-start(f32[32,2,32,256]{3,2,1,0:T(8,128)} %range_compress.2), calls=%async_computation | async-start | bytes 4194304 | tf_op jit(solution)/shard_map/all_to_all | solution.py:526
  70.1 1.6 %constant_dynamic-slice_fusion = f32[2,1024,64]{2,1,0:T(8,128)S(1)} fusion(f32[2,1024,512]{2,1,0:T(8,128)} %param.24, s32[]{:T(128)S(6)} %select_n.3), kind=kLoop, calls=%fused_computation.2 | loop fusion | bytes 1048580 | tf_op jit(solution)/shard_map/dynamic_slice | solution.py:519
  71.7 1.1 copy.28
  72.8 7.0 %reshape.19 = f32[2,128,8,2,8,4]{2,1,5,4,3,0:T(8,128)} reshape(f32[2,1024,64]{1,2,0:T(8,128)} %copy.28) | data formatting | bytes 1048576 | tf_op jit(solution)/shard_map/reshape | solution.py:520
  79.9 5.3 %copy.29 = f32[2,2,8,4,8,128]{5,4,3,2,1,0:T(8,128)S(1)} copy(f32[2,2,8,4,8,128]{2,5,3,4,0,1:T(8,128)} %bitcast.14) | data formatting | bytes 1048576 | tf_op jit(solution)/shard_map/transpose | solution.py:522
  85.3 1.2 copy-done.2
  86.5 1.2 copy-done.4
  87.8 5.5 %azimuth_focus.2.refs_8_ = f32[8,2,2,8,256]{4,3,2,1,0:T(8,128)S(1)} custom-call(f32[4,8,2,32,256]{4,3,2,1,0:T(8,128)} %bitcast.17, f32[2,2,8,32,128]{4,3,2,1,0:T(8,128)S(1)} %bitcast.12, bf16[8,256,256]{2,1,0:T(8,128)(2,1)S(1)} %copy-done, bf16[8,256,256]{2,1,0:T(8,128)(2,1)S(1)} %copy-done.1, bf16[8,256,256]{2,1,0:T(8,128)(2,1)S(1)} %copy-done.2, ...), custom_call_target="tpu_custom_call" | custom-call | flops 1610612736 | bytes 6291456 | tf_op jit(solution)/shard_map/azimuth_focus/pallas_call | solution.py:468
  93.2 1.3 collective-permute-start
  94.6 11.1 %all_gather.4 = f32[8,8,2]{0,2,1:T(2,128)S(1)} all-gather(f32[8,1,2]{0,2,1:T(2,128)S(1)} %broadcast_multiply_fusion), channel_id=1, replica_groups=mesh['acq'=8,'strip'=4] {'acq'}, dimensions={1}, use_global_device_ids=true | all-gather | bytes 576 | tf_op jit(solution)/shard_map/all_gather | solution.py:544
  105.8 13.2 %all-to-all-done = f32[32,2,32,256]{3,2,1,0:T(8,128)} async-done(((f32[32,2,32,256]{3,2,1,0:T(8,128)}), f32[32,2,32,256]{3,2,1,0:T(8,128)}, u32[]{:S(2)}, u32[]{:S(2)}) %all-to-all-start) | async-done | bytes 2097184 | tf_op jit(solution)/shard_map/all_to_all | solution.py:526
  119.0 1.2 copy-done.3
  120.2 1.2 copy-done.5
  121.5 7.7 %azimuth_focus.3 = f32[8,2,16,256]{3,2,1,0:T(8,128)S(1)} custom-call(f32[4,8,2,32,256]{4,3,2,1,0:T(8,128)} %bitcast.1.refs_0_, f32[2,2,8,32,128]{4,3,2,1,0:T(8,128)S(1)} %bitcast.13, bf16[8,256,256]{2,1,0:T(8,128)(2,1)S(1)} %copy-done, bf16[8,256,256]{2,1,0:T(8,128)(2,1)S(1)} %copy-done.1, bf16[8,256,256]{2,1,0:T(8,128)(2,1)S(1)} %copy-done.3, ...), custom_call_target="tpu_custom_call" | custom-call | flops 1610612736 | bytes 6291456 | tf_op jit(solution)/shard_map/azimuth_focus/pallas_call | solution.py:468
  129.2 10.2 %all_to_all.15 = f32[8,2,16,256]{3,2,1,0:T(8,128)S(1)} all-to-all(f32[8,2,16,256]{3,2,1,0:T(8,128)S(1)} %azimuth_focus.3), channel_id=1, replica_groups=mesh['acq'=8,'strip'=4] {'acq'}, dimensions={0} | all-to-all | bytes 524288 | tf_op jit(solution)/shard_map/all_to_all | solution.py:565
  139.4 0.7 copy.31
  (35 shorter events, 0.2 us)
Async XLA Ops:
  0.0 1.0 copy-start.6
  1.0 1.0 copy-start.8
  2.1 0.8 copy-start.11
  2.8 0.7 copy-start.13
  3.6 13.5 %copy-start.7 = (bf16[512,512]{1,0:T(8,128)(2,1)S(1)}, bf16[512,512]{1,0:T(8,128)(2,1)}, u32[]{:S(2)}) copy-start(bf16[512,512]{1,0:T(8,128)(2,1)} %constant.33.clone.table_high) | copy-start | bytes 1572868
  3.6 13.5 %copy-start.9 = (bf16[512,512]{1,0:T(8,128)(2,1)S(1)}, bf16[512,512]{1,0:T(8,128)(2,1)}, u32[]{:S(2)}) copy-start(bf16[512,512]{1,0:T(8,128)(2,1)} %constant.34.clone.table_low) | copy-start | bytes 1572868
  3.6 13.5 %copy-start.12 = (f32[4,8,256]{2,1,0:T(8,128)S(1)}, f32[4,8,256]{2,1,0:T(8,128)}, u32[]{:S(2)}) copy-start(f32[4,8,256]{2,1,0:T(8,128)} %constant.35.clone.turn_ref) | copy-start | bytes 98308
  3.6 13.6 %copy-start.14 = (f32[2,2048]{1,0:T(2,128)S(1)}, f32[2,2048]{1,0:T(2,128)}, u32[]{:S(2)}) copy-start(f32[2,2048]{1,0:T(2,128)} %filter_ref.3) | copy-start | bytes 49156
  9.8 56.2 %all-to-all-start.1 = ((f32[32,2,32,256]{3,2,1,0:T(8,128)}), f32[32,2,32,256]{3,2,1,0:T(8,128)S(1)}, u32[]{:S(2)}, u32[]{:S(2)}) async-start(f32[32,2,32,256]{3,2,1,0:T(8,128)} %range_compress.3), calls=%async_computation.1 | async-start | bytes 4194304 | tf_op jit(solution)/shard_map/all_to_all | solution.py:526
  66.0 13.9 %copy-start.15 = (f32[32,2,32,256]{3,2,1,0:T(8,128)}, f32[32,2,32,256]{3,2,1,0:T(8,128)S(1)}, u32[]{:S(2)}) copy-start(f32[32,2,32,256]{3,2,1,0:T(8,128)S(1)} %all-to-all-done.1) | copy-start | bytes 6291460
  66.0 53.0 %all-to-all-start = ((f32[32,2,32,256]{3,2,1,0:T(8,128)}), f32[32,2,32,256]{3,2,1,0:T(8,128)}, u32[]{:S(2)}, u32[]{:S(2)}) async-start(f32[32,2,32,256]{3,2,1,0:T(8,128)} %range_compress.2), calls=%async_computation | async-start | bytes 4194304 | tf_op jit(solution)/shard_map/all_to_all | solution.py:526
  79.9 5.4 %copy-start.17 = (s32[1,2]{1,0:T(1,128)S(1)}, s32[1,2]{1,0:T(1,128)}, u32[]{:S(2)}) copy-start(s32[1,2]{1,0:T(1,128)} %param.25) | copy-start | bytes 28
  79.9 5.4 %copy-start.18 = (s32[2]{0:T(128)S(1)}, s32[2]{0:T(128)}, u32[]{:S(2)}) copy-start(s32[2]{0:T(128)} %constant.32.clone) | copy-start | bytes 28
  79.9 5.4 %copy-start = (bf16[8,256,256]{2,1,0:T(8,128)(2,1)S(1)}, bf16[8,256,256]{2,1,0:T(8,128)(2,1)}, u32[]{:S(2)}) copy-start(bf16[8,256,256]{2,1,0:T(8,128)(2,1)} %constant.36.clone.refs_2_) | copy-start | bytes 3145732
  79.9 5.4 %copy-start.1 = (bf16[8,256,256]{2,1,0:T(8,128)(2,1)S(1)}, bf16[8,256,256]{2,1,0:T(8,128)(2,1)}, u32[]{:S(2)}) copy-start(bf16[8,256,256]{2,1,0:T(8,128)(2,1)} %constant.37.clone.refs_3_) | copy-start | bytes 3145732
  79.9 5.4 %copy-start.10 = (bf16[1024,256]{1,0:T(8,128)(2,1)S(1)}, bf16[1024,256]{1,0:T(8,128)(2,1)}, u32[]{:S(2)}) copy-start(bf16[1024,256]{1,0:T(8,128)(2,1)} %constant.40.clone.refs_6_) | copy-start | bytes 1572868
  85.2 9.3 %copy-start.16 = (f32[8,1,2]{0,2,1:T(2,128)S(1)}, f32[8,1,2]{0,2,1:T(2,128)}, u32[]{:S(2)}) copy-start(f32[8,1,2]{0,2,1:T(2,128)} %param.26) | copy-start | bytes 196
  85.3 1.2 copy-start.2
  86.5 1.2 copy-start.4
  93.2 25.8 %collective-permute-start = (f32[8,2,2,1,256]{4,3,2,1,0:T(1,128)S(1)}, f32[8,2,2,1,256]{4,3,2,1,0:T(1,128)S(1)}, u32[]{:S(2)}, u32[]{:S(2)}) collective-permute-start(f32[8,2,2,1,256]{4,3,2,1,0:T(1,128)S(1)} %slice.4), channel_id=1, source_target_pairs={{4,0},{8,4},{12,8},{16,12},{20,16},{24,20},{28,24},{1,28},{5,1},{9... | collective-permute-start | bytes 98312 | tf_op jit(solution)/shard_map/ppermute | solution.py:556
  119.0 1.2 copy-start.3
  120.2 1.2 copy-start.5

commit v3 on v2

--- a/solution.py
+++ b/solution.py
@@ -23,6 +23,10 @@
 
 def sub(left, right):
     return (left[0] - right[0], left[1] - right[1])
+
+
+def times(value, cosine, sine):
+    return (value[0] * cosine - value[1] * sine, value[0] * sine + value[1] * cosine)
 
 
 def turn(value, sign):
@@ -119,7 +123,9 @@
 def lag_tables(plan):
     base, samples = plan.base, plan.samples
     index = np.arange(base)
-    table = host_parts(real_form(*unit(index[:, None] * index[None, :], samples, -1.0)) / samples)
+    table = host_parts(
+        np.concatenate(unit(index[:, None] * index[None, :], samples, -1.0), axis=1) / samples
+    )
     block = np.arange(RADIX)[:, None]
     turns = np.stack(
         unit(block * index[None, :], RADIX, -1.0)
@@ -133,18 +139,18 @@
     lane = lax.broadcasted_iota(jnp.int32, (RADIX, base), 1)
     chosen = lane % RADIX == lax.broadcasted_iota(jnp.int32, (RADIX, base), 0)
     rows = []
-    for e in range(RADIX):
-        both = []
-        for c in range(2):
+    for c in range(2):
+        for e in range(RADIX):
             block = jnp.broadcast_to(filter_ref[c : c + 1, e * base : (e + 1) * base], (RADIX, base))
-            both.append(jnp.where(chosen, block, 0.0))
-        rows.append(jnp.concatenate(both, axis=1))
+            rows.append(jnp.where(chosen, block, 0.0))
     high, low = two_parts(jnp.concatenate(rows, axis=0))
     sums = three_products(high, low, table_high[...], table_low[...], ((1,), (0,)))
     real, imag = 0.0, 0.0
     for e in range(RADIX):
-        part_real = sums[e * RADIX : (e + 1) * RADIX, :base]
-        part_imag = sums[e * RADIX : (e + 1) * RADIX, base:]
+        by_real = sums[e * RADIX : (e + 1) * RADIX]
+        by_imag = sums[(RADIX + e) * RADIX : (RADIX + e + 1) * RADIX]
+        part_real = by_real[:, :base] - by_imag[:, base:]
+        part_imag = by_real[:, base:] + by_imag[:, :base]
         cosine, sine = turn_ref[0, e : e + 1, :], turn_ref[1, e : e + 1, :]
         real = real + part_real * cosine - part_imag * sine
         imag = imag + part_real * sine + part_imag * cosine
@@ -162,8 +168,8 @@
 
 
 def compress_kernel(
-    plan, part, filter_ref, table_high, table_low, turn_ref, raw_ref, out_ref,
-    raw, t_high, t_low, y_high, y_low, z_ref, sems,
+    plan, part, filter_ref, high_any, low_any, turn_any, raw_ref, out_ref,
+    table_high, table_low, turn_ref, raw, t_high, t_low, y_high, y_low, z_ref, sems, table_sems,
 ):
     base, blocks = plan.base, plan.blocks
     tiles = plan.rows // ROWS
@@ -175,7 +181,17 @@
         rows = pl.ds(at * piece, piece)
         return pltpu.make_async_copy(raw_ref.at[:, rows, :], raw.at[:, rows, :], sems.at[at])
 
+    tables = fetch(
+        [
+            pltpu.make_async_copy(source, target, table_sems.at[at])
+            for at, (source, target) in enumerate(
+                ((high_any, table_high), (low_any, table_low), (turn_any, turn_ref))
+            )
+        ]
+    )
     fetch([raw_copy(at) for at in range(pieces)])
+    for copy in tables:
+        copy.wait()
     lags = lag_vectors(plan, filter_ref, table_high, table_low, turn_ref)
 
     for d in range(RADIX):
@@ -245,14 +261,16 @@
     chunk = plan.blocks * plan.rows
     whole = pl.BlockSpec(memory_space=pltpu.VMEM)
     bytes_moved = 4 * (raw.size + raw.size // plan.parts)
+    tables = lag_tables(plan)
     return pl.pallas_call(
         functools.partial(compress_kernel, plan, part),
         out_shape=jax.ShapeDtypeStruct(
             (plan.strips * plan.epochs, 2, plan.rows, plan.pulses), jnp.float32
         ),
-        in_specs=[whole] * 4 + [pl.BlockSpec(memory_space=pl.ANY)],
+        in_specs=[whole] + [pl.BlockSpec(memory_space=pltpu.HBM)] * 4,
         out_specs=whole,
         scratch_shapes=[
+            *[pltpu.VMEM(table.shape, table.dtype) for table in tables],
             pltpu.VMEM(raw.shape, jnp.float32),
             pltpu.VMEM((RADIX, 2 * chunk, 2 * plan.base), jnp.bfloat16),
             pltpu.VMEM((RADIX, 2 * chunk, 2 * plan.base), jnp.bfloat16),
@@ -260,6 +278,7 @@
             pltpu.VMEM((RADIX, plan.pulses, 2 * plan.base), jnp.bfloat16),
             pltpu.VMEM((RADIX, 2 * chunk, plan.pulses), jnp.float32),
             pltpu.SemaphoreType.DMA((4,)),
+            pltpu.SemaphoreType.DMA((3,)),
         ],
         compiler_params=pltpu.CompilerParams(vmem_limit_bytes=VMEM_BYTES),
         cost_estimate=pl.CostEstimate(
@@ -268,68 +287,78 @@
             transcendentals=0,
         ),
         name="range_compress",
-    )(range_filter, *lag_tables(plan), raw)
+    )(range_filter, *tables, raw)
 
 
 def focus_kernel(plan, part, final, *refs):
-    field_any, filter_any, fh_any, fl_any, bh_any, bl_any, sum_any = refs[:7]
+    field_any, filter_any, high_any, low_any, twiddle_any, sum_any = refs[:6]
     if final:
-        weight_ref, before_ref, halo_ref, out_ref = refs[7:11]
+        weight_ref, before_ref, halo_ref, out_ref = refs[6:10]
     else:
-        (out_ref,) = refs[7:8]
-    scratch = refs[11 if final else 8 :]
+        (out_ref,) = refs[6:7]
+    scratch = refs[10 if final else 7 :]
     (
-        field_ref, filter_ref, fh_ref, fl_ref, bh_ref, bl_ref, sum_ref,
-        z_ref, scene_ref, product_ref, field_sems, table_sems,
-    ) = scratch[:12]
+        field_ref, filter_ref, table_high, table_low, twiddle_ref, sum_ref,
+        y_high, y_low, z_ref, scene_ref, product_ref, field_sems, table_sems,
+    ) = scratch[:13]
     rows, lanes, epochs, looks = plan.rows, plan.lanes, plan.epochs, plan.looks
+    step = 2 * ROWS
+    group = max(1, step // rows)
     per_block = field_ref.shape[-1] // lanes
 
     def field_copy(j):
         return pltpu.make_async_copy(field_any.at[:, j], field_ref.at[:, j], field_sems.at[j])
 
+    tables = [
+        pltpu.make_async_copy(source, target, table_sems.at[at])
+        for at, (source, target) in enumerate(
+            (
+                (twiddle_any, twiddle_ref),
+                (high_any, table_high),
+                (low_any, table_low),
+                (filter_any.at[part], filter_ref),
+                (sum_any, sum_ref),
+            )
+        )
+    ]
+    fetch(tables[:1])
     fetch([field_copy(j) for j in range(epochs)])
-    tables = fetch(
-        [
-            pltpu.make_async_copy(source, target, table_sems.at[at])
-            for at, (source, target) in enumerate(
-                (
-                    (fh_any, fh_ref),
-                    (fl_any, fl_ref),
-                    (filter_any.at[part], filter_ref),
-                    (bh_any, bh_ref),
-                    (bl_any, bl_ref),
-                    (sum_any, sum_ref),
-                )
-            )
+    fetch(tables[1:])
+    tables[0].wait()
+
+    def rows_of(strip, j, c, top, start):
+        some = [
+            field_ref[strip, j * group + g, c, top : top + min(rows, step), start : start + lanes]
+            for g in range(group)
         ]
-    )
+        return some[0] if group == 1 else jnp.concatenate(some, axis=0)
 
     def forward(j, carry):
-        field_copy(j).wait()
-        for top in range(0, rows, ROWS):
+        for g in range(group):
+            field_copy(j * group + g).wait()
+        for top in range(0, rows, step):
             x = []
             for a in range(RADIX):
                 strip, start = a // per_block, a % per_block * lanes
-                x.append(
-                    tuple(
-                        field_ref[strip, j, c, top : top + ROWS, start : start + lanes]
-                        for c in range(2)
-                    )
-                )
+                x.append(tuple(rows_of(strip, j, c, top, start) for c in range(2)))
+            at = pl.ds(pl.multiple_of(j * group * rows + top, step), step)
             for d, value in enumerate(dft8(x, -1.0)):
+                if d > 0:
+                    value = times(value, twiddle_ref[0, d : d + 1, :], twiddle_ref[1, d : d + 1, :])
                 for c in range(2):
-                    at = pl.ds(pl.multiple_of(j * rows + top, ROWS), ROWS)
-                    z_ref[d, at, c * lanes : (c + 1) * lanes] = value[c]
+                    high, low = two_parts(value[c])
+                    y_high[d, at, c * lanes : (c + 1) * lanes] = high
+                    y_low[d, at, c * lanes : (c + 1) * lanes] = low
         return carry
 
-    lax.fori_loop(0, epochs, forward, 0)
-    for copy in tables:
+    lax.fori_loop(0, epochs // group, forward, 0)
+    for copy in tables[1:]:
         copy.wait()
 
     for d in range(RADIX):
-        high, low = two_parts(z_ref[d])
-        spectrum = three_products(high, low, fh_ref[d], fl_ref[d], ((1,), (0,)))
+        spectrum = three_products(
+            y_high[d], y_low[d], table_high[...], table_low[...], ((1,), (0,))
+        )
         spectrum = spectrum.reshape(epochs, rows, 2 * lanes)
         real, imag = spectrum[:, :, :lanes], spectrum[:, :, lanes:]
         by_real, by_imag = filter_ref[0, d][None], filter_ref[1, d][None]
@@ -337,7 +366,7 @@
             [real * by_real - imag * by_imag, real * by_imag + imag * by_real], axis=2
         )
         high, low = two_parts(spectrum.reshape(epochs * rows, 2 * lanes))
-        z_ref[d] = three_products(high, low, bh_ref[d], bl_ref[d], ((1,), (0,)))
+        z_ref[d] = three_products(high, low, table_high[...], table_low[...], ((1,), (1,)))
 
     scene_ref[0] = jnp.zeros_like(scene_ref[0])
     scene_ref[1] = jnp.zeros_like(scene_ref[1])
@@ -346,7 +375,11 @@
         for top in range(0, rows, ROWS):
             at = pl.ds(pl.multiple_of(j * rows + top, ROWS), ROWS)
             z = [
-                tuple(z_ref[d, at, c * lanes : (c + 1) * lanes] for c in range(2))
+                times(
+                    tuple(z_ref[d, at, c * lanes : (c + 1) * lanes] for c in range(2)),
+                    twiddle_ref[2, d : d + 1, :],
+                    twiddle_ref[3, d : d + 1, :],
+                )
                 for d in range(RADIX)
             ]
             for a, value in enumerate(dft8(z, 1.0)):
@@ -382,12 +415,17 @@
     products = product_ref[...].reshape(total, plan.azimuth)
     high, low = two_parts(products)
     weights = sum_ref[...]
-    looked = jnp.dot(high, weights, preferred_element_type=jnp.float32) + jnp.dot(
-        low, weights, preferred_element_type=jnp.float32
-    )
+    looked = []
+    for start in range(0, plan.azimuth, weights.shape[0]):
+        columns = slice(start, start + weights.shape[0])
+        looked.append(
+            jnp.dot(high[:, columns], weights, preferred_element_type=jnp.float32)
+            + jnp.dot(low[:, columns], weights, preferred_element_type=jnp.float32)
+        )
+    looked = jnp.concatenate(looked, axis=1)
     looked = looked.reshape(epochs, 2, 2, looks, plan.azimuth_looks)
     if final:
-        looked_ref, slope_ref = scratch[12:]
+        looked_ref, slope_ref = scratch[13:]
         for at, before in enumerate(before_ref):
             looked_ref[:, :, :, at * looks : (at + 1) * looks, :] = before[...]
         looked_ref[:, :, :, part * looks :, :] = looked
@@ -426,14 +464,12 @@
 
 def focus_tables(plan):
     lanes = plan.lanes
-    b = np.arange(lanes)[None, :, None]
-    k = RADIX * np.arange(lanes)[None, None, :] + np.arange(RADIX)[:, None, None]
-    cosine, sine = unit(b * k, plan.azimuth, -1.0)
-    ahead = host_parts(real_form(cosine, sine))
-    cosine, sine = cosine.swapaxes(1, 2), -sine.swapaxes(1, 2)
-    back = host_parts(real_form(cosine, sine) / plan.azimuth)
-    sums = (np.arange(plan.azimuth)[:, None] // LOOK == np.arange(plan.azimuth_looks)[None, :]) / LOOK
-    return ahead + back + (sums.astype(ml_dtypes.bfloat16),)
+    index = np.arange(lanes)
+    table = host_parts(real_form(*unit(index[:, None] * index[None, :], lanes, -1.0)))
+    cosine, sine = unit(np.arange(RADIX)[:, None] * index[None, :], plan.azimuth, -1.0)
+    twiddles = np.stack([cosine, sine, cosine / plan.azimuth, -sine / plan.azimuth])
+    sums = np.arange(plan.azimuth // 2)[:, None] // LOOK == np.arange(plan.azimuth_looks // 2)[None, :]
+    return table + (twiddles.astype(np.float32), (sums / LOOK).astype(ml_dtypes.bfloat16))
 
 
 def focus(plan, part, field, spectrum, finish=None):
@@ -444,16 +480,18 @@
     looked = (plan.epochs, 2, 2, plan.looks, plan.azimuth_looks)
     gradients = (plan.epochs, 2, plan.looks * plan.parts, plan.azimuth_looks)
     operands = [field, spectrum, *tables]
-    in_specs = [pl.BlockSpec(memory_space=pl.ANY)] * 7
+    in_specs = [pl.BlockSpec(memory_space=pltpu.HBM)] * 6
     scratch = [
         pltpu.VMEM(field.shape, jnp.float32),
         pltpu.VMEM(spectrum.shape[1:], jnp.float32),
-        *[pltpu.VMEM(table.shape, jnp.bfloat16) for table in tables],
+        *[pltpu.VMEM(table.shape, table.dtype) for table in tables],
+        pltpu.VMEM((RADIX, total, 2 * lanes), jnp.bfloat16),
+        pltpu.VMEM((RADIX, total, 2 * lanes), jnp.bfloat16),
         pltpu.VMEM((RADIX, total, 2 * lanes), jnp.float32),
         pltpu.VMEM((plan.epochs + 2, 2, plan.rows, plan.azimuth), jnp.float32),
         pltpu.VMEM((plan.epochs, 2, 2, plan.looks, plan.azimuth), jnp.float32),
         pltpu.SemaphoreType.DMA((plan.epochs,)),
-        pltpu.SemaphoreType.DMA((6,)),
+        pltpu.SemaphoreType.DMA((5,)),
     ]
     shape = looked
     if finish is not None:
@@ -485,8 +523,8 @@
     if count is None:
         focus_kernel(plan, part, False, *refs)
         return
-    before = refs[8 : 8 + count]
-    focus_kernel(plan, part, True, *refs[:8], before, *refs[8 + count :])
+    before = refs[7 : 7 + count]
+    focus_kernel(plan, part, True, *refs[:7], before, *refs[7 + count :])
 
 
 def slope_kernel(plan, weight_ref, looked_ref, halo_ref, out_ref, slope_ref):

time: 141 us -> 139 us (0.986)
  local copies, waits for them, and re-layouts: 24.3 us -> 22.2 us
    unnamed x38 -> x34, local copies, waits for them, and re-layouts: 8.5 us -> 6.34 us
where the time goes in v3:
time: 139 us; the launch traced here: 138 us
  waiting for transfers between devices  57.1 us (41%)
  Pallas kernels  24.8 us (18%)
  local copies, waits for them, and re-layouts  22.2 us (16%)
  blocking collectives  21.4 us (15%)
  starting transfers between devices  12.6 us (9%)
    all_to_all x2, waiting for transfers between devices, exchange(): lax.all_to_all(block, OWNERS, split_axis=0, concat_axis=0, tiled=True)  57.1 us
    pallas_call x2, Pallas kernels, focus(): pl.pallas_call(functools.partial(focus_kernel_flat, plan, part, len(befor...  12.8 us
    pallas_call x2, Pallas kernels, compress(): pl.pallas_call(functools.partial(compress_kernel, plan, part), out_shape=...  12 us
    all_to_all x2, starting transfers between devices, exchange(): lax.all_to_all(block, OWNERS, split_axis=0, concat_axis=0, tiled=True)  11.3 us
    all_gather x1, blocking collectives, per_device(): lax.all_gather(inversion[:, 0, :] * usable[None, :], 'acq', axis=1, tiled...  11.2 us
    all_to_all x1, blocking collectives, per_device(): lax.all_to_all(gradients, 'acq', split_axis=0, concat_axis=0, tiled=True)  10.2 us
    reshape x1, local copies, waits for them, and re-layouts, own_filter(): own = own.reshape(2, plan.lanes, RADIX, plan.parts, plan.looks, LOOK)  7.05 us
    unnamed x34, local copies, waits for them, and re-layouts  6.34 us
  transfers between devices with their start and end apart: 3, of which 2 were waited for; matrix products, arithmetic and copies ran while one was open for 11% of the time, Pallas kernels for 8%

profile of v3, /device:TPU:0, one launch (start us, length us, event | category | flops | bytes accessed | tf_op | source)
XLA Modules:
  0.0 138.3 jit_solution(11077878117853479211)
XLA Ops:
  0.0 0.9 copy-done.2
  1.0 0.9 copy-done.4
  1.9 0.8 copy-done.6
  2.7 0.7 copy-done.8
  3.4 6.0 %range_compress.3 = f32[32,2,32,256]{3,2,1,0:T(8,128)} custom-call(f32[2,2048]{1,0:T(2,128)S(1)} %copy-done.8, bf16[256,512]{1,0:T(8,128)(2,1)S(1)} %copy-done.2, bf16[256,512]{1,0:T(8,128)(2,1)S(1)} %copy-done.4, f32[4,8,256]{2,1,0:T(8,128)S(1)} %copy-done.6, f32[2,256,2048]{2,1,0:T(8,128)} %bitcast.17), custom_call_target="tpu_custom_call" | custom-call | flops 1610612736 | bytes 6291456 | tf_op jit(solution)/shard_map/range_compress/pallas_call | solution.py:265
  9.4 7.3 %all-to-all-start.1 = ((f32[32,2,32,256]{3,2,1,0:T(8,128)}), f32[32,2,32,256]{3,2,1,0:T(8,128)S(1)}, u32[]{:S(2)}, u32[]{:S(2)}) async-start(f32[32,2,32,256]{3,2,1,0:T(8,128)} %range_compress.3), calls=%async_computation.1 | async-start | bytes 4194304 | tf_op jit(solution)/shard_map/all_to_all | solution.py:564
  16.7 6.0 %range_compress.2 = f32[32,2,32,256]{3,2,1,0:T(8,128)} custom-call(f32[2,2048]{1,0:T(2,128)S(1)} %copy-done.9, bf16[256,512]{1,0:T(8,128)(2,1)S(1)} %copy-done.3, bf16[256,512]{1,0:T(8,128)(2,1)S(1)} %copy-done.5, f32[4,8,256]{2,1,0:T(8,128)S(1)} %copy-done.7, f32[2,256,2048]{2,1,0:T(8,128)} %bitcast.18), custom_call_target="tpu_custom_call" | custom-call | flops 1610612736 | bytes 6291456 | tf_op jit(solution)/shard_map/range_compress/pallas_call | solution.py:265
  22.8 42.8 %all-to-all-done.1 = f32[32,2,32,256]{3,2,1,0:T(8,128)S(1)} async-done(((f32[32,2,32,256]{3,2,1,0:T(8,128)}), f32[32,2,32,256]{3,2,1,0:T(8,128)S(1)}, u32[]{:S(2)}, u32[]{:S(2)}) %all-to-all-start.1) | async-done | bytes 2097184 | tf_op jit(solution)/shard_map/all_to_all | solution.py:564
  65.6 1.3 copy-done
  66.9 4.0 %all-to-all-start = ((f32[32,2,32,256]{3,2,1,0:T(8,128)}), f32[32,2,32,256]{3,2,1,0:T(8,128)S(1)}, u32[]{:S(2)}, u32[]{:S(2)}) async-start(f32[32,2,32,256]{3,2,1,0:T(8,128)} %range_compress.2), calls=%async_computation | async-start | bytes 4194304 | tf_op jit(solution)/shard_map/all_to_all | solution.py:564
  70.9 1.6 %constant_dynamic-slice_fusion = f32[2,1024,64]{2,1,0:T(8,128)S(1)} fusion(f32[2,1024,512]{2,1,0:T(8,128)} %param.22, s32[]{:T(128)S(6)} %select_n.3), kind=kLoop, calls=%fused_computation.2 | loop fusion | bytes 1048580 | tf_op jit(solution)/shard_map/dynamic_slice | solution.py:557
  72.5 1.2 copy.26
  73.7 7.0 %reshape.19 = f32[2,128,8,2,8,4]{2,1,5,4,3,0:T(8,128)} reshape(f32[2,1024,64]{1,2,0:T(8,128)} %copy.26) | data formatting | bytes 1048576 | tf_op jit(solution)/shard_map/reshape | solution.py:558
  80.8 5.2 %copy.27 = f32[2,2,8,4,8,128]{5,4,3,2,1,0:T(8,128)S(1)} copy(f32[2,2,8,4,8,128]{2,5,3,4,0,1:T(8,128)} %bitcast.16) | data formatting | bytes 1048576 | tf_op jit(solution)/shard_map/transpose | solution.py:560
  86.1 1.6 %copy-done.1 = f32[32,2,32,256]{3,2,1,0:T(8,128)S(1)} copy-done((f32[32,2,32,256]{3,2,1,0:T(8,128)S(1)}, f32[32,2,32,256]{3,2,1,0:T(8,128)}, u32[]{:S(2)}) %copy-start.1) | copy-done | bytes 2097176
  87.7 5.3 %azimuth_focus.2.refs_7_ = f32[8,2,2,8,256]{4,3,2,1,0:T(8,128)S(1)} custom-call(f32[4,8,2,32,256]{4,3,2,1,0:T(8,128)S(1)} %bitcast.13, f32[2,2,8,32,128]{4,3,2,1,0:T(8,128)S(1)} %bitcast.14, bf16[256,256]{1,0:T(8,128)(2,1)S(1)} %copy-done.10, bf16[256,256]{1,0:T(8,128)(2,1)S(1)} %copy-done.11, f32[4,8,128]{2,1,0:T(8,128)S(1)} %copy-done.13, ...), custom_call_target="tpu_custom_call" | custom-call | flops 1610612736 | bytes 6291456 | tf_op jit(solution)/shard_map/azimuth_focus/pallas_call | solution.py:506
  93.0 1.3 collective-permute-start
  94.3 0.1 broadcast_multiply_fusion
  94.4 11.2 %all_gather.4 = f32[8,8,2]{0,2,1:T(2,128)S(1)} all-gather(f32[8,1,2]{0,2,1:T(2,128)S(1)} %broadcast_multiply_fusion), channel_id=1, replica_groups=mesh['acq'=8,'strip'=4] {'acq'}, dimensions={1}, use_global_device_ids=true | all-gather | bytes 576 | tf_op jit(solution)/shard_map/all_gather | solution.py:582
  105.5 0.1 copy.28.refs_6_
  105.6 14.3 %all-to-all-done = f32[32,2,32,256]{3,2,1,0:T(8,128)S(1)} async-done(((f32[32,2,32,256]{3,2,1,0:T(8,128)}), f32[32,2,32,256]{3,2,1,0:T(8,128)S(1)}, u32[]{:S(2)}, u32[]{:S(2)}) %all-to-all-start) | async-done | bytes 2097184 | tf_op jit(solution)/shard_map/all_to_all | solution.py:564
  119.8 7.5 %azimuth_focus.3 = f32[8,2,16,256]{3,2,1,0:T(8,128)S(1)} custom-call(f32[4,8,2,32,256]{4,3,2,1,0:T(8,128)S(1)} %bitcast.12, f32[2,2,8,32,128]{4,3,2,1,0:T(8,128)S(1)} %bitcast.15, bf16[256,256]{1,0:T(8,128)(2,1)S(1)} %copy-done.10, bf16[256,256]{1,0:T(8,128)(2,1)S(1)} %copy-done.11, f32[4,8,128]{2,1,0:T(8,128)S(1)} %copy-done.13, ...), custom_call_target="tpu_custom_call" | custom-call | flops 1610612736 | bytes 6291456 | tf_op jit(solution)/shard_map/azimuth_focus/pallas_call | solution.py:506
  127.4 10.2 %all_to_all.15 = f32[8,2,16,256]{3,2,1,0:T(8,128)S(1)} all-to-all(f32[8,2,16,256]{3,2,1,0:T(8,128)S(1)} %azimuth_focus.3), channel_id=1, replica_groups=mesh['acq'=8,'strip'=4] {'acq'}, dimensions={0} | all-to-all | bytes 524288 | tf_op jit(solution)/shard_map/all_to_all | solution.py:603
  137.6 0.7 copy.29
  (31 shorter events, 0.1 us)
Async XLA Ops:
  0.0 0.9 copy-start.2
  1.0 0.9 copy-start.4
  1.9 0.8 copy-start.6
  2.7 0.7 copy-start.8
  3.4 13.3 %copy-start.3 = (bf16[256,512]{1,0:T(8,128)(2,1)S(1)}, bf16[256,512]{1,0:T(8,128)(2,1)}, u32[]{:S(2)}) copy-start(bf16[256,512]{1,0:T(8,128)(2,1)} %constant.31.clone.high_any) | copy-start | bytes 786436
  3.4 13.3 %copy-start.5 = (bf16[256,512]{1,0:T(8,128)(2,1)S(1)}, bf16[256,512]{1,0:T(8,128)(2,1)}, u32[]{:S(2)}) copy-start(bf16[256,512]{1,0:T(8,128)(2,1)} %constant.32.clone.low_any) | copy-start | bytes 786436
  3.4 13.3 %copy-start.7 = (f32[4,8,256]{2,1,0:T(8,128)S(1)}, f32[4,8,256]{2,1,0:T(8,128)}, u32[]{:S(2)}) copy-start(f32[4,8,256]{2,1,0:T(8,128)} %constant.33.clone.turn_any) | copy-start | bytes 98308
  3.4 13.3 %copy-start.9 = (f32[2,2048]{1,0:T(2,128)S(1)}, f32[2,2048]{1,0:T(2,128)}, u32[]{:S(2)}) copy-start(f32[2,2048]{1,0:T(2,128)} %filter_ref.3) | copy-start | bytes 49156
  9.4 56.2 %all-to-all-start.1 = ((f32[32,2,32,256]{3,2,1,0:T(8,128)}), f32[32,2,32,256]{3,2,1,0:T(8,128)S(1)}, u32[]{:S(2)}, u32[]{:S(2)}) async-start(f32[32,2,32,256]{3,2,1,0:T(8,128)} %range_compress.3), calls=%async_computation.1 | async-start | bytes 4194304 | tf_op jit(solution)/shard_map/all_to_all | solution.py:564
  65.6 1.3 copy-start
  66.9 52.9 %all-to-all-start = ((f32[32,2,32,256]{3,2,1,0:T(8,128)}), f32[32,2,32,256]{3,2,1,0:T(8,128)S(1)}, u32[]{:S(2)}, u32[]{:S(2)}) async-start(f32[32,2,32,256]{3,2,1,0:T(8,128)} %range_compress.2), calls=%async_computation | async-start | bytes 4194304 | tf_op jit(solution)/shard_map/all_to_all | solution.py:564
  80.7 5.3 %copy-start.15 = (s32[1,2]{1,0:T(1,128)S(1)}, s32[1,2]{1,0:T(1,128)}, u32[]{:S(2)}) copy-start(s32[1,2]{1,0:T(1,128)} %param.23) | copy-start | bytes 28
  80.7 5.3 %copy-start.16 = (s32[2]{0:T(128)S(1)}, s32[2]{0:T(128)}, u32[]{:S(2)}) copy-start(s32[2]{0:T(128)} %constant.30.clone) | copy-start | bytes 28
  80.7 5.3 %copy-start.10 = (bf16[256,256]{1,0:T(8,128)(2,1)S(1)}, bf16[256,256]{1,0:T(8,128)(2,1)}, u32[]{:S(2)}) copy-start(bf16[256,256]{1,0:T(8,128)(2,1)} %constant.34.clone.refs_2_) | copy-start | bytes 393220
  80.7 5.3 %copy-start.11 = (bf16[256,256]{1,0:T(8,128)(2,1)S(1)}, bf16[256,256]{1,0:T(8,128)(2,1)}, u32[]{:S(2)}) copy-start(bf16[256,256]{1,0:T(8,128)(2,1)} %constant.35.clone.refs_3_) | copy-start | bytes 393220
  80.7 5.3 %copy-start.12 = (bf16[512,128]{1,0:T(8,128)(2,1)S(1)}, bf16[512,128]{1,0:T(8,128)(2,1)}, u32[]{:S(2)}) copy-start(bf16[512,128]{1,0:T(8,128)(2,1)} %constant.37.clone.refs_5_) | copy-start | bytes 393220
  80.8 5.3 %copy-start.13 = (f32[4,8,128]{2,1,0:T(8,128)S(1)}, f32[4,8,128]{2,1,0:T(8,128)}, u32[]{:S(2)}) copy-start(f32[4,8,128]{2,1,0:T(8,128)} %constant.36.clone.refs_4_) | copy-start | bytes 49156
  86.0 8.3 %copy-start.14 = (f32[8,1,2]{0,2,1:T(2,128)S(1)}, f32[8,1,2]{0,2,1:T(2,128)}, u32[]{:S(2)}) copy-start(f32[8,1,2]{0,2,1:T(2,128)} %param.24) | copy-start | bytes 196
  86.1 1.6 %copy-start.1 = (f32[32,2,32,256]{3,2,1,0:T(8,128)S(1)}, f32[32,2,32,256]{3,2,1,0:T(8,128)}, u32[]{:S(2)}) copy-start(f32[32,2,32,256]{3,2,1,0:T(8,128)} %copy-done) | copy-start | bytes 6291460
  93.0 26.9 %collective-permute-start = (f32[8,2,2,1,256]{4,3,2,1,0:T(1,128)S(1)}, f32[8,2,2,1,256]{4,3,2,1,0:T(1,128)S(1)}, u32[]{:S(2)}, u32[]{:S(2)}) collective-permute-start(f32[8,2,2,1,256]{4,3,2,1,0:T(1,128)S(1)} %slice.4), channel_id=1, source_target_pairs={{4,0},{8,4},{12,8},{16,12},{20,16},{24,20},{28,24},{1,28},{5,1},{9... | collective-permute-start | bytes 98312 | tf_op jit(solution)/shard_map/ppermute | solution.py:594

commit v4 on v3

--- a/solution.py
+++ b/solution.py
@@ -13,7 +13,7 @@
 LOOK = 4
 RADIX = 8
 ROWS = 8
-VMEM_BYTES = 48 * 1024 * 1024
+VMEM_BYTES = 60 * 1024 * 1024
 OWNERS = ("strip", "acq")
 
 
@@ -108,6 +108,9 @@
         self.blocks = self.base // self.owned
         self.lanes = self.azimuth // RADIX
         self.azimuth_looks = self.azimuth // LOOK
+
+    def outputs(self, form):
+        return self.strips if form == "slots" else 1
 
     def tile_shift(self, part, block, tile):
         start = block * self.owned + part * self.rows
@@ -168,9 +171,12 @@
 
 
 def compress_kernel(
-    plan, part, filter_ref, high_any, low_any, turn_any, raw_ref, out_ref,
-    table_high, table_low, turn_ref, raw, t_high, t_low, y_high, y_low, z_ref, sems, table_sems,
+    plan, part, form, filter_ref, high_any, low_any, turn_any, raw_ref, *refs
 ):
+    outs, scratch = refs[: plan.outputs(form)], refs[plan.outputs(form) :]
+    (
+        table_high, table_low, turn_ref, raw, t_high, t_low, y_high, y_low, z_ref, sems, table_sems,
+    ) = scratch
     base, blocks = plan.base, plan.blocks
     tiles = plan.rows // ROWS
     chunk = blocks * plan.rows
@@ -254,21 +260,32 @@
             ]
             for a, value in enumerate(dft8(z, 1.0)):
                 for c in range(2):
-                    out_ref[a * blocks + block, c, tile * ROWS : (tile + 1) * ROWS, :] = value[c]
-
-
-def compress(plan, part, range_filter, raw):
+                    slot, owner = divmod(a * blocks + block, plan.epochs)
+                    rows = slice(tile * ROWS, (tile + 1) * ROWS)
+                    if form == "slots":
+                        outs[slot][owner, c, rows, :] = value[c]
+                    elif form == "owners":
+                        outs[0][owner, slot, c, rows, :] = value[c]
+                    else:
+                        outs[0][slot, owner, c, rows, :] = value[c]
+
+
+def compress(plan, part, form, range_filter, raw):
     chunk = plan.blocks * plan.rows
     whole = pl.BlockSpec(memory_space=pltpu.VMEM)
     bytes_moved = 4 * (raw.size + raw.size // plan.parts)
     tables = lag_tables(plan)
+    slab = (2, plan.rows, plan.pulses)
+    shape = {
+        "slots": (plan.epochs,) + slab,
+        "owners": (plan.epochs, plan.strips) + slab,
+        "all": (plan.strips, plan.epochs) + slab,
+    }[form]
     return pl.pallas_call(
-        functools.partial(compress_kernel, plan, part),
-        out_shape=jax.ShapeDtypeStruct(
-            (plan.strips * plan.epochs, 2, plan.rows, plan.pulses), jnp.float32
-        ),
+        functools.partial(compress_kernel, plan, part, form),
+        out_shape=[jax.ShapeDtypeStruct(shape, jnp.float32)] * plan.outputs(form),
         in_specs=[whole] + [pl.BlockSpec(memory_space=pltpu.HBM)] * 4,
-        out_specs=whole,
+        out_specs=[whole] * plan.outputs(form),
         scratch_shapes=[
             *[pltpu.VMEM(table.shape, table.dtype) for table in tables],
             pltpu.VMEM(raw.shape, jnp.float32),
@@ -290,13 +307,13 @@
     )(range_filter, *tables, raw)
 
 
-def focus_kernel(plan, part, final, *refs):
-    field_any, filter_any, high_any, low_any, twiddle_any, sum_any = refs[:6]
+def focus_kernel(plan, part, final, field_at, *refs):
+    filter_any, high_any, low_any, twiddle_any, sum_any = refs[:5]
     if final:
-        weight_ref, before_ref, halo_ref, out_ref = refs[6:10]
+        weight_ref, before_ref, halo_ref, out_ref = refs[5:9]
     else:
-        (out_ref,) = refs[6:7]
-    scratch = refs[10 if final else 7 :]
+        (out_ref,) = refs[5:6]
+    scratch = refs[9 if final else 6 :]
     (
         field_ref, filter_ref, table_high, table_low, twiddle_ref, sum_ref,
         y_high, y_low, z_ref, scene_ref, product_ref, field_sems, table_sems,
@@ -306,8 +323,11 @@
     group = max(1, step // rows)
     per_block = field_ref.shape[-1] // lanes
 
-    def field_copy(j):
-        return pltpu.make_async_copy(field_any.at[:, j], field_ref.at[:, j], field_sems.at[j])
+    def field_copies(j):
+        return [
+            pltpu.make_async_copy(field_at(j, at), field_ref.at[at, j], field_sems.at[j, at])
+            for at in range(field_ref.shape[0])
+        ]
 
     tables = [
         pltpu.make_async_copy(source, target, table_sems.at[at])
@@ -322,7 +342,8 @@
         )
     ]
     fetch(tables[:1])
-    fetch([field_copy(j) for j in range(epochs)])
+    for j in range(epochs):
+        fetch(field_copies(j))
     fetch(tables[1:])
     tables[0].wait()
 
@@ -335,7 +356,8 @@
 
     def forward(j, carry):
         for g in range(group):
-            field_copy(j * group + g).wait()
+            for copy in field_copies(j * group + g):
+                copy.wait()
         for top in range(0, rows, step):
             x = []
             for a in range(RADIX):
@@ -472,17 +494,19 @@
     return table + (twiddles.astype(np.float32), (sums / LOOK).astype(ml_dtypes.bfloat16))
 
 
-def focus(plan, part, field, spectrum, finish=None):
+def focus(plan, part, fields, by_owner, spectrum, finish=None):
     lanes = plan.lanes
     total = plan.epochs * plan.rows
     tables = focus_tables(plan)
     whole = pl.BlockSpec(memory_space=pltpu.VMEM)
     looked = (plan.epochs, 2, 2, plan.looks, plan.azimuth_looks)
     gradients = (plan.epochs, 2, plan.looks * plan.parts, plan.azimuth_looks)
-    operands = [field, spectrum, *tables]
-    in_specs = [pl.BlockSpec(memory_space=pltpu.HBM)] * 6
+    operands = [*fields, spectrum, *tables]
+    in_specs = [pl.BlockSpec(memory_space=pltpu.HBM)] * len(operands)
+    blocks = plan.azimuth // fields[0].shape[-1]
+    before = ()
     scratch = [
-        pltpu.VMEM(field.shape, jnp.float32),
+        pltpu.VMEM((blocks, plan.epochs) + fields[0].shape[-3:], jnp.float32),
         pltpu.VMEM(spectrum.shape[1:], jnp.float32),
         *[pltpu.VMEM(table.shape, table.dtype) for table in tables],
         pltpu.VMEM((RADIX, total, 2 * lanes), jnp.bfloat16),
@@ -490,41 +514,50 @@
         pltpu.VMEM((RADIX, total, 2 * lanes), jnp.float32),
         pltpu.VMEM((plan.epochs + 2, 2, plan.rows, plan.azimuth), jnp.float32),
         pltpu.VMEM((plan.epochs, 2, 2, plan.looks, plan.azimuth), jnp.float32),
-        pltpu.SemaphoreType.DMA((plan.epochs,)),
+        pltpu.SemaphoreType.DMA((plan.epochs, blocks)),
         pltpu.SemaphoreType.DMA((5,)),
     ]
     shape = looked
     if finish is not None:
         weights, before, halo = finish
         shape = gradients
-        operands += [weights, before, halo]
-        in_specs += [pl.BlockSpec(memory_space=pltpu.SMEM), [whole] * len(before), whole]
+        operands += [weights, *before, halo]
+        in_specs += [pl.BlockSpec(memory_space=pltpu.SMEM)] + [whole] * (len(before) + 1)
         scratch += [
             pltpu.VMEM((plan.epochs, 2, 2, plan.looks * plan.parts, plan.azimuth_looks), jnp.float32),
             pltpu.VMEM((2 * plan.epochs,) + gradients[1:], jnp.float32),
         ]
+
+    def kernel(*refs):
+        some, refs = refs[: len(fields)], refs[len(fields) :]
+
+        def field_at(j, at):
+            if len(some) > 1:
+                return some[at].at[j]
+            return some[0].at[j, at] if by_owner else some[0].at[at, j]
+
+        if finish is None:
+            focus_kernel(plan, part, False, field_at, *refs)
+        else:
+            count = len(before)
+            focus_kernel(
+                plan, part, True, field_at, *refs[:6], refs[6 : 6 + count], *refs[6 + count :]
+            )
+
     return pl.pallas_call(
-        functools.partial(focus_kernel_flat, plan, part, len(before) if finish else None),
+        kernel,
         out_shape=jax.ShapeDtypeStruct(shape, jnp.float32),
-        in_specs=jax.tree.leaves(in_specs),
+        in_specs=in_specs,
         out_specs=whole,
         scratch_shapes=scratch,
         compiler_params=pltpu.CompilerParams(vmem_limit_bytes=VMEM_BYTES),
         cost_estimate=pl.CostEstimate(
             flops=2 * 6 * RADIX * total * 4 * lanes * lanes,
-            bytes_accessed=4 * field.size + 4 * 1024 * 1024,
+            bytes_accessed=4 * blocks * fields[0].size + 4 * 1024 * 1024,
             transcendentals=0,
         ),
         name="azimuth_focus",
-    )(*jax.tree.leaves(operands))
-
-
-def focus_kernel_flat(plan, part, count, *refs):
-    if count is None:
-        focus_kernel(plan, part, False, *refs)
-        return
-    before = refs[7 : 7 + count]
-    focus_kernel(plan, part, True, *refs[:7], before, *refs[7 + count :])
+    )(*operands)
 
 
 def slope_kernel(plan, weight_ref, looked_ref, halo_ref, out_ref, slope_ref):
@@ -552,25 +585,46 @@
     )(weights, looked, halo)
 
 
-def own_filter(plan, azimuth_filter):
+def strip_turn(length, sign):
+    strips = lax.axis_size("strip")
+    step = lax.axis_index("strip") * jnp.arange(length, dtype=jnp.int32) % strips
+    angle = sign * 2.0 * math.pi / strips * step.astype(jnp.float32)
+    return jnp.cos(angle), jnp.sin(angle)
+
+
+def own_filter(plan, azimuth_filter, shifted):
     start = lax.axis_index("acq") * plan.owned
     own = lax.dynamic_slice_in_dim(azimuth_filter, start, plan.owned, axis=2)
+    if shifted:
+        cosine, sine = strip_turn(plan.azimuth, -1.0)
+        own = jnp.stack(times(own, cosine[:, None], sine[:, None]))
     own = own.reshape(2, plan.lanes, RADIX, plan.parts, plan.looks, LOOK)
     order = (3, 0, 2, 5, 4, 1) if plan.planes else (3, 0, 2, 4, 5, 1)
     return own.transpose(order).reshape(plan.parts, 2, RADIX, plan.rows, plan.lanes)
 
 
-def exchange(plan, block):
+def exchange_all(plan, block):
+    shape = block.shape
+    block = block.reshape((plan.strips * plan.epochs,) + shape[2:])
     received = lax.all_to_all(block, OWNERS, split_axis=0, concat_axis=0, tiled=True)
     join = max(1, plan.lanes // plan.pulses)
-    received = received.reshape(
-        plan.strips // join, join, plan.epochs, 2, plan.rows, plan.pulses
-    )
+    received = received.reshape((plan.strips // join, join) + shape[1:])
     if join > 1:
         received = received.transpose(0, 2, 3, 4, 1, 5)
-    return received.reshape(
-        plan.strips // join, plan.epochs, 2, plan.rows, join * plan.pulses
-    )
+    return received.reshape(plan.strips // join, plan.epochs, 2, plan.rows, join * plan.pulses)
+
+
+def to_owners(block):
+    return lax.all_to_all(block, "acq", split_axis=0, concat_axis=0, tiled=True)
+
+
+def to_strips(plan, slots):
+    strips = plan.strips
+    moved = [slots[0]]
+    for k in range(1, strips):
+        route = [(i, (i + k) % strips) for i in range(strips)]
+        moved.append(lax.ppermute(slots[k], "strip", route))
+    return [moved[-place % strips] for place in range(strips)]
 
 
 def per_device(raw_echoes, range_filter, azimuth_filter, pair_mask, inversion):
@@ -582,12 +636,21 @@
     weights = lax.all_gather(inversion[:, 0, :] * usable[None, :], "acq", axis=1, tiled=False)
     weights = weights.reshape(epochs, 2 * epochs)
 
-    spectrum = own_filter(plan, azimuth_filter)
-    fields = [
-        exchange(plan, compress(plan, part, range_filter, raw_echoes[0]))
-        for part in range(plan.parts)
-    ]
-    before = [focus(plan, part, fields[part], spectrum) for part in range(max(1, plan.parts - 1))]
+    raw = raw_echoes[0]
+    if plan.parts == 1:
+        spectrum = own_filter(plan, azimuth_filter, False)
+        (block,) = compress(plan, 0, "all", range_filter, raw)
+        before = [focus(plan, 0, [exchange_all(plan, block)], False, spectrum)]
+    else:
+        spectrum = own_filter(plan, azimuth_filter, True)
+        turned = jnp.stack(times(range_filter, *strip_turn(plan.samples, 1.0)))
+        slots = compress(plan, 0, "slots", turned, raw)
+        (block,) = compress(plan, 1, "owners", turned, raw)
+        first = to_strips(plan, slots)
+        block = to_owners(block)
+        second = to_strips(plan, [block[:, k] for k in range(strips)])
+        first = to_owners(jnp.stack(first, axis=1))
+        before = [focus(plan, 0, [first], True, spectrum)]
 
     owners = strips * epochs
     device = [i % epochs * strips + i // epochs for i in range(owners)]
@@ -597,7 +660,7 @@
         [(device[i], device[i - 1]) for i in range(1, owners)],
     )
     if plan.parts > 1:
-        gradients = focus(plan, plan.parts - 1, fields[-1], spectrum, (weights, before, halo))
+        gradients = focus(plan, 1, second, True, spectrum, (weights, before, halo))
     else:
         gradients = slopes_to_epochs(plan, weights, before[0], halo)
     gathered = lax.all_to_all(gradients, "acq", split_axis=0, concat_axis=0, tiled=True)

time: 139 us -> 155 us (1.12)
  Pallas kernels: 24.8 us -> 33 us
  starting transfers between devices: 12.6 us -> 20.4 us
  other arithmetic: 0.08 us -> 5.31 us
  local copies, waits for them, and re-layouts: 22.2 us -> 19.2 us
    all_to_all x2, waiting for transfers between devices: 57.1 us -> 4.73 us  [to_owners(): return lax.all_to_all(block, 'acq', split_axis=0, concat_axis=0, tiled=True)]
    ppermute x0 -> x6, waiting for transfers between devices: none -> 51.1 us  [to_strips(): moved.append(lax.ppermute(slots[k], 'strip', route))]
    another operation x0 -> x4, local copies, waits for them, and re-layouts: none -> 12.8 us  [own_filter(): own = jnp.stack(times(own, cosine[:, None], sine[:, None]))]
    ppermute x0 -> x6, starting transfers between devices: none -> 9.54 us  [to_strips(): moved.append(lax.ppermute(slots[k], 'strip', route))]
    pallas_call x4, Pallas kernels: 24.8 us -> 33 us  [the longest x2 16.7 us: compress(): pl.pallas_call(functools.partial(compress_kernel, plan, part, form), out_...]
    reshape x1 -> x0, local copies, waits for them, and re-layouts: 7.05 us -> none  [own_filter(): own = own.reshape(2, plan.lanes, RADIX, plan.parts, plan.looks, LOOK)]
    transpose x1 -> x0, local copies, waits for them, and re-layouts: 5.23 us -> none  [own_filter(): own.transpose(order).reshape(plan.parts, 2, RADIX, plan.rows, plan.lanes)]
    unnamed x34 -> x14, local copies, waits for them, and re-layouts: 6.34 us -> 1.18 us
  transfers between devices with their start and end apart: 3 -> 9, of which waited for: 2 -> 4; matrix products, arithmetic and copies ran while one was open for 11% -> 14% of each run, Pallas kernels for 8% -> 10%
where the time goes in v4:
time: 155 us; the launch traced here: 154 us
  waiting for transfers between devices  55.8 us (36%)
  Pallas kernels  33 us (21%)
  starting transfers between devices  20.4 us (13%)
  blocking collectives  20.3 us (13%)
  local copies, waits for them, and re-layouts  19.2 us (12%)
  other arithmetic  5.31 us (3%)
    ppermute x6, waiting for transfers between devices, to_strips(): moved.append(lax.ppermute(slots[k], 'strip', route))  51.1 us
    pallas_call x2, Pallas kernels, compress(): pl.pallas_call(functools.partial(compress_kernel, plan, part, form), out_...  16.7 us
    pallas_call x2, Pallas kernels, focus(): pl.pallas_call(kernel, out_shape=jax.ShapeDtypeStruct(shape, jnp.float32)...  16.4 us
    another operation x4, local copies, waits for them, and re-layouts, own_filter(): own = jnp.stack(times(own, cosine[:, None], sine[:, None]))  12.8 us
    all_to_all x1, blocking collectives, per_device(): lax.all_to_all(gradients, 'acq', split_axis=0, concat_axis=0, tiled=True)  10.7 us
    all_gather x1, blocking collectives, per_device(): lax.all_gather(inversion[:, 0, :] * usable[None, :], 'acq', axis=1, tiled...  9.62 us
    all_to_all x2, starting transfers between devices, to_owners(): return lax.all_to_all(block, 'acq', split_axis=0, concat_axis=0, tiled=True)  9.55 us
    ppermute x6, starting transfers between devices, to_strips(): moved.append(lax.ppermute(slots[k], 'strip', route))  9.54 us
  transfers between devices with their start and end apart: 9, of which 4 were waited for; matrix products, arithmetic and copies ran while one was open for 14% of the time, Pallas kernels for 10%

profile of v4, /device:TPU:0, one launch (start us, length us, event | category | flops | bytes accessed | tf_op | source)
XLA Modules:
  0.0 154.2 jit_solution(18333919687942500971)
XLA Ops:
  0.0 1.1 multiply_subtract_fusion.1
  1.7 8.4 %range_compress.2 = f32[8,4,2,32,256]{4,3,2,1,0:T(8,128)} custom-call(f32[2,2048]{1,0:T(2,128)} %pad_maximum_fusion.1.filter_ref, bf16[256,512]{1,0:T(8,128)(2,1)} %constant.60.clone.high_any, bf16[256,512]{1,0:T(8,128)(2,1)} %constant.61.clone.low_any, f32[4,8,256]{2,1,0:T(8,128)} %constant.62.clone.turn_any, f32[2,256,2048]{2,1,0:T(8,128)} %bitcast.35), custom_call_target="tpu_custom_call" | custom-call | flops 1610612736 | bytes 6291456 | tf_op jit(solution)/shard_map/range_compress/pallas_call | solution.py:284
  10.1 5.2 %all-to-all-start = ((f32[8,4,2,32,256]{4,3,2,1,0:T(8,128)}), f32[8,4,2,32,256]{4,3,2,1,0:T(8,128)S(1)}, u32[]{:S(2)}, u32[]{:S(2)}) async-start(f32[8,4,2,32,256]{4,3,2,1,0:T(8,128)} %range_compress.2), calls=%async_computation | async-start | bytes 4194304 | tf_op jit(solution)/shard_map/all_to_all | solution.py:618
  15.3 8.3 %range_compress.3 = (f32[8,2,32,256]{3,2,1,0:T(8,128)}, f32[8,2,32,256]{3,2,1,0:T(8,128)}, f32[8,2,32,256]{3,2,1,0:T(8,128)}, f32[8,2,32,256]{3,2,1,0:T(8,128)}) custom-call(f32[2,2048]{1,0:T(2,128)} %pad_maximum_fusion.1.filter_ref, bf16[256,512]{1,0:T(8,128)(2,1)} %constant.60.clone.high_any, bf16[256,512]{1,0:T(8,128)(2,1)} %constant.61.clone.low_any, ...), custom_call_target="tpu_custom_call" | custom-call | flops 1610612736 | bytes 6291456 | tf_op jit(solution)/shard_map/range_compress/pallas_call | solution.py:284
  23.6 3.6 %collective-permute-start.3 = (f32[8,2,32,256]{3,2,1,0:T(8,128)}, f32[8,2,32,256]{3,2,1,0:T(8,128)S(1)}, u32[]{:S(2)}, u32[]{:S(2)}) collective-permute-start(f32[8,2,32,256]{3,2,1,0:T(8,128)} %get-tuple-element.10), channel_id=1, source_target_pairs={{0,3},{1,0},{2,1},{3,2},{4,7},{5,4},{6,5},{7,6},{8,11},{9,8},{10,9... | collective-permute-start | bytes 1572872 | tf_op jit(solution)/shard_map/ppermute | solution.py:626
  28.3 11.6 %collective-permute-done.3 = f32[8,2,32,256]{3,2,1,0:T(8,128)S(1)} collective-permute-done((f32[8,2,32,256]{3,2,1,0:T(8,128)}, f32[8,2,32,256]{3,2,1,0:T(8,128)S(1)}, u32[]{:S(2)}, u32[]{:S(2)}) %collective-permute-start.3) | collective-permute-done | bytes 524320 | tf_op jit(solution)/shard_map/ppermute | solution.py:626
  39.9 33.0 %collective-permute-done.4 = f32[8,2,32,256]{3,2,1,0:T(8,128)S(1)} collective-permute-done((f32[8,2,32,256]{3,2,1,0:T(8,128)}, f32[8,2,32,256]{3,2,1,0:T(8,128)S(1)}, u32[]{:S(2)}, u32[]{:S(2)}) %collective-permute-start.4) | collective-permute-done | bytes 524320 | tf_op jit(solution)/shard_map/ppermute | solution.py:626
  72.9 2.5 %pad_maximum_fusion = f32[8,4,2,32,256]{4,3,2,1,0:T(8,128)} fusion(f32[8,1,2,32,256]{4,3,2,1,0:T(8,128)S(1)} %bitcast.41, f32[8,1,2,32,256]{4,3,2,1,0:T(8,128)S(1)} %bitcast.40, f32[8,1,2,32,256]{4,3,2,1,0:T(8,128)S(1)} %bitcast.39, f32[8,1,2,32,256]{4,3,2,1,0:T(8,128)} %bitcast.38), kind=kLoop, calls=%fused_computation | loop fusion | flops 1572864 | bytes 4194304 | tf_op jit(solution)/shard_map/stack | solution.py:652
  75.5 4.4 %all-to-all-start.1 = ((f32[8,4,2,32,256]{4,3,2,1,0:T(8,128)}), f32[8,4,2,32,256]{4,3,2,1,0:T(8,128)}, u32[]{:S(2)}, u32[]{:S(2)}) async-start(f32[8,4,2,32,256]{4,3,2,1,0:T(8,128)} %pad_maximum_fusion), calls=%async_computation.1 | async-start | bytes 4194304 | tf_op jit(solution)/shard_map/all_to_all | solution.py:618
  79.8 1.5 %constant_dynamic-slice_fusion = (f32[1,1024,64]{2,1,0:T(8,128)S(1)}, f32[1,1024,64]{2,1,0:T(8,128)S(1)}) fusion(f32[2,1024,512]{2,1,0:T(8,128)} %param.22, s32[]{:T(128)S(6)} %select_n.35, s32[]{:T(128)S(6)} %add.46), kind=kLoop, calls=%fused_computation.33 | loop fusion | bytes 1048584 | tf_op jit(solution)/shard_map/slice | solution.py:29
  81.9 1.2 slice_bitcast_fusion
  83.2 2.8 %collective-permute-start.1 = (f32[8,2,32,256]{3,2,1,0:T(8,128)}, f32[8,2,32,256]{3,2,1,0:T(8,128)S(1)}, u32[]{:S(2)}, u32[]{:S(2)}) collective-permute-start(f32[8,2,32,256]{3,2,1,0:T(8,128)} %get-tuple-element.16), channel_id=1, source_target_pairs={{0,2},{1,3},{2,0},{3,1},{4,6},{5,7},{6,4},{7,5},{8,10},{9,11},{10,... | collective-permute-start | bytes 1572872 | tf_op jit(solution)/shard_map/ppermute | solution.py:626
  86.0 2.0 %collective-permute-start.2 = (f32[8,2,32,256]{3,2,1,0:T(8,128)S(1)}, f32[8,2,32,256]{3,2,1,0:T(8,128)}, u32[]{:S(2)}, u32[]{:S(2)}) collective-permute-start(f32[8,2,32,256]{3,2,1,0:T(8,128)S(1)} %get-tuple-element.15), channel_id=1, source_target_pairs={{0,1},{1,2},{2,3},{3,0},{4,5},{5,6},{6,7},{7,4},{8,9},{9,10},{10,1... | collective-permute-start | bytes 1572872 | tf_op jit(solution)/shard_map/ppermute | solution.py:626
  88.0 3.6 %stack.30 = f32[1,128,8,2,8,4]{2,1,5,4,3,0:T(8,128)} reshape(f32[1,1024,64]{1,2,0:T(8,128)S(1)} %get-tuple-element.19) | data formatting | bytes 524288 | tf_op jit(solution)/shard_map/stack | solution.py:600
  91.7 2.8 %copy.47 = f32[1,128,8,2,8,4]{1,4,5,3,2,0:T(8,128)S(1)} copy(f32[1,128,8,2,8,4]{2,1,5,4,3,0:T(8,128)} %stack.30) | data formatting | bytes 524288 | tf_op jit(solution)/shard_map/stack | solution.py:600
  94.5 3.6 %stack.31 = f32[1,128,8,2,8,4]{2,1,5,4,3,0:T(8,128)} reshape(f32[1,1024,64]{1,2,0:T(8,128)S(1)} %get-tuple-element.20) | data formatting | bytes 524288 | tf_op jit(solution)/shard_map/stack | solution.py:600
  98.1 2.8 %copy.48 = f32[1,128,8,2,8,4]{1,4,5,3,2,0:T(8,128)S(1)} copy(f32[1,128,8,2,8,4]{2,1,5,4,3,0:T(8,128)} %stack.31) | data formatting | bytes 524288 | tf_op jit(solution)/shard_map/stack | solution.py:600
  101.8 4.7 %all-to-all-done.1.refs_0_ = f32[8,4,2,32,256]{4,3,2,1,0:T(8,128)} async-done(((f32[8,4,2,32,256]{4,3,2,1,0:T(8,128)}), f32[8,4,2,32,256]{4,3,2,1,0:T(8,128)}, u32[]{:S(2)}, u32[]{:S(2)}) %all-to-all-start.1) | async-done | bytes 2097184 | tf_op jit(solution)/shard_map/all_to_all | solution.py:618
  106.5 6.9 %azimuth_focus.2.refs_10_ = f32[8,2,2,8,256]{4,3,2,1,0:T(8,128)} custom-call(f32[8,4,2,32,256]{4,3,2,1,0:T(8,128)} %all-to-all-done.1.refs_0_, f32[2,2,8,32,128]{4,3,2,1,0:T(8,128)} %copy_bitcast_fusion.refs_1_.refs_4_, bf16[256,256]{1,0:T(8,128)(2,1)} %constant.63.clone.refs_2_.refs_5_, bf16[256,256]{1,0:T(8,128)(2,1)} %constant.64.clone.refs_3_.refs_6_, ...), custom_call_target="tpu_custom_call" | custom-call | flops 1610612736 | bytes 12582912 | tf_op jit(solution)/shard_map/azimuth_focus/pallas_call | solution.py:547
  114.3 1.3 collective-permute-start.6
  115.7 9.6 %all_gather.4 = f32[8,8,2]{0,2,1:T(2,128)S(1)} all-gather(f32[8,1,2]{0,2,1:T(2,128)S(1)} %broadcast_multiply_fusion), channel_id=1, replica_groups=mesh['acq'=8,'strip'=4] {'acq'}, dimensions={1}, use_global_device_ids=true | all-gather | bytes 576 | tf_op jit(solution)/shard_map/all_gather | solution.py:636
  126.0 6.4 %collective-permute-done.1.refs_2_ = f32[8,2,32,256]{3,2,1,0:T(8,128)S(1)} collective-permute-done((f32[8,2,32,256]{3,2,1,0:T(8,128)}, f32[8,2,32,256]{3,2,1,0:T(8,128)S(1)}, u32[]{:S(2)}, u32[]{:S(2)}) %collective-permute-start.1) | collective-permute-done | bytes 524320 | tf_op jit(solution)/shard_map/ppermute | solution.py:626
  133.3 9.5 %azimuth_focus.3 = f32[8,2,16,256]{3,2,1,0:T(8,128)} custom-call(f32[8,2,32,256]{3,2,1,0:T(8,128)} %get-tuple-element.18.refs_0_, f32[8,2,32,256]{3,2,1,0:T(8,128)} %copy-done.3, f32[8,2,32,256]{3,2,1,0:T(8,128)} %copy-done.4, f32[8,2,32,256]{3,2,1,0:T(8,128)} %collective-permute-done.2.refs_3_, f32[2,2,8,32,128]{4,3,2,1,0:T(8,128)} %copy_bitcast_fusion.refs_1_.refs_4_, ...), custom_call_target="tpu_custom_call" | custom-call | flops 1610612736 | bytes 6291456 | tf_op jit(solution)/shard_map/azimuth_focus/pallas_call | solution.py:547
  142.8 10.7 %all_to_all.15 = f32[8,2,16,256]{3,2,1,0:T(8,128)S(1)} all-to-all(f32[8,2,16,256]{3,2,1,0:T(8,128)} %azimuth_focus.3), channel_id=1, replica_groups=mesh['acq'=8,'strip'=4] {'acq'}, dimensions={0} | all-to-all | bytes 524288 | tf_op jit(solution)/shard_map/all_to_all | solution.py:666
  (31 shorter events, 6.3 us)
Async XLA Ops:
  10.1 65.3 %all-to-all-start = ((f32[8,4,2,32,256]{4,3,2,1,0:T(8,128)}), f32[8,4,2,32,256]{4,3,2,1,0:T(8,128)S(1)}, u32[]{:S(2)}, u32[]{:S(2)}) async-start(f32[8,4,2,32,256]{4,3,2,1,0:T(8,128)} %range_compress.2), calls=%async_computation | async-start | bytes 4194304 | tf_op jit(solution)/shard_map/all_to_all | solution.py:618
  23.6 16.3 %collective-permute-start.3 = (f32[8,2,32,256]{3,2,1,0:T(8,128)}, f32[8,2,32,256]{3,2,1,0:T(8,128)S(1)}, u32[]{:S(2)}, u32[]{:S(2)}) collective-permute-start(f32[8,2,32,256]{3,2,1,0:T(8,128)} %get-tuple-element.10), channel_id=1, source_target_pairs={{0,3},{1,0},{2,1},{3,2},{4,7},{5,4},{6,5},{7,6},{8,11},{9,8},{10,9... | collective-permute-start | bytes 1572872 | tf_op jit(solution)/shard_map/ppermute | solution.py:626
  27.2 45.7 %collective-permute-start.4 = (f32[8,2,32,256]{3,2,1,0:T(8,128)}, f32[8,2,32,256]{3,2,1,0:T(8,128)S(1)}, u32[]{:S(2)}, u32[]{:S(2)}) collective-permute-start(f32[8,2,32,256]{3,2,1,0:T(8,128)} %get-tuple-element.11), channel_id=1, source_target_pairs={{0,2},{1,3},{2,0},{3,1},{4,6},{5,7},{6,4},{7,5},{8,10},{9,11},{10,... | collective-permute-start | bytes 1572872 | tf_op jit(solution)/shard_map/ppermute | solution.py:626
  27.2 45.7 %collective-permute-start.5 = (f32[8,2,32,256]{3,2,1,0:T(8,128)}, f32[8,2,32,256]{3,2,1,0:T(8,128)S(1)}, u32[]{:S(2)}, u32[]{:S(2)}) collective-permute-start(f32[8,2,32,256]{3,2,1,0:T(8,128)} %get-tuple-element.12), channel_id=1, source_target_pairs={{0,1},{1,2},{2,3},{3,0},{4,5},{5,6},{6,7},{7,4},{8,9},{9,10},{10,1... | collective-permute-start | bytes 1572872 | tf_op jit(solution)/shard_map/ppermute | solution.py:626
  75.5 31.0 %all-to-all-start.1 = ((f32[8,4,2,32,256]{4,3,2,1,0:T(8,128)}), f32[8,4,2,32,256]{4,3,2,1,0:T(8,128)}, u32[]{:S(2)}, u32[]{:S(2)}) async-start(f32[8,4,2,32,256]{4,3,2,1,0:T(8,128)} %pad_maximum_fusion), calls=%async_computation.1 | async-start | bytes 4194304 | tf_op jit(solution)/shard_map/all_to_all | solution.py:618
  81.9 6.1 %copy-start.1 = (s32[1,2]{1,0:T(1,128)S(1)}, s32[1,2]{1,0:T(1,128)}, u32[]{:S(2)}) copy-start(s32[1,2]{1,0:T(1,128)} %param.23) | copy-start | bytes 28
  81.9 6.1 %copy-start.2 = (s32[2]{0:T(128)S(1)}, s32[2]{0:T(128)}, u32[]{:S(2)}) copy-start(s32[2]{0:T(128)} %constant.59.clone) | copy-start | bytes 28
  83.2 42.8 %collective-permute-start = (f32[8,2,32,256]{3,2,1,0:T(8,128)}, f32[8,2,32,256]{3,2,1,0:T(8,128)S(1)}, u32[]{:S(2)}, u32[]{:S(2)}) collective-permute-start(f32[8,2,32,256]{3,2,1,0:T(8,128)} %get-tuple-element.17), channel_id=1, source_target_pairs={{0,3},{1,0},{2,1},{3,2},{4,7},{5,4},{6,5},{7,6},{8,11},{9,8},{10,9... | collective-permute-start | bytes 1572872 | tf_op jit(solution)/shard_map/ppermute | solution.py:626
  83.2 49.3 %collective-permute-start.1 = (f32[8,2,32,256]{3,2,1,0:T(8,128)}, f32[8,2,32,256]{3,2,1,0:T(8,128)S(1)}, u32[]{:S(2)}, u32[]{:S(2)}) collective-permute-start(f32[8,2,32,256]{3,2,1,0:T(8,128)} %get-tuple-element.16), channel_id=1, source_target_pairs={{0,2},{1,3},{2,0},{3,1},{4,6},{5,7},{6,4},{7,5},{8,10},{9,11},{10,... | collective-permute-start | bytes 1572872 | tf_op jit(solution)/shard_map/ppermute | solution.py:626
  86.0 46.5 %collective-permute-start.2 = (f32[8,2,32,256]{3,2,1,0:T(8,128)S(1)}, f32[8,2,32,256]{3,2,1,0:T(8,128)}, u32[]{:S(2)}, u32[]{:S(2)}) collective-permute-start(f32[8,2,32,256]{3,2,1,0:T(8,128)S(1)} %get-tuple-element.15), channel_id=1, source_target_pairs={{0,1},{1,2},{2,3},{3,0},{4,5},{5,6},{6,7},{7,4},{8,9},{9,10},{10,1... | collective-permute-start | bytes 1572872 | tf_op jit(solution)/shard_map/ppermute | solution.py:626
  101.8 13.9 %copy-start = (f32[8,1,2]{0,2,1:T(2,128)S(1)}, f32[8,1,2]{0,2,1:T(2,128)}, u32[]{:S(2)}) copy-start(f32[8,1,2]{0,2,1:T(2,128)} %param.24) | copy-start | bytes 196
  114.3 18.1 %collective-permute-start.6 = (f32[8,2,2,1,256]{4,3,2,1,0:T(1,128)S(1)}, f32[8,2,2,1,256]{4,3,2,1,0:T(1,128)S(1)}, u32[]{:S(2)}, u32[]{:S(2)}) collective-permute-start(f32[8,2,2,1,256]{4,3,2,1,0:T(1,128)S(1)} %slice.44), channel_id=1, source_target_pairs={{4,0},{8,4},{12,8},{16,12},{20,16},{24,20},{28,24},{1,28},{5,1},{9... | collective-permute-start | bytes 98312 | tf_op jit(solution)/shard_map/ppermute | solution.py:657
  126.0 6.5 %copy-start.3 = (f32[8,2,32,256]{3,2,1,0:T(8,128)}, f32[8,2,32,256]{3,2,1,0:T(8,128)S(1)}, u32[]{:S(2)}) copy-start(f32[8,2,32,256]{3,2,1,0:T(8,128)S(1)} %collective-permute-done.refs_1_) | copy-start | bytes 1572868
  132.4 0.8 copy-start.4
  132.5 0.8 copy-start.5

commit v5 on v4

--- a/solution.py
+++ b/solution.py
@@ -101,16 +101,14 @@
         self.azimuth = pulses * strips
         self.base = samples // RADIX
         self.owned = samples // (strips * epochs)
-        self.parts = 2 if self.owned % (2 * LOOK * ROWS) == 0 else 1
+        even = all(size & (size - 1) == 0 for size in (strips, epochs))
+        self.parts = 2 if even and self.owned % (2 * LOOK * ROWS) == 0 else 1
         self.rows = self.owned // self.parts
         self.looks = self.rows // LOOK
         self.planes = self.looks % ROWS == 0
         self.blocks = self.base // self.owned
         self.lanes = self.azimuth // RADIX
         self.azimuth_looks = self.azimuth // LOOK
-
-    def outputs(self, form):
-        return self.strips if form == "slots" else 1
 
     def tile_shift(self, part, block, tile):
         start = block * self.owned + part * self.rows
@@ -171,12 +169,9 @@
 
 
 def compress_kernel(
-    plan, part, form, filter_ref, high_any, low_any, turn_any, raw_ref, *refs
+    plan, part, relative, filter_ref, high_any, low_any, turn_any, raw_ref, out_ref,
+    table_high, table_low, turn_ref, raw, t_high, t_low, y_high, y_low, z_ref, sems, table_sems,
 ):
-    outs, scratch = refs[: plan.outputs(form)], refs[plan.outputs(form) :]
-    (
-        table_high, table_low, turn_ref, raw, t_high, t_low, y_high, y_low, z_ref, sems, table_sems,
-    ) = scratch
     base, blocks = plan.base, plan.blocks
     tiles = plan.rows // ROWS
     chunk = blocks * plan.rows
@@ -260,32 +255,27 @@
             ]
             for a, value in enumerate(dft8(z, 1.0)):
                 for c in range(2):
-                    slot, owner = divmod(a * blocks + block, plan.epochs)
+                    strip, owner = divmod(a * blocks + block, plan.epochs)
                     rows = slice(tile * ROWS, (tile + 1) * ROWS)
-                    if form == "slots":
-                        outs[slot][owner, c, rows, :] = value[c]
-                    elif form == "owners":
-                        outs[0][owner, slot, c, rows, :] = value[c]
+                    if relative:
+                        place = owner ^ lax.axis_index("acq"), strip ^ lax.axis_index("strip")
                     else:
-                        outs[0][slot, owner, c, rows, :] = value[c]
-
-
-def compress(plan, part, form, range_filter, raw):
+                        place = strip, owner
+                    out_ref[place[0], place[1], c, rows, :] = value[c]
+
+
+def compress(plan, part, relative, range_filter, raw):
     chunk = plan.blocks * plan.rows
     whole = pl.BlockSpec(memory_space=pltpu.VMEM)
     bytes_moved = 4 * (raw.size + raw.size // plan.parts)
     tables = lag_tables(plan)
-    slab = (2, plan.rows, plan.pulses)
-    shape = {
-        "slots": (plan.epochs,) + slab,
-        "owners": (plan.epochs, plan.strips) + slab,
-        "all": (plan.strips, plan.epochs) + slab,
-    }[form]
+    places = (plan.strips, plan.epochs)
+    places = places[::-1] if relative else places
     return pl.pallas_call(
-        functools.partial(compress_kernel, plan, part, form),
-        out_shape=[jax.ShapeDtypeStruct(shape, jnp.float32)] * plan.outputs(form),
+        functools.partial(compress_kernel, plan, part, relative),
+        out_shape=jax.ShapeDtypeStruct(places + (2, plan.rows, plan.pulses), jnp.float32),
         in_specs=[whole] + [pl.BlockSpec(memory_space=pltpu.HBM)] * 4,
-        out_specs=[whole] * plan.outputs(form),
+        out_specs=whole,
         scratch_shapes=[
             *[pltpu.VMEM(table.shape, table.dtype) for table in tables],
             pltpu.VMEM(raw.shape, jnp.float32),
@@ -307,7 +297,7 @@
     )(range_filter, *tables, raw)
 
 
-def focus_kernel(plan, part, final, field_at, *refs):
+def focus_kernel(plan, part, final, field_at, own, *refs):
     filter_any, high_any, low_any, twiddle_any, sum_any = refs[:5]
     if final:
         weight_ref, before_ref, halo_ref, out_ref = refs[5:9]
@@ -323,9 +313,11 @@
     group = max(1, step // rows)
     per_block = field_ref.shape[-1] // lanes
 
-    def field_copies(j):
+    def field_copies(slot):
         return [
-            pltpu.make_async_copy(field_at(j, at), field_ref.at[at, j], field_sems.at[j, at])
+            pltpu.make_async_copy(
+                field_at(slot, at), field_ref.at[at ^ own[1], slot ^ own[0]], field_sems.at[slot, at]
+            )
             for at in range(field_ref.shape[0])
         ]
 
@@ -349,21 +341,22 @@
 
     def rows_of(strip, j, c, top, start):
         some = [
-            field_ref[strip, j * group + g, c, top : top + min(rows, step), start : start + lanes]
+            field_ref[strip, j + g, c, top : top + min(rows, step), start : start + lanes]
             for g in range(group)
         ]
         return some[0] if group == 1 else jnp.concatenate(some, axis=0)
 
-    def forward(j, carry):
+    def forward(at, carry):
         for g in range(group):
-            for copy in field_copies(j * group + g):
+            for copy in field_copies(at * group + g):
                 copy.wait()
+        j = at * group ^ own[0]
         for top in range(0, rows, step):
             x = []
             for a in range(RADIX):
                 strip, start = a // per_block, a % per_block * lanes
                 x.append(tuple(rows_of(strip, j, c, top, start) for c in range(2)))
-            at = pl.ds(pl.multiple_of(j * group * rows + top, step), step)
+            at = pl.ds(pl.multiple_of(j * rows + top, step), step)
             for d, value in enumerate(dft8(x, -1.0)):
                 if d > 0:
                     value = times(value, twiddle_ref[0, d : d + 1, :], twiddle_ref[1, d : d + 1, :])
@@ -494,7 +487,7 @@
     return table + (twiddles.astype(np.float32), (sums / LOOK).astype(ml_dtypes.bfloat16))
 
 
-def focus(plan, part, fields, by_owner, spectrum, finish=None):
+def focus(plan, part, fields, spectrum, finish=None):
     lanes = plan.lanes
     total = plan.epochs * plan.rows
     tables = focus_tables(plan)
@@ -531,17 +524,18 @@
     def kernel(*refs):
         some, refs = refs[: len(fields)], refs[len(fields) :]
 
+        relative = len(some) > 1
+        own = (lax.axis_index("acq"), lax.axis_index("strip")) if relative else (0, 0)
+
         def field_at(j, at):
-            if len(some) > 1:
-                return some[at].at[j]
-            return some[0].at[j, at] if by_owner else some[0].at[at, j]
+            return some[at].at[j] if relative else some[0].at[at, j]
 
         if finish is None:
-            focus_kernel(plan, part, False, field_at, *refs)
+            focus_kernel(plan, part, False, field_at, own, *refs)
         else:
             count = len(before)
             focus_kernel(
-                plan, part, True, field_at, *refs[:6], refs[6 : 6 + count], *refs[6 + count :]
+                plan, part, True, field_at, own, *refs[:6], refs[6 : 6 + count], *refs[6 + count :]
             )
 
     return pl.pallas_call(
@@ -585,19 +579,9 @@
     )(weights, looked, halo)
 
 
-def strip_turn(length, sign):
-    strips = lax.axis_size("strip")
-    step = lax.axis_index("strip") * jnp.arange(length, dtype=jnp.int32) % strips
-    angle = sign * 2.0 * math.pi / strips * step.astype(jnp.float32)
-    return jnp.cos(angle), jnp.sin(angle)
-
-
-def own_filter(plan, azimuth_filter, shifted):
+def own_filter(plan, azimuth_filter):
     start = lax.axis_index("acq") * plan.owned
     own = lax.dynamic_slice_in_dim(azimuth_filter, start, plan.owned, axis=2)
-    if shifted:
-        cosine, sine = strip_turn(plan.azimuth, -1.0)
-        own = jnp.stack(times(own, cosine[:, None], sine[:, None]))
     own = own.reshape(2, plan.lanes, RADIX, plan.parts, plan.looks, LOOK)
     order = (3, 0, 2, 5, 4, 1) if plan.planes else (3, 0, 2, 4, 5, 1)
     return own.transpose(order).reshape(plan.parts, 2, RADIX, plan.rows, plan.lanes)
@@ -614,43 +598,40 @@
     return received.reshape(plan.strips // join, plan.epochs, 2, plan.rows, join * plan.pulses)
 
 
-def to_owners(block):
-    return lax.all_to_all(block, "acq", split_axis=0, concat_axis=0, tiled=True)
-
-
-def to_strips(plan, slots):
-    strips = plan.strips
-    moved = [slots[0]]
-    for k in range(1, strips):
-        route = [(i, (i + k) % strips) for i in range(strips)]
-        moved.append(lax.ppermute(slots[k], "strip", route))
-    return [moved[-place % strips] for place in range(strips)]
+def partners(slots, axis):
+    size = lax.axis_size(axis)
+    routes = [[(i, i ^ k) for i in range(size)] for k in range(size)]
+    return slots[:1] + [lax.ppermute(slots[k], axis, routes[k]) for k in range(1, size)]
+
+
+def all_weights(pair_mask, inversion):
+    lags = jnp.array([1, 2], dtype=jnp.int32)
+    usable = pair_mask[0].astype(jnp.float32) * (lax.axis_index("acq") >= lags).astype(jnp.float32)
+    weights = lax.all_gather(inversion[:, 0, :] * usable[None, :], "acq", axis=1, tiled=False)
+    return weights.reshape(weights.shape[0], -1)
 
 
 def per_device(raw_echoes, range_filter, azimuth_filter, pair_mask, inversion):
     strips, epochs = lax.axis_size("strip"), lax.axis_size("acq")
     plan = Plan(strips, epochs, raw_echoes.shape[2], raw_echoes.shape[3])
 
-    lags = jnp.array([1, 2], dtype=jnp.int32)
-    usable = pair_mask[0].astype(jnp.float32) * (lax.axis_index("acq") >= lags).astype(jnp.float32)
-    weights = lax.all_gather(inversion[:, 0, :] * usable[None, :], "acq", axis=1, tiled=False)
-    weights = weights.reshape(epochs, 2 * epochs)
-
     raw = raw_echoes[0]
-    if plan.parts == 1:
-        spectrum = own_filter(plan, azimuth_filter, False)
-        (block,) = compress(plan, 0, "all", range_filter, raw)
-        before = [focus(plan, 0, [exchange_all(plan, block)], False, spectrum)]
-    else:
-        spectrum = own_filter(plan, azimuth_filter, True)
-        turned = jnp.stack(times(range_filter, *strip_turn(plan.samples, 1.0)))
-        slots = compress(plan, 0, "slots", turned, raw)
-        (block,) = compress(plan, 1, "owners", turned, raw)
-        first = to_strips(plan, slots)
-        block = to_owners(block)
-        second = to_strips(plan, [block[:, k] for k in range(strips)])
-        first = to_owners(jnp.stack(first, axis=1))
-        before = [focus(plan, 0, [first], True, spectrum)]
+    block = compress(plan, 0, False, range_filter, raw)
+    if plan.parts > 1:
+        range_filter, block = lax.optimization_barrier((range_filter, block))
+        other = compress(plan, 1, True, range_filter, raw)
+        other, azimuth_filter, pair_mask, inversion = lax.optimization_barrier(
+            (other, azimuth_filter, pair_mask, inversion)
+        )
+    weights = all_weights(pair_mask, inversion)
+    spectrum = own_filter(plan, azimuth_filter)
+    field = exchange_all(plan, block)
+    if plan.parts > 1:
+        other = partners([other[k] for k in range(epochs)], "acq")
+        *other, weights, spectrum = lax.optimization_barrier((*other, weights, spectrum))
+        slots = [jnp.stack([part[k] for part in other]) for k in range(strips)]
+        slots = partners(slots, "strip")
+    before = [focus(plan, 0, [field], spectrum)]
 
     owners = strips * epochs
     device = [i % epochs * strips + i // epochs for i in range(owners)]
@@ -660,7 +641,7 @@
         [(device[i], device[i - 1]) for i in range(1, owners)],
     )
     if plan.parts > 1:
-        gradients = focus(plan, 1, second, True, spectrum, (weights, before, halo))
+        gradients = focus(plan, 1, slots, spectrum, (weights, before, halo))
     else:
         gradients = slopes_to_epochs(plan, weights, before[0], halo)
     gathered = lax.all_to_all(gradients, "acq", split_axis=0, concat_axis=0, tiled=True)

time: 155 us -> 143 us (0.923)
  the two profiles are of different devices: /device:TPU:0 before, /device:TPU:16 now
where the time goes in v5:
time: 143 us; the launch traced here: 142 us
  waiting for transfers between devices  41 us (29%)
  Pallas kernels  33.2 us (23%)
  blocking collectives  25.4 us (18%)
  local copies, waits for them, and re-layouts  23.2 us (16%)
  starting transfers between devices  19 us (13%)
    ppermute x10, waiting for transfers between devices, partners(): lax.ppermute(slots[k], axis, routes[k])  40.9 us
    pallas_call x2, Pallas kernels, compress(): pl.pallas_call(functools.partial(compress_kernel, plan, part, relative),...  16.8 us
    pallas_call x2, Pallas kernels, focus(): pl.pallas_call(kernel, out_shape=jax.ShapeDtypeStruct(shape, jnp.float32)...  16.4 us
    all_gather x1, blocking collectives, all_weights(): lax.all_gather(inversion[:, 0, :] * usable[None, :], 'acq', axis=1, tiled...  15.2 us
    ppermute x10, starting transfers between devices, partners(): lax.ppermute(slots[k], axis, routes[k])  10.7 us
    all_to_all x1, blocking collectives, per_device(): lax.all_to_all(gradients, 'acq', split_axis=0, concat_axis=0, tiled=True)  10.3 us
    reshape x1, local copies, waits for them, and re-layouts, own_filter(): own = own.reshape(2, plan.lanes, RADIX, plan.parts, plan.looks, LOOK)  6.21 us
    all_to_all x1, starting transfers between devices, exchange_all(): lax.all_to_all(block, OWNERS, split_axis=0, concat_axis=0, tiled=True)  6 us
  transfers between devices with their start and end apart: 12, of which 4 were waited for; matrix products, arithmetic and copies ran while one was open for 15% of the time, Pallas kernels for 11%

profile of v5, /device:TPU:16, one launch (start us, length us, event | category | flops | bytes accessed | tf_op | source)
XLA Modules:
  0.0 142.2 jit_solution(9759929828239878894)
XLA Ops:
  0.0 8.4 %range_compress.2 = f32[4,8,2,32,256]{4,3,2,1,0:T(8,128)} custom-call(f32[2,2048]{1,0:T(2,128)} %filter_ref.2, bf16[256,512]{1,0:T(8,128)(2,1)} %constant.30.clone.high_any, bf16[256,512]{1,0:T(8,128)(2,1)} %constant.31.clone.low_any, f32[4,8,256]{2,1,0:T(8,128)} %constant.32.clone.turn_any, f32[2,256,2048]{2,1,0:T(8,128)} %bitcast.29), custom_call_target="tpu_custom_call" | custom-call | flops 1610612736 | bytes 6291456 | tf_op jit(solution)/shard_map/range_compress/pallas_call | solution.py:274
  8.4 6.0 %all-to-all-start = ((f32[32,2,32,256]{3,2,1,0:T(8,128)}), f32[32,2,32,256]{3,2,1,0:T(8,128)}, u32[]{:S(2)}, u32[]{:S(2)}) async-start(f32[32,2,32,256]{3,2,1,0:T(8,128)} %bitcast.31), calls=%async_computation | async-start | bytes 4194304 | tf_op jit(solution)/shard_map/all_to_all | solution.py:593
  14.4 8.5 %range_compress.3 = f32[8,4,2,32,256]{4,3,2,1,0:T(8,128)} custom-call(f32[2,2048]{1,0:T(2,128)} %filter_ref.2, bf16[256,512]{1,0:T(8,128)(2,1)} %constant.30.clone.high_any, bf16[256,512]{1,0:T(8,128)(2,1)} %constant.31.clone.low_any, f32[4,8,256]{2,1,0:T(8,128)} %constant.32.clone.turn_any, f32[2,256,2048]{2,1,0:T(8,128)} %bitcast.30), custom_call_target="tpu_custom_call" | custom-call | flops 1610612736 | bytes 6291456 | tf_op jit(solution)/shard_map/range_compress/pallas_call | solution.py:274
  22.9 1.6 %slice_bitcast_fusion = (f32[4,2,32,256]{3,2,1,0:T(8,128)S(1)}, f32[4,2,32,256]{3,2,1,0:T(8,128)S(1)}, f32[4,2,32,256]{3,2,1,0:T(8,128)S(1)}, f32[4,2,32,256]{3,...) fusion(f32[8,4,2,32,256]{4,3,2,1,0:T(8,128)} %range_compress.3), kind=kLoop, calls=%fused_computation | loop fusion | bytes 4194304 | tf_op jit(solution)/shard_map/squeeze | solution.py:630
  24.8 1.5 %collective-permute-start.1 = (f32[4,2,32,256]{3,2,1,0:T(8,128)S(1)}, f32[4,2,32,256]{3,2,1,0:T(8,128)S(1)}, u32[]{:S(2)}, u32[]{:S(2)}) collective-permute-start(f32[4,2,32,256]{3,2,1,0:T(8,128)S(1)} %get-tuple-element.42), channel_id=1, source_target_pairs={{0,8},{4,12},{8,0},{12,4},{16,24},{20,28},{24,16},{28,20},{1,9},{5... | collective-permute-start | bytes 786440 | tf_op jit(solution)/shard_map/ppermute | solution.py:604
  26.5 1.5 %collective-permute-start.3 = (f32[4,2,32,256]{3,2,1,0:T(8,128)S(1)}, f32[4,2,32,256]{3,2,1,0:T(8,128)}, u32[]{:S(2)}, u32[]{:S(2)}) collective-permute-start(f32[4,2,32,256]{3,2,1,0:T(8,128)S(1)} %get-tuple-element.40), channel_id=1, source_target_pairs={{0,16},{4,20},{8,24},{12,28},{16,0},{20,4},{24,8},{28,12},{1,17},{... | collective-permute-start | bytes 786440 | tf_op jit(solution)/shard_map/ppermute | solution.py:604
  28.3 2.5 %collective-permute-start.5 = (f32[4,2,32,256]{3,2,1,0:T(8,128)S(1)}, f32[4,2,32,256]{3,2,1,0:T(8,128)}, u32[]{:S(2)}, u32[]{:S(2)}) collective-permute-start(f32[4,2,32,256]{3,2,1,0:T(8,128)S(1)} %get-tuple-element.38), channel_id=1, source_target_pairs={{0,24},{4,28},{8,16},{12,20},{16,8},{20,12},{24,0},{28,4},{1,25},{... | collective-permute-start | bytes 786440 | tf_op jit(solution)/shard_map/ppermute | solution.py:604
  30.8 6.1 %collective-permute-done.1 = f32[4,2,32,256]{3,2,1,0:T(8,128)S(1)} collective-permute-done((f32[4,2,32,256]{3,2,1,0:T(8,128)S(1)}, f32[4,2,32,256]{3,2,1,0:T(8,128)S(1)}, u32[]{:S(2)}, u32[]{:S(2)}) %collective-permute-start.1) | collective-permute-done | bytes 262176 | tf_op jit(solution)/shard_map/ppermute | solution.py:604
  38.5 1.6 %constant_dynamic-slice_fusion = f32[2,1024,64]{2,1,0:T(8,128)S(1)} fusion(f32[2,1024,512]{2,1,0:T(8,128)} %param.22, s32[]{:T(128)S(6)} %select_n.3), kind=kLoop, calls=%fused_computation.42 | loop fusion | bytes 1048580 | tf_op jit(solution)/shard_map/dynamic_slice | solution.py:584
  40.4 6.2 %reshape.23 = f32[2,128,8,2,8,4]{2,1,5,4,3,0:T(8,128)} reshape(f32[2,1024,64]{1,2,0:T(8,128)S(1)} %copy.26) | data formatting | bytes 1048576 | tf_op jit(solution)/shard_map/reshape | solution.py:585
  46.6 5.9 %copy.27 = f32[2,2,8,4,8,128]{5,4,3,2,1,0:T(8,128)} copy(f32[2,2,8,4,8,128]{2,5,3,4,0,1:T(8,128)} %bitcast.28) | data formatting | bytes 1048576 | tf_op jit(solution)/shard_map/transpose | solution.py:587
  52.6 15.2 %all_gather.4 = f32[8,8,2]{0,2,1:T(2,128)S(1)} all-gather(f32[8,1,2]{0,2,1:T(2,128)S(1)} %broadcast_multiply_fusion), channel_id=1, replica_groups=mesh['acq'=8,'strip'=4] {'acq'}, dimensions={1}, use_global_device_ids=true | all-gather | bytes 576 | tf_op jit(solution)/shard_map/all_gather | solution.py:610
  67.9 1.0 constant_dynamic-update-slice_fusion.28
  68.9 1.0 constant_dynamic-update-slice_fusion.27
  72.2 1.0 collective-permute-start.8
  73.2 2.1 %collective-permute-start.9 = (f32[8,2,32,256]{3,2,1,0:T(8,128)S(1)}, f32[8,2,32,256]{3,2,1,0:T(8,128)}, u32[]{:S(2)}, u32[]{:S(2)}) collective-permute-start(f32[8,2,32,256]{3,2,1,0:T(8,128)S(1)} %get-tuple-element.45), channel_id=1, source_target_pairs={{0,3},{1,2},{2,1},{3,0},{4,7},{5,6},{6,5},{7,4},{8,11},{9,10},{10,... | collective-permute-start | bytes 1572872 | tf_op jit(solution)/shard_map/ppermute | solution.py:604
  75.4 6.9 %azimuth_focus.2.refs_10_ = f32[8,2,2,8,256]{4,3,2,1,0:T(8,128)} custom-call(f32[4,8,2,32,256]{4,3,2,1,0:T(8,128)} %bitcast.14.refs_0_, f32[2,2,8,32,128]{4,3,2,1,0:T(8,128)} %bitcast.33, bf16[256,256]{1,0:T(8,128)(2,1)} %constant.34.clone.refs_2_.refs_5_, bf16[256,256]{1,0:T(8,128)(2,1)} %constant.35.clone.refs_3_.refs_6_, ...), custom_call_target="tpu_custom_call" | custom-call | flops 1610612736 | bytes 12582912 | tf_op jit(solution)/shard_map/azimuth_focus/pallas_call | solution.py:541
  82.3 1.0 slice.164
  83.2 2.4 %collective-permute-start.10 = (f32[8,2,2,1,256]{4,3,2,1,0:T(1,128)S(1)}, f32[8,2,2,1,256]{4,3,2,1,0:T(1,128)S(1)}, u32[]{:S(2)}, u32[]{:S(2)}) collective-permute-start(f32[8,2,2,1,256]{4,3,2,1,0:T(1,128)S(1)} %slice.164), channel_id=1, source_target_pairs={{4,0},{8,4},{12,8},{16,12},{20,16},{24,20},{28,24},{1,28},{5,1},{9... | collective-permute-start | bytes 98312 | tf_op jit(solution)/shard_map/ppermute | solution.py:638
  86.2 7.1 %collective-permute-done.7.refs_1_ = f32[8,2,32,256]{3,2,1,0:T(8,128)S(1)} collective-permute-done((f32[8,2,32,256]{3,2,1,0:T(8,128)S(1)}, f32[8,2,32,256]{3,2,1,0:T(8,128)S(1)}, u32[]{:S(2)}, u32[]{:S(2)}) %collective-permute-start.7) | collective-permute-done | bytes 524320 | tf_op jit(solution)/shard_map/ppermute | solution.py:604
  93.3 14.5 %collective-permute-done.8.refs_2_ = f32[8,2,32,256]{3,2,1,0:T(8,128)S(1)} collective-permute-done((f32[8,2,32,256]{3,2,1,0:T(8,128)S(1)}, f32[8,2,32,256]{3,2,1,0:T(8,128)S(1)}, u32[]{:S(2)}, u32[]{:S(2)}) %collective-permute-start.8) | collective-permute-done | bytes 524320 | tf_op jit(solution)/shard_map/ppermute | solution.py:604
  107.9 13.2 %collective-permute-done.9.refs_3_ = f32[8,2,32,256]{3,2,1,0:T(8,128)} collective-permute-done((f32[8,2,32,256]{3,2,1,0:T(8,128)S(1)}, f32[8,2,32,256]{3,2,1,0:T(8,128)}, u32[]{:S(2)}, u32[]{:S(2)}) %collective-permute-start.9) | collective-permute-done | bytes 524320 | tf_op jit(solution)/shard_map/ppermute | solution.py:604
  121.7 9.5 %azimuth_focus.3 = f32[8,2,16,256]{3,2,1,0:T(8,128)} custom-call(f32[8,2,32,256]{3,2,1,0:T(8,128)} %copy-done.4, f32[8,2,32,256]{3,2,1,0:T(8,128)} %copy-done.8, f32[8,2,32,256]{3,2,1,0:T(8,128)} %copy-done.9, f32[8,2,32,256]{3,2,1,0:T(8,128)} %collective-permute-done.9.refs_3_, f32[2,2,8,32,128]{4,3,2,1,0:T(8,128)} %bitcast.34, ...), custom_call_target="tpu_custom_call" | custom-call | flops 1610612736 | bytes 6291456 | tf_op jit(solution)/shard_map/azimuth_focus/pallas_call | solution.py:541
  131.2 10.3 %all_to_all.10 = f32[8,2,16,256]{3,2,1,0:T(8,128)S(1)} all-to-all(f32[8,2,16,256]{3,2,1,0:T(8,128)} %azimuth_focus.3), channel_id=1, replica_groups=mesh['acq'=8,'strip'=4] {'acq'}, dimensions={0} | all-to-all | bytes 524288 | tf_op jit(solution)/shard_map/all_to_all | solution.py:647
  (46 shorter events, 7.3 us)
Async XLA Ops:
  8.4 67.0 %all-to-all-start = ((f32[32,2,32,256]{3,2,1,0:T(8,128)}), f32[32,2,32,256]{3,2,1,0:T(8,128)}, u32[]{:S(2)}, u32[]{:S(2)}) async-start(f32[32,2,32,256]{3,2,1,0:T(8,128)} %bitcast.31), calls=%async_computation | async-start | bytes 4194304 | tf_op jit(solution)/shard_map/all_to_all | solution.py:593
  14.4 13.9 %copy-start.6 = (s32[1,2]{1,0:T(1,128)S(1)}, s32[1,2]{1,0:T(1,128)}, u32[]{:S(2)}) copy-start(s32[1,2]{1,0:T(1,128)} %param.23) | copy-start | bytes 28
  14.4 13.9 %copy-start.7 = (s32[2]{0:T(128)S(1)}, s32[2]{0:T(128)}, u32[]{:S(2)}) copy-start(s32[2]{0:T(128)} %constant.33.clone) | copy-start | bytes 28
  24.6 3.7 %collective-permute-start = (f32[4,2,32,256]{3,2,1,0:T(8,128)S(1)}, f32[4,2,32,256]{3,2,1,0:T(8,128)S(1)}, u32[]{:S(2)}, u32[]{:S(2)}) collective-permute-start(f32[4,2,32,256]{3,2,1,0:T(8,128)S(1)} %get-tuple-element.43), channel_id=1, source_target_pairs={{0,4},{4,0},{8,12},{12,8},{16,20},{20,16},{24,28},{28,24},{1,5},{5... | collective-permute-start | bytes 786440 | tf_op jit(solution)/shard_map/ppermute | solution.py:604
  24.8 12.1 %collective-permute-start.1 = (f32[4,2,32,256]{3,2,1,0:T(8,128)S(1)}, f32[4,2,32,256]{3,2,1,0:T(8,128)S(1)}, u32[]{:S(2)}, u32[]{:S(2)}) collective-permute-start(f32[4,2,32,256]{3,2,1,0:T(8,128)S(1)} %get-tuple-element.42), channel_id=1, source_target_pairs={{0,8},{4,12},{8,0},{12,4},{16,24},{20,28},{24,16},{28,20},{1,9},{5... | collective-permute-start | bytes 786440 | tf_op jit(solution)/shard_map/ppermute | solution.py:604
  26.2 41.5 %collective-permute-start.2 = (f32[4,2,32,256]{3,2,1,0:T(8,128)S(1)}, f32[4,2,32,256]{3,2,1,0:T(8,128)}, u32[]{:S(2)}, u32[]{:S(2)}) collective-permute-start(f32[4,2,32,256]{3,2,1,0:T(8,128)S(1)} %get-tuple-element.41), channel_id=1, source_target_pairs={{0,12},{4,8},{8,4},{12,0},{16,28},{20,24},{24,20},{28,16},{1,13},{... | collective-permute-start | bytes 786440 | tf_op jit(solution)/shard_map/ppermute | solution.py:604
  26.5 41.3 %collective-permute-start.3 = (f32[4,2,32,256]{3,2,1,0:T(8,128)S(1)}, f32[4,2,32,256]{3,2,1,0:T(8,128)}, u32[]{:S(2)}, u32[]{:S(2)}) collective-permute-start(f32[4,2,32,256]{3,2,1,0:T(8,128)S(1)} %get-tuple-element.40), channel_id=1, source_target_pairs={{0,16},{4,20},{8,24},{12,28},{16,0},{20,4},{24,8},{28,12},{1,17},{... | collective-permute-start | bytes 786440 | tf_op jit(solution)/shard_map/ppermute | solution.py:604
  28.0 39.8 %collective-permute-start.4 = (f32[4,2,32,256]{3,2,1,0:T(8,128)S(1)}, f32[4,2,32,256]{3,2,1,0:T(8,128)S(1)}, u32[]{:S(2)}, u32[]{:S(2)}) collective-permute-start(f32[4,2,32,256]{3,2,1,0:T(8,128)S(1)} %get-tuple-element.39), channel_id=1, source_target_pairs={{0,20},{4,16},{8,28},{12,24},{16,4},{20,0},{24,12},{28,8},{1,21},{... | collective-permute-start | bytes 786440 | tf_op jit(solution)/shard_map/ppermute | solution.py:604
  28.3 8.6 %copy-start.2 = (f32[4,2,32,256]{3,2,1,0:T(8,128)}, f32[4,2,32,256]{3,2,1,0:T(8,128)S(1)}, u32[]{:S(2)}) copy-start(f32[4,2,32,256]{3,2,1,0:T(8,128)S(1)} %collective-permute-done) | copy-start | bytes 786436
  28.3 39.5 %collective-permute-start.5 = (f32[4,2,32,256]{3,2,1,0:T(8,128)S(1)}, f32[4,2,32,256]{3,2,1,0:T(8,128)}, u32[]{:S(2)}, u32[]{:S(2)}) collective-permute-start(f32[4,2,32,256]{3,2,1,0:T(8,128)S(1)} %get-tuple-element.38), channel_id=1, source_target_pairs={{0,24},{4,28},{8,16},{12,20},{16,8},{20,12},{24,0},{28,4},{1,25},{... | collective-permute-start | bytes 786440 | tf_op jit(solution)/shard_map/ppermute | solution.py:604
  36.9 0.7 copy-start
  37.6 30.2 %collective-permute-start.6 = (f32[4,2,32,256]{3,2,1,0:T(8,128)S(1)}, f32[4,2,32,256]{3,2,1,0:T(8,128)}, u32[]{:S(2)}, u32[]{:S(2)}) collective-permute-start(f32[4,2,32,256]{3,2,1,0:T(8,128)S(1)} %get-tuple-element.37), channel_id=1, source_target_pairs={{0,28},{4,24},{8,20},{12,16},{16,12},{20,8},{24,4},{28,0},{1,29},{... | collective-permute-start | bytes 786440 | tf_op jit(solution)/shard_map/ppermute | solution.py:604
  46.6 5.9 %copy-start.5 = (f32[8,1,2]{0,2,1:T(2,128)S(1)}, f32[8,1,2]{0,2,1:T(2,128)}, u32[]{:S(2)}) copy-start(f32[8,1,2]{0,2,1:T(2,128)} %param.24) | copy-start | bytes 196
  46.6 21.2 %copy-start.3 = (f32[4,2,32,256]{3,2,1,0:T(8,128)S(1)}, f32[4,2,32,256]{3,2,1,0:T(8,128)}, u32[]{:S(2)}) copy-start(f32[4,2,32,256]{3,2,1,0:T(8,128)} %copy-done.2) | copy-start | bytes 786436
  46.6 21.3 %copy-start.1 = (f32[4,2,32,256]{3,2,1,0:T(8,128)S(1)}, f32[4,2,32,256]{3,2,1,0:T(8,128)}, u32[]{:S(2)}) copy-start(f32[4,2,32,256]{3,2,1,0:T(8,128)} %copy-done) | copy-start | bytes 786436
  71.8 1.4 copy-start.4
  71.8 21.5 %collective-permute-start.7 = (f32[8,2,32,256]{3,2,1,0:T(8,128)S(1)}, f32[8,2,32,256]{3,2,1,0:T(8,128)S(1)}, u32[]{:S(2)}, u32[]{:S(2)}) collective-permute-start(f32[8,2,32,256]{3,2,1,0:T(8,128)S(1)} %get-tuple-element.47), channel_id=1, source_target_pairs={{0,1},{1,0},{2,3},{3,2},{4,5},{5,4},{6,7},{7,6},{8,9},{9,8},{10,11... | collective-permute-start | bytes 1572872 | tf_op jit(solution)/shard_map/ppermute | solution.py:604
  72.2 35.6 %collective-permute-start.8 = (f32[8,2,32,256]{3,2,1,0:T(8,128)S(1)}, f32[8,2,32,256]{3,2,1,0:T(8,128)S(1)}, u32[]{:S(2)}, u32[]{:S(2)}) collective-permute-start(f32[8,2,32,256]{3,2,1,0:T(8,128)S(1)} %get-tuple-element.46), channel_id=1, source_target_pairs={{0,2},{1,3},{2,0},{3,1},{4,6},{5,7},{6,4},{7,5},{8,10},{9,11},{10,... | collective-permute-start | bytes 1572872 | tf_op jit(solution)/shard_map/ppermute | solution.py:604
  73.2 47.8 %collective-permute-start.9 = (f32[8,2,32,256]{3,2,1,0:T(8,128)S(1)}, f32[8,2,32,256]{3,2,1,0:T(8,128)}, u32[]{:S(2)}, u32[]{:S(2)}) collective-permute-start(f32[8,2,32,256]{3,2,1,0:T(8,128)S(1)} %get-tuple-element.45), channel_id=1, source_target_pairs={{0,3},{1,2},{2,1},{3,0},{4,7},{5,6},{6,5},{7,4},{8,11},{9,10},{10,... | collective-permute-start | bytes 1572872 | tf_op jit(solution)/shard_map/ppermute | solution.py:604
  83.2 37.8 %collective-permute-start.10 = (f32[8,2,2,1,256]{4,3,2,1,0:T(1,128)S(1)}, f32[8,2,2,1,256]{4,3,2,1,0:T(1,128)S(1)}, u32[]{:S(2)}, u32[]{:S(2)}) collective-permute-start(f32[8,2,2,1,256]{4,3,2,1,0:T(1,128)S(1)} %slice.164), channel_id=1, source_target_pairs={{4,0},{8,4},{12,8},{16,12},{20,16},{24,20},{28,24},{1,28},{5,1},{9... | collective-permute-start | bytes 98312 | tf_op jit(solution)/shard_map/ppermute | solution.py:638
  93.3 27.7 %copy-start.8 = (f32[8,2,32,256]{3,2,1,0:T(8,128)}, f32[8,2,32,256]{3,2,1,0:T(8,128)S(1)}, u32[]{:S(2)}) copy-start(f32[8,2,32,256]{3,2,1,0:T(8,128)S(1)} %collective-permute-done.7.refs_1_) | copy-start | bytes 1572868
  107.9 13.2 %copy-start.9 = (f32[8,2,32,256]{3,2,1,0:T(8,128)}, f32[8,2,32,256]{3,2,1,0:T(8,128)S(1)}, u32[]{:S(2)}) copy-start(f32[8,2,32,256]{3,2,1,0:T(8,128)S(1)} %collective-permute-done.8.refs_2_) | copy-start | bytes 1572868
  121.1 0.6 copy-start.10

commit v6 on v5

--- a/solution.py
+++ b/solution.py
@@ -13,7 +13,8 @@
 LOOK = 4
 RADIX = 8
 ROWS = 8
-VMEM_BYTES = 60 * 1024 * 1024
+RANGE_VMEM = 60 * 1024 * 1024
+FOCUS_VMEM = 28 * 1024 * 1024
 OWNERS = ("strip", "acq")
 
 
@@ -191,6 +192,24 @@
         ]
     )
     fetch([raw_copy(at) for at in range(pieces)])
+    def spread_pulses(at, carry):
+        rows = pl.ds(pl.multiple_of(at * 2 * ROWS, 2 * ROWS), 2 * ROWS)
+        x = [
+            tuple(raw[c, rows, a * base : (a + 1) * base] for c in range(2))
+            for a in range(RADIX)
+        ]
+        for d, value in enumerate(dft8(x, -1.0)):
+            for c in range(2):
+                high, low = two_parts(value[c])
+                y_high[d, rows, c * base : (c + 1) * base] = high
+                y_low[d, rows, c * base : (c + 1) * base] = low
+        return carry
+
+    steps = piece // (2 * ROWS)
+    for at in range(pieces):
+        raw_copy(at).wait()
+        lax.fori_loop(at * steps, (at + 1) * steps, spread_pulses, 0)
+
     for copy in tables:
         copy.wait()
     lags = lag_vectors(plan, filter_ref, table_high, table_low, turn_ref)
@@ -224,26 +243,6 @@
             t_low[d, top, base:] = -imag_low
             t_low[d, bottom, :base] = imag_low
             t_low[d, bottom, base:] = real_low
-
-    def spread_pulses(at, carry):
-        rows = pl.ds(pl.multiple_of(at * 2 * ROWS, 2 * ROWS), 2 * ROWS)
-        x = [
-            tuple(raw[c, rows, a * base : (a + 1) * base] for c in range(2))
-            for a in range(RADIX)
-        ]
-        for d, value in enumerate(dft8(x, -1.0)):
-            for c in range(2):
-                high, low = two_parts(value[c])
-                y_high[d, rows, c * base : (c + 1) * base] = high
-                y_low[d, rows, c * base : (c + 1) * base] = low
-        return carry
-
-    steps = piece // (2 * ROWS)
-    for at in range(pieces):
-        raw_copy(at).wait()
-        lax.fori_loop(at * steps, (at + 1) * steps, spread_pulses, 0)
-
-    for d in range(RADIX):
         z_ref[d] = three_products(t_high[d], t_low[d], y_high[d], y_low[d], ((1,), (1,)))
 
     for block in range(blocks):
@@ -287,7 +286,7 @@
             pltpu.SemaphoreType.DMA((4,)),
             pltpu.SemaphoreType.DMA((3,)),
         ],
-        compiler_params=pltpu.CompilerParams(vmem_limit_bytes=VMEM_BYTES),
+        compiler_params=pltpu.CompilerParams(vmem_limit_bytes=RANGE_VMEM),
         cost_estimate=pl.CostEstimate(
             flops=6 * RADIX * 4 * chunk * plan.base * plan.pulses,
             bytes_accessed=bytes_moved,
@@ -348,8 +347,9 @@
 
     def forward(at, carry):
         for g in range(group):
-            for copy in field_copies(at * group + g):
-                copy.wait()
+            for block in range(field_ref.shape[0]):
+                place = field_ref.at[block, at * group + g]
+                pltpu.make_async_copy(place, place, field_sems.at[at * group + g, block]).wait()
         j = at * group ^ own[0]
         for top in range(0, rows, step):
             x = []
@@ -528,7 +528,9 @@
         own = (lax.axis_index("acq"), lax.axis_index("strip")) if relative else (0, 0)
 
         def field_at(j, at):
-            return some[at].at[j] if relative else some[0].at[at, j]
+            if not relative:
+                return some[0].at[at, j]
+            return some[j].at[0] if at == 0 else some[plan.epochs + at - 1].at[j]
 
         if finish is None:
             focus_kernel(plan, part, False, field_at, own, *refs)
@@ -544,10 +546,10 @@
         in_specs=in_specs,
         out_specs=whole,
         scratch_shapes=scratch,
-        compiler_params=pltpu.CompilerParams(vmem_limit_bytes=VMEM_BYTES),
+        compiler_params=pltpu.CompilerParams(vmem_limit_bytes=FOCUS_VMEM),
         cost_estimate=pl.CostEstimate(
             flops=2 * 6 * RADIX * total * 4 * lanes * lanes,
-            bytes_accessed=4 * blocks * fields[0].size + 4 * 1024 * 1024,
+            bytes_accessed=4 * total * 2 * plan.azimuth + 4 * 1024 * 1024,
             transcendentals=0,
         ),
         name="azimuth_focus",
@@ -571,7 +573,7 @@
         scratch_shapes=[
             pltpu.VMEM((2 * plan.epochs, 2, looks, plan.azimuth_looks), jnp.float32)
         ],
-        compiler_params=pltpu.CompilerParams(vmem_limit_bytes=VMEM_BYTES),
+        compiler_params=pltpu.CompilerParams(vmem_limit_bytes=FOCUS_VMEM),
         cost_estimate=pl.CostEstimate(
             flops=8 * looked.size * plan.epochs, bytes_accessed=5 * looked.size, transcendentals=0
         ),
@@ -598,10 +600,39 @@
     return received.reshape(plan.strips // join, plan.epochs, 2, plan.rows, join * plan.pulses)
 
 
-def partners(slots, axis):
+def partners(slots, axis, first=0):
     size = lax.axis_size(axis)
-    routes = [[(i, i ^ k) for i in range(size)] for k in range(size)]
-    return slots[:1] + [lax.ppermute(slots[k], axis, routes[k]) for k in range(1, size)]
+    moved = []
+    for k, slot in enumerate(slots, first):
+        moved.append(slot if k == 0 else lax.ppermute(slot, axis, [(i, i ^ k) for i in range(size)]))
+    return moved
+
+
+def regroup(plan, others):
+    far = range(1, plan.strips)
+
+    def kernel(*refs):
+        ins, outs, sems = refs[: plan.epochs], refs[plan.epochs : -1], refs[-1]
+        copies = fetch(
+            [
+                pltpu.make_async_copy(ins[m].at[k], outs[k - 1].at[m], sems.at[m, k])
+                for k in far
+                for m in range(plan.epochs)
+            ]
+        )
+        for copy in copies:
+            copy.wait()
+
+    shape = jax.ShapeDtypeStruct((plan.epochs,) + others[0].shape[1:], jnp.float32)
+    place = pl.BlockSpec(memory_space=pltpu.HBM)
+    return pl.pallas_call(
+        kernel,
+        out_shape=[shape for _ in far],
+        in_specs=[place] * plan.epochs,
+        out_specs=[place for _ in far],
+        scratch_shapes=[pltpu.SemaphoreType.DMA((plan.epochs, plan.strips))],
+        name="regroup",
+    )(*others)
 
 
 def all_weights(pair_mask, inversion):
@@ -620,18 +651,16 @@
     if plan.parts > 1:
         range_filter, block = lax.optimization_barrier((range_filter, block))
         other = compress(plan, 1, True, range_filter, raw)
-        other, azimuth_filter, pair_mask, inversion = lax.optimization_barrier(
-            (other, azimuth_filter, pair_mask, inversion)
-        )
-    weights = all_weights(pair_mask, inversion)
+        other, azimuth_filter = lax.optimization_barrier((other, azimuth_filter))
     spectrum = own_filter(plan, azimuth_filter)
     field = exchange_all(plan, block)
     if plan.parts > 1:
         other = partners([other[k] for k in range(epochs)], "acq")
-        *other, weights, spectrum = lax.optimization_barrier((*other, weights, spectrum))
-        slots = [jnp.stack([part[k] for part in other]) for k in range(strips)]
-        slots = partners(slots, "strip")
+        *other, spectrum = lax.optimization_barrier((*other, spectrum))
+        slots = partners(regroup(plan, other), "strip", 1)
     before = [focus(plan, 0, [field], spectrum)]
+    before[0], pair_mask, inversion = lax.optimization_barrier((before[0], pair_mask, inversion))
+    weights = all_weights(pair_mask, inversion)
 
     owners = strips * epochs
     device = [i % epochs * strips + i // epochs for i in range(owners)]
@@ -641,7 +670,7 @@
         [(device[i], device[i - 1]) for i in range(1, owners)],
     )
     if plan.parts > 1:
-        gradients = focus(plan, 1, slots, spectrum, (weights, before, halo))
+        gradients = focus(plan, 1, other + slots, spectrum, (weights, before, halo))
     else:
         gradients = slopes_to_epochs(plan, weights, before[0], halo)
     gathered = lax.all_to_all(gradients, "acq", split_axis=0, concat_axis=0, tiled=True)

time: 143 us -> 187 us (1.31)
  the two profiles are of different devices: /device:TPU:16 before, /device:TPU:8 now
where the time goes in v6:
time: 187 us
  Pallas kernels  79.8 us (43%)
  waiting for transfers between devices  42 us (22%)
  local copies, waits for them, and re-layouts  24.3 us (13%)
  starting transfers between devices  22 us (12%)
  blocking collectives  18.2 us (10%)
    pallas_call x1, Pallas kernels, regroup(): pl.pallas_call(kernel, out_shape=[shape for _ in far], in_specs=[place] *...  49 us
    ppermute x10, waiting for transfers between devices, partners(): lax.ppermute(slot, axis, [(i, i ^ k) for i in range(size)])  42 us
    pallas_call x2, Pallas kernels, focus(): pl.pallas_call(kernel, out_shape=jax.ShapeDtypeStruct(shape, jnp.float32)...  16.2 us
    pallas_call x2, Pallas kernels, compress(): pl.pallas_call(functools.partial(compress_kernel, plan, part, relative),...  14.6 us
    ppermute x10, starting transfers between devices, partners(): lax.ppermute(slot, axis, [(i, i ^ k) for i in range(size)])  12.4 us
    all_to_all x1, blocking collectives, per_device(): lax.all_to_all(gradients, 'acq', split_axis=0, concat_axis=0, tiled=True)  10 us
    all_gather x1, blocking collectives, all_weights(): lax.all_gather(inversion[:, 0, :] * usable[None, :], 'acq', axis=1, tiled...  8.2 us
    reshape x1, local copies, waits for them, and re-layouts, own_filter(): own = own.reshape(2, plan.lanes, RADIX, plan.parts, plan.looks, LOOK)  6.21 us
  transfers between devices with their start and end apart: 12, of which 4 were waited for; matrix products, arithmetic and copies ran while one was open for 10% of the time, Pallas kernels for 34%

profile of v6, /device:TPU:8, one launch (start us, length us, event | category | flops | bytes accessed | tf_op | source)
XLA Modules:
  0.0 186.8 jit_solution(4191486489173191237)
XLA Ops:
  0.0 7.3 %range_compress.2 = f32[4,8,2,32,256]{4,3,2,1,0:T(8,128)} custom-call(f32[2,2048]{1,0:T(2,128)} %filter_ref.2, bf16[256,512]{1,0:T(8,128)(2,1)} %constant.30.clone.high_any, bf16[256,512]{1,0:T(8,128)(2,1)} %constant.31.clone.low_any, f32[4,8,256]{2,1,0:T(8,128)} %constant.32.clone.turn_any, f32[2,256,2048]{2,1,0:T(8,128)} %bitcast.32), custom_call_target="tpu_custom_call" | custom-call | flops 1610612736 | bytes 6291456 | tf_op jit(solution)/shard_map/range_compress/pallas_call | solution.py:273
  7.3 6.1 %all-to-all-start = ((f32[32,2,32,256]{3,2,1,0:T(8,128)}), f32[32,2,32,256]{3,2,1,0:T(8,128)S(1)}, u32[]{:S(2)}, u32[]{:S(2)}) async-start(f32[32,2,32,256]{3,2,1,0:T(8,128)} %bitcast.34), calls=%async_computation | async-start | bytes 4194304 | tf_op jit(solution)/shard_map/all_to_all | solution.py:595
  13.4 7.3 %range_compress.3 = f32[8,4,2,32,256]{4,3,2,1,0:T(8,128)} custom-call(f32[2,2048]{1,0:T(2,128)} %filter_ref.2, bf16[256,512]{1,0:T(8,128)(2,1)} %constant.30.clone.high_any, bf16[256,512]{1,0:T(8,128)(2,1)} %constant.31.clone.low_any, f32[4,8,256]{2,1,0:T(8,128)} %constant.32.clone.turn_any, f32[2,256,2048]{2,1,0:T(8,128)} %bitcast.33), custom_call_target="tpu_custom_call" | custom-call | flops 1610612736 | bytes 6291456 | tf_op jit(solution)/shard_map/range_compress/pallas_call | solution.py:273
  20.7 2.7 %slice_bitcast_fusion = (f32[4,2,32,256]{3,2,1,0:T(8,128)S(1)}, f32[4,2,32,256]{3,2,1,0:T(8,128)S(1)}, f32[4,2,32,256]{3,2,1,0:T(8,128)}, f32[4,2,32,256]{3,2,1,...) fusion(f32[8,4,2,32,256]{4,3,2,1,0:T(8,128)} %range_compress.3), kind=kLoop, calls=%fused_computation | loop fusion | bytes 4194304 | tf_op jit(solution)/shard_map/squeeze | solution.py:658
  23.3 2.1 %collective-permute-start.6 = (f32[4,2,32,256]{3,2,1,0:T(8,128)S(1)}, f32[4,2,32,256]{3,2,1,0:T(8,128)S(1)}, u32[]{:S(2)}, u32[]{:S(2)}) collective-permute-start(f32[4,2,32,256]{3,2,1,0:T(8,128)S(1)} %get-tuple-element.43), channel_id=1, source_target_pairs={{0,28},{4,24},{8,20},{12,16},{16,12},{20,8},{24,4},{28,0},{1,29},{... | collective-permute-start | bytes 786440 | tf_op jit(solution)/shard_map/ppermute | solution.py:607
  26.0 1.1 collective-permute-start.4
  27.7 1.2 collective-permute-start.2
  29.0 9.5 %collective-permute-done.6.refs_7_ = f32[4,2,32,256]{3,2,1,0:T(8,128)S(1)} collective-permute-done((f32[4,2,32,256]{3,2,1,0:T(8,128)S(1)}, f32[4,2,32,256]{3,2,1,0:T(8,128)S(1)}, u32[]{:S(2)}, u32[]{:S(2)}) %collective-permute-start.6) | collective-permute-done | bytes 262176 | tf_op jit(solution)/shard_map/ppermute | solution.py:607
  38.4 3.3 %collective-permute-start.1 = (f32[4,2,32,256]{3,2,1,0:T(8,128)}, f32[4,2,32,256]{3,2,1,0:T(8,128)}, u32[]{:S(2)}, u32[]{:S(2)}) collective-permute-start(f32[4,2,32,256]{3,2,1,0:T(8,128)} %get-tuple-element.48), channel_id=1, source_target_pairs={{0,8},{4,12},{8,0},{12,4},{16,24},{20,28},{24,16},{28,20},{1,9},{5... | collective-permute-start | bytes 786440 | tf_op jit(solution)/shard_map/ppermute | solution.py:607
  41.7 9.1 %collective-permute-done.5.refs_6_ = f32[4,2,32,256]{3,2,1,0:T(8,128)S(1)} collective-permute-done((f32[4,2,32,256]{3,2,1,0:T(8,128)S(1)}, f32[4,2,32,256]{3,2,1,0:T(8,128)S(1)}, u32[]{:S(2)}, u32[]{:S(2)}) %collective-permute-start.5) | collective-permute-done | bytes 262176 | tf_op jit(solution)/shard_map/ppermute | solution.py:607
  50.8 2.6 %constant_dynamic-slice_fusion = f32[2,1024,64]{2,1,0:T(8,128)} fusion(f32[2,1024,512]{2,1,0:T(8,128)} %param.22, s32[]{:T(128)S(6)} %select_n.3), kind=kLoop, calls=%fused_computation.10 | loop fusion | bytes 1048580 | tf_op jit(solution)/shard_map/dynamic_slice | solution.py:586
  53.4 1.5 copy.26
  55.0 6.2 %reshape.22 = f32[2,128,8,2,8,4]{2,1,5,4,3,0:T(8,128)} reshape(f32[2,1024,64]{1,2,0:T(8,128)S(1)} %copy.26) | data formatting | bytes 1048576 | tf_op jit(solution)/shard_map/reshape | solution.py:587
  61.2 5.2 %copy.27 = f32[2,2,8,4,8,128]{5,4,3,2,1,0:T(8,128)S(1)} copy(f32[2,2,8,4,8,128]{2,5,3,4,0,1:T(8,128)} %bitcast.31) | data formatting | bytes 1048576 | tf_op jit(solution)/shard_map/transpose | solution.py:589
  66.5 49.0 %regroup.1 = (f32[8,2,32,256]{3,2,1,0:T(8,128)}, f32[8,2,32,256]{3,2,1,0:T(8,128)}, f32[8,2,32,256]{3,2,1,0:T(8,128)}) custom-call(f32[4,2,32,256]{3,2,1,0:T(8,128)} %get-tuple-element.27.refs_0_, f32[4,2,32,256]{3,2,1,0:T(8,128)} %collective-permute-done.refs_1_, f32[4,2,32,256]{3,2,1,0:T(8,128)} %collective-permute-done.1.refs_2_, ...), custom_call_target="tpu_custom_call" | custom-call | tf_op jit(solution)/shard_map/regroup/pallas_call | solution.py:628
  115.6 3.1 %collective-permute-start.8 = (f32[8,2,32,256]{3,2,1,0:T(8,128)}, f32[8,2,32,256]{3,2,1,0:T(8,128)}, u32[]{:S(2)}, u32[]{:S(2)}) collective-permute-start(f32[8,2,32,256]{3,2,1,0:T(8,128)} %get-tuple-element.36), channel_id=1, source_target_pairs={{0,2},{1,3},{2,0},{3,1},{4,6},{5,7},{6,4},{7,5},{8,10},{9,11},{10,... | collective-permute-start | bytes 1572872 | tf_op jit(solution)/shard_map/ppermute | solution.py:607
  120.9 8.1 %azimuth_focus.2.refs_17_ = f32[8,2,2,8,256]{4,3,2,1,0:T(8,128)S(1)} custom-call(f32[4,8,2,32,256]{4,3,2,1,0:T(8,128)S(1)} %bitcast.28, f32[2,2,8,32,128]{4,3,2,1,0:T(8,128)S(1)} %bitcast.29, bf16[256,256]{1,0:T(8,128)(2,1)S(1)} %copy-done.10, bf16[256,256]{1,0:T(8,128)(2,1)S(1)} %copy-done.8, f32[4,8,128]{2,1,0:T(8,128)S(1)} %copy-done.12, ...), custom_call_target="tpu_custom_call" | custom-call | flops 1610612736 | bytes 6291456 | tf_op jit(solution)/shard_map/azimuth_focus/pallas_call | solution.py:543
  129.7 3.5 %collective-permute-start.10 = (f32[8,2,2,1,256]{4,3,2,1,0:T(1,128)S(1)}, f32[8,2,2,1,256]{4,3,2,1,0:T(1,128)S(1)}, u32[]{:S(2)}, u32[]{:S(2)}) collective-permute-start(f32[8,2,2,1,256]{4,3,2,1,0:T(1,128)S(1)} %slice.35), channel_id=1, source_target_pairs={{4,0},{8,4},{12,8},{16,12},{20,16},{24,20},{28,24},{1,28},{5,1},{9... | collective-permute-start | bytes 98312 | tf_op jit(solution)/shard_map/ppermute | solution.py:667
  133.4 8.2 %all_gather.4 = f32[8,8,2]{0,2,1:T(2,128)S(1)} all-gather(f32[8,1,2]{0,2,1:T(2,128)S(1)} %broadcast_multiply_fusion), channel_id=1, replica_groups=mesh['acq'=8,'strip'=4] {'acq'}, dimensions={1}, use_global_device_ids=true | all-gather | bytes 576 | tf_op jit(solution)/shard_map/all_gather | solution.py:641
  141.7 12.1 %collective-permute-done.8.refs_9_ = f32[8,2,32,256]{3,2,1,0:T(8,128)} collective-permute-done((f32[8,2,32,256]{3,2,1,0:T(8,128)}, f32[8,2,32,256]{3,2,1,0:T(8,128)}, u32[]{:S(2)}, u32[]{:S(2)}) %collective-permute-start.8) | collective-permute-done | bytes 524320 | tf_op jit(solution)/shard_map/ppermute | solution.py:607
  153.8 11.3 %collective-permute-done.9.refs_10_ = f32[8,2,32,256]{3,2,1,0:T(8,128)} collective-permute-done((f32[8,2,32,256]{3,2,1,0:T(8,128)}, f32[8,2,32,256]{3,2,1,0:T(8,128)}, u32[]{:S(2)}, u32[]{:S(2)}) %collective-permute-start.9) | collective-permute-done | bytes 524320 | tf_op jit(solution)/shard_map/ppermute | solution.py:607
  165.1 0.9 copy-done.6
  167.9 8.1 %azimuth_focus.3 = f32[8,2,16,256]{3,2,1,0:T(8,128)S(1)} custom-call(f32[4,2,32,256]{3,2,1,0:T(8,128)S(1)} %copy-done, f32[4,2,32,256]{3,2,1,0:T(8,128)} %collective-permute-done.refs_1_, f32[4,2,32,256]{3,2,1,0:T(8,128)} %collective-permute-done.1.refs_2_, f32[4,2,32,256]{3,2,1,0:T(8,128)} %collective-permute-done.2.refs_3_, ...), custom_call_target="tpu_custom_call" | custom-call | flops 1610612736 | bytes 6291456 | tf_op jit(solution)/shard_map/azimuth_focus/pallas_call | solution.py:543
  176.0 10.0 %all_to_all.10 = f32[8,2,16,256]{3,2,1,0:T(8,128)S(1)} all-to-all(f32[8,2,16,256]{3,2,1,0:T(8,128)S(1)} %azimuth_focus.3), channel_id=1, replica_groups=mesh['acq'=8,'strip'=4] {'acq'}, dimensions={0} | all-to-all | bytes 524288 | tf_op jit(solution)/shard_map/all_to_all | solution.py:676
  (49 shorter events, 6.9 us)
Async XLA Ops:
  7.3 111.8 %all-to-all-start = ((f32[32,2,32,256]{3,2,1,0:T(8,128)}), f32[32,2,32,256]{3,2,1,0:T(8,128)S(1)}, u32[]{:S(2)}, u32[]{:S(2)}) async-start(f32[32,2,32,256]{3,2,1,0:T(8,128)} %bitcast.34), calls=%async_computation | async-start | bytes 4194304 | tf_op jit(solution)/shard_map/all_to_all | solution.py:595
  23.3 15.1 %collective-permute-start.6 = (f32[4,2,32,256]{3,2,1,0:T(8,128)S(1)}, f32[4,2,32,256]{3,2,1,0:T(8,128)S(1)}, u32[]{:S(2)}, u32[]{:S(2)}) collective-permute-start(f32[4,2,32,256]{3,2,1,0:T(8,128)S(1)} %get-tuple-element.43), channel_id=1, source_target_pairs={{0,28},{4,24},{8,20},{12,16},{16,12},{20,8},{24,4},{28,0},{1,29},{... | collective-permute-start | bytes 786440 | tf_op jit(solution)/shard_map/ppermute | solution.py:607
  25.5 25.3 %collective-permute-start.5 = (f32[4,2,32,256]{3,2,1,0:T(8,128)S(1)}, f32[4,2,32,256]{3,2,1,0:T(8,128)S(1)}, u32[]{:S(2)}, u32[]{:S(2)}) collective-permute-start(f32[4,2,32,256]{3,2,1,0:T(8,128)S(1)} %get-tuple-element.44), channel_id=1, source_target_pairs={{0,24},{4,28},{8,16},{12,20},{16,8},{20,12},{24,0},{28,4},{1,25},{... | collective-permute-start | bytes 786440 | tf_op jit(solution)/shard_map/ppermute | solution.py:607
  26.0 40.4 %collective-permute-start.4 = (f32[4,2,32,256]{3,2,1,0:T(8,128)}, f32[4,2,32,256]{3,2,1,0:T(8,128)}, u32[]{:S(2)}, u32[]{:S(2)}) collective-permute-start(f32[4,2,32,256]{3,2,1,0:T(8,128)} %get-tuple-element.45), channel_id=1, source_target_pairs={{0,20},{4,16},{8,28},{12,24},{16,4},{20,0},{24,12},{28,8},{1,21},{... | collective-permute-start | bytes 786440 | tf_op jit(solution)/shard_map/ppermute | solution.py:607
  27.2 39.3 %collective-permute-start.3 = (f32[4,2,32,256]{3,2,1,0:T(8,128)}, f32[4,2,32,256]{3,2,1,0:T(8,128)}, u32[]{:S(2)}, u32[]{:S(2)}) collective-permute-start(f32[4,2,32,256]{3,2,1,0:T(8,128)} %get-tuple-element.46), channel_id=1, source_target_pairs={{0,16},{4,20},{8,24},{12,28},{16,0},{20,4},{24,8},{28,12},{1,17},{... | collective-permute-start | bytes 786440 | tf_op jit(solution)/shard_map/ppermute | solution.py:607
  27.7 38.7 %collective-permute-start.2 = (f32[4,2,32,256]{3,2,1,0:T(8,128)}, f32[4,2,32,256]{3,2,1,0:T(8,128)}, u32[]{:S(2)}, u32[]{:S(2)}) collective-permute-start(f32[4,2,32,256]{3,2,1,0:T(8,128)} %get-tuple-element.47), channel_id=1, source_target_pairs={{0,12},{4,8},{8,4},{12,0},{16,28},{20,24},{24,20},{28,16},{1,13},{... | collective-permute-start | bytes 786440 | tf_op jit(solution)/shard_map/ppermute | solution.py:607
  38.4 22.8 %copy-start.1 = (f32[4,2,32,256]{3,2,1,0:T(8,128)}, f32[4,2,32,256]{3,2,1,0:T(8,128)S(1)}, u32[]{:S(2)}) copy-start(f32[4,2,32,256]{3,2,1,0:T(8,128)S(1)} %collective-permute-done.6.refs_7_) | copy-start | bytes 786436
  38.4 28.0 %collective-permute-start.1 = (f32[4,2,32,256]{3,2,1,0:T(8,128)}, f32[4,2,32,256]{3,2,1,0:T(8,128)}, u32[]{:S(2)}, u32[]{:S(2)}) collective-permute-start(f32[4,2,32,256]{3,2,1,0:T(8,128)} %get-tuple-element.48), channel_id=1, source_target_pairs={{0,8},{4,12},{8,0},{12,4},{16,24},{20,28},{24,16},{28,20},{1,9},{5... | collective-permute-start | bytes 786440 | tf_op jit(solution)/shard_map/ppermute | solution.py:607
  50.8 10.4 %copy-start.3 = (f32[4,2,32,256]{3,2,1,0:T(8,128)}, f32[4,2,32,256]{3,2,1,0:T(8,128)S(1)}, u32[]{:S(2)}) copy-start(f32[4,2,32,256]{3,2,1,0:T(8,128)S(1)} %collective-permute-done.5.refs_6_) | copy-start | bytes 786436
  50.8 15.7 %collective-permute-start = (f32[4,2,32,256]{3,2,1,0:T(8,128)}, f32[4,2,32,256]{3,2,1,0:T(8,128)}, u32[]{:S(2)}, u32[]{:S(2)}) collective-permute-start(f32[4,2,32,256]{3,2,1,0:T(8,128)} %get-tuple-element.49), channel_id=1, source_target_pairs={{0,4},{4,0},{8,12},{12,8},{16,20},{20,16},{24,28},{28,24},{1,5},{5... | collective-permute-start | bytes 786440 | tf_op jit(solution)/shard_map/ppermute | solution.py:607
  61.2 57.9 %copy-start.7 = (bf16[512,128]{1,0:T(8,128)(2,1)S(1)}, bf16[512,128]{1,0:T(8,128)(2,1)}, u32[]{:S(2)}) copy-start(bf16[512,128]{1,0:T(8,128)(2,1)} %constant.36.clone.refs_5_.refs_15_) | copy-start | bytes 393220
  61.2 57.9 %copy-start.12 = (f32[4,8,128]{2,1,0:T(8,128)S(1)}, f32[4,8,128]{2,1,0:T(8,128)}, u32[]{:S(2)}) copy-start(f32[4,8,128]{2,1,0:T(8,128)} %constant.35.clone.refs_4_.refs_14_) | copy-start | bytes 49156
  66.4 98.7 %copy-start = (f32[4,2,32,256]{3,2,1,0:T(8,128)S(1)}, f32[4,2,32,256]{3,2,1,0:T(8,128)}, u32[]{:S(2)}) copy-start(f32[4,2,32,256]{3,2,1,0:T(8,128)} %get-tuple-element.27.refs_0_) | copy-start | bytes 786436
  66.4 98.7 %copy-start.2 = (f32[4,2,32,256]{3,2,1,0:T(8,128)S(1)}, f32[4,2,32,256]{3,2,1,0:T(8,128)}, u32[]{:S(2)}) copy-start(f32[4,2,32,256]{3,2,1,0:T(8,128)} %copy-done.1) | copy-start | bytes 786436
  66.4 98.7 %copy-start.4 = (f32[4,2,32,256]{3,2,1,0:T(8,128)S(1)}, f32[4,2,32,256]{3,2,1,0:T(8,128)}, u32[]{:S(2)}) copy-start(f32[4,2,32,256]{3,2,1,0:T(8,128)} %copy-done.3) | copy-start | bytes 786436
  115.5 26.1 %collective-permute-start.7 = (f32[8,2,32,256]{3,2,1,0:T(8,128)}, f32[8,2,32,256]{3,2,1,0:T(8,128)}, u32[]{:S(2)}, u32[]{:S(2)}) collective-permute-start(f32[8,2,32,256]{3,2,1,0:T(8,128)} %get-tuple-element.35), channel_id=1, source_target_pairs={{0,1},{1,0},{2,3},{3,2},{4,5},{5,4},{6,7},{7,6},{8,9},{9,8},{10,11... | collective-permute-start | bytes 1572872 | tf_op jit(solution)/shard_map/ppermute | solution.py:607
  115.6 38.2 %collective-permute-start.8 = (f32[8,2,32,256]{3,2,1,0:T(8,128)}, f32[8,2,32,256]{3,2,1,0:T(8,128)}, u32[]{:S(2)}, u32[]{:S(2)}) collective-permute-start(f32[8,2,32,256]{3,2,1,0:T(8,128)} %get-tuple-element.36), channel_id=1, source_target_pairs={{0,2},{1,3},{2,0},{3,1},{4,6},{5,7},{6,4},{7,5},{8,10},{9,11},{10,... | collective-permute-start | bytes 1572872 | tf_op jit(solution)/shard_map/ppermute | solution.py:607
  118.7 46.4 %collective-permute-start.9 = (f32[8,2,32,256]{3,2,1,0:T(8,128)}, f32[8,2,32,256]{3,2,1,0:T(8,128)}, u32[]{:S(2)}, u32[]{:S(2)}) collective-permute-start(f32[8,2,32,256]{3,2,1,0:T(8,128)} %get-tuple-element.37), channel_id=1, source_target_pairs={{0,3},{1,2},{2,1},{3,0},{4,7},{5,6},{6,5},{7,4},{8,11},{9,10},{10,... | collective-permute-start | bytes 1572872 | tf_op jit(solution)/shard_map/ppermute | solution.py:607
  119.1 14.2 %copy-start.14 = (s32[1,2]{1,0:T(1,128)S(1)}, s32[1,2]{1,0:T(1,128)}, u32[]{:S(2)}) copy-start(s32[1,2]{1,0:T(1,128)} %param.23) | copy-start | bytes 28
  119.1 14.2 %copy-start.13 = (f32[8,1,2]{0,2,1:T(2,128)S(1)}, f32[8,1,2]{0,2,1:T(2,128)}, u32[]{:S(2)}) copy-start(f32[8,1,2]{0,2,1:T(2,128)} %param.24) | copy-start | bytes 196
  119.1 0.9 copy-start.8
  120.9 12.4 %copy-start.15 = (s32[2]{0:T(128)S(1)}, s32[2]{0:T(128)}, u32[]{:S(2)}) copy-start(s32[2]{0:T(128)} %constant.37.clone) | copy-start | bytes 28
  129.7 35.4 %collective-permute-start.10 = (f32[8,2,2,1,256]{4,3,2,1,0:T(1,128)S(1)}, f32[8,2,2,1,256]{4,3,2,1,0:T(1,128)S(1)}, u32[]{:S(2)}, u32[]{:S(2)}) collective-permute-start(f32[8,2,2,1,256]{4,3,2,1,0:T(1,128)S(1)} %slice.35), channel_id=1, source_target_pairs={{4,0},{8,4},{12,8},{16,12},{20,16},{24,20},{28,24},{1,28},{5,1},{9... | collective-permute-start | bytes 98312 | tf_op jit(solution)/shard_map/ppermute | solution.py:667
  165.1 1.0 copy-start.6
  (4 other events, 3.4 us)

commit v7 on v6

--- a/solution.py
+++ b/solution.py
@@ -14,7 +14,8 @@
 RADIX = 8
 ROWS = 8
 RANGE_VMEM = 60 * 1024 * 1024
-FOCUS_VMEM = 28 * 1024 * 1024
+LAYOUT_VMEM = 8 * 1024 * 1024
+FOCUS_VMEM = 60 * 1024 * 1024
 OWNERS = ("strip", "acq")
 
 
@@ -103,7 +104,7 @@
         self.base = samples // RADIX
         self.owned = samples // (strips * epochs)
         even = all(size & (size - 1) == 0 for size in (strips, epochs))
-        self.parts = 2 if even and self.owned % (2 * LOOK * ROWS) == 0 else 1
+        self.parts = 2 if even and self.owned in (64, 128) else 1
         self.rows = self.owned // self.parts
         self.looks = self.rows // LOOK
         self.planes = self.looks % ROWS == 0
@@ -170,9 +171,13 @@
 
 
 def compress_kernel(
-    plan, part, relative, filter_ref, high_any, low_any, turn_any, raw_ref, out_ref,
-    table_high, table_low, turn_ref, raw, t_high, t_low, y_high, y_low, z_ref, sems, table_sems,
+    plan, part, relative, filter_ref, high_any, low_any, turn_any, raw_ref, *refs
 ):
+    outs = refs[: plan.epochs if relative else 1]
+    (
+        table_high, table_low, turn_ref, raw, t_high, t_low, y_high, y_low, z_ref, sems, table_sems,
+    ) = refs[len(outs) :][:11]
+    out_ref = refs[-2] if relative else outs[0]
     base, blocks = plan.base, plan.blocks
     tiles = plan.rows // ROWS
     chunk = blocks * plan.rows
@@ -261,6 +266,15 @@
                     else:
                         place = strip, owner
                     out_ref[place[0], place[1], c, rows, :] = value[c]
+    if relative:
+        copies = fetch(
+            [
+                pltpu.make_async_copy(out_ref.at[m], out, refs[-1].at[m])
+                for m, out in enumerate(outs)
+            ]
+        )
+        for copy in copies:
+            copy.wait()
 
 
 def compress(plan, part, relative, range_filter, raw):
@@ -268,13 +282,21 @@
     whole = pl.BlockSpec(memory_space=pltpu.VMEM)
     bytes_moved = 4 * (raw.size + raw.size // plan.parts)
     tables = lag_tables(plan)
-    places = (plan.strips, plan.epochs)
-    places = places[::-1] if relative else places
+    slab = (2, plan.rows, plan.pulses)
+    shape = (plan.strips,) + (slab if relative else (plan.epochs,) + slab)
+    scratch, out_specs = [], whole
+    if relative:
+        out_specs = [pl.BlockSpec(memory_space=pltpu.HBM)] * plan.epochs
+        scratch = [
+            pltpu.VMEM((plan.epochs,) + shape, jnp.float32),
+            pltpu.SemaphoreType.DMA((plan.epochs,)),
+        ]
+    shape = jax.ShapeDtypeStruct(shape, jnp.float32)
     return pl.pallas_call(
         functools.partial(compress_kernel, plan, part, relative),
-        out_shape=jax.ShapeDtypeStruct(places + (2, plan.rows, plan.pulses), jnp.float32),
+        out_shape=[shape] * plan.epochs if relative else shape,
         in_specs=[whole] + [pl.BlockSpec(memory_space=pltpu.HBM)] * 4,
-        out_specs=whole,
+        out_specs=out_specs,
         scratch_shapes=[
             *[pltpu.VMEM(table.shape, table.dtype) for table in tables],
             pltpu.VMEM(raw.shape, jnp.float32),
@@ -285,6 +307,7 @@
             pltpu.VMEM((RADIX, 2 * chunk, plan.pulses), jnp.float32),
             pltpu.SemaphoreType.DMA((4,)),
             pltpu.SemaphoreType.DMA((3,)),
+            *scratch,
         ],
         compiler_params=pltpu.CompilerParams(vmem_limit_bytes=RANGE_VMEM),
         cost_estimate=pl.CostEstimate(
@@ -299,7 +322,7 @@
 def focus_kernel(plan, part, final, field_at, own, *refs):
     filter_any, high_any, low_any, twiddle_any, sum_any = refs[:5]
     if final:
-        weight_ref, before_ref, halo_ref, out_ref = refs[5:9]
+        weight_ref, before_any, halo_any, out_ref = refs[5:9]
     else:
         (out_ref,) = refs[5:6]
     scratch = refs[9 if final else 6 :]
@@ -312,14 +335,18 @@
     group = max(1, step // rows)
     per_block = field_ref.shape[-1] // lanes
 
-    def field_copies(slot):
-        return [
+    half = epochs // 2
+    fields = [
+        [
             pltpu.make_async_copy(
-                field_at(slot, at), field_ref.at[at ^ own[1], slot ^ own[0]], field_sems.at[slot, at]
+                field_at(at).at[pl.ds(side * half, half)],
+                field_ref.at[at, pl.ds(side * half, half)],
+                field_sems.at[at, side],
             )
             for at in range(field_ref.shape[0])
         ]
-
+        for side in range(2)
+    ]
     tables = [
         pltpu.make_async_copy(source, target, table_sems.at[at])
         for at, (source, target) in enumerate(
@@ -333,29 +360,35 @@
         )
     ]
     fetch(tables[:1])
-    for j in range(epochs):
-        fetch(field_copies(j))
+    for copies in fields:
+        fetch(copies)
     fetch(tables[1:])
+    if final:
+        looked_ref, slope_ref, halo_ref, late_sems = scratch[13:]
+        late = [
+            pltpu.make_async_copy(
+                before, looked_ref.at[:, :, :, pl.ds(at * looks, looks), :], late_sems.at[at]
+            )
+            for at, before in enumerate(before_any)
+        ]
+        late = fetch(late + [pltpu.make_async_copy(halo_any, halo_ref, late_sems.at[part])])
     tables[0].wait()
 
-    def rows_of(strip, j, c, top, start):
+    def rows_of(strip, slot, c, top, start):
         some = [
-            field_ref[strip, j + g, c, top : top + min(rows, step), start : start + lanes]
+            field_ref[strip, slot + g, c, top : top + min(rows, step), start : start + lanes]
             for g in range(group)
         ]
         return some[0] if group == 1 else jnp.concatenate(some, axis=0)
 
     def forward(at, carry):
-        for g in range(group):
-            for block in range(field_ref.shape[0]):
-                place = field_ref.at[block, at * group + g]
-                pltpu.make_async_copy(place, place, field_sems.at[at * group + g, block]).wait()
-        j = at * group ^ own[0]
+        slot = at * group
+        j = slot ^ own[0]
         for top in range(0, rows, step):
             x = []
             for a in range(RADIX):
                 strip, start = a // per_block, a % per_block * lanes
-                x.append(tuple(rows_of(strip, j, c, top, start) for c in range(2)))
+                x.append(tuple(rows_of(strip ^ own[1], slot, c, top, start) for c in range(2)))
             at = pl.ds(pl.multiple_of(j * rows + top, step), step)
             for d, value in enumerate(dft8(x, -1.0)):
                 if d > 0:
@@ -366,7 +399,10 @@
                     y_low[d, at, c * lanes : (c + 1) * lanes] = low
         return carry
 
-    lax.fori_loop(0, epochs // group, forward, 0)
+    for side, copies in enumerate(fields):
+        for copy in copies:
+            copy.wait()
+        lax.fori_loop(side * half // group, (side + 1) * half // group, forward, 0)
     for copy in tables[1:]:
         copy.wait()
 
@@ -440,9 +476,8 @@
     looked = jnp.concatenate(looked, axis=1)
     looked = looked.reshape(epochs, 2, 2, looks, plan.azimuth_looks)
     if final:
-        looked_ref, slope_ref = scratch[13:]
-        for at, before in enumerate(before_ref):
-            looked_ref[:, :, :, at * looks : (at + 1) * looks, :] = before[...]
+        for copy in late:
+            copy.wait()
         looked_ref[:, :, :, part * looks :, :] = looked
         slopes_and_sums(plan, weight_ref, looked_ref, halo_ref, out_ref, slope_ref)
     else:
@@ -507,7 +542,7 @@
         pltpu.VMEM((RADIX, total, 2 * lanes), jnp.float32),
         pltpu.VMEM((plan.epochs + 2, 2, plan.rows, plan.azimuth), jnp.float32),
         pltpu.VMEM((plan.epochs, 2, 2, plan.looks, plan.azimuth), jnp.float32),
-        pltpu.SemaphoreType.DMA((plan.epochs, blocks)),
+        pltpu.SemaphoreType.DMA((blocks, 2)),
         pltpu.SemaphoreType.DMA((5,)),
     ]
     shape = looked
@@ -515,10 +550,13 @@
         weights, before, halo = finish
         shape = gradients
         operands += [weights, *before, halo]
-        in_specs += [pl.BlockSpec(memory_space=pltpu.SMEM)] + [whole] * (len(before) + 1)
+        in_specs += [pl.BlockSpec(memory_space=pltpu.SMEM)]
+        in_specs += [pl.BlockSpec(memory_space=pltpu.HBM)] * (len(before) + 1)
         scratch += [
             pltpu.VMEM((plan.epochs, 2, 2, plan.looks * plan.parts, plan.azimuth_looks), jnp.float32),
             pltpu.VMEM((2 * plan.epochs,) + gradients[1:], jnp.float32),
+            pltpu.VMEM(halo.shape, jnp.float32),
+            pltpu.SemaphoreType.DMA((plan.parts,)),
         ]
 
     def kernel(*refs):
@@ -527,10 +565,8 @@
         relative = len(some) > 1
         own = (lax.axis_index("acq"), lax.axis_index("strip")) if relative else (0, 0)
 
-        def field_at(j, at):
-            if not relative:
-                return some[0].at[at, j]
-            return some[j].at[0] if at == 0 else some[plan.epochs + at - 1].at[j]
+        def field_at(at):
+            return some[at] if relative else some[0].at[at]
 
         if finish is None:
             focus_kernel(plan, part, False, field_at, own, *refs)
@@ -589,6 +625,46 @@
     return own.transpose(order).reshape(plan.parts, 2, RADIX, plan.rows, plan.lanes)
 
 
+def own_filter_kernel(plan, filter_any, out_ref, block_ref, turned_ref, sem):
+    width = block_ref.shape[-1]
+    acq = lax.axis_index("acq")
+    start = acq * plan.owned // width * width
+    inside = acq * plan.owned % width
+    copy = pltpu.make_async_copy(
+        filter_any.at[:, :, pl.ds(pl.multiple_of(start, width), width)], block_ref, sem
+    )
+    copy.start()
+    copy.wait()
+    for c in range(2):
+        for d in range(RADIX):
+            turned_ref[...] = block_ref[c, pl.ds(d, plan.lanes, stride=RADIX), :].T
+            for part in range(plan.parts):
+                for tile in range(plan.rows // ROWS):
+                    row = plan.tile_shift(part, 0, tile)
+                    rows = pl.ds(inside + row, ROWS, stride=plan.tile_stride())
+                    out_ref[part, c, d, tile * ROWS : (tile + 1) * ROWS, :] = turned_ref[rows, :]
+
+
+def own_filter_by_kernel(plan, azimuth_filter):
+    width = 128
+    return pl.pallas_call(
+        functools.partial(own_filter_kernel, plan),
+        out_shape=jax.ShapeDtypeStruct(
+            (plan.parts, 2, RADIX, plan.rows, plan.lanes), jnp.float32
+        ),
+        in_specs=[pl.BlockSpec(memory_space=pltpu.HBM)],
+        out_specs=pl.BlockSpec(memory_space=pltpu.VMEM),
+        scratch_shapes=[
+            pltpu.VMEM((2, plan.azimuth, width), jnp.float32),
+            pltpu.VMEM((width, plan.lanes), jnp.float32),
+            pltpu.SemaphoreType.DMA,
+        ],
+        compiler_params=pltpu.CompilerParams(vmem_limit_bytes=LAYOUT_VMEM),
+        cost_estimate=pl.CostEstimate(flops=0, bytes_accessed=1024, transcendentals=0),
+        name="own_filter",
+    )(azimuth_filter)
+
+
 def exchange_all(plan, block):
     shape = block.shape
     block = block.reshape((plan.strips * plan.epochs,) + shape[2:])
@@ -600,37 +676,47 @@
     return received.reshape(plan.strips // join, plan.epochs, 2, plan.rows, join * plan.pulses)
 
 
-def partners(slots, axis, first=0):
+def partners(slots, axis):
     size = lax.axis_size(axis)
     moved = []
-    for k, slot in enumerate(slots, first):
+    for k, slot in enumerate(slots):
         moved.append(slot if k == 0 else lax.ppermute(slot, axis, [(i, i ^ k) for i in range(size)]))
     return moved
 
 
 def regroup(plan, others):
-    far = range(1, plan.strips)
-
     def kernel(*refs):
-        ins, outs, sems = refs[: plan.epochs], refs[plan.epochs : -1], refs[-1]
-        copies = fetch(
+        ins, outs = refs[: plan.epochs], refs[plan.epochs : plan.epochs + plan.strips]
+        stage, in_sems, out_sems = refs[plan.epochs + plan.strips :]
+        inward = fetch(
             [
-                pltpu.make_async_copy(ins[m].at[k], outs[k - 1].at[m], sems.at[m, k])
-                for k in far
+                pltpu.make_async_copy(ins[m].at[k], stage.at[k, m], in_sems.at[k, m])
+                for k in range(plan.strips)
                 for m in range(plan.epochs)
             ]
         )
-        for copy in copies:
+        outward = []
+        for k in range(plan.strips):
+            for copy in inward[k * plan.epochs : (k + 1) * plan.epochs]:
+                copy.wait()
+            outward += fetch([pltpu.make_async_copy(stage.at[k], outs[k], out_sems.at[k])])
+        for copy in outward:
             copy.wait()
 
-    shape = jax.ShapeDtypeStruct((plan.epochs,) + others[0].shape[1:], jnp.float32)
+    slab = (plan.epochs,) + others[0].shape[1:]
     place = pl.BlockSpec(memory_space=pltpu.HBM)
     return pl.pallas_call(
         kernel,
-        out_shape=[shape for _ in far],
+        out_shape=[jax.ShapeDtypeStruct(slab, jnp.float32)] * plan.strips,
         in_specs=[place] * plan.epochs,
-        out_specs=[place for _ in far],
-        scratch_shapes=[pltpu.SemaphoreType.DMA((plan.epochs, plan.strips))],
+        out_specs=[place] * plan.strips,
+        scratch_shapes=[
+            pltpu.VMEM((plan.strips,) + slab, jnp.float32),
+            pltpu.SemaphoreType.DMA((plan.strips, plan.epochs)),
+            pltpu.SemaphoreType.DMA((plan.strips,)),
+        ],
+        compiler_params=pltpu.CompilerParams(vmem_limit_bytes=LAYOUT_VMEM),
+        cost_estimate=pl.CostEstimate(flops=0, bytes_accessed=1024, transcendentals=0),
         name="regroup",
     )(*others)
 
@@ -651,13 +737,15 @@
     if plan.parts > 1:
         range_filter, block = lax.optimization_barrier((range_filter, block))
         other = compress(plan, 1, True, range_filter, raw)
-        other, azimuth_filter = lax.optimization_barrier((other, azimuth_filter))
-    spectrum = own_filter(plan, azimuth_filter)
+        *other, azimuth_filter = lax.optimization_barrier((*other, azimuth_filter))
+        spectrum = own_filter_by_kernel(plan, azimuth_filter)
+    else:
+        spectrum = own_filter(plan, azimuth_filter)
     field = exchange_all(plan, block)
     if plan.parts > 1:
-        other = partners([other[k] for k in range(epochs)], "acq")
+        other = partners(other, "acq")
         *other, spectrum = lax.optimization_barrier((*other, spectrum))
-        slots = partners(regroup(plan, other), "strip", 1)
+        slots = partners(regroup(plan, other), "strip")
     before = [focus(plan, 0, [field], spectrum)]
     before[0], pair_mask, inversion = lax.optimization_barrier((before[0], pair_mask, inversion))
     weights = all_weights(pair_mask, inversion)
@@ -670,7 +758,7 @@
         [(device[i], device[i - 1]) for i in range(1, owners)],
     )
     if plan.parts > 1:
-        gradients = focus(plan, 1, other + slots, spectrum, (weights, before, halo))
+        gradients = focus(plan, 1, slots, spectrum, (weights, before, halo))
     else:
         gradients = slopes_to_epochs(plan, weights, before[0], halo)
     gathered = lax.all_to_all(gradients, "acq", split_axis=0, concat_axis=0, tiled=True)

time: 187 us -> 137 us (0.73)
  Pallas kernels: 79.8 us -> 33.8 us
  local copies, waits for them, and re-layouts: 24.3 us -> 6.74 us
  waiting for transfers between devices: 42 us -> 58.2 us
  starting transfers between devices: 22 us -> 19.1 us
    pallas_call x1 -> x2, Pallas kernels: 49 us -> 3.71 us  [the longest x1 3.21 us: regroup(): pl.pallas_call(kernel, out_shape=[jax.ShapeDtypeStruct(slab, jnp.float32)...]
    ppermute x10, waiting for transfers between devices: 42 us -> 58.2 us  [partners(): lax.ppermute(slot, axis, [(i, i ^ k) for i in range(size)])]
    reshape x1 -> x0, local copies, waits for them, and re-layouts: 6.21 us -> none  [own_filter(): own = own.reshape(2, plan.lanes, RADIX, plan.parts, plan.looks, LOOK)]
    transpose x1 -> x0, local copies, waits for them, and re-layouts: 5.18 us -> none  [own_filter(): own.transpose(order).reshape(plan.parts, 2, RADIX, plan.rows, plan.lanes)]
    dynamic_slice x2 -> x0, local copies, waits for them, and re-layouts: 4.18 us -> none  [own_filter(): own = lax.dynamic_slice_in_dim(azimuth_filter, start, plan.owned, axis=2)]
    squeeze x1 -> x0, local copies, waits for them, and re-layouts: 2.66 us -> none  [per_device(): other = partners([other[k] for k in range(epochs)], 'acq')]
    ppermute x10, starting transfers between devices: 12.4 us -> 10 us  [partners(): lax.ppermute(slot, axis, [(i, i ^ k) for i in range(size)])]
    unnamed x32 -> x20, local copies, waits for them, and re-layouts: 5.3 us -> 4.4 us
  transfers between devices with their start and end apart: 12 -> 12, of which waited for: 4 -> 6; matrix products, arithmetic and copies ran while one was open for 10% -> 1% of each run, Pallas kernels for 34% -> 13%
where the time goes in v7:
time: 137 us
  waiting for transfers between devices  58.2 us (42%)
  Pallas kernels  33.8 us (25%)
  starting transfers between devices  19.1 us (14%)
  blocking collectives  18.5 us (14%)
  local copies, waits for them, and re-layouts  6.74 us (5%)
    ppermute x10, waiting for transfers between devices, partners(): lax.ppermute(slot, axis, [(i, i ^ k) for i in range(size)])  58.2 us
    pallas_call x2, Pallas kernels, focus(): pl.pallas_call(kernel, out_shape=jax.ShapeDtypeStruct(shape, jnp.float32)...  15.6 us
    pallas_call x2, Pallas kernels, compress(): pl.pallas_call(functools.partial(compress_kernel, plan, part, relative),...  14.6 us
    all_to_all x1, blocking collectives, per_device(): lax.all_to_all(gradients, 'acq', split_axis=0, concat_axis=0, tiled=True)  10.3 us
    ppermute x10, starting transfers between devices, partners(): lax.ppermute(slot, axis, [(i, i ^ k) for i in range(size)])  10 us
    all_gather x1, blocking collectives, all_weights(): lax.all_gather(inversion[:, 0, :] * usable[None, :], 'acq', axis=1, tiled...  8.23 us
    all_to_all x1, starting transfers between devices, exchange_all(): lax.all_to_all(block, OWNERS, split_axis=0, concat_axis=0, tiled=True)  6.11 us
    unnamed x20, local copies, waits for them, and re-layouts  4.4 us
  transfers between devices with their start and end apart: 12, of which 6 were waited for; matrix products, arithmetic and copies ran while one was open for 1% of the time, Pallas kernels for 13%

profile of v7, /device:TPU:8, one launch (start us, length us, event | category | flops | bytes accessed | tf_op | source)
XLA Modules:
  0.0 136.6 jit_solution(5544307478093526702)
XLA Ops:
  0.0 7.2 %range_compress.2 = f32[4,8,2,32,256]{4,3,2,1,0:T(8,128)} custom-call(f32[2,2048]{1,0:T(2,128)} %filter_ref.2, bf16[256,512]{1,0:T(8,128)(2,1)} %constant.24.clone.high_any, bf16[256,512]{1,0:T(8,128)(2,1)} %constant.25.clone.low_any, f32[4,8,256]{2,1,0:T(8,128)} %constant.26.clone.turn_any, f32[2,256,2048]{2,1,0:T(8,128)} %bitcast.9), custom_call_target="tpu_custom_call" | custom-call | flops 1610612736 | bytes 6291456 | tf_op jit(solution)/shard_map/range_compress/pallas_call | solution.py:295
  7.2 6.1 %all-to-all-start = ((f32[32,2,32,256]{3,2,1,0:T(8,128)}), f32[32,2,32,256]{3,2,1,0:T(8,128)}, u32[]{:S(2)}, u32[]{:S(2)}) async-start(f32[32,2,32,256]{3,2,1,0:T(8,128)} %bitcast.8), calls=%async_computation | async-start | bytes 4194304 | tf_op jit(solution)/shard_map/all_to_all | solution.py:671
  13.3 7.3 %range_compress.3 = (f32[4,2,32,256]{3,2,1,0:T(8,128)}, f32[4,2,32,256]{3,2,1,0:T(8,128)}, f32[4,2,32,256]{3,2,1,0:T(8,128)}, f32[4,2,32,256]{3,2,1,0:T(8,128)},...) custom-call(f32[2,2048]{1,0:T(2,128)} %filter_ref.2, ...), custom_call_target="tpu_custom_call" | custom-call | flops 1610612736 | bytes 6291456 | tf_op jit(solution)/shard_map/range_compress/pallas_call | solution.py:295
  20.9 1.5 %collective-permute-start.1 = (f32[4,2,32,256]{3,2,1,0:T(8,128)}, f32[4,2,32,256]{3,2,1,0:T(8,128)S(1)}, u32[]{:S(2)}, u32[]{:S(2)}) collective-permute-start(f32[4,2,32,256]{3,2,1,0:T(8,128)} %get-tuple-element.51), channel_id=1, source_target_pairs={{0,8},{4,12},{8,0},{12,4},{16,24},{20,28},{24,16},{28,20},{1,9},{5... | collective-permute-start | bytes 786440 | tf_op jit(solution)/shard_map/ppermute | solution.py:683
  22.6 1.5 %collective-permute-start.3 = (f32[4,2,32,256]{3,2,1,0:T(8,128)}, f32[4,2,32,256]{3,2,1,0:T(8,128)S(1)}, u32[]{:S(2)}, u32[]{:S(2)}) collective-permute-start(f32[4,2,32,256]{3,2,1,0:T(8,128)} %get-tuple-element.53), channel_id=1, source_target_pairs={{0,16},{4,20},{8,24},{12,28},{16,0},{20,4},{24,8},{28,12},{1,17},{... | collective-permute-start | bytes 786440 | tf_op jit(solution)/shard_map/ppermute | solution.py:683
  24.4 2.4 %collective-permute-start.5 = (f32[4,2,32,256]{3,2,1,0:T(8,128)}, f32[4,2,32,256]{3,2,1,0:T(8,128)S(1)}, u32[]{:S(2)}, u32[]{:S(2)}) collective-permute-start(f32[4,2,32,256]{3,2,1,0:T(8,128)} %get-tuple-element.55), channel_id=1, source_target_pairs={{0,24},{4,28},{8,16},{12,20},{16,8},{20,12},{24,0},{28,4},{1,25},{... | collective-permute-start | bytes 786440 | tf_op jit(solution)/shard_map/ppermute | solution.py:683
  26.8 7.6 %collective-permute-done.1.refs_2_ = f32[4,2,32,256]{3,2,1,0:T(8,128)S(1)} collective-permute-done((f32[4,2,32,256]{3,2,1,0:T(8,128)}, f32[4,2,32,256]{3,2,1,0:T(8,128)S(1)}, u32[]{:S(2)}, u32[]{:S(2)}) %collective-permute-start.1) | collective-permute-done | bytes 262176 | tf_op jit(solution)/shard_map/ppermute | solution.py:683
  34.9 2.2 %copy-done = f32[2,1024,512]{2,1,0:T(8,128)S(1)} copy-done((f32[2,1024,512]{2,1,0:T(8,128)S(1)}, f32[2,1024,512]{2,1,0:T(8,128)}, u32[]{:S(2)}) %copy-start) | copy-done | bytes 4194328
  37.6 0.8 copy-done.1
  38.4 8.3 %collective-permute-done.2.refs_3_ = f32[4,2,32,256]{3,2,1,0:T(8,128)S(1)} collective-permute-done((f32[4,2,32,256]{3,2,1,0:T(8,128)}, f32[4,2,32,256]{3,2,1,0:T(8,128)S(1)}, u32[]{:S(2)}, u32[]{:S(2)}) %collective-permute-start.2) | collective-permute-done | bytes 262176 | tf_op jit(solution)/shard_map/ppermute | solution.py:683
  46.7 8.7 %collective-permute-done.5.refs_6_ = f32[4,2,32,256]{3,2,1,0:T(8,128)S(1)} collective-permute-done((f32[4,2,32,256]{3,2,1,0:T(8,128)}, f32[4,2,32,256]{3,2,1,0:T(8,128)S(1)}, u32[]{:S(2)}, u32[]{:S(2)}) %collective-permute-start.5) | collective-permute-done | bytes 262176 | tf_op jit(solution)/shard_map/ppermute | solution.py:683
  55.4 7.4 %collective-permute-done.6.refs_7_ = f32[4,2,32,256]{3,2,1,0:T(8,128)S(1)} collective-permute-done((f32[4,2,32,256]{3,2,1,0:T(8,128)}, f32[4,2,32,256]{3,2,1,0:T(8,128)S(1)}, u32[]{:S(2)}, u32[]{:S(2)}) %collective-permute-start.6) | collective-permute-done | bytes 262176 | tf_op jit(solution)/shard_map/ppermute | solution.py:683
  62.8 3.2 %regroup.1 = (f32[8,2,32,256]{3,2,1,0:T(8,128)S(1)}, f32[8,2,32,256]{3,2,1,0:T(8,128)S(1)}, f32[8,2,32,256]{3,2,1,0:T(8,128)S(1)}, f32[8,2,32,256]{3,2,1,0:T(8,128)S(1)}) custom-call(f32[4,2,32,256]{3,2,1,0:T(8,128)S(1)} %copy-done.2, f32[4,2,32,256]{3,2,1,0:T(8,128)S(1)} %collective-permute-done.refs_1_, ...), custom_call_target="tpu_custom_call" | custom-call | bytes 1024 | tf_op jit(solution)/shard_map/regroup/pallas_call | solution.py:708
  66.0 0.8 copy-done.3
  66.8 2.3 %collective-permute-start.8 = (f32[8,2,32,256]{3,2,1,0:T(8,128)S(1)}, f32[8,2,32,256]{3,2,1,0:T(8,128)S(1)}, u32[]{:S(2)}, u32[]{:S(2)}) collective-permute-start(f32[8,2,32,256]{3,2,1,0:T(8,128)S(1)} %get-tuple-element.68), channel_id=1, source_target_pairs={{0,2},{1,3},{2,0},{3,1},{4,6},{5,7},{6,4},{7,5},{8,10},{9,11},{10,... | collective-permute-start | bytes 1572872 | tf_op jit(solution)/shard_map/ppermute | solution.py:683
  69.2 1.2 collective-permute-start.9
  70.3 6.5 %azimuth_focus.2.refs_10_ = f32[8,2,2,8,256]{4,3,2,1,0:T(8,128)} custom-call(f32[4,8,2,32,256]{4,3,2,1,0:T(8,128)} %bitcast.2.refs_0_, f32[2,2,8,32,128]{4,3,2,1,0:T(8,128)} %copy-done.1, bf16[256,256]{1,0:T(8,128)(2,1)} %constant.27.clone.refs_2_.refs_5_, bf16[256,256]{1,0:T(8,128)(2,1)} %constant.28.clone.refs_3_.refs_6_, ...), custom_call_target="tpu_custom_call" | custom-call | flops 1610612736 | bytes 6291456 | tf_op jit(solution)/shard_map/azimuth_focus/pallas_call | solution.py:579
  76.9 1.0 slice.3
  77.8 3.0 %collective-permute-start.10 = (f32[8,2,2,1,256]{4,3,2,1,0:T(1,128)S(1)}, f32[8,2,2,1,256]{4,3,2,1,0:T(1,128)S(1)}, u32[]{:S(2)}, u32[]{:S(2)}) collective-permute-start(f32[8,2,2,1,256]{4,3,2,1,0:T(1,128)S(1)} %slice.3), channel_id=1, source_target_pairs={{4,0},{8,4},{12,8},{16,12},{20,16},{24,20},{28,24},{1,28},{5,1},{9... | collective-permute-start | bytes 98312 | tf_op jit(solution)/shard_map/ppermute | solution.py:755
  80.9 8.2 %all_gather.4 = f32[8,8,2]{0,2,1:T(2,128)S(1)} all-gather(f32[8,1,2]{0,2,1:T(2,128)S(1)} %broadcast_multiply_fusion), channel_id=1, replica_groups=mesh['acq'=8,'strip'=4] {'acq'}, dimensions={1}, use_global_device_ids=true | all-gather | bytes 576 | tf_op jit(solution)/shard_map/all_gather | solution.py:727
  89.8 14.2 %collective-permute-done.8.refs_2_ = f32[8,2,32,256]{3,2,1,0:T(8,128)S(1)} collective-permute-done((f32[8,2,32,256]{3,2,1,0:T(8,128)S(1)}, f32[8,2,32,256]{3,2,1,0:T(8,128)S(1)}, u32[]{:S(2)}, u32[]{:S(2)}) %collective-permute-start.8) | collective-permute-done | bytes 524320 | tf_op jit(solution)/shard_map/ppermute | solution.py:683
  104.0 12.0 %collective-permute-done.9.refs_3_ = f32[8,2,32,256]{3,2,1,0:T(8,128)} collective-permute-done((f32[8,2,32,256]{3,2,1,0:T(8,128)S(1)}, f32[8,2,32,256]{3,2,1,0:T(8,128)}, u32[]{:S(2)}, u32[]{:S(2)}) %collective-permute-start.9) | collective-permute-done | bytes 524320 | tf_op jit(solution)/shard_map/ppermute | solution.py:683
  116.6 9.0 %azimuth_focus.3 = f32[8,2,16,256]{3,2,1,0:T(8,128)} custom-call(f32[8,2,32,256]{3,2,1,0:T(8,128)} %copy-done.3, f32[8,2,32,256]{3,2,1,0:T(8,128)} %copy-done.7, f32[8,2,32,256]{3,2,1,0:T(8,128)} %copy-done.8, f32[8,2,32,256]{3,2,1,0:T(8,128)} %collective-permute-done.9.refs_3_, f32[2,2,8,32,128]{4,3,2,1,0:T(8,128)} %copy-done.1, ...), custom_call_target="tpu_custom_call" | custom-call | flops 1610612736 | bytes 6291456 | tf_op jit(solution)/shard_map/azimuth_focus/pallas_call | solution.py:579
  125.7 10.3 %all_to_all.10 = f32[8,2,16,256]{3,2,1,0:T(8,128)S(1)} all-to-all(f32[8,2,16,256]{3,2,1,0:T(8,128)} %azimuth_focus.3), channel_id=1, replica_groups=mesh['acq'=8,'strip'=4] {'acq'}, dimensions={0} | all-to-all | bytes 524288 | tf_op jit(solution)/shard_map/all_to_all | solution.py:764
  (33 shorter events, 3.8 us)
Async XLA Ops:
  7.2 63.1 %all-to-all-start = ((f32[32,2,32,256]{3,2,1,0:T(8,128)}), f32[32,2,32,256]{3,2,1,0:T(8,128)}, u32[]{:S(2)}, u32[]{:S(2)}) async-start(f32[32,2,32,256]{3,2,1,0:T(8,128)} %bitcast.8), calls=%async_computation | async-start | bytes 4194304 | tf_op jit(solution)/shard_map/all_to_all | solution.py:671
  20.7 3.7 %collective-permute-start = (f32[4,2,32,256]{3,2,1,0:T(8,128)}, f32[4,2,32,256]{3,2,1,0:T(8,128)S(1)}, u32[]{:S(2)}, u32[]{:S(2)}) collective-permute-start(f32[4,2,32,256]{3,2,1,0:T(8,128)} %get-tuple-element.50), channel_id=1, source_target_pairs={{0,4},{4,0},{8,12},{12,8},{16,20},{20,16},{24,28},{28,24},{1,5},{5... | collective-permute-start | bytes 786440 | tf_op jit(solution)/shard_map/ppermute | solution.py:683
  20.9 13.5 %collective-permute-start.1 = (f32[4,2,32,256]{3,2,1,0:T(8,128)}, f32[4,2,32,256]{3,2,1,0:T(8,128)S(1)}, u32[]{:S(2)}, u32[]{:S(2)}) collective-permute-start(f32[4,2,32,256]{3,2,1,0:T(8,128)} %get-tuple-element.51), channel_id=1, source_target_pairs={{0,8},{4,12},{8,0},{12,4},{16,24},{20,28},{24,16},{28,20},{1,9},{5... | collective-permute-start | bytes 786440 | tf_op jit(solution)/shard_map/ppermute | solution.py:683
  22.4 24.3 %collective-permute-start.2 = (f32[4,2,32,256]{3,2,1,0:T(8,128)}, f32[4,2,32,256]{3,2,1,0:T(8,128)S(1)}, u32[]{:S(2)}, u32[]{:S(2)}) collective-permute-start(f32[4,2,32,256]{3,2,1,0:T(8,128)} %get-tuple-element.52), channel_id=1, source_target_pairs={{0,12},{4,8},{8,4},{12,0},{16,28},{20,24},{24,20},{28,16},{1,13},{... | collective-permute-start | bytes 786440 | tf_op jit(solution)/shard_map/ppermute | solution.py:683
  22.6 24.1 %collective-permute-start.3 = (f32[4,2,32,256]{3,2,1,0:T(8,128)}, f32[4,2,32,256]{3,2,1,0:T(8,128)S(1)}, u32[]{:S(2)}, u32[]{:S(2)}) collective-permute-start(f32[4,2,32,256]{3,2,1,0:T(8,128)} %get-tuple-element.53), channel_id=1, source_target_pairs={{0,16},{4,20},{8,24},{12,28},{16,0},{20,4},{24,8},{28,12},{1,17},{... | collective-permute-start | bytes 786440 | tf_op jit(solution)/shard_map/ppermute | solution.py:683
  24.1 22.6 %collective-permute-start.4 = (f32[4,2,32,256]{3,2,1,0:T(8,128)}, f32[4,2,32,256]{3,2,1,0:T(8,128)S(1)}, u32[]{:S(2)}, u32[]{:S(2)}) collective-permute-start(f32[4,2,32,256]{3,2,1,0:T(8,128)} %get-tuple-element.54), channel_id=1, source_target_pairs={{0,20},{4,16},{8,28},{12,24},{16,4},{20,0},{24,12},{28,8},{1,21},{... | collective-permute-start | bytes 786440 | tf_op jit(solution)/shard_map/ppermute | solution.py:683
  24.4 31.0 %collective-permute-start.5 = (f32[4,2,32,256]{3,2,1,0:T(8,128)}, f32[4,2,32,256]{3,2,1,0:T(8,128)S(1)}, u32[]{:S(2)}, u32[]{:S(2)}) collective-permute-start(f32[4,2,32,256]{3,2,1,0:T(8,128)} %get-tuple-element.55), channel_id=1, source_target_pairs={{0,24},{4,28},{8,16},{12,20},{16,8},{20,12},{24,0},{28,4},{1,25},{... | collective-permute-start | bytes 786440 | tf_op jit(solution)/shard_map/ppermute | solution.py:683
  34.4 28.4 %collective-permute-start.6 = (f32[4,2,32,256]{3,2,1,0:T(8,128)}, f32[4,2,32,256]{3,2,1,0:T(8,128)S(1)}, u32[]{:S(2)}, u32[]{:S(2)}) collective-permute-start(f32[4,2,32,256]{3,2,1,0:T(8,128)} %get-tuple-element.56), channel_id=1, source_target_pairs={{0,28},{4,24},{8,20},{12,16},{16,12},{20,8},{24,4},{28,0},{1,29},{... | collective-permute-start | bytes 786440 | tf_op jit(solution)/shard_map/ppermute | solution.py:683
  34.9 2.2 %copy-start = (f32[2,1024,512]{2,1,0:T(8,128)S(1)}, f32[2,1024,512]{2,1,0:T(8,128)}, u32[]{:S(2)}) copy-start(f32[2,1024,512]{2,1,0:T(8,128)} %filter_any) | copy-start | bytes 12582916
  37.1 25.7 %copy-start.2 = (f32[4,2,32,256]{3,2,1,0:T(8,128)S(1)}, f32[4,2,32,256]{3,2,1,0:T(8,128)}, u32[]{:S(2)}) copy-start(f32[4,2,32,256]{3,2,1,0:T(8,128)} %get-tuple-element.58.refs_0_) | copy-start | bytes 786436
  37.6 0.8 copy-start.1
  38.4 42.4 %copy-start.5 = (s32[1,2]{1,0:T(1,128)S(1)}, s32[1,2]{1,0:T(1,128)}, u32[]{:S(2)}) copy-start(s32[1,2]{1,0:T(1,128)} %param.23) | copy-start | bytes 28
  38.4 42.4 %copy-start.6 = (s32[2]{0:T(128)S(1)}, s32[2]{0:T(128)}, u32[]{:S(2)}) copy-start(s32[2]{0:T(128)} %constant.31.clone) | copy-start | bytes 28
  38.4 42.5 %copy-start.4 = (f32[8,1,2]{0,2,1:T(2,128)S(1)}, f32[8,1,2]{0,2,1:T(2,128)}, u32[]{:S(2)}) copy-start(f32[8,1,2]{0,2,1:T(2,128)} %param.24) | copy-start | bytes 196
  66.0 0.8 copy-start.3
  66.8 23.0 %collective-permute-start.7 = (f32[8,2,32,256]{3,2,1,0:T(8,128)S(1)}, f32[8,2,32,256]{3,2,1,0:T(8,128)S(1)}, u32[]{:S(2)}, u32[]{:S(2)}) collective-permute-start(f32[8,2,32,256]{3,2,1,0:T(8,128)S(1)} %get-tuple-element.67), channel_id=1, source_target_pairs={{0,1},{1,0},{2,3},{3,2},{4,5},{5,4},{6,7},{7,6},{8,9},{9,8},{10,11... | collective-permute-start | bytes 1572872 | tf_op jit(solution)/shard_map/ppermute | solution.py:683
  66.8 37.1 %collective-permute-start.8 = (f32[8,2,32,256]{3,2,1,0:T(8,128)S(1)}, f32[8,2,32,256]{3,2,1,0:T(8,128)S(1)}, u32[]{:S(2)}, u32[]{:S(2)}) collective-permute-start(f32[8,2,32,256]{3,2,1,0:T(8,128)S(1)} %get-tuple-element.68), channel_id=1, source_target_pairs={{0,2},{1,3},{2,0},{3,1},{4,6},{5,7},{6,4},{7,5},{8,10},{9,11},{10,... | collective-permute-start | bytes 1572872 | tf_op jit(solution)/shard_map/ppermute | solution.py:683
  69.2 46.9 %collective-permute-start.9 = (f32[8,2,32,256]{3,2,1,0:T(8,128)S(1)}, f32[8,2,32,256]{3,2,1,0:T(8,128)}, u32[]{:S(2)}, u32[]{:S(2)}) collective-permute-start(f32[8,2,32,256]{3,2,1,0:T(8,128)S(1)} %get-tuple-element.69), channel_id=1, source_target_pairs={{0,3},{1,2},{2,1},{3,0},{4,7},{5,6},{6,5},{7,4},{8,11},{9,10},{10,... | collective-permute-start | bytes 1572872 | tf_op jit(solution)/shard_map/ppermute | solution.py:683
  77.8 38.2 %collective-permute-start.10 = (f32[8,2,2,1,256]{4,3,2,1,0:T(1,128)S(1)}, f32[8,2,2,1,256]{4,3,2,1,0:T(1,128)S(1)}, u32[]{:S(2)}, u32[]{:S(2)}) collective-permute-start(f32[8,2,2,1,256]{4,3,2,1,0:T(1,128)S(1)} %slice.3), channel_id=1, source_target_pairs={{4,0},{8,4},{12,8},{16,12},{20,16},{24,20},{28,24},{1,28},{5,1},{9... | collective-permute-start | bytes 98312 | tf_op jit(solution)/shard_map/ppermute | solution.py:755
  89.8 26.2 %copy-start.7 = (f32[8,2,32,256]{3,2,1,0:T(8,128)}, f32[8,2,32,256]{3,2,1,0:T(8,128)S(1)}, u32[]{:S(2)}) copy-start(f32[8,2,32,256]{3,2,1,0:T(8,128)S(1)} %collective-permute-done.7.refs_1_) | copy-start | bytes 1572868
  104.0 12.0 %copy-start.8 = (f32[8,2,32,256]{3,2,1,0:T(8,128)}, f32[8,2,32,256]{3,2,1,0:T(8,128)S(1)}, u32[]{:S(2)}) copy-start(f32[8,2,32,256]{3,2,1,0:T(8,128)S(1)} %collective-permute-done.8.refs_2_) | copy-start | bytes 1572868
  116.0 0.6 copy-start.9

commit v8 on v7

--- a/solution.py
+++ b/solution.py
@@ -13,9 +13,9 @@
 LOOK = 4
 RADIX = 8
 ROWS = 8
-RANGE_VMEM = 60 * 1024 * 1024
+RANGE_VMEM = 63 * 1024 * 1024
 LAYOUT_VMEM = 8 * 1024 * 1024
-FOCUS_VMEM = 60 * 1024 * 1024
+FOCUS_VMEM = 32 * 1024 * 1024
 OWNERS = ("strip", "acq")
 
 
@@ -103,7 +103,7 @@
         self.azimuth = pulses * strips
         self.base = samples // RADIX
         self.owned = samples // (strips * epochs)
-        even = all(size & (size - 1) == 0 for size in (strips, epochs))
+        even = strips != epochs and all(size & (size - 1) == 0 for size in (strips, epochs))
         self.parts = 2 if even and self.owned in (64, 128) else 1
         self.rows = self.owned // self.parts
         self.looks = self.rows // LOOK
@@ -171,9 +171,10 @@
 
 
 def compress_kernel(
-    plan, part, relative, filter_ref, high_any, low_any, turn_any, raw_ref, *refs
+    plan, part, form, filter_ref, high_any, low_any, turn_any, raw_ref, *refs
 ):
-    outs = refs[: plan.epochs if relative else 1]
+    relative = form != "all"
+    outs = refs[: {"all": 1, "epochs": plan.epochs, "strips": plan.strips}[form]]
     (
         table_high, table_low, turn_ref, raw, t_high, t_low, y_high, y_low, z_ref, sems, table_sems,
     ) = refs[len(outs) :][:11]
@@ -263,6 +264,7 @@
                     rows = slice(tile * ROWS, (tile + 1) * ROWS)
                     if relative:
                         place = owner ^ lax.axis_index("acq"), strip ^ lax.axis_index("strip")
+                        place = place if form == "epochs" else place[::-1]
                     else:
                         place = strip, owner
                     out_ref[place[0], place[1], c, rows, :] = value[c]
@@ -277,24 +279,27 @@
             copy.wait()
 
 
-def compress(plan, part, relative, range_filter, raw):
+def compress(plan, part, form, range_filter, raw):
     chunk = plan.blocks * plan.rows
     whole = pl.BlockSpec(memory_space=pltpu.VMEM)
     bytes_moved = 4 * (raw.size + raw.size // plan.parts)
     tables = lag_tables(plan)
     slab = (2, plan.rows, plan.pulses)
-    shape = (plan.strips,) + (slab if relative else (plan.epochs,) + slab)
     scratch, out_specs = [], whole
-    if relative:
-        out_specs = [pl.BlockSpec(memory_space=pltpu.HBM)] * plan.epochs
+    shape = jax.ShapeDtypeStruct((plan.strips, plan.epochs) + slab, jnp.float32)
+    if form != "all":
+        count, inner = plan.epochs, plan.strips
+        if form == "strips":
+            count, inner = inner, count
+        out_specs = [pl.BlockSpec(memory_space=pltpu.HBM)] * count
         scratch = [
-            pltpu.VMEM((plan.epochs,) + shape, jnp.float32),
-            pltpu.SemaphoreType.DMA((plan.epochs,)),
-        ]
-    shape = jax.ShapeDtypeStruct(shape, jnp.float32)
+            pltpu.VMEM((count, inner) + slab, jnp.float32),
+            pltpu.SemaphoreType.DMA((count,)),
+        ]
+        shape = [jax.ShapeDtypeStruct((inner,) + slab, jnp.float32)] * count
     return pl.pallas_call(
-        functools.partial(compress_kernel, plan, part, relative),
-        out_shape=[shape] * plan.epochs if relative else shape,
+        functools.partial(compress_kernel, plan, part, form),
+        out_shape=shape,
         in_specs=[whole] + [pl.BlockSpec(memory_space=pltpu.HBM)] * 4,
         out_specs=out_specs,
         scratch_shapes=[
@@ -338,12 +343,8 @@
     half = epochs // 2
     fields = [
         [
-            pltpu.make_async_copy(
-                field_at(at).at[pl.ds(side * half, half)],
-                field_ref.at[at, pl.ds(side * half, half)],
-                field_sems.at[at, side],
-            )
-            for at in range(field_ref.shape[0])
+            pltpu.make_async_copy(source, field_ref.at[place], field_sems.at[side, at])
+            for at, (source, place) in enumerate(field_at(pl.ds(side * half, half)))
         ]
         for side in range(2)
     ]
@@ -531,6 +532,7 @@
     gradients = (plan.epochs, 2, plan.looks * plan.parts, plan.azimuth_looks)
     operands = [*fields, spectrum, *tables]
     in_specs = [pl.BlockSpec(memory_space=pltpu.HBM)] * len(operands)
+    assert plan.strips != plan.epochs or len(fields) == 1
     blocks = plan.azimuth // fields[0].shape[-1]
     before = ()
     scratch = [
@@ -542,7 +544,7 @@
         pltpu.VMEM((RADIX, total, 2 * lanes), jnp.float32),
         pltpu.VMEM((plan.epochs + 2, 2, plan.rows, plan.azimuth), jnp.float32),
         pltpu.VMEM((plan.epochs, 2, 2, plan.looks, plan.azimuth), jnp.float32),
-        pltpu.SemaphoreType.DMA((blocks, 2)),
+        pltpu.SemaphoreType.DMA((2, max(blocks, plan.epochs // 2))),
         pltpu.SemaphoreType.DMA((5,)),
     ]
     shape = looked
@@ -565,8 +567,13 @@
         relative = len(some) > 1
         own = (lax.axis_index("acq"), lax.axis_index("strip")) if relative else (0, 0)
 
-        def field_at(at):
-            return some[at] if relative else some[0].at[at]
+        def field_at(some_epochs):
+            if not relative:
+                return [(some[0].at[at, some_epochs], (at, some_epochs)) for at in range(blocks)]
+            if len(some) == plan.strips:
+                return [(block.at[some_epochs], (at, some_epochs)) for at, block in enumerate(some)]
+            inside = range(some_epochs.start, some_epochs.start + some_epochs.size)
+            return [(some[m], (slice(None), m)) for m in inside]
 
         if finish is None:
             focus_kernel(plan, part, False, field_at, own, *refs)
@@ -684,41 +691,45 @@
     return moved
 
 
-def regroup(plan, others):
+def regroup(blocks):
+    count, inner = len(blocks), blocks[0].shape[0]
+
     def kernel(*refs):
-        ins, outs = refs[: plan.epochs], refs[plan.epochs : plan.epochs + plan.strips]
-        stage, in_sems, out_sems = refs[plan.epochs + plan.strips :]
-        inward = fetch(
-            [
-                pltpu.make_async_copy(ins[m].at[k], stage.at[k, m], in_sems.at[k, m])
-                for k in range(plan.strips)
-                for m in range(plan.epochs)
-            ]
-        )
+        ins, outs = refs[:count], refs[count : count + inner]
+        stage, in_sems, out_sems = refs[count + inner :]
+        inward = [
+            fetch(
+                [
+                    pltpu.make_async_copy(ins[m].at[k], stage.at[k, m], in_sems.at[k, m])
+                    for m in range(count)
+                ]
+            )
+            for k in range(inner)
+        ]
         outward = []
-        for k in range(plan.strips):
-            for copy in inward[k * plan.epochs : (k + 1) * plan.epochs]:
+        for k in range(inner):
+            for copy in inward[k]:
                 copy.wait()
             outward += fetch([pltpu.make_async_copy(stage.at[k], outs[k], out_sems.at[k])])
         for copy in outward:
             copy.wait()
 
-    slab = (plan.epochs,) + others[0].shape[1:]
+    slab = (count,) + blocks[0].shape[1:]
     place = pl.BlockSpec(memory_space=pltpu.HBM)
     return pl.pallas_call(
         kernel,
-        out_shape=[jax.ShapeDtypeStruct(slab, jnp.float32)] * plan.strips,
-        in_specs=[place] * plan.epochs,
-        out_specs=[place] * plan.strips,
+        out_shape=[jax.ShapeDtypeStruct(slab, jnp.float32)] * inner,
+        in_specs=[place] * count,
+        out_specs=[place] * inner,
         scratch_shapes=[
-            pltpu.VMEM((plan.strips,) + slab, jnp.float32),
-            pltpu.SemaphoreType.DMA((plan.strips, plan.epochs)),
-            pltpu.SemaphoreType.DMA((plan.strips,)),
+            pltpu.VMEM((inner,) + slab, jnp.float32),
+            pltpu.SemaphoreType.DMA((inner, count)),
+            pltpu.SemaphoreType.DMA((inner,)),
         ],
         compiler_params=pltpu.CompilerParams(vmem_limit_bytes=LAYOUT_VMEM),
         cost_estimate=pl.CostEstimate(flops=0, bytes_accessed=1024, transcendentals=0),
         name="regroup",
-    )(*others)
+    )(*blocks)
 
 
 def all_weights(pair_mask, inversion):
@@ -733,19 +744,16 @@
     plan = Plan(strips, epochs, raw_echoes.shape[2], raw_echoes.shape[3])
 
     raw = raw_echoes[0]
-    block = compress(plan, 0, False, range_filter, raw)
+    block = compress(plan, 0, "all", range_filter, raw)
     if plan.parts > 1:
         range_filter, block = lax.optimization_barrier((range_filter, block))
-        other = compress(plan, 1, True, range_filter, raw)
-        *other, azimuth_filter = lax.optimization_barrier((*other, azimuth_filter))
+        other = compress(plan, 1, "all", range_filter, raw)
+        other, azimuth_filter = lax.optimization_barrier((other, azimuth_filter))
         spectrum = own_filter_by_kernel(plan, azimuth_filter)
+        field, other = exchange_all(plan, block), exchange_all(plan, other)
     else:
         spectrum = own_filter(plan, azimuth_filter)
-    field = exchange_all(plan, block)
-    if plan.parts > 1:
-        other = partners(other, "acq")
-        *other, spectrum = lax.optimization_barrier((*other, spectrum))
-        slots = partners(regroup(plan, other), "strip")
+        field = exchange_all(plan, block)
     before = [focus(plan, 0, [field], spectrum)]
     before[0], pair_mask, inversion = lax.optimization_barrier((before[0], pair_mask, inversion))
     weights = all_weights(pair_mask, inversion)
@@ -758,7 +766,7 @@
         [(device[i], device[i - 1]) for i in range(1, owners)],
     )
     if plan.parts > 1:
-        gradients = focus(plan, 1, slots, spectrum, (weights, before, halo))
+        gradients = focus(plan, 1, [other], spectrum, (weights, before, halo))
     else:
         gradients = slopes_to_epochs(plan, weights, before[0], halo)
     gathered = lax.all_to_all(gradients, "acq", split_axis=0, concat_axis=0, tiled=True)

time: 137 us -> 136 us (level)
  the two profiles are of different devices: /device:TPU:8 before, /device:TPU:0 now
where the time goes in v8:
time: 136 us; the launch traced here: 135 us
  waiting for transfers between devices  68.4 us (50%)
  Pallas kernels  28.4 us (21%)
  blocking collectives  21.8 us (16%)
  starting transfers between devices  12.7 us (9%)
  local copies, waits for them, and re-layouts  3.49 us (3%)
    all_to_all x2, waiting for transfers between devices, exchange_all(): lax.all_to_all(block, OWNERS, split_axis=0, concat_axis=0, tiled=True)  68.4 us
    pallas_call x2, Pallas kernels, compress(): pl.pallas_call(functools.partial(compress_kernel, plan, part, form), out_...  14.5 us
    pallas_call x2, Pallas kernels, focus(): pl.pallas_call(kernel, out_shape=jax.ShapeDtypeStruct(shape, jnp.float32)...  13.4 us
    all_gather x1, blocking collectives, all_weights(): lax.all_gather(inversion[:, 0, :] * usable[None, :], 'acq', axis=1, tiled...  11.5 us
    all_to_all x2, starting transfers between devices, exchange_all(): lax.all_to_all(block, OWNERS, split_axis=0, concat_axis=0, tiled=True)  11.4 us
    all_to_all x1, blocking collectives, per_device(): lax.all_to_all(gradients, 'acq', split_axis=0, concat_axis=0, tiled=True)  10.2 us
  transfers between devices with their start and end apart: 3, of which 2 were waited for; matrix products, arithmetic and copies ran while one was open for 0% of the time, Pallas kernels for 10%

profile of v8, /device:TPU:0, one launch (start us, length us, event | category | flops | bytes accessed | tf_op | source)
XLA Modules:
  0.0 135.0 jit_solution(2048358138989071331)
XLA Ops:
  0.0 7.2 %range_compress.2 = f32[4,8,2,32,256]{4,3,2,1,0:T(8,128)} custom-call(f32[2,2048]{1,0:T(2,128)} %filter_ref.2, bf16[256,512]{1,0:T(8,128)(2,1)} %constant.24.clone.high_any, bf16[256,512]{1,0:T(8,128)(2,1)} %constant.25.clone.low_any, f32[4,8,256]{2,1,0:T(8,128)} %constant.26.clone.turn_any, f32[2,256,2048]{2,1,0:T(8,128)} %bitcast.11), custom_call_target="tpu_custom_call" | custom-call | flops 1610612736 | bytes 6291456 | tf_op jit(solution)/shard_map/range_compress/pallas_call | solution.py:300
  7.2 7.4 %all-to-all-start.1 = ((f32[32,2,32,256]{3,2,1,0:T(8,128)}), f32[32,2,32,256]{3,2,1,0:T(8,128)}, u32[]{:S(2)}, u32[]{:S(2)}) async-start(f32[32,2,32,256]{3,2,1,0:T(8,128)} %bitcast.14), calls=%async_computation.1 | async-start | bytes 4194304 | tf_op jit(solution)/shard_map/all_to_all | solution.py:678
  14.7 7.3 %range_compress.3 = f32[4,8,2,32,256]{4,3,2,1,0:T(8,128)} custom-call(f32[2,2048]{1,0:T(2,128)} %filter_ref.2, bf16[256,512]{1,0:T(8,128)(2,1)} %constant.24.clone.high_any, bf16[256,512]{1,0:T(8,128)(2,1)} %constant.25.clone.low_any, f32[4,8,256]{2,1,0:T(8,128)} %constant.26.clone.turn_any, f32[2,256,2048]{2,1,0:T(8,128)} %bitcast.12), custom_call_target="tpu_custom_call" | custom-call | flops 1610612736 | bytes 6291456 | tf_op jit(solution)/shard_map/range_compress/pallas_call | solution.py:300
  22.0 41.6 %all-to-all-done.1 = f32[32,2,32,256]{3,2,1,0:T(8,128)} async-done(((f32[32,2,32,256]{3,2,1,0:T(8,128)}), f32[32,2,32,256]{3,2,1,0:T(8,128)}, u32[]{:S(2)}, u32[]{:S(2)}) %all-to-all-start.1) | async-done | bytes 2097184 | tf_op jit(solution)/shard_map/all_to_all | solution.py:678
  63.6 4.0 %all-to-all-start = ((f32[32,2,32,256]{3,2,1,0:T(8,128)}), f32[32,2,32,256]{3,2,1,0:T(8,128)S(1)}, u32[]{:S(2)}, u32[]{:S(2)}) async-start(f32[32,2,32,256]{3,2,1,0:T(8,128)} %bitcast.13), calls=%async_computation | async-start | bytes 4194304 | tf_op jit(solution)/shard_map/all_to_all | solution.py:678
  67.6 0.0 copy-start
  67.6 2.2 %copy-done = f32[2,1024,512]{2,1,0:T(8,128)S(1)} copy-done((f32[2,1024,512]{2,1,0:T(8,128)S(1)}, f32[2,1024,512]{2,1,0:T(8,128)}, u32[]{:S(2)}) %copy-start) | copy-done | bytes 4194328
  69.8 0.5 own_filter.1.refs_1_
  70.3 0.4 copy-done.1
  70.7 0.1 copy-done.2
  70.7 0.1 copy-done.3
  70.8 0.0 copy-done.4
  70.8 5.8 %azimuth_focus.2.refs_7_ = f32[8,2,2,8,256]{4,3,2,1,0:T(8,128)S(1)} custom-call(f32[4,8,2,32,256]{4,3,2,1,0:T(8,128)} %bitcast.4.refs_0_, f32[2,2,8,32,128]{4,3,2,1,0:T(8,128)S(1)} %own_filter.1.refs_1_, bf16[256,256]{1,0:T(8,128)(2,1)S(1)} %copy-done.3, bf16[256,256]{1,0:T(8,128)(2,1)S(1)} %copy-done.2, f32[4,8,128]{2,1,0:T(8,128)S(1)} %copy-done.4, ...), custom_call_target="tpu_custom_call" | custom-call | flops 1610612736 | bytes 6291456 | tf_op jit(solution)/shard_map/azimuth_focus/pallas_call | solution.py:586
  76.6 1.3 collective-permute-start
  77.9 0.0 copy-done.6
  78.0 0.0 copy-done.7
  78.0 0.1 broadcast_multiply_fusion
  78.1 11.5 %all_gather.4 = f32[8,8,2]{0,2,1:T(2,128)S(1)} all-gather(f32[8,1,2]{0,2,1:T(2,128)S(1)} %broadcast_multiply_fusion), channel_id=1, replica_groups=mesh['acq'=8,'strip'=4] {'acq'}, dimensions={1}, use_global_device_ids=true | all-gather | bytes 576 | tf_op jit(solution)/shard_map/all_gather | solution.py:738
  89.6 0.1 copy.24.refs_6_
  89.7 26.8 %all-to-all-done = f32[32,2,32,256]{3,2,1,0:T(8,128)S(1)} async-done(((f32[32,2,32,256]{3,2,1,0:T(8,128)}), f32[32,2,32,256]{3,2,1,0:T(8,128)S(1)}, u32[]{:S(2)}, u32[]{:S(2)}) %all-to-all-start) | async-done | bytes 2097184 | tf_op jit(solution)/shard_map/all_to_all | solution.py:678
  116.5 0.0 collective-permute-done.refs_8_
  116.5 7.6 %azimuth_focus.3 = f32[8,2,16,256]{3,2,1,0:T(8,128)S(1)} custom-call(f32[4,8,2,32,256]{4,3,2,1,0:T(8,128)S(1)} %bitcast.10, f32[2,2,8,32,128]{4,3,2,1,0:T(8,128)S(1)} %own_filter.1.refs_1_, bf16[256,256]{1,0:T(8,128)(2,1)S(1)} %copy-done.3, bf16[256,256]{1,0:T(8,128)(2,1)S(1)} %copy-done.2, f32[4,8,128]{2,1,0:T(8,128)S(1)} %copy-done.4, ...), custom_call_target="tpu_custom_call" | custom-call | flops 1610612736 | bytes 6291456 | tf_op jit(solution)/shard_map/azimuth_focus/pallas_call | solution.py:586
  124.1 10.2 %all_to_all.15 = f32[8,2,16,256]{3,2,1,0:T(8,128)S(1)} all-to-all(f32[8,2,16,256]{3,2,1,0:T(8,128)S(1)} %azimuth_focus.3), channel_id=1, replica_groups=mesh['acq'=8,'strip'=4] {'acq'}, dimensions={0} | all-to-all | bytes 524288 | tf_op jit(solution)/shard_map/all_to_all | solution.py:772
  134.3 0.7 copy.25
  (10 shorter events, 0.0 us)
Async XLA Ops:
  7.2 56.3 %all-to-all-start.1 = ((f32[32,2,32,256]{3,2,1,0:T(8,128)}), f32[32,2,32,256]{3,2,1,0:T(8,128)}, u32[]{:S(2)}, u32[]{:S(2)}) async-start(f32[32,2,32,256]{3,2,1,0:T(8,128)} %bitcast.14), calls=%async_computation.1 | async-start | bytes 4194304 | tf_op jit(solution)/shard_map/all_to_all | solution.py:678
  63.6 52.9 %all-to-all-start = ((f32[32,2,32,256]{3,2,1,0:T(8,128)}), f32[32,2,32,256]{3,2,1,0:T(8,128)S(1)}, u32[]{:S(2)}, u32[]{:S(2)}) async-start(f32[32,2,32,256]{3,2,1,0:T(8,128)} %bitcast.13), calls=%async_computation | async-start | bytes 4194304 | tf_op jit(solution)/shard_map/all_to_all | solution.py:678
  67.6 2.2 %copy-start = (f32[2,1024,512]{2,1,0:T(8,128)S(1)}, f32[2,1024,512]{2,1,0:T(8,128)}, u32[]{:S(2)}) copy-start(f32[2,1024,512]{2,1,0:T(8,128)} %filter_any) | copy-start | bytes 12582916
  69.8 0.9 copy-start.1
  69.8 1.0 copy-start.2
  69.8 1.0 copy-start.3
  69.8 1.0 copy-start.4
  70.8 7.1 %copy-start.6 = (s32[1,2]{1,0:T(1,128)S(1)}, s32[1,2]{1,0:T(1,128)}, u32[]{:S(2)}) copy-start(s32[1,2]{1,0:T(1,128)} %param.23) | copy-start | bytes 28
  70.8 7.2 %copy-start.7 = (s32[2]{0:T(128)S(1)}, s32[2]{0:T(128)}, u32[]{:S(2)}) copy-start(s32[2]{0:T(128)} %constant.31.clone) | copy-start | bytes 28
  70.8 7.2 %copy-start.5 = (f32[8,1,2]{0,2,1:T(2,128)S(1)}, f32[8,1,2]{0,2,1:T(2,128)}, u32[]{:S(2)}) copy-start(f32[8,1,2]{0,2,1:T(2,128)} %param.24) | copy-start | bytes 196
  76.6 39.8 %collective-permute-start = (f32[8,2,2,1,256]{4,3,2,1,0:T(1,128)S(1)}, f32[8,2,2,1,256]{4,3,2,1,0:T(1,128)S(1)}, u32[]{:S(2)}, u32[]{:S(2)}) collective-permute-start(f32[8,2,2,1,256]{4,3,2,1,0:T(1,128)S(1)} %slice.3), channel_id=1, source_target_pairs={{4,0},{8,4},{12,8},{16,12},{20,16},{24,20},{28,24},{1,28},{5,1},{9... | collective-permute-start | bytes 98312 | tf_op jit(solution)/shard_map/ppermute | solution.py:763

commit v9 on v8

--- a/solution.py
+++ b/solution.py
@@ -1,3 +1,4 @@
+import copy
 import functools
 import math
 
@@ -103,24 +104,26 @@
         self.azimuth = pulses * strips
         self.base = samples // RADIX
         self.owned = samples // (strips * epochs)
-        even = strips != epochs and all(size & (size - 1) == 0 for size in (strips, epochs))
+        even = all(size & (size - 1) == 0 for size in (strips, epochs))
         self.parts = 2 if even and self.owned in (64, 128) else 1
-        self.rows = self.owned // self.parts
+        self.start, self.rows = 0, self.owned
         self.looks = self.rows // LOOK
-        self.planes = self.looks % ROWS == 0
+        self.all_looks = self.looks
         self.blocks = self.base // self.owned
         self.lanes = self.azimuth // RADIX
         self.azimuth_looks = self.azimuth // LOOK
 
-    def tile_shift(self, part, block, tile):
-        start = block * self.owned + part * self.rows
-        if self.planes:
-            plane, look = divmod(tile * ROWS, self.looks)
-            return start + LOOK * look + plane
-        return start + tile * ROWS
-
-    def tile_stride(self):
-        return LOOK if self.planes else 1
+    def part(self, number):
+        if self.parts == 1:
+            return self
+        own = copy.copy(self)
+        size = self.owned // 4
+        own.start, own.rows = (0, 3 * size) if number == 0 else (3 * size, size)
+        own.looks = own.rows // LOOK
+        return own
+
+    def tile_shift(self, block, tile):
+        return block * self.owned + self.start + tile * ROWS
 
 
 def lag_tables(plan):
@@ -165,16 +168,15 @@
 
 
 def fetch(copies):
-    for copy in copies:
-        copy.start()
+    for move in copies:
+        move.start()
     return copies
 
 
 def compress_kernel(
-    plan, part, form, filter_ref, high_any, low_any, turn_any, raw_ref, *refs
+    plan, relative, filter_ref, high_any, low_any, turn_any, raw_ref, *refs
 ):
-    relative = form != "all"
-    outs = refs[: {"all": 1, "epochs": plan.epochs, "strips": plan.strips}[form]]
+    outs = refs[: plan.epochs if relative else 1]
     (
         table_high, table_low, turn_ref, raw, t_high, t_low, y_high, y_low, z_ref, sems, table_sems,
     ) = refs[len(outs) :][:11]
@@ -216,8 +218,8 @@
         raw_copy(at).wait()
         lax.fori_loop(at * steps, (at + 1) * steps, spread_pulses, 0)
 
-    for copy in tables:
-        copy.wait()
+    for move in tables:
+        move.wait()
     lags = lag_vectors(plan, filter_ref, table_high, table_low, turn_ref)
 
     for d in range(RADIX):
@@ -226,7 +228,7 @@
                 jnp.broadcast_to(lag[d : d + 1, :], (ROWS, 2 * base)),
                 0,
                 1,
-                stride=plan.tile_stride(),
+                stride=1,
                 stride_axis=0,
             )
             for lag in lags
@@ -234,7 +236,7 @@
         for pair in range(blocks * tiles // 2):
             real, imag = [], []
             for at in (2 * pair, 2 * pair + 1):
-                shift = plan.tile_shift(part, at // tiles, at % tiles)
+                shift = plan.tile_shift(at // tiles, at % tiles)
                 real.append(pltpu.roll(spread[0], shift, 1)[:, :base])
                 imag.append(pltpu.roll(spread[1], shift, 1)[:, :base])
             real_high, real_low = two_parts(jnp.concatenate(real, axis=0))
@@ -264,7 +266,6 @@
                     rows = slice(tile * ROWS, (tile + 1) * ROWS)
                     if relative:
                         place = owner ^ lax.axis_index("acq"), strip ^ lax.axis_index("strip")
-                        place = place if form == "epochs" else place[::-1]
                     else:
                         place = strip, owner
                     out_ref[place[0], place[1], c, rows, :] = value[c]
@@ -275,31 +276,28 @@
                 for m, out in enumerate(outs)
             ]
         )
-        for copy in copies:
-            copy.wait()
-
-
-def compress(plan, part, form, range_filter, raw):
+        for move in copies:
+            move.wait()
+
+
+def compress(plan, relative, range_filter, raw):
     chunk = plan.blocks * plan.rows
     whole = pl.BlockSpec(memory_space=pltpu.VMEM)
-    bytes_moved = 4 * (raw.size + raw.size // plan.parts)
+    bytes_moved = 8 * raw.size
     tables = lag_tables(plan)
     slab = (2, plan.rows, plan.pulses)
+    shape = (plan.strips,) + (slab if relative else (plan.epochs,) + slab)
     scratch, out_specs = [], whole
-    shape = jax.ShapeDtypeStruct((plan.strips, plan.epochs) + slab, jnp.float32)
-    if form != "all":
-        count, inner = plan.epochs, plan.strips
-        if form == "strips":
-            count, inner = inner, count
-        out_specs = [pl.BlockSpec(memory_space=pltpu.HBM)] * count
+    if relative:
+        out_specs = [pl.BlockSpec(memory_space=pltpu.HBM)] * plan.epochs
         scratch = [
-            pltpu.VMEM((count, inner) + slab, jnp.float32),
-            pltpu.SemaphoreType.DMA((count,)),
+            pltpu.VMEM((plan.epochs,) + shape, jnp.float32),
+            pltpu.SemaphoreType.DMA((plan.epochs,)),
         ]
-        shape = [jax.ShapeDtypeStruct((inner,) + slab, jnp.float32)] * count
+    shape = jax.ShapeDtypeStruct(shape, jnp.float32)
     return pl.pallas_call(
-        functools.partial(compress_kernel, plan, part, form),
-        out_shape=shape,
+        functools.partial(compress_kernel, plan, relative),
+        out_shape=[shape] * plan.epochs if relative else shape,
         in_specs=[whole] + [pl.BlockSpec(memory_space=pltpu.HBM)] * 4,
         out_specs=out_specs,
         scratch_shapes=[
@@ -324,7 +322,7 @@
     )(range_filter, *tables, raw)
 
 
-def focus_kernel(plan, part, final, field_at, own, *refs):
+def focus_kernel(plan, final, field_at, own, *refs):
     filter_any, high_any, low_any, twiddle_any, sum_any = refs[:5]
     if final:
         weight_ref, before_any, halo_any, out_ref = refs[5:9]
@@ -343,8 +341,12 @@
     half = epochs // 2
     fields = [
         [
-            pltpu.make_async_copy(source, field_ref.at[place], field_sems.at[side, at])
-            for at, (source, place) in enumerate(field_at(pl.ds(side * half, half)))
+            pltpu.make_async_copy(
+                field_at(at).at[pl.ds(side * half, half)],
+                field_ref.at[at, pl.ds(side * half, half)],
+                field_sems.at[at, side],
+            )
+            for at in range(field_ref.shape[0])
         ]
         for side in range(2)
     ]
@@ -355,7 +357,7 @@
                 (twiddle_any, twiddle_ref),
                 (high_any, table_high),
                 (low_any, table_low),
-                (filter_any.at[part], filter_ref),
+                (filter_any, filter_ref),
                 (sum_any, sum_ref),
             )
         )
@@ -366,13 +368,12 @@
     fetch(tables[1:])
     if final:
         looked_ref, slope_ref, halo_ref, late_sems = scratch[13:]
-        late = [
-            pltpu.make_async_copy(
-                before, looked_ref.at[:, :, :, pl.ds(at * looks, looks), :], late_sems.at[at]
-            )
-            for at, before in enumerate(before_any)
-        ]
-        late = fetch(late + [pltpu.make_async_copy(halo_any, halo_ref, late_sems.at[part])])
+        late = fetch(
+            [
+                pltpu.make_async_copy(before_any, looked_ref, late_sems.at[0]),
+                pltpu.make_async_copy(halo_any, halo_ref, late_sems.at[1]),
+            ]
+        )
     tables[0].wait()
 
     def rows_of(strip, slot, c, top, start):
@@ -401,11 +402,11 @@
         return carry
 
     for side, copies in enumerate(fields):
-        for copy in copies:
-            copy.wait()
+        for move in copies:
+            move.wait()
         lax.fori_loop(side * half // group, (side + 1) * half // group, forward, 0)
-    for copy in tables[1:]:
-        copy.wait()
+    for move in tables[1:]:
+        move.wait()
 
     for d in range(RADIX):
         spectrum = three_products(
@@ -436,35 +437,31 @@
             ]
             for a, value in enumerate(dft8(z, 1.0)):
                 for c in range(2):
-                    scene_ref[j + 2, c, top : top + ROWS, a * lanes : (a + 1) * lanes] = value[c]
+                    scene_ref[j + 2, c, a, top : top + ROWS, :] = value[c]
         return carry
 
     lax.fori_loop(0, epochs, backward, 0)
-
-    def look(value):
-        if plan.planes:
-            return sum(value[q * looks : (q + 1) * looks] for q in range(1, LOOK)) + value[:looks]
-        return value.reshape(looks, LOOK, value.shape[-1]).sum(axis=1)
 
     def interfere(j, carry):
         for a in range(RADIX):
             columns = pl.ds(a * lanes, lanes)
-            later = (scene_ref[j + 2, 0, :, columns], scene_ref[j + 2, 1, :, columns])
-            for lag in (1, 2):
-                earlier = (
-                    scene_ref[j + 2 - lag, 0, :, columns],
-                    scene_ref[j + 2 - lag, 1, :, columns],
-                )
-                real = earlier[0] * later[0] + earlier[1] * later[1]
-                imag = earlier[1] * later[0] - earlier[0] * later[1]
-                product_ref[j, lag - 1, 0, :, columns] = look(real)
-                product_ref[j, lag - 1, 1, :, columns] = look(imag)
+            sums = [0.0] * 4
+            for q in range(LOOK):
+                rows_at = pl.ds(q, looks, stride=LOOK)
+                later, *earlier = [
+                    tuple(scene_ref[j + 2 - lag, c, a, rows_at, :] for c in range(2))
+                    for lag in range(3)
+                ]
+                for at, value in enumerate(earlier):
+                    sums[2 * at] += value[0] * later[0] + value[1] * later[1]
+                    sums[2 * at + 1] += value[1] * later[0] - value[0] * later[1]
+            place = pl.ds(pl.multiple_of(j * 4 * looks, ROWS), 4 * looks)
+            product_ref[place, columns] = jnp.concatenate(sums, axis=0)
         return carry
 
     lax.fori_loop(0, epochs, interfere, 0)
 
-    total = epochs * 4 * looks
-    products = product_ref[...].reshape(total, plan.azimuth)
+    products = product_ref[...]
     high, low = two_parts(products)
     weights = sum_ref[...]
     looked = []
@@ -477,18 +474,21 @@
     looked = jnp.concatenate(looked, axis=1)
     looked = looked.reshape(epochs, 2, 2, looks, plan.azimuth_looks)
     if final:
-        for copy in late:
-            copy.wait()
-        looked_ref[:, :, :, part * looks :, :] = looked
+        for move in late:
+            move.wait()
+        looked_ref[:, :, :, plan.all_looks - looks :, :] = looked
         slopes_and_sums(plan, weight_ref, looked_ref, halo_ref, out_ref, slope_ref)
     else:
-        out_ref[...] = looked
+        out_ref[:, :, :, :looks, :] = looked
+        if looks < plan.all_looks:
+            rest = (epochs, 2, 2, plan.all_looks - looks, plan.azimuth_looks)
+            out_ref[:, :, :, looks:, :] = jnp.zeros(rest, jnp.float32)
 
 
 def slopes_and_sums(plan, weight_ref, looked_ref, halo_ref, out_ref, slope_ref):
     epochs = plan.epochs
     columns = plan.azimuth_looks
-    inner = lax.broadcasted_iota(jnp.int32, (plan.looks * plan.parts, columns), 1) < columns - 1
+    inner = lax.broadcasted_iota(jnp.int32, (plan.all_looks, columns), 1) < columns - 1
 
     def slopes(at, carry):
         j, lag = at // 2, at % 2
@@ -523,42 +523,40 @@
     return table + (twiddles.astype(np.float32), (sums / LOOK).astype(ml_dtypes.bfloat16))
 
 
-def focus(plan, part, fields, spectrum, finish=None):
+def focus(plan, fields, spectrum, finish=None):
     lanes = plan.lanes
     total = plan.epochs * plan.rows
     tables = focus_tables(plan)
     whole = pl.BlockSpec(memory_space=pltpu.VMEM)
-    looked = (plan.epochs, 2, 2, plan.looks, plan.azimuth_looks)
-    gradients = (plan.epochs, 2, plan.looks * plan.parts, plan.azimuth_looks)
+    looked = (plan.epochs, 2, 2, plan.all_looks, plan.azimuth_looks)
+    gradients = (plan.epochs, 2, plan.all_looks, plan.azimuth_looks)
     operands = [*fields, spectrum, *tables]
     in_specs = [pl.BlockSpec(memory_space=pltpu.HBM)] * len(operands)
-    assert plan.strips != plan.epochs or len(fields) == 1
     blocks = plan.azimuth // fields[0].shape[-1]
-    before = ()
     scratch = [
         pltpu.VMEM((blocks, plan.epochs) + fields[0].shape[-3:], jnp.float32),
-        pltpu.VMEM(spectrum.shape[1:], jnp.float32),
+        pltpu.VMEM(spectrum.shape, jnp.float32),
         *[pltpu.VMEM(table.shape, table.dtype) for table in tables],
         pltpu.VMEM((RADIX, total, 2 * lanes), jnp.bfloat16),
         pltpu.VMEM((RADIX, total, 2 * lanes), jnp.bfloat16),
         pltpu.VMEM((RADIX, total, 2 * lanes), jnp.float32),
-        pltpu.VMEM((plan.epochs + 2, 2, plan.rows, plan.azimuth), jnp.float32),
-        pltpu.VMEM((plan.epochs, 2, 2, plan.looks, plan.azimuth), jnp.float32),
-        pltpu.SemaphoreType.DMA((2, max(blocks, plan.epochs // 2))),
+        pltpu.VMEM((plan.epochs + 2, 2, RADIX, plan.rows, lanes), jnp.float32),
+        pltpu.VMEM((plan.epochs * 4 * plan.looks, plan.azimuth), jnp.float32),
+        pltpu.SemaphoreType.DMA((blocks, 2)),
         pltpu.SemaphoreType.DMA((5,)),
     ]
     shape = looked
     if finish is not None:
         weights, before, halo = finish
         shape = gradients
-        operands += [weights, *before, halo]
+        operands += [weights, before, halo]
         in_specs += [pl.BlockSpec(memory_space=pltpu.SMEM)]
-        in_specs += [pl.BlockSpec(memory_space=pltpu.HBM)] * (len(before) + 1)
+        in_specs += [pl.BlockSpec(memory_space=pltpu.HBM)] * 2
         scratch += [
-            pltpu.VMEM((plan.epochs, 2, 2, plan.looks * plan.parts, plan.azimuth_looks), jnp.float32),
+            pltpu.VMEM(looked, jnp.float32),
             pltpu.VMEM((2 * plan.epochs,) + gradients[1:], jnp.float32),
             pltpu.VMEM(halo.shape, jnp.float32),
-            pltpu.SemaphoreType.DMA((plan.parts,)),
+            pltpu.SemaphoreType.DMA((2,)),
         ]
 
     def kernel(*refs):
@@ -567,21 +565,10 @@
         relative = len(some) > 1
         own = (lax.axis_index("acq"), lax.axis_index("strip")) if relative else (0, 0)
 
-        def field_at(some_epochs):
-            if not relative:
-                return [(some[0].at[at, some_epochs], (at, some_epochs)) for at in range(blocks)]
-            if len(some) == plan.strips:
-                return [(block.at[some_epochs], (at, some_epochs)) for at, block in enumerate(some)]
-            inside = range(some_epochs.start, some_epochs.start + some_epochs.size)
-            return [(some[m], (slice(None), m)) for m in inside]
-
-        if finish is None:
-            focus_kernel(plan, part, False, field_at, own, *refs)
-        else:
-            count = len(before)
-            focus_kernel(
-                plan, part, True, field_at, own, *refs[:6], refs[6 : 6 + count], *refs[6 + count :]
-            )
+        def field_at(at):
+            return some[at] if relative else some[0].at[at]
+
+        focus_kernel(plan, finish is not None, field_at, own, *refs)
 
     return pl.pallas_call(
         kernel,
@@ -605,7 +592,7 @@
 
 def slopes_to_epochs(plan, weights, looked, halo):
     whole = pl.BlockSpec(memory_space=pltpu.VMEM)
-    looks = plan.looks * plan.parts
+    looks = plan.all_looks
     return pl.pallas_call(
         functools.partial(slope_kernel, plan),
         out_shape=jax.ShapeDtypeStruct(
@@ -627,40 +614,39 @@
 def own_filter(plan, azimuth_filter):
     start = lax.axis_index("acq") * plan.owned
     own = lax.dynamic_slice_in_dim(azimuth_filter, start, plan.owned, axis=2)
-    own = own.reshape(2, plan.lanes, RADIX, plan.parts, plan.looks, LOOK)
-    order = (3, 0, 2, 5, 4, 1) if plan.planes else (3, 0, 2, 4, 5, 1)
-    return own.transpose(order).reshape(plan.parts, 2, RADIX, plan.rows, plan.lanes)
-
-
-def own_filter_kernel(plan, filter_any, out_ref, block_ref, turned_ref, sem):
+    return own.reshape(2, plan.lanes, RADIX, plan.owned).transpose(0, 2, 3, 1)
+
+
+def own_filter_kernel(plan, filter_any, *refs):
+    *outs, block_ref, turned_ref, sem = refs
     width = block_ref.shape[-1]
     acq = lax.axis_index("acq")
     start = acq * plan.owned // width * width
     inside = acq * plan.owned % width
-    copy = pltpu.make_async_copy(
+    move = pltpu.make_async_copy(
         filter_any.at[:, :, pl.ds(pl.multiple_of(start, width), width)], block_ref, sem
     )
-    copy.start()
-    copy.wait()
+    move.start()
+    move.wait()
     for c in range(2):
         for d in range(RADIX):
             turned_ref[...] = block_ref[c, pl.ds(d, plan.lanes, stride=RADIX), :].T
-            for part in range(plan.parts):
-                for tile in range(plan.rows // ROWS):
-                    row = plan.tile_shift(part, 0, tile)
-                    rows = pl.ds(inside + row, ROWS, stride=plan.tile_stride())
-                    out_ref[part, c, d, tile * ROWS : (tile + 1) * ROWS, :] = turned_ref[rows, :]
+            for number, out_ref in enumerate(outs):
+                part = plan.part(number)
+                start = pl.multiple_of(inside + part.start, ROWS)
+                out_ref[c, d] = turned_ref[pl.ds(start, part.rows), :]
 
 
 def own_filter_by_kernel(plan, azimuth_filter):
     width = 128
     return pl.pallas_call(
         functools.partial(own_filter_kernel, plan),
-        out_shape=jax.ShapeDtypeStruct(
-            (plan.parts, 2, RADIX, plan.rows, plan.lanes), jnp.float32
-        ),
+        out_shape=[
+            jax.ShapeDtypeStruct((2, RADIX, plan.part(number).rows, plan.lanes), jnp.float32)
+            for number in range(plan.parts)
+        ],
         in_specs=[pl.BlockSpec(memory_space=pltpu.HBM)],
-        out_specs=pl.BlockSpec(memory_space=pltpu.VMEM),
+        out_specs=[pl.BlockSpec(memory_space=pltpu.VMEM)] * plan.parts,
         scratch_shapes=[
             pltpu.VMEM((2, plan.azimuth, width), jnp.float32),
             pltpu.VMEM((width, plan.lanes), jnp.float32),
@@ -708,11 +694,11 @@
         ]
         outward = []
         for k in range(inner):
-            for copy in inward[k]:
-                copy.wait()
+            for move in inward[k]:
+                move.wait()
             outward += fetch([pltpu.make_async_copy(stage.at[k], outs[k], out_sems.at[k])])
-        for copy in outward:
-            copy.wait()
+        for move in outward:
+            move.wait()
 
     slab = (count,) + blocks[0].shape[1:]
     place = pl.BlockSpec(memory_space=pltpu.HBM)
@@ -744,33 +730,39 @@
     plan = Plan(strips, epochs, raw_echoes.shape[2], raw_echoes.shape[3])
 
     raw = raw_echoes[0]
-    block = compress(plan, 0, "all", range_filter, raw)
+    big, small = plan.part(0), plan.part(1)
+    block = compress(big, False, range_filter, raw)
     if plan.parts > 1:
         range_filter, block = lax.optimization_barrier((range_filter, block))
-        other = compress(plan, 1, "all", range_filter, raw)
-        other, azimuth_filter = lax.optimization_barrier((other, azimuth_filter))
-        spectrum = own_filter_by_kernel(plan, azimuth_filter)
-        field, other = exchange_all(plan, block), exchange_all(plan, other)
+        other = compress(small, True, range_filter, raw)
+        *other, azimuth_filter, pair_mask, inversion = lax.optimization_barrier(
+            (*other, azimuth_filter, pair_mask, inversion)
+        )
+        weights = all_weights(pair_mask, inversion)
+        spectrum, other_spectrum = own_filter_by_kernel(plan, azimuth_filter)
+        field = exchange_all(big, block)
+        other = partners(other, "acq")
+        *other, spectrum, weights = lax.optimization_barrier((*other, spectrum, weights))
+        other = partners(regroup(other), "strip")
     else:
+        weights = all_weights(pair_mask, inversion)
         spectrum = own_filter(plan, azimuth_filter)
         field = exchange_all(plan, block)
-    before = [focus(plan, 0, [field], spectrum)]
-    before[0], pair_mask, inversion = lax.optimization_barrier((before[0], pair_mask, inversion))
-    weights = all_weights(pair_mask, inversion)
+    before = focus(big, [field], spectrum)
 
     owners = strips * epochs
     device = [i % epochs * strips + i // epochs for i in range(owners)]
     halo = lax.ppermute(
-        before[0][:, :, :, :1, :],
+        before[:, :, :, :1, :],
         ("acq", "strip"),
         [(device[i], device[i - 1]) for i in range(1, owners)],
     )
     if plan.parts > 1:
-        gradients = focus(plan, 1, [other], spectrum, (weights, before, halo))
+        gradients = focus(small, other, other_spectrum, (weights, before, halo))
     else:
-        gradients = slopes_to_epochs(plan, weights, before[0], halo)
+        gradients = slopes_to_epochs(plan, weights, before, halo)
     gathered = lax.all_to_all(gradients, "acq", split_axis=0, concat_axis=0, tiled=True)
-    gathered = gathered.reshape(epochs, 2, plan.looks * plan.parts, plan.azimuth_looks)
+    gathered = gathered.reshape(epochs, 2, plan.all_looks, plan.azimuth_looks)
     return gathered.swapaxes(0, 1).reshape(1, 2, -1, plan.azimuth_looks)
 
 

time: 136 us -> 133 us (0.978)
  waiting for transfers between devices: 68.4 us -> 43.7 us
  blocking collectives: 21.8 us -> 30.6 us
  starting transfers between devices: 12.7 us -> 20.1 us
  Pallas kernels: 28.4 us -> 34.1 us
    all_to_all x2 -> x1, waiting for transfers between devices: 68.4 us -> 32.7 us  [exchange_all(): lax.all_to_all(block, OWNERS, split_axis=0, concat_axis=0, tiled=True)]
    ppermute x1 -> x11, starting transfers between devices: 1.29 us -> 12.7 us  [the longest x10 11.4 us: partners(): lax.ppermute(slot, axis, [(i, i ^ k) for i in range(size)])]
    ppermute x1 -> x11, waiting for transfers between devices: 0.01 us -> 11.1 us  [the longest x10 9.33 us: partners(): lax.ppermute(slot, axis, [(i, i ^ k) for i in range(size)])]
    all_gather x1, blocking collectives: 11.5 us -> 17.9 us  [all_weights(): lax.all_gather(inversion[:, 0, :] * usable[None, :], 'acq', axis=1, tiled...]
    all_to_all x2 -> x1, starting transfers between devices: 11.4 us -> 7.42 us  [exchange_all(): lax.all_to_all(block, OWNERS, split_axis=0, concat_axis=0, tiled=True)]
    pallas_call x3 -> x4, Pallas kernels: 15 us -> 17.9 us  [the longest x2 15.6 us: compress(): pl.pallas_call(functools.partial(compress_kernel, plan, relative), out_sh...]
    pallas_call x2, Pallas kernels: 13.4 us -> 16.2 us  [focus(): pl.pallas_call(kernel, out_shape=jax.ShapeDtypeStruct(shape, jnp.float32)...]
    all_to_all x1, blocking collectives: 10.2 us -> 12.7 us  [per_device(): lax.all_to_all(gradients, 'acq', split_axis=0, concat_axis=0, tiled=True)]
  transfers between devices with their start and end apart: 3 -> 12, of which waited for: 2 -> 3; matrix products, arithmetic and copies ran while one was open for 0% -> 0% of each run, Pallas kernels for 10% -> 13%
where the time goes in v9:
time: 133 us; the launch traced here: 132 us
  waiting for transfers between devices  43.7 us (33%)
  Pallas kernels  34.1 us (26%)
  blocking collectives  30.6 us (23%)
  starting transfers between devices  20.1 us (15%)
  local copies, waits for them, and re-layouts  3.38 us (3%)
    all_to_all x1, waiting for transfers between devices, exchange_all(): lax.all_to_all(block, OWNERS, split_axis=0, concat_axis=0, tiled=True)  32.7 us
    all_gather x1, blocking collectives, all_weights(): lax.all_gather(inversion[:, 0, :] * usable[None, :], 'acq', axis=1, tiled...  17.9 us
    pallas_call x2, Pallas kernels, focus(): pl.pallas_call(kernel, out_shape=jax.ShapeDtypeStruct(shape, jnp.float32)...  16.2 us
    pallas_call x2, Pallas kernels, compress(): pl.pallas_call(functools.partial(compress_kernel, plan, relative), out_sh...  15.6 us
    all_to_all x1, blocking collectives, per_device(): lax.all_to_all(gradients, 'acq', split_axis=0, concat_axis=0, tiled=True)  12.7 us
    ppermute x10, starting transfers between devices, partners(): lax.ppermute(slot, axis, [(i, i ^ k) for i in range(size)])  11.4 us
    ppermute x10, waiting for transfers between devices, partners(): lax.ppermute(slot, axis, [(i, i ^ k) for i in range(size)])  9.33 us
    all_to_all x1, starting transfers between devices, exchange_all(): lax.all_to_all(block, OWNERS, split_axis=0, concat_axis=0, tiled=True)  7.42 us
  transfers between devices with their start and end apart: 12, of which 3 were waited for; matrix products, arithmetic and copies ran while one was open for 0% of the time, Pallas kernels for 13%

profile of v9, /device:TPU:0, one launch (start us, length us, event | category | flops | bytes accessed | tf_op | source)
XLA Modules:
  0.0 132.2 jit_solution(15181444109750039630)
XLA Ops:
  0.0 8.6 %range_compress.2 = f32[4,8,2,48,256]{4,3,2,1,0:T(8,128)} custom-call(f32[2,2048]{1,0:T(2,128)} %filter_ref.2, bf16[256,512]{1,0:T(8,128)(2,1)} %constant.24.clone.high_any, bf16[256,512]{1,0:T(8,128)(2,1)} %constant.25.clone.low_any, f32[4,8,256]{2,1,0:T(8,128)} %constant.26.clone.turn_any, f32[2,256,2048]{2,1,0:T(8,128)} %bitcast.8), custom_call_target="tpu_custom_call" | custom-call | flops 2415919104 | bytes 8388608 | tf_op jit(solution)/shard_map/range_compress/pallas_call | solution.py:298
  8.6 7.4 %all-to-all-start = ((f32[32,2,48,256]{3,2,1,0:T(8,128)}), f32[32,2,48,256]{3,2,1,0:T(8,128)}, u32[]{:S(2)}, u32[]{:S(2)}) async-start(f32[32,2,48,256]{3,2,1,0:T(8,128)} %bitcast.10), calls=%async_computation | async-start | bytes 6291456 | tf_op jit(solution)/shard_map/all_to_all | solution.py:664
  16.1 7.0 %range_compress.3 = (f32[4,2,16,256]{3,2,1,0:T(8,128)}, f32[4,2,16,256]{3,2,1,0:T(8,128)}, f32[4,2,16,256]{3,2,1,0:T(8,128)}, f32[4,2,16,256]{3,2,1,0:T(8,128)},...) custom-call(f32[2,2048]{1,0:T(2,128)} %filter_ref.2, ...), custom_call_target="tpu_custom_call" | custom-call | flops 805306368 | bytes 8388608 | tf_op jit(solution)/shard_map/range_compress/pallas_call | solution.py:298
  23.1 0.3 collective-permute-start
  23.4 1.7 %collective-permute-start.1 = (f32[4,2,16,256]{3,2,1,0:T(8,128)}, f32[4,2,16,256]{3,2,1,0:T(8,128)S(1)}, u32[]{:S(2)}, u32[]{:S(2)}) collective-permute-start(f32[4,2,16,256]{3,2,1,0:T(8,128)} %get-tuple-element.53), channel_id=1, source_target_pairs={{0,8},{4,12},{8,0},{12,4},{16,24},{20,28},{24,16},{28,20},{1,9},{5... | collective-permute-start | bytes 393224 | tf_op jit(solution)/shard_map/ppermute | solution.py:676
  25.0 1.7 %collective-permute-start.3 = (f32[4,2,16,256]{3,2,1,0:T(8,128)}, f32[4,2,16,256]{3,2,1,0:T(8,128)S(1)}, u32[]{:S(2)}, u32[]{:S(2)}) collective-permute-start(f32[4,2,16,256]{3,2,1,0:T(8,128)} %get-tuple-element.55), channel_id=1, source_target_pairs={{0,16},{4,20},{8,24},{12,28},{16,0},{20,4},{24,8},{28,12},{1,17},{... | collective-permute-start | bytes 393224 | tf_op jit(solution)/shard_map/ppermute | solution.py:676
  26.8 2.2 %copy-done = f32[2,1024,512]{2,1,0:T(8,128)S(1)} copy-done((f32[2,1024,512]{2,1,0:T(8,128)S(1)}, f32[2,1024,512]{2,1,0:T(8,128)}, u32[]{:S(2)}) %copy-start) | copy-done | bytes 4194328
  29.0 0.5 own_filter.1
  29.6 0.3 copy-done.10
  29.9 2.6 %collective-permute-start.5 = (f32[4,2,16,256]{3,2,1,0:T(8,128)S(1)}, f32[4,2,16,256]{3,2,1,0:T(8,128)S(1)}, u32[]{:S(2)}, u32[]{:S(2)}) collective-permute-start(f32[4,2,16,256]{3,2,1,0:T(8,128)S(1)} %copy-done.10), channel_id=1, source_target_pairs={{0,24},{4,28},{8,16},{12,20},{16,8},{20,12},{24,0},{28,4},{1,25},{... | collective-permute-start | bytes 393224 | tf_op jit(solution)/shard_map/ppermute | solution.py:676
  32.5 9.3 %collective-permute-done.1.refs_2_ = f32[4,2,16,256]{3,2,1,0:T(8,128)S(1)} collective-permute-done((f32[4,2,16,256]{3,2,1,0:T(8,128)}, f32[4,2,16,256]{3,2,1,0:T(8,128)S(1)}, u32[]{:S(2)}, u32[]{:S(2)}) %collective-permute-start.1) | collective-permute-done | bytes 131104 | tf_op jit(solution)/shard_map/ppermute | solution.py:676
  41.8 0.6 collective-permute-start.6
  42.5 17.9 %all_gather.4 = f32[8,8,2]{0,2,1:T(2,128)S(1)} all-gather(f32[8,1,2]{0,2,1:T(2,128)S(1)} %broadcast_multiply_fusion), channel_id=1, replica_groups=mesh['acq'=8,'strip'=4] {'acq'}, dimensions={1}, use_global_device_ids=true | all-gather | bytes 576 | tf_op jit(solution)/shard_map/all_gather | solution.py:724
  60.5 1.8 %regroup.1 = (f32[8,2,16,256]{3,2,1,0:T(8,128)S(1)}, f32[8,2,16,256]{3,2,1,0:T(8,128)S(1)}, f32[8,2,16,256]{3,2,1,0:T(8,128)S(1)}, f32[8,2,16,256]{3,2,1,0:T(8,128)S(1)}) custom-call(f32[4,2,16,256]{3,2,1,0:T(8,128)S(1)} %copy-done.1, f32[4,2,16,256]{3,2,1,0:T(8,128)S(1)} %collective-permute-done.refs_1_, ...), custom_call_target="tpu_custom_call" | custom-call | bytes 1024 | tf_op jit(solution)/shard_map/regroup/pallas_call | solution.py:705
  62.3 0.5 collective-permute-start.7
  62.8 3.2 %collective-permute-start.8 = (f32[8,2,16,256]{3,2,1,0:T(8,128)S(1)}, f32[8,2,16,256]{3,2,1,0:T(8,128)S(1)}, u32[]{:S(2)}, u32[]{:S(2)}) collective-permute-start(f32[8,2,16,256]{3,2,1,0:T(8,128)S(1)} %get-tuple-element.73), channel_id=1, source_target_pairs={{0,2},{1,3},{2,0},{3,1},{4,6},{5,7},{6,4},{7,5},{8,10},{9,11},{10,... | collective-permute-start | bytes 786440 | tf_op jit(solution)/shard_map/ppermute | solution.py:676
  66.0 0.7 collective-permute-start.9
  66.8 32.7 %all-to-all-done = f32[32,2,48,256]{3,2,1,0:T(8,128)} async-done(((f32[32,2,48,256]{3,2,1,0:T(8,128)}), f32[32,2,48,256]{3,2,1,0:T(8,128)}, u32[]{:S(2)}, u32[]{:S(2)}) %all-to-all-start) | async-done | bytes 3145760 | tf_op jit(solution)/shard_map/all_to_all | solution.py:664
  99.5 8.2 %azimuth_focus.2.refs_10_ = f32[8,2,2,16,256]{4,3,2,1,0:T(8,128)S(1)} custom-call(f32[4,8,2,48,256]{4,3,2,1,0:T(8,128)} %bitcast.4.refs_0_, f32[2,8,48,128]{3,2,1,0:T(8,128)S(1)} %get-tuple-element.78.refs_1_, bf16[256,256]{1,0:T(8,128)(2,1)S(1)} %copy-done.4, bf16[256,256]{1,0:T(8,128)(2,1)S(1)} %copy-done.3, f32[4,8,128]{2,1,0:T(8,128)S(1)} %copy-done.5, ...), custom_call_target="tpu_custom_call" | custom-call | flops 2415919104 | bytes 7340032 | tf_op jit(solution)/shard_map/azimuth_focus/pallas_call | solution.py:573
  107.7 1.3 collective-permute-start.10
  109.1 1.7 %collective-permute-done.10.refs_11_ = f32[8,2,2,1,256]{4,3,2,1,0:T(1,128)S(1)} collective-permute-done((f32[8,2,2,1,256]{4,3,2,1,0:T(1,128)S(1)}, f32[8,2,2,1,256]{4,3,2,1,0:T(1,128)S(1)}, u32[]{:S(2)}, u32[]{:S(2)}) %collective-permute-start.10) | collective-permute-done | bytes 32800 | tf_op jit(solution)/shard_map/ppermute | solution.py:755
  110.8 8.0 %azimuth_focus.3 = f32[8,2,16,256]{3,2,1,0:T(8,128)S(1)} custom-call(f32[8,2,16,256]{3,2,1,0:T(8,128)S(1)} %get-tuple-element.71.refs_0_, f32[8,2,16,256]{3,2,1,0:T(8,128)S(1)} %collective-permute-done.7.refs_1_, f32[8,2,16,256]{3,2,1,0:T(8,128)S(1)} %collective-permute-done.8.refs_2_, f32[8,2,16,256]{3,2,1,0:T(8,128)S(1)} %collective-permute-done.9.refs_3_, ...), custom_call_target="tpu_custom_call" | custom-call | flops 805306368 | bytes 5242880 | tf_op jit(solution)/shard_map/azimuth_focus/pallas_call | solution.py:573
  118.8 12.7 %all_to_all.10 = f32[8,2,16,256]{3,2,1,0:T(8,128)S(1)} all-to-all(f32[8,2,16,256]{3,2,1,0:T(8,128)S(1)} %azimuth_focus.3), channel_id=1, replica_groups=mesh['acq'=8,'strip'=4] {'acq'}, dimensions={0} | all-to-all | bytes 524288 | tf_op jit(solution)/shard_map/all_to_all | solution.py:764
  131.5 0.7 copy.25
  (35 shorter events, 0.4 us)
Async XLA Ops:
  8.6 90.8 %all-to-all-start = ((f32[32,2,48,256]{3,2,1,0:T(8,128)}), f32[32,2,48,256]{3,2,1,0:T(8,128)}, u32[]{:S(2)}, u32[]{:S(2)}) async-start(f32[32,2,48,256]{3,2,1,0:T(8,128)} %bitcast.10), calls=%async_computation | async-start | bytes 6291456 | tf_op jit(solution)/shard_map/all_to_all | solution.py:664
  16.0 13.5 %copy-start.7 = (s32[1,2]{1,0:T(1,128)S(1)}, s32[1,2]{1,0:T(1,128)}, u32[]{:S(2)}) copy-start(s32[1,2]{1,0:T(1,128)} %param.23) | copy-start | bytes 28
  16.1 13.5 %copy-start.8 = (s32[2]{0:T(128)S(1)}, s32[2]{0:T(128)}, u32[]{:S(2)}) copy-start(s32[2]{0:T(128)} %constant.27.clone) | copy-start | bytes 28
  16.1 26.4 %copy-start.6 = (f32[8,1,2]{0,2,1:T(2,128)S(1)}, f32[8,1,2]{0,2,1:T(2,128)}, u32[]{:S(2)}) copy-start(f32[8,1,2]{0,2,1:T(2,128)} %param.24) | copy-start | bytes 196
  16.1 83.4 %copy-start.2 = (bf16[512,128]{1,0:T(8,128)(2,1)S(1)}, bf16[512,128]{1,0:T(8,128)(2,1)}, u32[]{:S(2)}) copy-start(bf16[512,128]{1,0:T(8,128)(2,1)} %constant.31.clone.refs_5_.refs_8_) | copy-start | bytes 393220
  16.1 83.4 %copy-start.3 = (bf16[256,256]{1,0:T(8,128)(2,1)S(1)}, bf16[256,256]{1,0:T(8,128)(2,1)}, u32[]{:S(2)}) copy-start(bf16[256,256]{1,0:T(8,128)(2,1)} %constant.29.clone.refs_3_.refs_6_) | copy-start | bytes 393220
  16.1 83.3 %copy-start.4 = (bf16[256,256]{1,0:T(8,128)(2,1)S(1)}, bf16[256,256]{1,0:T(8,128)(2,1)}, u32[]{:S(2)}) copy-start(bf16[256,256]{1,0:T(8,128)(2,1)} %constant.28.clone.refs_2_.refs_5_) | copy-start | bytes 393220
  16.1 83.3 %copy-start.5 = (f32[4,8,128]{2,1,0:T(8,128)S(1)}, f32[4,8,128]{2,1,0:T(8,128)}, u32[]{:S(2)}) copy-start(f32[4,8,128]{2,1,0:T(8,128)} %constant.30.clone.refs_4_.refs_7_) | copy-start | bytes 49156
  23.1 6.5 %collective-permute-start = (f32[4,2,16,256]{3,2,1,0:T(8,128)}, f32[4,2,16,256]{3,2,1,0:T(8,128)S(1)}, u32[]{:S(2)}, u32[]{:S(2)}) collective-permute-start(f32[4,2,16,256]{3,2,1,0:T(8,128)} %get-tuple-element.52), channel_id=1, source_target_pairs={{0,4},{4,0},{8,12},{12,8},{16,20},{20,16},{24,28},{28,24},{1,5},{5... | collective-permute-start | bytes 393224 | tf_op jit(solution)/shard_map/ppermute | solution.py:676
  23.4 18.5 %collective-permute-start.1 = (f32[4,2,16,256]{3,2,1,0:T(8,128)}, f32[4,2,16,256]{3,2,1,0:T(8,128)S(1)}, u32[]{:S(2)}, u32[]{:S(2)}) collective-permute-start(f32[4,2,16,256]{3,2,1,0:T(8,128)} %get-tuple-element.53), channel_id=1, source_target_pairs={{0,8},{4,12},{8,0},{12,4},{16,24},{20,28},{24,16},{28,20},{1,9},{5... | collective-permute-start | bytes 393224 | tf_op jit(solution)/shard_map/ppermute | solution.py:676
  25.0 35.4 %collective-permute-start.2 = (f32[4,2,16,256]{3,2,1,0:T(8,128)}, f32[4,2,16,256]{3,2,1,0:T(8,128)S(1)}, u32[]{:S(2)}, u32[]{:S(2)}) collective-permute-start(f32[4,2,16,256]{3,2,1,0:T(8,128)} %get-tuple-element.54), channel_id=1, source_target_pairs={{0,12},{4,8},{8,4},{12,0},{16,28},{20,24},{24,20},{28,16},{1,13},{... | collective-permute-start | bytes 393224 | tf_op jit(solution)/shard_map/ppermute | solution.py:676
  25.0 35.4 %collective-permute-start.3 = (f32[4,2,16,256]{3,2,1,0:T(8,128)}, f32[4,2,16,256]{3,2,1,0:T(8,128)S(1)}, u32[]{:S(2)}, u32[]{:S(2)}) collective-permute-start(f32[4,2,16,256]{3,2,1,0:T(8,128)} %get-tuple-element.55), channel_id=1, source_target_pairs={{0,16},{4,20},{8,24},{12,28},{16,0},{20,4},{24,8},{28,12},{1,17},{... | collective-permute-start | bytes 393224 | tf_op jit(solution)/shard_map/ppermute | solution.py:676
  26.7 33.7 %collective-permute-start.4 = (f32[4,2,16,256]{3,2,1,0:T(8,128)}, f32[4,2,16,256]{3,2,1,0:T(8,128)S(1)}, u32[]{:S(2)}, u32[]{:S(2)}) collective-permute-start(f32[4,2,16,256]{3,2,1,0:T(8,128)} %get-tuple-element.56), channel_id=1, source_target_pairs={{0,20},{4,16},{8,28},{12,24},{16,4},{20,0},{24,12},{28,8},{1,21},{... | collective-permute-start | bytes 393224 | tf_op jit(solution)/shard_map/ppermute | solution.py:676
  26.8 2.2 %copy-start = (f32[2,1024,512]{2,1,0:T(8,128)S(1)}, f32[2,1024,512]{2,1,0:T(8,128)}, u32[]{:S(2)}) copy-start(f32[2,1024,512]{2,1,0:T(8,128)} %filter_any) | copy-start | bytes 12582916
  29.0 0.9 copy-start.10
  29.0 12.8 %copy-start.9 = (f32[4,2,16,256]{3,2,1,0:T(8,128)S(1)}, f32[4,2,16,256]{3,2,1,0:T(8,128)}, u32[]{:S(2)}) copy-start(f32[4,2,16,256]{3,2,1,0:T(8,128)} %get-tuple-element.58) | copy-start | bytes 393220
  29.0 31.4 %copy-start.1 = (f32[4,2,16,256]{3,2,1,0:T(8,128)S(1)}, f32[4,2,16,256]{3,2,1,0:T(8,128)}, u32[]{:S(2)}) copy-start(f32[4,2,16,256]{3,2,1,0:T(8,128)} %get-tuple-element.63.refs_0_) | copy-start | bytes 393220
  29.9 30.5 %collective-permute-start.5 = (f32[4,2,16,256]{3,2,1,0:T(8,128)S(1)}, f32[4,2,16,256]{3,2,1,0:T(8,128)S(1)}, u32[]{:S(2)}, u32[]{:S(2)}) collective-permute-start(f32[4,2,16,256]{3,2,1,0:T(8,128)S(1)} %copy-done.10), channel_id=1, source_target_pairs={{0,24},{4,28},{8,16},{12,20},{16,8},{20,12},{24,0},{28,4},{1,25},{... | collective-permute-start | bytes 393224 | tf_op jit(solution)/shard_map/ppermute | solution.py:676
  41.8 18.6 %collective-permute-start.6 = (f32[4,2,16,256]{3,2,1,0:T(8,128)S(1)}, f32[4,2,16,256]{3,2,1,0:T(8,128)S(1)}, u32[]{:S(2)}, u32[]{:S(2)}) collective-permute-start(f32[4,2,16,256]{3,2,1,0:T(8,128)S(1)} %copy-done.9), channel_id=1, source_target_pairs={{0,28},{4,24},{8,20},{12,16},{16,12},{20,8},{24,4},{28,0},{1,29},{... | collective-permute-start | bytes 393224 | tf_op jit(solution)/shard_map/ppermute | solution.py:676
  62.3 46.8 %collective-permute-start.7 = (f32[8,2,16,256]{3,2,1,0:T(8,128)S(1)}, f32[8,2,16,256]{3,2,1,0:T(8,128)S(1)}, u32[]{:S(2)}, u32[]{:S(2)}) collective-permute-start(f32[8,2,16,256]{3,2,1,0:T(8,128)S(1)} %get-tuple-element.72), channel_id=1, source_target_pairs={{0,1},{1,0},{2,3},{3,2},{4,5},{5,4},{6,7},{7,6},{8,9},{9,8},{10,11... | collective-permute-start | bytes 786440 | tf_op jit(solution)/shard_map/ppermute | solution.py:676
  62.8 46.3 %collective-permute-start.8 = (f32[8,2,16,256]{3,2,1,0:T(8,128)S(1)}, f32[8,2,16,256]{3,2,1,0:T(8,128)S(1)}, u32[]{:S(2)}, u32[]{:S(2)}) collective-permute-start(f32[8,2,16,256]{3,2,1,0:T(8,128)S(1)} %get-tuple-element.73), channel_id=1, source_target_pairs={{0,2},{1,3},{2,0},{3,1},{4,6},{5,7},{6,4},{7,5},{8,10},{9,11},{10,... | collective-permute-start | bytes 786440 | tf_op jit(solution)/shard_map/ppermute | solution.py:676
  66.0 43.0 %collective-permute-start.9 = (f32[8,2,16,256]{3,2,1,0:T(8,128)S(1)}, f32[8,2,16,256]{3,2,1,0:T(8,128)S(1)}, u32[]{:S(2)}, u32[]{:S(2)}) collective-permute-start(f32[8,2,16,256]{3,2,1,0:T(8,128)S(1)} %get-tuple-element.74), channel_id=1, source_target_pairs={{0,3},{1,2},{2,1},{3,0},{4,7},{5,6},{6,5},{7,4},{8,11},{9,10},{10,... | collective-permute-start | bytes 786440 | tf_op jit(solution)/shard_map/ppermute | solution.py:676
  107.7 3.1 %collective-permute-start.10 = (f32[8,2,2,1,256]{4,3,2,1,0:T(1,128)S(1)}, f32[8,2,2,1,256]{4,3,2,1,0:T(1,128)S(1)}, u32[]{:S(2)}, u32[]{:S(2)}) collective-permute-start(f32[8,2,2,1,256]{4,3,2,1,0:T(1,128)S(1)} %slice.4), channel_id=1, source_target_pairs={{4,0},{8,4},{12,8},{16,12},{20,16},{24,20},{28,24},{1,28},{5,1},{9... | collective-permute-start | bytes 98312 | tf_op jit(solution)/shard_map/ppermute | solution.py:755

commit v10 on v9

--- a/solution.py
+++ b/solution.py
@@ -118,7 +118,7 @@
             return self
         own = copy.copy(self)
         size = self.owned // 4
-        own.start, own.rows = (0, 3 * size) if number == 0 else (3 * size, size)
+        own.start, own.rows = (0, size) if number == 0 else (size, 3 * size)
         own.looks = own.rows // LOOK
         return own
 
@@ -730,25 +730,22 @@
     plan = Plan(strips, epochs, raw_echoes.shape[2], raw_echoes.shape[3])
 
     raw = raw_echoes[0]
-    big, small = plan.part(0), plan.part(1)
+    small, big = plan.part(0), plan.part(1)
     block = compress(big, False, range_filter, raw)
     if plan.parts > 1:
         range_filter, block = lax.optimization_barrier((range_filter, block))
         other = compress(small, True, range_filter, raw)
-        *other, azimuth_filter, pair_mask, inversion = lax.optimization_barrier(
-            (*other, azimuth_filter, pair_mask, inversion)
-        )
-        weights = all_weights(pair_mask, inversion)
-        spectrum, other_spectrum = own_filter_by_kernel(plan, azimuth_filter)
+        *other, azimuth_filter = lax.optimization_barrier((*other, azimuth_filter))
+        other_spectrum, spectrum = own_filter_by_kernel(plan, azimuth_filter)
         field = exchange_all(big, block)
         other = partners(other, "acq")
-        *other, spectrum, weights = lax.optimization_barrier((*other, spectrum, weights))
+        *other, other_spectrum = lax.optimization_barrier((*other, other_spectrum))
         other = partners(regroup(other), "strip")
+        before = focus(small, other, other_spectrum)
+        before, pair_mask, inversion = lax.optimization_barrier((before, pair_mask, inversion))
     else:
-        weights = all_weights(pair_mask, inversion)
-        spectrum = own_filter(plan, azimuth_filter)
-        field = exchange_all(plan, block)
-    before = focus(big, [field], spectrum)
+        before = focus(plan, [exchange_all(plan, block)], own_filter(plan, azimuth_filter))
+    weights = all_weights(pair_mask, inversion)
 
     owners = strips * epochs
     device = [i % epochs * strips + i // epochs for i in range(owners)]
@@ -758,7 +755,7 @@
         [(device[i], device[i - 1]) for i in range(1, owners)],
     )
     if plan.parts > 1:
-        gradients = focus(small, other, other_spectrum, (weights, before, halo))
+        gradients = focus(big, [field], spectrum, (weights, before, halo))
     else:
         gradients = slopes_to_epochs(plan, weights, before, halo)
     gathered = lax.all_to_all(gradients, "acq", split_axis=0, concat_axis=0, tiled=True)

time: 133 us -> 146 us (1.098)
  the two profiles are of different devices: /device:TPU:0 before, /device:TPU:8 now
where the time goes in v10:
time: 146 us; the launch traced here: 145 us
  waiting for transfers between devices  71.7 us (49%)
  Pallas kernels  34 us (23%)
  blocking collectives  18.7 us (13%)
  starting transfers between devices  17.7 us (12%)
  local copies, waits for them, and re-layouts  3.05 us (2%)
    ppermute x10, waiting for transfers between devices, partners(): lax.ppermute(slot, axis, [(i, i ^ k) for i in range(size)])  71.7 us
    pallas_call x2, Pallas kernels, focus(): pl.pallas_call(kernel, out_shape=jax.ShapeDtypeStruct(shape, jnp.float32)...  16.1 us
    pallas_call x2, Pallas kernels, compress(): pl.pallas_call(functools.partial(compress_kernel, plan, relative), out_sh...  15.6 us
    ppermute x10, starting transfers between devices, partners(): lax.ppermute(slot, axis, [(i, i ^ k) for i in range(size)])  9.64 us
    all_to_all x1, blocking collectives, per_device(): lax.all_to_all(gradients, 'acq', split_axis=0, concat_axis=0, tiled=True)  9.46 us
    all_gather x1, blocking collectives, all_weights(): lax.all_gather(inversion[:, 0, :] * usable[None, :], 'acq', axis=1, tiled...  9.27 us
    all_to_all x1, starting transfers between devices, exchange_all(): lax.all_to_all(block, OWNERS, split_axis=0, concat_axis=0, tiled=True)  6.1 us
  transfers between devices with their start and end apart: 12, of which 8 were waited for; matrix products, arithmetic and copies ran while one was open for 0% of the time, Pallas kernels for 10%

profile of v10, /device:TPU:8, one launch (start us, length us, event | category | flops | bytes accessed | tf_op | source)
XLA Modules:
  0.0 145.4 jit_solution(9810395285138702566)
XLA Ops:
  0.0 8.7 %range_compress.2 = f32[4,8,2,48,256]{4,3,2,1,0:T(8,128)} custom-call(f32[2,2048]{1,0:T(2,128)} %filter_ref.2, bf16[256,512]{1,0:T(8,128)(2,1)} %constant.24.clone.high_any, bf16[256,512]{1,0:T(8,128)(2,1)} %constant.25.clone.low_any, f32[4,8,256]{2,1,0:T(8,128)} %constant.26.clone.turn_any, f32[2,256,2048]{2,1,0:T(8,128)} %bitcast.8), custom_call_target="tpu_custom_call" | custom-call | flops 2415919104 | bytes 8388608 | tf_op jit(solution)/shard_map/range_compress/pallas_call | solution.py:298
  8.7 6.1 %all-to-all-start = ((f32[32,2,48,256]{3,2,1,0:T(8,128)}), f32[32,2,48,256]{3,2,1,0:T(8,128)}, u32[]{:S(2)}, u32[]{:S(2)}) async-start(f32[32,2,48,256]{3,2,1,0:T(8,128)} %bitcast.10), calls=%async_computation | async-start | bytes 6291456 | tf_op jit(solution)/shard_map/all_to_all | solution.py:664
  14.8 7.0 %range_compress.3 = (f32[4,2,16,256]{3,2,1,0:T(8,128)}, f32[4,2,16,256]{3,2,1,0:T(8,128)}, f32[4,2,16,256]{3,2,1,0:T(8,128)}, f32[4,2,16,256]{3,2,1,0:T(8,128)},...) custom-call(f32[2,2048]{1,0:T(2,128)} %filter_ref.2, ...), custom_call_target="tpu_custom_call" | custom-call | flops 805306368 | bytes 8388608 | tf_op jit(solution)/shard_map/range_compress/pallas_call | solution.py:298
  22.1 1.5 %collective-permute-start.1 = (f32[4,2,16,256]{3,2,1,0:T(8,128)}, f32[4,2,16,256]{3,2,1,0:T(8,128)S(1)}, u32[]{:S(2)}, u32[]{:S(2)}) collective-permute-start(f32[4,2,16,256]{3,2,1,0:T(8,128)} %get-tuple-element.56), channel_id=1, source_target_pairs={{0,8},{4,12},{8,0},{12,4},{16,24},{20,28},{24,16},{28,20},{1,9},{5... | collective-permute-start | bytes 393224 | tf_op jit(solution)/shard_map/ppermute | solution.py:676
  23.8 1.5 %collective-permute-start.3 = (f32[4,2,16,256]{3,2,1,0:T(8,128)}, f32[4,2,16,256]{3,2,1,0:T(8,128)S(1)}, u32[]{:S(2)}, u32[]{:S(2)}) collective-permute-start(f32[4,2,16,256]{3,2,1,0:T(8,128)} %get-tuple-element.58), channel_id=1, source_target_pairs={{0,16},{4,20},{8,24},{12,28},{16,0},{20,4},{24,8},{28,12},{1,17},{... | collective-permute-start | bytes 393224 | tf_op jit(solution)/shard_map/ppermute | solution.py:676
  25.6 2.4 %collective-permute-start.5 = (f32[4,2,16,256]{3,2,1,0:T(8,128)}, f32[4,2,16,256]{3,2,1,0:T(8,128)S(1)}, u32[]{:S(2)}, u32[]{:S(2)}) collective-permute-start(f32[4,2,16,256]{3,2,1,0:T(8,128)} %get-tuple-element.60), channel_id=1, source_target_pairs={{0,24},{4,28},{8,16},{12,20},{16,8},{20,12},{24,0},{28,4},{1,25},{... | collective-permute-start | bytes 393224 | tf_op jit(solution)/shard_map/ppermute | solution.py:676
  27.9 10.2 %collective-permute-done.1.refs_2_ = f32[4,2,16,256]{3,2,1,0:T(8,128)S(1)} collective-permute-done((f32[4,2,16,256]{3,2,1,0:T(8,128)}, f32[4,2,16,256]{3,2,1,0:T(8,128)S(1)}, u32[]{:S(2)}, u32[]{:S(2)}) %collective-permute-start.1) | collective-permute-done | bytes 131104 | tf_op jit(solution)/shard_map/ppermute | solution.py:676
  38.1 2.2 %copy-done = f32[2,1024,512]{2,1,0:T(8,128)S(1)} copy-done((f32[2,1024,512]{2,1,0:T(8,128)S(1)}, f32[2,1024,512]{2,1,0:T(8,128)}, u32[]{:S(2)}) %copy-start) | copy-done | bytes 4194328
  41.1 2.7 %collective-permute-done.4.refs_5_ = f32[4,2,16,256]{3,2,1,0:T(8,128)S(1)} collective-permute-done((f32[4,2,16,256]{3,2,1,0:T(8,128)}, f32[4,2,16,256]{3,2,1,0:T(8,128)S(1)}, u32[]{:S(2)}, u32[]{:S(2)}) %collective-permute-start.4) | collective-permute-done | bytes 131104 | tf_op jit(solution)/shard_map/ppermute | solution.py:676
  43.8 6.1 %collective-permute-done.5.refs_6_ = f32[4,2,16,256]{3,2,1,0:T(8,128)S(1)} collective-permute-done((f32[4,2,16,256]{3,2,1,0:T(8,128)}, f32[4,2,16,256]{3,2,1,0:T(8,128)S(1)}, u32[]{:S(2)}, u32[]{:S(2)}) %collective-permute-start.5) | collective-permute-done | bytes 131104 | tf_op jit(solution)/shard_map/ppermute | solution.py:676
  49.9 7.1 %collective-permute-done.6.refs_7_ = f32[4,2,16,256]{3,2,1,0:T(8,128)S(1)} collective-permute-done((f32[4,2,16,256]{3,2,1,0:T(8,128)}, f32[4,2,16,256]{3,2,1,0:T(8,128)S(1)}, u32[]{:S(2)}, u32[]{:S(2)}) %collective-permute-start.6) | collective-permute-done | bytes 131104 | tf_op jit(solution)/shard_map/ppermute | solution.py:676
  57.1 1.8 %regroup.1 = (f32[8,2,16,256]{3,2,1,0:T(8,128)S(1)}, f32[8,2,16,256]{3,2,1,0:T(8,128)S(1)}, f32[8,2,16,256]{3,2,1,0:T(8,128)S(1)}, f32[8,2,16,256]{3,2,1,0:T(8,128)S(1)}) custom-call(f32[4,2,16,256]{3,2,1,0:T(8,128)S(1)} %copy-done.1, f32[4,2,16,256]{3,2,1,0:T(8,128)S(1)} %collective-permute-done.refs_1_, ...), custom_call_target="tpu_custom_call" | custom-call | bytes 1024 | tf_op jit(solution)/shard_map/regroup/pallas_call | solution.py:705
  58.9 1.9 %collective-permute-start.7 = (f32[8,2,16,256]{3,2,1,0:T(8,128)S(1)}, f32[8,2,16,256]{3,2,1,0:T(8,128)S(1)}, u32[]{:S(2)}, u32[]{:S(2)}) collective-permute-start(f32[8,2,16,256]{3,2,1,0:T(8,128)S(1)} %get-tuple-element.72), channel_id=1, source_target_pairs={{0,1},{1,0},{2,3},{3,2},{4,5},{5,4},{6,7},{7,6},{8,9},{9,8},{10,11... | collective-permute-start | bytes 786440 | tf_op jit(solution)/shard_map/ppermute | solution.py:676
  60.8 0.7 collective-permute-start.8
  61.5 0.9 collective-permute-start.9
  62.4 10.8 %collective-permute-done.7.refs_1_ = f32[8,2,16,256]{3,2,1,0:T(8,128)S(1)} collective-permute-done((f32[8,2,16,256]{3,2,1,0:T(8,128)S(1)}, f32[8,2,16,256]{3,2,1,0:T(8,128)S(1)}, u32[]{:S(2)}, u32[]{:S(2)}) %collective-permute-start.7) | collective-permute-done | bytes 262176 | tf_op jit(solution)/shard_map/ppermute | solution.py:676
  73.3 27.2 %collective-permute-done.8.refs_2_ = f32[8,2,16,256]{3,2,1,0:T(8,128)S(1)} collective-permute-done((f32[8,2,16,256]{3,2,1,0:T(8,128)S(1)}, f32[8,2,16,256]{3,2,1,0:T(8,128)S(1)}, u32[]{:S(2)}, u32[]{:S(2)}) %collective-permute-start.8) | collective-permute-done | bytes 262176 | tf_op jit(solution)/shard_map/ppermute | solution.py:676
  100.5 7.2 %collective-permute-done.9.refs_3_ = f32[8,2,16,256]{3,2,1,0:T(8,128)S(1)} collective-permute-done((f32[8,2,16,256]{3,2,1,0:T(8,128)S(1)}, f32[8,2,16,256]{3,2,1,0:T(8,128)S(1)}, u32[]{:S(2)}, u32[]{:S(2)}) %collective-permute-start.9) | collective-permute-done | bytes 262176 | tf_op jit(solution)/shard_map/ppermute | solution.py:676
  107.7 5.6 %azimuth_focus.2.refs_7_ = f32[8,2,2,16,256]{4,3,2,1,0:T(8,128)S(1)} custom-call(f32[8,2,16,256]{3,2,1,0:T(8,128)S(1)} %get-tuple-element.71.refs_0_, f32[8,2,16,256]{3,2,1,0:T(8,128)S(1)} %collective-permute-done.7.refs_1_, f32[8,2,16,256]{3,2,1,0:T(8,128)S(1)} %collective-permute-done.8.refs_2_, f32[8,2,16,256]{3,2,1,0:T(8,128)S(1)} %collective-permute-done.9.refs_3_, ...), custom_call_target="tpu_custom_call" | custom-call | flops 805306368 | bytes 5242880 | tf_op jit(solution)/shard_map/azimuth_focus/pallas_call | solution.py:573
  113.4 1.9 %collective-permute-start.10 = (f32[8,2,2,1,256]{4,3,2,1,0:T(1,128)S(1)}, f32[8,2,2,1,256]{4,3,2,1,0:T(1,128)S(1)}, u32[]{:S(2)}, u32[]{:S(2)}) collective-permute-start(f32[8,2,2,1,256]{4,3,2,1,0:T(1,128)S(1)} %slice.3), channel_id=1, source_target_pairs={{4,0},{8,4},{12,8},{16,12},{20,16},{24,20},{28,24},{1,28},{5,1},{9... | collective-permute-start | bytes 98312 | tf_op jit(solution)/shard_map/ppermute | solution.py:752
  115.4 9.3 %all_gather.4 = f32[8,8,2]{0,2,1:T(2,128)S(1)} all-gather(f32[8,1,2]{0,2,1:T(2,128)S(1)} %broadcast_multiply_fusion), channel_id=1, replica_groups=mesh['acq'=8,'strip'=4] {'acq'}, dimensions={1}, use_global_device_ids=true | all-gather | bytes 576 | tf_op jit(solution)/shard_map/all_gather | solution.py:724
  124.8 10.5 %azimuth_focus.3 = f32[8,2,16,256]{3,2,1,0:T(8,128)S(1)} custom-call(f32[4,8,2,48,256]{4,3,2,1,0:T(8,128)} %bitcast.2.refs_0_, f32[2,8,48,128]{3,2,1,0:T(8,128)S(1)} %get-tuple-element.53.refs_1_, bf16[256,256]{1,0:T(8,128)(2,1)S(1)} %copy-done.2, bf16[256,256]{1,0:T(8,128)(2,1)S(1)} %copy-done.3, f32[4,8,128]{2,1,0:T(8,128)S(1)} %copy-done.5, ...), custom_call_target="tpu_custom_call" | custom-call | flops 2415919104 | bytes 7340032 | tf_op jit(solution)/shard_map/azimuth_focus/pallas_call | solution.py:573
  135.2 9.5 %all_to_all.10 = f32[8,2,16,256]{3,2,1,0:T(8,128)S(1)} all-to-all(f32[8,2,16,256]{3,2,1,0:T(8,128)S(1)} %azimuth_focus.3), channel_id=1, replica_groups=mesh['acq'=8,'strip'=4] {'acq'}, dimensions={0} | all-to-all | bytes 524288 | tf_op jit(solution)/shard_map/all_to_all | solution.py:761
  144.7 0.7 copy.25
  (31 shorter events, 1.8 us)
Async XLA Ops:
  8.7 116.1 %all-to-all-start = ((f32[32,2,48,256]{3,2,1,0:T(8,128)}), f32[32,2,48,256]{3,2,1,0:T(8,128)}, u32[]{:S(2)}, u32[]{:S(2)}) async-start(f32[32,2,48,256]{3,2,1,0:T(8,128)} %bitcast.10), calls=%async_computation | async-start | bytes 6291456 | tf_op jit(solution)/shard_map/all_to_all | solution.py:664
  14.8 92.9 %copy-start.2 = (bf16[256,256]{1,0:T(8,128)(2,1)S(1)}, bf16[256,256]{1,0:T(8,128)(2,1)}, u32[]{:S(2)}) copy-start(bf16[256,256]{1,0:T(8,128)(2,1)} %constant.27.clone.refs_5_.refs_2_) | copy-start | bytes 393220
  14.8 92.9 %copy-start.3 = (bf16[256,256]{1,0:T(8,128)(2,1)S(1)}, bf16[256,256]{1,0:T(8,128)(2,1)}, u32[]{:S(2)}) copy-start(bf16[256,256]{1,0:T(8,128)(2,1)} %constant.28.clone.refs_6_.refs_3_) | copy-start | bytes 393220
  14.8 92.9 %copy-start.4 = (bf16[512,128]{1,0:T(8,128)(2,1)S(1)}, bf16[512,128]{1,0:T(8,128)(2,1)}, u32[]{:S(2)}) copy-start(bf16[512,128]{1,0:T(8,128)(2,1)} %constant.30.clone.refs_8_.refs_5_) | copy-start | bytes 393220
  14.8 92.9 %copy-start.5 = (f32[4,8,128]{2,1,0:T(8,128)S(1)}, f32[4,8,128]{2,1,0:T(8,128)}, u32[]{:S(2)}) copy-start(f32[4,8,128]{2,1,0:T(8,128)} %constant.29.clone.refs_7_.refs_4_) | copy-start | bytes 49156
  21.8 93.5 %copy-start.7 = (s32[1,2]{1,0:T(1,128)S(1)}, s32[1,2]{1,0:T(1,128)}, u32[]{:S(2)}) copy-start(s32[1,2]{1,0:T(1,128)} %param.23) | copy-start | bytes 28
  21.8 93.5 %copy-start.8 = (s32[2]{0:T(128)S(1)}, s32[2]{0:T(128)}, u32[]{:S(2)}) copy-start(s32[2]{0:T(128)} %constant.31.clone) | copy-start | bytes 28
  21.8 93.5 %copy-start.6 = (f32[8,1,2]{0,2,1:T(2,128)S(1)}, f32[8,1,2]{0,2,1:T(2,128)}, u32[]{:S(2)}) copy-start(f32[8,1,2]{0,2,1:T(2,128)} %param.24) | copy-start | bytes 196
  21.8 3.7 %collective-permute-start = (f32[4,2,16,256]{3,2,1,0:T(8,128)}, f32[4,2,16,256]{3,2,1,0:T(8,128)S(1)}, u32[]{:S(2)}, u32[]{:S(2)}) collective-permute-start(f32[4,2,16,256]{3,2,1,0:T(8,128)} %get-tuple-element.55), channel_id=1, source_target_pairs={{0,4},{4,0},{8,12},{12,8},{16,20},{20,16},{24,28},{28,24},{1,5},{5... | collective-permute-start | bytes 393224 | tf_op jit(solution)/shard_map/ppermute | solution.py:676
  22.1 16.1 %collective-permute-start.1 = (f32[4,2,16,256]{3,2,1,0:T(8,128)}, f32[4,2,16,256]{3,2,1,0:T(8,128)S(1)}, u32[]{:S(2)}, u32[]{:S(2)}) collective-permute-start(f32[4,2,16,256]{3,2,1,0:T(8,128)} %get-tuple-element.56), channel_id=1, source_target_pairs={{0,8},{4,12},{8,0},{12,4},{16,24},{20,28},{24,16},{28,20},{1,9},{5... | collective-permute-start | bytes 393224 | tf_op jit(solution)/shard_map/ppermute | solution.py:676
  23.5 17.6 %collective-permute-start.2 = (f32[4,2,16,256]{3,2,1,0:T(8,128)}, f32[4,2,16,256]{3,2,1,0:T(8,128)S(1)}, u32[]{:S(2)}, u32[]{:S(2)}) collective-permute-start(f32[4,2,16,256]{3,2,1,0:T(8,128)} %get-tuple-element.57), channel_id=1, source_target_pairs={{0,12},{4,8},{8,4},{12,0},{16,28},{20,24},{24,20},{28,16},{1,13},{... | collective-permute-start | bytes 393224 | tf_op jit(solution)/shard_map/ppermute | solution.py:676
  23.8 17.4 %collective-permute-start.3 = (f32[4,2,16,256]{3,2,1,0:T(8,128)}, f32[4,2,16,256]{3,2,1,0:T(8,128)S(1)}, u32[]{:S(2)}, u32[]{:S(2)}) collective-permute-start(f32[4,2,16,256]{3,2,1,0:T(8,128)} %get-tuple-element.58), channel_id=1, source_target_pairs={{0,16},{4,20},{8,24},{12,28},{16,0},{20,4},{24,8},{28,12},{1,17},{... | collective-permute-start | bytes 393224 | tf_op jit(solution)/shard_map/ppermute | solution.py:676
  25.2 18.6 %collective-permute-start.4 = (f32[4,2,16,256]{3,2,1,0:T(8,128)}, f32[4,2,16,256]{3,2,1,0:T(8,128)S(1)}, u32[]{:S(2)}, u32[]{:S(2)}) collective-permute-start(f32[4,2,16,256]{3,2,1,0:T(8,128)} %get-tuple-element.59), channel_id=1, source_target_pairs={{0,20},{4,16},{8,28},{12,24},{16,4},{20,0},{24,12},{28,8},{1,21},{... | collective-permute-start | bytes 393224 | tf_op jit(solution)/shard_map/ppermute | solution.py:676
  25.6 24.4 %collective-permute-start.5 = (f32[4,2,16,256]{3,2,1,0:T(8,128)}, f32[4,2,16,256]{3,2,1,0:T(8,128)S(1)}, u32[]{:S(2)}, u32[]{:S(2)}) collective-permute-start(f32[4,2,16,256]{3,2,1,0:T(8,128)} %get-tuple-element.60), channel_id=1, source_target_pairs={{0,24},{4,28},{8,16},{12,20},{16,8},{20,12},{24,0},{28,4},{1,25},{... | collective-permute-start | bytes 393224 | tf_op jit(solution)/shard_map/ppermute | solution.py:676
  38.1 18.9 %collective-permute-start.6 = (f32[4,2,16,256]{3,2,1,0:T(8,128)}, f32[4,2,16,256]{3,2,1,0:T(8,128)S(1)}, u32[]{:S(2)}, u32[]{:S(2)}) collective-permute-start(f32[4,2,16,256]{3,2,1,0:T(8,128)} %get-tuple-element.61), channel_id=1, source_target_pairs={{0,28},{4,24},{8,20},{12,16},{16,12},{20,8},{24,4},{28,0},{1,29},{... | collective-permute-start | bytes 393224 | tf_op jit(solution)/shard_map/ppermute | solution.py:676
  38.1 2.2 %copy-start = (f32[2,1024,512]{2,1,0:T(8,128)S(1)}, f32[2,1024,512]{2,1,0:T(8,128)}, u32[]{:S(2)}) copy-start(f32[2,1024,512]{2,1,0:T(8,128)} %filter_any) | copy-start | bytes 12582916
  40.3 16.8 %copy-start.1 = (f32[4,2,16,256]{3,2,1,0:T(8,128)S(1)}, f32[4,2,16,256]{3,2,1,0:T(8,128)}, u32[]{:S(2)}) copy-start(f32[4,2,16,256]{3,2,1,0:T(8,128)} %get-tuple-element.63.refs_0_) | copy-start | bytes 393220
  58.9 14.4 %collective-permute-start.7 = (f32[8,2,16,256]{3,2,1,0:T(8,128)S(1)}, f32[8,2,16,256]{3,2,1,0:T(8,128)S(1)}, u32[]{:S(2)}, u32[]{:S(2)}) collective-permute-start(f32[8,2,16,256]{3,2,1,0:T(8,128)S(1)} %get-tuple-element.72), channel_id=1, source_target_pairs={{0,1},{1,0},{2,3},{3,2},{4,5},{5,4},{6,7},{7,6},{8,9},{9,8},{10,11... | collective-permute-start | bytes 786440 | tf_op jit(solution)/shard_map/ppermute | solution.py:676
  60.8 39.7 %collective-permute-start.8 = (f32[8,2,16,256]{3,2,1,0:T(8,128)S(1)}, f32[8,2,16,256]{3,2,1,0:T(8,128)S(1)}, u32[]{:S(2)}, u32[]{:S(2)}) collective-permute-start(f32[8,2,16,256]{3,2,1,0:T(8,128)S(1)} %get-tuple-element.73), channel_id=1, source_target_pairs={{0,2},{1,3},{2,0},{3,1},{4,6},{5,7},{6,4},{7,5},{8,10},{9,11},{10,... | collective-permute-start | bytes 786440 | tf_op jit(solution)/shard_map/ppermute | solution.py:676
  61.5 46.2 %collective-permute-start.9 = (f32[8,2,16,256]{3,2,1,0:T(8,128)S(1)}, f32[8,2,16,256]{3,2,1,0:T(8,128)S(1)}, u32[]{:S(2)}, u32[]{:S(2)}) collective-permute-start(f32[8,2,16,256]{3,2,1,0:T(8,128)S(1)} %get-tuple-element.74), channel_id=1, source_target_pairs={{0,3},{1,2},{2,1},{3,0},{4,7},{5,6},{6,5},{7,4},{8,11},{9,10},{10,... | collective-permute-start | bytes 786440 | tf_op jit(solution)/shard_map/ppermute | solution.py:676
  113.4 11.4 %collective-permute-start.10 = (f32[8,2,2,1,256]{4,3,2,1,0:T(1,128)S(1)}, f32[8,2,2,1,256]{4,3,2,1,0:T(1,128)S(1)}, u32[]{:S(2)}, u32[]{:S(2)}) collective-permute-start(f32[8,2,2,1,256]{4,3,2,1,0:T(1,128)S(1)} %slice.3), channel_id=1, source_target_pairs={{4,0},{8,4},{12,8},{16,12},{20,16},{24,20},{28,24},{1,28},{5,1},{9... | collective-permute-start | bytes 98312 | tf_op jit(solution)/shard_map/ppermute | solution.py:752

commit v11 on v9

--- a/solution.py
+++ b/solution.py
@@ -408,18 +408,28 @@
     for move in tables[1:]:
         move.wait()
 
-    for d in range(RADIX):
+    each = epochs * rows
+    per = max(1, 1024 // each)
+    while RADIX % per:
+        per -= 1
+    for d in range(0, RADIX, per):
+        some = slice(d, d + per)
         spectrum = three_products(
-            y_high[d], y_low[d], table_high[...], table_low[...], ((1,), (0,))
+            y_high[some].reshape(per * each, 2 * lanes),
+            y_low[some].reshape(per * each, 2 * lanes),
+            table_high[...],
+            table_low[...],
+            ((1,), (0,)),
+        ).reshape(per, epochs, rows, 2 * lanes)
+        real, imag = spectrum[..., :lanes], spectrum[..., lanes:]
+        by_real, by_imag = filter_ref[0, some][:, None], filter_ref[1, some][:, None]
+        spectrum = jnp.concatenate(
+            [real * by_real - imag * by_imag, real * by_imag + imag * by_real], axis=3
         )
-        spectrum = spectrum.reshape(epochs, rows, 2 * lanes)
-        real, imag = spectrum[:, :, :lanes], spectrum[:, :, lanes:]
-        by_real, by_imag = filter_ref[0, d][None], filter_ref[1, d][None]
-        spectrum = jnp.concatenate(
-            [real * by_real - imag * by_imag, real * by_imag + imag * by_real], axis=2
-        )
-        high, low = two_parts(spectrum.reshape(epochs * rows, 2 * lanes))
-        z_ref[d] = three_products(high, low, table_high[...], table_low[...], ((1,), (1,)))
+        high, low = two_parts(spectrum.reshape(per * each, 2 * lanes))
+        z_ref[some] = three_products(
+            high, low, table_high[...], table_low[...], ((1,), (1,))
+        ).reshape(per, each, 2 * lanes)
 
     scene_ref[0] = jnp.zeros_like(scene_ref[0])
     scene_ref[1] = jnp.zeros_like(scene_ref[1])

time: 133 us -> 133 us (level)
  no operation moved by 1% of the time
where the time goes in v11:
time: 133 us; the launch traced here: 132 us
  waiting for transfers between devices  43.7 us (33%)
  Pallas kernels  34.1 us (26%)
  blocking collectives  30.6 us (23%)
  starting transfers between devices  20.1 us (15%)
  local copies, waits for them, and re-layouts  3.38 us (3%)
    all_to_all x1, waiting for transfers between devices, exchange_all(): lax.all_to_all(block, OWNERS, split_axis=0, concat_axis=0, tiled=True)  32.7 us
    all_gather x1, blocking collectives, all_weights(): lax.all_gather(inversion[:, 0, :] * usable[None, :], 'acq', axis=1, tiled...  17.9 us
    pallas_call x2, Pallas kernels, focus(): pl.pallas_call(kernel, out_shape=jax.ShapeDtypeStruct(shape, jnp.float32)...  16.2 us
    pallas_call x2, Pallas kernels, compress(): pl.pallas_call(functools.partial(compress_kernel, plan, relative), out_sh...  15.6 us
    all_to_all x1, blocking collectives, per_device(): lax.all_to_all(gradients, 'acq', split_axis=0, concat_axis=0, tiled=True)  12.7 us
    ppermute x10, starting transfers between devices, partners(): lax.ppermute(slot, axis, [(i, i ^ k) for i in range(size)])  11.4 us
    ppermute x10, waiting for transfers between devices, partners(): lax.ppermute(slot, axis, [(i, i ^ k) for i in range(size)])  9.33 us
    all_to_all x1, starting transfers between devices, exchange_all(): lax.all_to_all(block, OWNERS, split_axis=0, concat_axis=0, tiled=True)  7.42 us
  transfers between devices with their start and end apart: 12, of which 3 were waited for; matrix products, arithmetic and copies ran while one was open for 0% of the time, Pallas kernels for 13%

profile of v11, /device:TPU:0, one launch (start us, length us, event | category | flops | bytes accessed | tf_op | source)
XLA Modules:
  0.0 132.2 jit_solution(16159784756031017844)
XLA Ops:
  0.0 8.6 %range_compress.2 = f32[4,8,2,48,256]{4,3,2,1,0:T(8,128)} custom-call(f32[2,2048]{1,0:T(2,128)} %filter_ref.2, bf16[256,512]{1,0:T(8,128)(2,1)} %constant.24.clone.high_any, bf16[256,512]{1,0:T(8,128)(2,1)} %constant.25.clone.low_any, f32[4,8,256]{2,1,0:T(8,128)} %constant.26.clone.turn_any, f32[2,256,2048]{2,1,0:T(8,128)} %bitcast.8), custom_call_target="tpu_custom_call" | custom-call | flops 2415919104 | bytes 8388608 | tf_op jit(solution)/shard_map/range_compress/pallas_call | solution.py:298
  8.6 7.4 %all-to-all-start = ((f32[32,2,48,256]{3,2,1,0:T(8,128)}), f32[32,2,48,256]{3,2,1,0:T(8,128)}, u32[]{:S(2)}, u32[]{:S(2)}) async-start(f32[32,2,48,256]{3,2,1,0:T(8,128)} %bitcast.10), calls=%async_computation | async-start | bytes 6291456 | tf_op jit(solution)/shard_map/all_to_all | solution.py:674
  16.1 7.0 %range_compress.3 = (f32[4,2,16,256]{3,2,1,0:T(8,128)}, f32[4,2,16,256]{3,2,1,0:T(8,128)}, f32[4,2,16,256]{3,2,1,0:T(8,128)}, f32[4,2,16,256]{3,2,1,0:T(8,128)},...) custom-call(f32[2,2048]{1,0:T(2,128)} %filter_ref.2, ...), custom_call_target="tpu_custom_call" | custom-call | flops 805306368 | bytes 8388608 | tf_op jit(solution)/shard_map/range_compress/pallas_call | solution.py:298
  23.1 0.3 collective-permute-start
  23.4 1.7 %collective-permute-start.1 = (f32[4,2,16,256]{3,2,1,0:T(8,128)}, f32[4,2,16,256]{3,2,1,0:T(8,128)S(1)}, u32[]{:S(2)}, u32[]{:S(2)}) collective-permute-start(f32[4,2,16,256]{3,2,1,0:T(8,128)} %get-tuple-element.53), channel_id=1, source_target_pairs={{0,8},{4,12},{8,0},{12,4},{16,24},{20,28},{24,16},{28,20},{1,9},{5... | collective-permute-start | bytes 393224 | tf_op jit(solution)/shard_map/ppermute | solution.py:686
  25.0 1.7 %collective-permute-start.3 = (f32[4,2,16,256]{3,2,1,0:T(8,128)}, f32[4,2,16,256]{3,2,1,0:T(8,128)S(1)}, u32[]{:S(2)}, u32[]{:S(2)}) collective-permute-start(f32[4,2,16,256]{3,2,1,0:T(8,128)} %get-tuple-element.55), channel_id=1, source_target_pairs={{0,16},{4,20},{8,24},{12,28},{16,0},{20,4},{24,8},{28,12},{1,17},{... | collective-permute-start | bytes 393224 | tf_op jit(solution)/shard_map/ppermute | solution.py:686
  26.8 2.2 %copy-done = f32[2,1024,512]{2,1,0:T(8,128)S(1)} copy-done((f32[2,1024,512]{2,1,0:T(8,128)S(1)}, f32[2,1024,512]{2,1,0:T(8,128)}, u32[]{:S(2)}) %copy-start) | copy-done | bytes 4194328
  29.0 0.5 own_filter.1
  29.6 0.3 copy-done.10
  29.9 2.6 %collective-permute-start.5 = (f32[4,2,16,256]{3,2,1,0:T(8,128)S(1)}, f32[4,2,16,256]{3,2,1,0:T(8,128)S(1)}, u32[]{:S(2)}, u32[]{:S(2)}) collective-permute-start(f32[4,2,16,256]{3,2,1,0:T(8,128)S(1)} %copy-done.10), channel_id=1, source_target_pairs={{0,24},{4,28},{8,16},{12,20},{16,8},{20,12},{24,0},{28,4},{1,25},{... | collective-permute-start | bytes 393224 | tf_op jit(solution)/shard_map/ppermute | solution.py:686
  32.5 9.3 %collective-permute-done.1.refs_2_ = f32[4,2,16,256]{3,2,1,0:T(8,128)S(1)} collective-permute-done((f32[4,2,16,256]{3,2,1,0:T(8,128)}, f32[4,2,16,256]{3,2,1,0:T(8,128)S(1)}, u32[]{:S(2)}, u32[]{:S(2)}) %collective-permute-start.1) | collective-permute-done | bytes 131104 | tf_op jit(solution)/shard_map/ppermute | solution.py:686
  41.8 0.6 collective-permute-start.6
  42.5 17.9 %all_gather.4 = f32[8,8,2]{0,2,1:T(2,128)S(1)} all-gather(f32[8,1,2]{0,2,1:T(2,128)S(1)} %broadcast_multiply_fusion), channel_id=1, replica_groups=mesh['acq'=8,'strip'=4] {'acq'}, dimensions={1}, use_global_device_ids=true | all-gather | bytes 576 | tf_op jit(solution)/shard_map/all_gather | solution.py:734
  60.5 1.8 %regroup.1 = (f32[8,2,16,256]{3,2,1,0:T(8,128)S(1)}, f32[8,2,16,256]{3,2,1,0:T(8,128)S(1)}, f32[8,2,16,256]{3,2,1,0:T(8,128)S(1)}, f32[8,2,16,256]{3,2,1,0:T(8,128)S(1)}) custom-call(f32[4,2,16,256]{3,2,1,0:T(8,128)S(1)} %copy-done.1, f32[4,2,16,256]{3,2,1,0:T(8,128)S(1)} %collective-permute-done.refs_1_, ...), custom_call_target="tpu_custom_call" | custom-call | bytes 1024 | tf_op jit(solution)/shard_map/regroup/pallas_call | solution.py:715
  62.3 0.5 collective-permute-start.7
  62.8 3.2 %collective-permute-start.8 = (f32[8,2,16,256]{3,2,1,0:T(8,128)S(1)}, f32[8,2,16,256]{3,2,1,0:T(8,128)S(1)}, u32[]{:S(2)}, u32[]{:S(2)}) collective-permute-start(f32[8,2,16,256]{3,2,1,0:T(8,128)S(1)} %get-tuple-element.73), channel_id=1, source_target_pairs={{0,2},{1,3},{2,0},{3,1},{4,6},{5,7},{6,4},{7,5},{8,10},{9,11},{10,... | collective-permute-start | bytes 786440 | tf_op jit(solution)/shard_map/ppermute | solution.py:686
  66.0 0.7 collective-permute-start.9
  66.8 32.7 %all-to-all-done = f32[32,2,48,256]{3,2,1,0:T(8,128)} async-done(((f32[32,2,48,256]{3,2,1,0:T(8,128)}), f32[32,2,48,256]{3,2,1,0:T(8,128)}, u32[]{:S(2)}, u32[]{:S(2)}) %all-to-all-start) | async-done | bytes 3145760 | tf_op jit(solution)/shard_map/all_to_all | solution.py:674
  99.5 8.4 %azimuth_focus.2.refs_10_ = f32[8,2,2,16,256]{4,3,2,1,0:T(8,128)S(1)} custom-call(f32[4,8,2,48,256]{4,3,2,1,0:T(8,128)} %bitcast.4.refs_0_, f32[2,8,48,128]{3,2,1,0:T(8,128)S(1)} %get-tuple-element.78.refs_1_, bf16[256,256]{1,0:T(8,128)(2,1)S(1)} %copy-done.4, bf16[256,256]{1,0:T(8,128)(2,1)S(1)} %copy-done.3, f32[4,8,128]{2,1,0:T(8,128)S(1)} %copy-done.5, ...), custom_call_target="tpu_custom_call" | custom-call | flops 2415919104 | bytes 7340032 | tf_op jit(solution)/shard_map/azimuth_focus/pallas_call | solution.py:583
  107.9 1.3 collective-permute-start.10
  109.3 1.7 %collective-permute-done.10.refs_11_ = f32[8,2,2,1,256]{4,3,2,1,0:T(1,128)S(1)} collective-permute-done((f32[8,2,2,1,256]{4,3,2,1,0:T(1,128)S(1)}, f32[8,2,2,1,256]{4,3,2,1,0:T(1,128)S(1)}, u32[]{:S(2)}, u32[]{:S(2)}) %collective-permute-start.10) | collective-permute-done | bytes 32800 | tf_op jit(solution)/shard_map/ppermute | solution.py:765
  111.0 7.8 %azimuth_focus.3 = f32[8,2,16,256]{3,2,1,0:T(8,128)S(1)} custom-call(f32[8,2,16,256]{3,2,1,0:T(8,128)S(1)} %get-tuple-element.71.refs_0_, f32[8,2,16,256]{3,2,1,0:T(8,128)S(1)} %collective-permute-done.7.refs_1_, f32[8,2,16,256]{3,2,1,0:T(8,128)S(1)} %collective-permute-done.8.refs_2_, f32[8,2,16,256]{3,2,1,0:T(8,128)S(1)} %collective-permute-done.9.refs_3_, ...), custom_call_target="tpu_custom_call" | custom-call | flops 805306368 | bytes 5242880 | tf_op jit(solution)/shard_map/azimuth_focus/pallas_call | solution.py:583
  118.8 12.7 %all_to_all.10 = f32[8,2,16,256]{3,2,1,0:T(8,128)S(1)} all-to-all(f32[8,2,16,256]{3,2,1,0:T(8,128)S(1)} %azimuth_focus.3), channel_id=1, replica_groups=mesh['acq'=8,'strip'=4] {'acq'}, dimensions={0} | all-to-all | bytes 524288 | tf_op jit(solution)/shard_map/all_to_all | solution.py:774
  131.5 0.7 copy.25
  (35 shorter events, 0.4 us)
Async XLA Ops:
  8.6 90.8 %all-to-all-start = ((f32[32,2,48,256]{3,2,1,0:T(8,128)}), f32[32,2,48,256]{3,2,1,0:T(8,128)}, u32[]{:S(2)}, u32[]{:S(2)}) async-start(f32[32,2,48,256]{3,2,1,0:T(8,128)} %bitcast.10), calls=%async_computation | async-start | bytes 6291456 | tf_op jit(solution)/shard_map/all_to_all | solution.py:674
  16.0 13.5 %copy-start.7 = (s32[1,2]{1,0:T(1,128)S(1)}, s32[1,2]{1,0:T(1,128)}, u32[]{:S(2)}) copy-start(s32[1,2]{1,0:T(1,128)} %param.23) | copy-start | bytes 28
  16.1 13.5 %copy-start.8 = (s32[2]{0:T(128)S(1)}, s32[2]{0:T(128)}, u32[]{:S(2)}) copy-start(s32[2]{0:T(128)} %constant.27.clone) | copy-start | bytes 28
  16.1 26.4 %copy-start.6 = (f32[8,1,2]{0,2,1:T(2,128)S(1)}, f32[8,1,2]{0,2,1:T(2,128)}, u32[]{:S(2)}) copy-start(f32[8,1,2]{0,2,1:T(2,128)} %param.24) | copy-start | bytes 196
  16.1 83.4 %copy-start.2 = (bf16[512,128]{1,0:T(8,128)(2,1)S(1)}, bf16[512,128]{1,0:T(8,128)(2,1)}, u32[]{:S(2)}) copy-start(bf16[512,128]{1,0:T(8,128)(2,1)} %constant.31.clone.refs_5_.refs_8_) | copy-start | bytes 393220
  16.1 83.4 %copy-start.3 = (bf16[256,256]{1,0:T(8,128)(2,1)S(1)}, bf16[256,256]{1,0:T(8,128)(2,1)}, u32[]{:S(2)}) copy-start(bf16[256,256]{1,0:T(8,128)(2,1)} %constant.29.clone.refs_3_.refs_6_) | copy-start | bytes 393220
  16.1 83.3 %copy-start.4 = (bf16[256,256]{1,0:T(8,128)(2,1)S(1)}, bf16[256,256]{1,0:T(8,128)(2,1)}, u32[]{:S(2)}) copy-start(bf16[256,256]{1,0:T(8,128)(2,1)} %constant.28.clone.refs_2_.refs_5_) | copy-start | bytes 393220
  16.1 83.3 %copy-start.5 = (f32[4,8,128]{2,1,0:T(8,128)S(1)}, f32[4,8,128]{2,1,0:T(8,128)}, u32[]{:S(2)}) copy-start(f32[4,8,128]{2,1,0:T(8,128)} %constant.30.clone.refs_4_.refs_7_) | copy-start | bytes 49156
  23.1 6.5 %collective-permute-start = (f32[4,2,16,256]{3,2,1,0:T(8,128)}, f32[4,2,16,256]{3,2,1,0:T(8,128)S(1)}, u32[]{:S(2)}, u32[]{:S(2)}) collective-permute-start(f32[4,2,16,256]{3,2,1,0:T(8,128)} %get-tuple-element.52), channel_id=1, source_target_pairs={{0,4},{4,0},{8,12},{12,8},{16,20},{20,16},{24,28},{28,24},{1,5},{5... | collective-permute-start | bytes 393224 | tf_op jit(solution)/shard_map/ppermute | solution.py:686
  23.4 18.5 %collective-permute-start.1 = (f32[4,2,16,256]{3,2,1,0:T(8,128)}, f32[4,2,16,256]{3,2,1,0:T(8,128)S(1)}, u32[]{:S(2)}, u32[]{:S(2)}) collective-permute-start(f32[4,2,16,256]{3,2,1,0:T(8,128)} %get-tuple-element.53), channel_id=1, source_target_pairs={{0,8},{4,12},{8,0},{12,4},{16,24},{20,28},{24,16},{28,20},{1,9},{5... | collective-permute-start | bytes 393224 | tf_op jit(solution)/shard_map/ppermute | solution.py:686
  25.0 35.4 %collective-permute-start.2 = (f32[4,2,16,256]{3,2,1,0:T(8,128)}, f32[4,2,16,256]{3,2,1,0:T(8,128)S(1)}, u32[]{:S(2)}, u32[]{:S(2)}) collective-permute-start(f32[4,2,16,256]{3,2,1,0:T(8,128)} %get-tuple-element.54), channel_id=1, source_target_pairs={{0,12},{4,8},{8,4},{12,0},{16,28},{20,24},{24,20},{28,16},{1,13},{... | collective-permute-start | bytes 393224 | tf_op jit(solution)/shard_map/ppermute | solution.py:686
  25.0 35.4 %collective-permute-start.3 = (f32[4,2,16,256]{3,2,1,0:T(8,128)}, f32[4,2,16,256]{3,2,1,0:T(8,128)S(1)}, u32[]{:S(2)}, u32[]{:S(2)}) collective-permute-start(f32[4,2,16,256]{3,2,1,0:T(8,128)} %get-tuple-element.55), channel_id=1, source_target_pairs={{0,16},{4,20},{8,24},{12,28},{16,0},{20,4},{24,8},{28,12},{1,17},{... | collective-permute-start | bytes 393224 | tf_op jit(solution)/shard_map/ppermute | solution.py:686
  26.7 33.7 %collective-permute-start.4 = (f32[4,2,16,256]{3,2,1,0:T(8,128)}, f32[4,2,16,256]{3,2,1,0:T(8,128)S(1)}, u32[]{:S(2)}, u32[]{:S(2)}) collective-permute-start(f32[4,2,16,256]{3,2,1,0:T(8,128)} %get-tuple-element.56), channel_id=1, source_target_pairs={{0,20},{4,16},{8,28},{12,24},{16,4},{20,0},{24,12},{28,8},{1,21},{... | collective-permute-start | bytes 393224 | tf_op jit(solution)/shard_map/ppermute | solution.py:686
  26.8 2.2 %copy-start = (f32[2,1024,512]{2,1,0:T(8,128)S(1)}, f32[2,1024,512]{2,1,0:T(8,128)}, u32[]{:S(2)}) copy-start(f32[2,1024,512]{2,1,0:T(8,128)} %filter_any) | copy-start | bytes 12582916
  29.0 0.9 copy-start.10
  29.0 12.8 %copy-start.9 = (f32[4,2,16,256]{3,2,1,0:T(8,128)S(1)}, f32[4,2,16,256]{3,2,1,0:T(8,128)}, u32[]{:S(2)}) copy-start(f32[4,2,16,256]{3,2,1,0:T(8,128)} %get-tuple-element.58) | copy-start | bytes 393220
  29.0 31.4 %copy-start.1 = (f32[4,2,16,256]{3,2,1,0:T(8,128)S(1)}, f32[4,2,16,256]{3,2,1,0:T(8,128)}, u32[]{:S(2)}) copy-start(f32[4,2,16,256]{3,2,1,0:T(8,128)} %get-tuple-element.63.refs_0_) | copy-start | bytes 393220
  29.9 30.5 %collective-permute-start.5 = (f32[4,2,16,256]{3,2,1,0:T(8,128)S(1)}, f32[4,2,16,256]{3,2,1,0:T(8,128)S(1)}, u32[]{:S(2)}, u32[]{:S(2)}) collective-permute-start(f32[4,2,16,256]{3,2,1,0:T(8,128)S(1)} %copy-done.10), channel_id=1, source_target_pairs={{0,24},{4,28},{8,16},{12,20},{16,8},{20,12},{24,0},{28,4},{1,25},{... | collective-permute-start | bytes 393224 | tf_op jit(solution)/shard_map/ppermute | solution.py:686
  41.8 18.6 %collective-permute-start.6 = (f32[4,2,16,256]{3,2,1,0:T(8,128)S(1)}, f32[4,2,16,256]{3,2,1,0:T(8,128)S(1)}, u32[]{:S(2)}, u32[]{:S(2)}) collective-permute-start(f32[4,2,16,256]{3,2,1,0:T(8,128)S(1)} %copy-done.9), channel_id=1, source_target_pairs={{0,28},{4,24},{8,20},{12,16},{16,12},{20,8},{24,4},{28,0},{1,29},{... | collective-permute-start | bytes 393224 | tf_op jit(solution)/shard_map/ppermute | solution.py:686
  62.3 47.0 %collective-permute-start.7 = (f32[8,2,16,256]{3,2,1,0:T(8,128)S(1)}, f32[8,2,16,256]{3,2,1,0:T(8,128)S(1)}, u32[]{:S(2)}, u32[]{:S(2)}) collective-permute-start(f32[8,2,16,256]{3,2,1,0:T(8,128)S(1)} %get-tuple-element.72), channel_id=1, source_target_pairs={{0,1},{1,0},{2,3},{3,2},{4,5},{5,4},{6,7},{7,6},{8,9},{9,8},{10,11... | collective-permute-start | bytes 786440 | tf_op jit(solution)/shard_map/ppermute | solution.py:686
  62.8 46.5 %collective-permute-start.8 = (f32[8,2,16,256]{3,2,1,0:T(8,128)S(1)}, f32[8,2,16,256]{3,2,1,0:T(8,128)S(1)}, u32[]{:S(2)}, u32[]{:S(2)}) collective-permute-start(f32[8,2,16,256]{3,2,1,0:T(8,128)S(1)} %get-tuple-element.73), channel_id=1, source_target_pairs={{0,2},{1,3},{2,0},{3,1},{4,6},{5,7},{6,4},{7,5},{8,10},{9,11},{10,... | collective-permute-start | bytes 786440 | tf_op jit(solution)/shard_map/ppermute | solution.py:686
  66.0 43.2 %collective-permute-start.9 = (f32[8,2,16,256]{3,2,1,0:T(8,128)S(1)}, f32[8,2,16,256]{3,2,1,0:T(8,128)S(1)}, u32[]{:S(2)}, u32[]{:S(2)}) collective-permute-start(f32[8,2,16,256]{3,2,1,0:T(8,128)S(1)} %get-tuple-element.74), channel_id=1, source_target_pairs={{0,3},{1,2},{2,1},{3,0},{4,7},{5,6},{6,5},{7,4},{8,11},{9,10},{10,... | collective-permute-start | bytes 786440 | tf_op jit(solution)/shard_map/ppermute | solution.py:686
  107.9 3.1 %collective-permute-start.10 = (f32[8,2,2,1,256]{4,3,2,1,0:T(1,128)S(1)}, f32[8,2,2,1,256]{4,3,2,1,0:T(1,128)S(1)}, u32[]{:S(2)}, u32[]{:S(2)}) collective-permute-start(f32[8,2,2,1,256]{4,3,2,1,0:T(1,128)S(1)} %slice.4), channel_id=1, source_target_pairs={{4,0},{8,4},{12,8},{16,12},{20,16},{24,20},{28,24},{1,28},{5,1},{9... | collective-permute-start | bytes 98312 | tf_op jit(solution)/shard_map/ppermute | solution.py:765

commit v12 on v9

--- a/solution.py
+++ b/solution.py
@@ -669,10 +669,10 @@
     return received.reshape(plan.strips // join, plan.epochs, 2, plan.rows, join * plan.pulses)
 
 
-def partners(slots, axis):
+def partners(slots, axis, first=0):
     size = lax.axis_size(axis)
     moved = []
-    for k, slot in enumerate(slots):
+    for k, slot in enumerate(slots, first):
         moved.append(slot if k == 0 else lax.ppermute(slot, axis, [(i, i ^ k) for i in range(size)]))
     return moved
 
@@ -743,7 +743,10 @@
         field = exchange_all(big, block)
         other = partners(other, "acq")
         *other, spectrum, weights = lax.optimization_barrier((*other, spectrum, weights))
-        other = partners(regroup(other), "strip")
+        other = list(regroup(other))
+        near = partners(other[:2], "strip")
+        near[1], *far = lax.optimization_barrier((near[1], *other[2:]))
+        other = near + partners(far, "strip", 2)
     else:
         weights = all_weights(pair_mask, inversion)
         spectrum = own_filter(plan, azimuth_filter)

time: 133 us -> 133 us (level)
    ppermute x10, waiting for transfers between devices: 9.33 us -> 21.8 us  [partners(): lax.ppermute(slot, axis, [(i, i ^ k) for i in range(size)])]
    all_to_all x1, waiting for transfers between devices: 32.7 us -> 21.1 us  [exchange_all(): lax.all_to_all(block, OWNERS, split_axis=0, concat_axis=0, tiled=True)]
  transfers between devices with their start and end apart: 12 -> 12, of which waited for: 3 -> 4; matrix products, arithmetic and copies ran while one was open for 0% -> 0% of each run, Pallas kernels for 13% -> 13%
where the time goes in v12:
time: 133 us; the launch traced here: 132 us
  waiting for transfers between devices  44.7 us (34%)
  Pallas kernels  34.1 us (26%)
  blocking collectives  30.6 us (23%)
  starting transfers between devices  19.2 us (14%)
  local copies, waits for them, and re-layouts  3.38 us (3%)
    ppermute x10, waiting for transfers between devices, partners(): lax.ppermute(slot, axis, [(i, i ^ k) for i in range(size)])  21.8 us
    all_to_all x1, waiting for transfers between devices, exchange_all(): lax.all_to_all(block, OWNERS, split_axis=0, concat_axis=0, tiled=True)  21.1 us
    all_gather x1, blocking collectives, all_weights(): lax.all_gather(inversion[:, 0, :] * usable[None, :], 'acq', axis=1, tiled...  17.9 us
    pallas_call x2, Pallas kernels, focus(): pl.pallas_call(kernel, out_shape=jax.ShapeDtypeStruct(shape, jnp.float32)...  16.2 us
    pallas_call x2, Pallas kernels, compress(): pl.pallas_call(functools.partial(compress_kernel, plan, relative), out_sh...  15.6 us
    all_to_all x1, blocking collectives, per_device(): lax.all_to_all(gradients, 'acq', split_axis=0, concat_axis=0, tiled=True)  12.7 us
    ppermute x10, starting transfers between devices, partners(): lax.ppermute(slot, axis, [(i, i ^ k) for i in range(size)])  10.5 us
    all_to_all x1, starting transfers between devices, exchange_all(): lax.all_to_all(block, OWNERS, split_axis=0, concat_axis=0, tiled=True)  7.42 us
  transfers between devices with their start and end apart: 12, of which 4 were waited for; matrix products, arithmetic and copies ran while one was open for 0% of the time, Pallas kernels for 13%

profile of v12, /device:TPU:0, one launch (start us, length us, event | category | flops | bytes accessed | tf_op | source)
XLA Modules:
  0.0 132.2 jit_solution(12157100942038464867)
XLA Ops:
  0.0 8.6 %range_compress.2 = f32[4,8,2,48,256]{4,3,2,1,0:T(8,128)} custom-call(f32[2,2048]{1,0:T(2,128)} %filter_ref.2, bf16[256,512]{1,0:T(8,128)(2,1)} %constant.24.clone.high_any, bf16[256,512]{1,0:T(8,128)(2,1)} %constant.25.clone.low_any, f32[4,8,256]{2,1,0:T(8,128)} %constant.26.clone.turn_any, f32[2,256,2048]{2,1,0:T(8,128)} %bitcast.8), custom_call_target="tpu_custom_call" | custom-call | flops 2415919104 | bytes 8388608 | tf_op jit(solution)/shard_map/range_compress/pallas_call | solution.py:298
  8.6 7.4 %all-to-all-start = ((f32[32,2,48,256]{3,2,1,0:T(8,128)}), f32[32,2,48,256]{3,2,1,0:T(8,128)}, u32[]{:S(2)}, u32[]{:S(2)}) async-start(f32[32,2,48,256]{3,2,1,0:T(8,128)} %bitcast.10), calls=%async_computation | async-start | bytes 6291456 | tf_op jit(solution)/shard_map/all_to_all | solution.py:664
  16.1 7.0 %range_compress.3 = (f32[4,2,16,256]{3,2,1,0:T(8,128)}, f32[4,2,16,256]{3,2,1,0:T(8,128)}, f32[4,2,16,256]{3,2,1,0:T(8,128)}, f32[4,2,16,256]{3,2,1,0:T(8,128)},...) custom-call(f32[2,2048]{1,0:T(2,128)} %filter_ref.2, ...), custom_call_target="tpu_custom_call" | custom-call | flops 805306368 | bytes 8388608 | tf_op jit(solution)/shard_map/range_compress/pallas_call | solution.py:298
  23.4 1.7 %collective-permute-start.1 = (f32[4,2,16,256]{3,2,1,0:T(8,128)}, f32[4,2,16,256]{3,2,1,0:T(8,128)S(1)}, u32[]{:S(2)}, u32[]{:S(2)}) collective-permute-start(f32[4,2,16,256]{3,2,1,0:T(8,128)} %get-tuple-element.56), channel_id=1, source_target_pairs={{0,8},{4,12},{8,0},{12,4},{16,24},{20,28},{24,16},{28,20},{1,9},{5... | collective-permute-start | bytes 393224 | tf_op jit(solution)/shard_map/ppermute | solution.py:676
  25.0 1.7 %collective-permute-start.3 = (f32[4,2,16,256]{3,2,1,0:T(8,128)}, f32[4,2,16,256]{3,2,1,0:T(8,128)S(1)}, u32[]{:S(2)}, u32[]{:S(2)}) collective-permute-start(f32[4,2,16,256]{3,2,1,0:T(8,128)} %get-tuple-element.58), channel_id=1, source_target_pairs={{0,16},{4,20},{8,24},{12,28},{16,0},{20,4},{24,8},{28,12},{1,17},{... | collective-permute-start | bytes 393224 | tf_op jit(solution)/shard_map/ppermute | solution.py:676
  26.8 2.2 %copy-done = f32[2,1024,512]{2,1,0:T(8,128)S(1)} copy-done((f32[2,1024,512]{2,1,0:T(8,128)S(1)}, f32[2,1024,512]{2,1,0:T(8,128)}, u32[]{:S(2)}) %copy-start) | copy-done | bytes 4194328
  29.0 0.5 own_filter.1
  29.6 0.3 copy-done.10
  29.9 2.6 %collective-permute-start.5 = (f32[4,2,16,256]{3,2,1,0:T(8,128)S(1)}, f32[4,2,16,256]{3,2,1,0:T(8,128)S(1)}, u32[]{:S(2)}, u32[]{:S(2)}) collective-permute-start(f32[4,2,16,256]{3,2,1,0:T(8,128)S(1)} %copy-done.10), channel_id=1, source_target_pairs={{0,24},{4,28},{8,16},{12,20},{16,8},{20,12},{24,0},{28,4},{1,25},{... | collective-permute-start | bytes 393224 | tf_op jit(solution)/shard_map/ppermute | solution.py:676
  32.5 9.3 %collective-permute-done.1.refs_2_ = f32[4,2,16,256]{3,2,1,0:T(8,128)S(1)} collective-permute-done((f32[4,2,16,256]{3,2,1,0:T(8,128)}, f32[4,2,16,256]{3,2,1,0:T(8,128)S(1)}, u32[]{:S(2)}, u32[]{:S(2)}) %collective-permute-start.1) | collective-permute-done | bytes 131104 | tf_op jit(solution)/shard_map/ppermute | solution.py:676
  41.8 0.6 collective-permute-start.6
  42.5 17.9 %all_gather.4 = f32[8,8,2]{0,2,1:T(2,128)S(1)} all-gather(f32[8,1,2]{0,2,1:T(2,128)S(1)} %broadcast_multiply_fusion), channel_id=1, replica_groups=mesh['acq'=8,'strip'=4] {'acq'}, dimensions={1}, use_global_device_ids=true | all-gather | bytes 576 | tf_op jit(solution)/shard_map/all_gather | solution.py:724
  60.5 1.8 %regroup.1 = (f32[8,2,16,256]{3,2,1,0:T(8,128)S(1)}, f32[8,2,16,256]{3,2,1,0:T(8,128)S(1)}, f32[8,2,16,256]{3,2,1,0:T(8,128)S(1)}, f32[8,2,16,256]{3,2,1,0:T(8,128)S(1)}) custom-call(f32[4,2,16,256]{3,2,1,0:T(8,128)S(1)} %copy-done.1, f32[4,2,16,256]{3,2,1,0:T(8,128)S(1)} %collective-permute-done.refs_1_, ...), custom_call_target="tpu_custom_call" | custom-call | bytes 1024 | tf_op jit(solution)/shard_map/regroup/pallas_call | solution.py:705
  62.3 0.5 collective-permute-start.7
  62.8 12.5 %collective-permute-done.7.refs_1_ = f32[8,2,16,256]{3,2,1,0:T(8,128)S(1)} collective-permute-done((f32[8,2,16,256]{3,2,1,0:T(8,128)S(1)}, f32[8,2,16,256]{3,2,1,0:T(8,128)S(1)}, u32[]{:S(2)}, u32[]{:S(2)}) %collective-permute-start.7) | collective-permute-done | bytes 262176 | tf_op jit(solution)/shard_map/ppermute | solution.py:676
  75.3 2.5 %collective-permute-start.8 = (f32[8,2,16,256]{3,2,1,0:T(8,128)S(1)}, f32[8,2,16,256]{3,2,1,0:T(8,128)S(1)}, u32[]{:S(2)}, u32[]{:S(2)}) collective-permute-start(f32[8,2,16,256]{3,2,1,0:T(8,128)S(1)} %get-tuple-element.79), channel_id=1, source_target_pairs={{0,2},{1,3},{2,0},{3,1},{4,6},{5,7},{6,4},{7,5},{8,10},{9,11},{10,... | collective-permute-start | bytes 786440 | tf_op jit(solution)/shard_map/ppermute | solution.py:676
  77.8 0.5 collective-permute-start.9
  78.3 21.1 %all-to-all-done = f32[32,2,48,256]{3,2,1,0:T(8,128)} async-done(((f32[32,2,48,256]{3,2,1,0:T(8,128)}), f32[32,2,48,256]{3,2,1,0:T(8,128)}, u32[]{:S(2)}, u32[]{:S(2)}) %all-to-all-start) | async-done | bytes 3145760 | tf_op jit(solution)/shard_map/all_to_all | solution.py:664
  99.5 8.2 %azimuth_focus.2.refs_10_ = f32[8,2,2,16,256]{4,3,2,1,0:T(8,128)S(1)} custom-call(f32[4,8,2,48,256]{4,3,2,1,0:T(8,128)} %bitcast.4.refs_0_, f32[2,8,48,128]{3,2,1,0:T(8,128)S(1)} %get-tuple-element.84.refs_1_, bf16[256,256]{1,0:T(8,128)(2,1)S(1)} %copy-done.4, bf16[256,256]{1,0:T(8,128)(2,1)S(1)} %copy-done.3, f32[4,8,128]{2,1,0:T(8,128)S(1)} %copy-done.5, ...), custom_call_target="tpu_custom_call" | custom-call | flops 2415919104 | bytes 7340032 | tf_op jit(solution)/shard_map/azimuth_focus/pallas_call | solution.py:573
  107.7 1.3 collective-permute-start.10
  109.1 1.7 %collective-permute-done.10.refs_11_ = f32[8,2,2,1,256]{4,3,2,1,0:T(1,128)S(1)} collective-permute-done((f32[8,2,2,1,256]{4,3,2,1,0:T(1,128)S(1)}, f32[8,2,2,1,256]{4,3,2,1,0:T(1,128)S(1)}, u32[]{:S(2)}, u32[]{:S(2)}) %collective-permute-start.10) | collective-permute-done | bytes 32800 | tf_op jit(solution)/shard_map/ppermute | solution.py:758
  110.8 8.0 %azimuth_focus.3 = f32[8,2,16,256]{3,2,1,0:T(8,128)S(1)} custom-call(f32[8,2,16,256]{3,2,1,0:T(8,128)S(1)} %get-tuple-element.74.refs_0_, f32[8,2,16,256]{3,2,1,0:T(8,128)S(1)} %collective-permute-done.7.refs_1_, f32[8,2,16,256]{3,2,1,0:T(8,128)S(1)} %collective-permute-done.8.refs_2_, f32[8,2,16,256]{3,2,1,0:T(8,128)S(1)} %collective-permute-done.9.refs_3_, ...), custom_call_target="tpu_custom_call" | custom-call | flops 805306368 | bytes 5242880 | tf_op jit(solution)/shard_map/azimuth_focus/pallas_call | solution.py:573
  118.8 12.7 %all_to_all.10 = f32[8,2,16,256]{3,2,1,0:T(8,128)S(1)} all-to-all(f32[8,2,16,256]{3,2,1,0:T(8,128)S(1)} %azimuth_focus.3), channel_id=1, replica_groups=mesh['acq'=8,'strip'=4] {'acq'}, dimensions={0} | all-to-all | bytes 524288 | tf_op jit(solution)/shard_map/all_to_all | solution.py:767
  131.5 0.7 copy.25
  (35 shorter events, 0.6 us)
Async XLA Ops:
  8.6 90.8 %all-to-all-start = ((f32[32,2,48,256]{3,2,1,0:T(8,128)}), f32[32,2,48,256]{3,2,1,0:T(8,128)}, u32[]{:S(2)}, u32[]{:S(2)}) async-start(f32[32,2,48,256]{3,2,1,0:T(8,128)} %bitcast.10), calls=%async_computation | async-start | bytes 6291456 | tf_op jit(solution)/shard_map/all_to_all | solution.py:664
  16.0 13.5 %copy-start.7 = (s32[1,2]{1,0:T(1,128)S(1)}, s32[1,2]{1,0:T(1,128)}, u32[]{:S(2)}) copy-start(s32[1,2]{1,0:T(1,128)} %param.23) | copy-start | bytes 28
  16.1 13.5 %copy-start.8 = (s32[2]{0:T(128)S(1)}, s32[2]{0:T(128)}, u32[]{:S(2)}) copy-start(s32[2]{0:T(128)} %constant.27.clone) | copy-start | bytes 28
  16.1 26.4 %copy-start.6 = (f32[8,1,2]{0,2,1:T(2,128)S(1)}, f32[8,1,2]{0,2,1:T(2,128)}, u32[]{:S(2)}) copy-start(f32[8,1,2]{0,2,1:T(2,128)} %param.24) | copy-start | bytes 196
  16.1 83.4 %copy-start.2 = (bf16[512,128]{1,0:T(8,128)(2,1)S(1)}, bf16[512,128]{1,0:T(8,128)(2,1)}, u32[]{:S(2)}) copy-start(bf16[512,128]{1,0:T(8,128)(2,1)} %constant.31.clone.refs_5_.refs_8_) | copy-start | bytes 393220
  16.1 83.4 %copy-start.3 = (bf16[256,256]{1,0:T(8,128)(2,1)S(1)}, bf16[256,256]{1,0:T(8,128)(2,1)}, u32[]{:S(2)}) copy-start(bf16[256,256]{1,0:T(8,128)(2,1)} %constant.29.clone.refs_3_.refs_6_) | copy-start | bytes 393220
  16.1 83.3 %copy-start.4 = (bf16[256,256]{1,0:T(8,128)(2,1)S(1)}, bf16[256,256]{1,0:T(8,128)(2,1)}, u32[]{:S(2)}) copy-start(bf16[256,256]{1,0:T(8,128)(2,1)} %constant.28.clone.refs_2_.refs_5_) | copy-start | bytes 393220
  16.1 83.3 %copy-start.5 = (f32[4,8,128]{2,1,0:T(8,128)S(1)}, f32[4,8,128]{2,1,0:T(8,128)}, u32[]{:S(2)}) copy-start(f32[4,8,128]{2,1,0:T(8,128)} %constant.30.clone.refs_4_.refs_7_) | copy-start | bytes 49156
  23.1 6.5 %collective-permute-start = (f32[4,2,16,256]{3,2,1,0:T(8,128)}, f32[4,2,16,256]{3,2,1,0:T(8,128)S(1)}, u32[]{:S(2)}, u32[]{:S(2)}) collective-permute-start(f32[4,2,16,256]{3,2,1,0:T(8,128)} %get-tuple-element.55), channel_id=1, source_target_pairs={{0,4},{4,0},{8,12},{12,8},{16,20},{20,16},{24,28},{28,24},{1,5},{5... | collective-permute-start | bytes 393224 | tf_op jit(solution)/shard_map/ppermute | solution.py:676
  23.4 18.5 %collective-permute-start.1 = (f32[4,2,16,256]{3,2,1,0:T(8,128)}, f32[4,2,16,256]{3,2,1,0:T(8,128)S(1)}, u32[]{:S(2)}, u32[]{:S(2)}) collective-permute-start(f32[4,2,16,256]{3,2,1,0:T(8,128)} %get-tuple-element.56), channel_id=1, source_target_pairs={{0,8},{4,12},{8,0},{12,4},{16,24},{20,28},{24,16},{28,20},{1,9},{5... | collective-permute-start | bytes 393224 | tf_op jit(solution)/shard_map/ppermute | solution.py:676
  25.0 35.4 %collective-permute-start.2 = (f32[4,2,16,256]{3,2,1,0:T(8,128)}, f32[4,2,16,256]{3,2,1,0:T(8,128)S(1)}, u32[]{:S(2)}, u32[]{:S(2)}) collective-permute-start(f32[4,2,16,256]{3,2,1,0:T(8,128)} %get-tuple-element.57), channel_id=1, source_target_pairs={{0,12},{4,8},{8,4},{12,0},{16,28},{20,24},{24,20},{28,16},{1,13},{... | collective-permute-start | bytes 393224 | tf_op jit(solution)/shard_map/ppermute | solution.py:676
  25.0 35.4 %collective-permute-start.3 = (f32[4,2,16,256]{3,2,1,0:T(8,128)}, f32[4,2,16,256]{3,2,1,0:T(8,128)S(1)}, u32[]{:S(2)}, u32[]{:S(2)}) collective-permute-start(f32[4,2,16,256]{3,2,1,0:T(8,128)} %get-tuple-element.58), channel_id=1, source_target_pairs={{0,16},{4,20},{8,24},{12,28},{16,0},{20,4},{24,8},{28,12},{1,17},{... | collective-permute-start | bytes 393224 | tf_op jit(solution)/shard_map/ppermute | solution.py:676
  26.7 33.7 %collective-permute-start.4 = (f32[4,2,16,256]{3,2,1,0:T(8,128)}, f32[4,2,16,256]{3,2,1,0:T(8,128)S(1)}, u32[]{:S(2)}, u32[]{:S(2)}) collective-permute-start(f32[4,2,16,256]{3,2,1,0:T(8,128)} %get-tuple-element.59), channel_id=1, source_target_pairs={{0,20},{4,16},{8,28},{12,24},{16,4},{20,0},{24,12},{28,8},{1,21},{... | collective-permute-start | bytes 393224 | tf_op jit(solution)/shard_map/ppermute | solution.py:676
  26.8 2.2 %copy-start = (f32[2,1024,512]{2,1,0:T(8,128)S(1)}, f32[2,1024,512]{2,1,0:T(8,128)}, u32[]{:S(2)}) copy-start(f32[2,1024,512]{2,1,0:T(8,128)} %filter_any) | copy-start | bytes 12582916
  29.0 0.9 copy-start.10
  29.0 12.8 %copy-start.9 = (f32[4,2,16,256]{3,2,1,0:T(8,128)S(1)}, f32[4,2,16,256]{3,2,1,0:T(8,128)}, u32[]{:S(2)}) copy-start(f32[4,2,16,256]{3,2,1,0:T(8,128)} %get-tuple-element.61) | copy-start | bytes 393220
  29.0 31.4 %copy-start.1 = (f32[4,2,16,256]{3,2,1,0:T(8,128)S(1)}, f32[4,2,16,256]{3,2,1,0:T(8,128)}, u32[]{:S(2)}) copy-start(f32[4,2,16,256]{3,2,1,0:T(8,128)} %get-tuple-element.66.refs_0_) | copy-start | bytes 393220
  29.9 30.5 %collective-permute-start.5 = (f32[4,2,16,256]{3,2,1,0:T(8,128)S(1)}, f32[4,2,16,256]{3,2,1,0:T(8,128)S(1)}, u32[]{:S(2)}, u32[]{:S(2)}) collective-permute-start(f32[4,2,16,256]{3,2,1,0:T(8,128)S(1)} %copy-done.10), channel_id=1, source_target_pairs={{0,24},{4,28},{8,16},{12,20},{16,8},{20,12},{24,0},{28,4},{1,25},{... | collective-permute-start | bytes 393224 | tf_op jit(solution)/shard_map/ppermute | solution.py:676
  41.8 18.6 %collective-permute-start.6 = (f32[4,2,16,256]{3,2,1,0:T(8,128)S(1)}, f32[4,2,16,256]{3,2,1,0:T(8,128)S(1)}, u32[]{:S(2)}, u32[]{:S(2)}) collective-permute-start(f32[4,2,16,256]{3,2,1,0:T(8,128)S(1)} %copy-done.9), channel_id=1, source_target_pairs={{0,28},{4,24},{8,20},{12,16},{16,12},{20,8},{24,4},{28,0},{1,29},{... | collective-permute-start | bytes 393224 | tf_op jit(solution)/shard_map/ppermute | solution.py:676
  62.3 13.0 %collective-permute-start.7 = (f32[8,2,16,256]{3,2,1,0:T(8,128)S(1)}, f32[8,2,16,256]{3,2,1,0:T(8,128)S(1)}, u32[]{:S(2)}, u32[]{:S(2)}) collective-permute-start(f32[8,2,16,256]{3,2,1,0:T(8,128)S(1)} %get-tuple-element.75), channel_id=1, source_target_pairs={{0,1},{1,0},{2,3},{3,2},{4,5},{5,4},{6,7},{7,6},{8,9},{9,8},{10,11... | collective-permute-start | bytes 786440 | tf_op jit(solution)/shard_map/ppermute | solution.py:676
  75.3 33.8 %collective-permute-start.8 = (f32[8,2,16,256]{3,2,1,0:T(8,128)S(1)}, f32[8,2,16,256]{3,2,1,0:T(8,128)S(1)}, u32[]{:S(2)}, u32[]{:S(2)}) collective-permute-start(f32[8,2,16,256]{3,2,1,0:T(8,128)S(1)} %get-tuple-element.79), channel_id=1, source_target_pairs={{0,2},{1,3},{2,0},{3,1},{4,6},{5,7},{6,4},{7,5},{8,10},{9,11},{10,... | collective-permute-start | bytes 786440 | tf_op jit(solution)/shard_map/ppermute | solution.py:676
  77.8 31.2 %collective-permute-start.9 = (f32[8,2,16,256]{3,2,1,0:T(8,128)S(1)}, f32[8,2,16,256]{3,2,1,0:T(8,128)S(1)}, u32[]{:S(2)}, u32[]{:S(2)}) collective-permute-start(f32[8,2,16,256]{3,2,1,0:T(8,128)S(1)} %get-tuple-element.80), channel_id=1, source_target_pairs={{0,3},{1,2},{2,1},{3,0},{4,7},{5,6},{6,5},{7,4},{8,11},{9,10},{10,... | collective-permute-start | bytes 786440 | tf_op jit(solution)/shard_map/ppermute | solution.py:676
  107.7 3.1 %collective-permute-start.10 = (f32[8,2,2,1,256]{4,3,2,1,0:T(1,128)S(1)}, f32[8,2,2,1,256]{4,3,2,1,0:T(1,128)S(1)}, u32[]{:S(2)}, u32[]{:S(2)}) collective-permute-start(f32[8,2,2,1,256]{4,3,2,1,0:T(1,128)S(1)} %slice.4), channel_id=1, source_target_pairs={{4,0},{8,4},{12,8},{16,12},{20,16},{24,20},{28,24},{1,28},{5,1},{9... | collective-permute-start | bytes 98312 | tf_op jit(solution)/shard_map/ppermute | solution.py:758
